TPU v7x, 32 devices: a whole 2x2x4 slice. The times are simulated.
32 devices in a mesh: ctx: 8 (over z, x), hx: 4 (over y, core).
Axes of the slice: x: 2, y: 2, z: 4, core: 2. Of those that a mesh axis runs over, the one named last changes fastest.
Arguments:
- query_latent: bfloat16 [16, 128, 512], P(None, 'hx'), may hold values from -2 to 2
- query_rope: bfloat16 [16, 8192], P(None, 'hx'), may hold values from -80 to 80
- cache_latent: bfloat16 [4, 16384, 512], P(None, ('ctx', 'hx')), may hold values from -16 to 16
- cache_rope: bfloat16 [4, 64, 16384], P(None, None, ('ctx', 'hx')), may hold values from -8 to 8
- suffix_latent: bfloat16 [16, 4096, 512], P(None, ('ctx', 'hx')), may hold values from -16 to 16
- suffix_rope: bfloat16 [16, 64, 4096], P(None, None, ('ctx', 'hx')), may hold values from -6 to 6
- lengths: int32 [4], replicated, may hold values from 4096 to 16384, as said below
- parents: int32 [16], replicated, may hold values from 0 to 15, as said below
- w_uv: bfloat16 [512, 16384], P(None, ('ctx', 'hx')), may hold values from -1.25 to 1.25
- w_o: bfloat16 [16384, 7168], P(('ctx', 'hx')), may hold values from -0.046875 to 0.046875
- hidden: bfloat16 [16, 7168], replicated, may hold values from -6 to 6
- norm_gain: float32 [7168], replicated, may hold values from 0.1 to 1.9
- w_gate: bfloat16 [32768, 7168], P(('ctx', 'hx')), may hold values from -0.0625 to 0.0625
- w_up: bfloat16 [32768, 7168], P(('ctx', 'hx')), may hold values from -0.0625 to 0.0625
- w_down: bfloat16 [32768, 7168], P(('ctx', 'hx')), may hold values from -0.25 to 0.25
- expert_ids: int32 [16, 8], replicated, may hold values from 0 to 15, all different within a row
- gate_weights: float32 [16, 8], replicated, may hold values from 0.1 to 0.6
Outputs:
- attended: bfloat16 [16, 7168], replicated
- updated: bfloat16 [16, 7168], P(None, ('ctx', 'hx'))
Inputs may be any that keep to these rules, and one draw needn't show every extreme that they name: `lengths`: one request has length 16384 and another 16384 // 4. parents[b] is a hypothesis of the same request as b. `expert_ids`: each row names 8 different experts.
All inputs are finite; a program needn't handle non-finite values.
Results may differ from a plain program's by a relative error of at most 0.012.
Values may be sent and summed in bfloat16 or wider, within the bound.
No kernel may reach another device: no remote copies, remote signals or barrier semaphores. Data moves between devices by JAX's collectives and lax.ppermute only.
A program may use at most 128 MiB of HBM per device.

v0:
```python
from functools import partial
import math

import jax
import jax.numpy as jnp
from jax import lax
from jax.sharding import PartitionSpec as P

DL = 512
DR = 64
DN = 128
DV = 128
EFF = 2048
REQ = 4
BEAMS = 4
HYPS = 16


MSCALE = 1.0 + 0.1 * math.log(40.0)
NEG = -1e30


def merged(value, axis, join):
    pieces = jax.tree.map(lambda part: lax.all_gather(part, axis), value)
    head = jax.tree.map(lambda part: part[0], pieces)
    tail = jax.tree.map(lambda part: part[1:], pieces)
    subtotal, _ = lax.scan(lambda subtotal, section: (join(subtotal, section), None), head, tail)
    return subtotal


def merge_pair(first_set, second_set):
    max_a, sum_a, acc_a = first_set
    max_b, sum_b, acc_b = second_set
    new_max = jnp.maximum(max_a, max_b)
    factor_a = jnp.exp(max_a - new_max)
    factor_b = jnp.exp(max_b - new_max)
    return (
        new_max,
        sum_a * factor_a + sum_b * factor_b,
        acc_a * factor_a[..., None] + acc_b * factor_b[..., None],
    )


def request_stats(
    q_lat, q_rope, pre_lat, pre_rope, suf_lat, suf_rope, is_live, softmax_scale, with_prefix
):
    suf_scores = jnp.einsum("bhl,bsl->bhs", q_lat, suf_lat, preferred_element_type=jnp.float32)
    suf_scores = (
        suf_scores
        + jnp.einsum("bhr,brs->bhs", q_rope, suf_rope, preferred_element_type=jnp.float32)
    ) * softmax_scale
    row_max = jnp.max(suf_scores, axis=2)
    beam_count, head_count, lat_width = q_lat.shape
    flat_lat = q_lat.reshape(beam_count * head_count, lat_width)
    flat_rope = q_rope.reshape(beam_count * head_count, q_rope.shape[2])
    pre_scores = lax.dot_general(
        flat_lat, pre_lat, (((1,), (1,)), ((), ())), preferred_element_type=jnp.float32
    )
    pre_scores = pre_scores + jnp.dot(flat_rope, pre_rope, preferred_element_type=jnp.float32)
    pre_scores = jnp.where(is_live[None, :], pre_scores * softmax_scale, NEG).reshape(
        beam_count, head_count, -1
    )
    row_max = jnp.maximum(row_max, jnp.max(pre_scores, axis=2))
    suf_weights = jnp.exp(suf_scores - row_max[..., None]).astype(jnp.bfloat16)
    weight_sum = jnp.sum(suf_weights.astype(jnp.float32), axis=2)
    weighted = jnp.einsum("bhs,bsl->bhl", suf_weights, suf_lat, preferred_element_type=jnp.float32)
    pre_weights = jnp.exp(pre_scores - row_max[..., None]).astype(jnp.bfloat16)
    weight_sum = weight_sum + jnp.sum(pre_weights.astype(jnp.float32), axis=2)
    prefix_part = jnp.dot(
        pre_weights.reshape(beam_count * head_count, -1),
        pre_lat,
        preferred_element_type=jnp.float32,
    )
    weighted = weighted + prefix_part.reshape(beam_count, head_count, lat_width)
    return (row_max, weight_sum, weighted)


def local(
    query_latent,
    query_rope,
    cache_latent,
    cache_rope,
    suffix_latent,
    suffix_rope,
    lengths,
    parents,
    w_uv,
    w_o,
    hidden,
    norm_gain,
    w_gate,
    w_up,
    w_down,
    expert_ids,
    gate_weights,
):
    q_lat, q_rope = (
        lax.all_gather(query_latent, "hx", axis=1, tiled=True),
        lax.all_gather(query_rope, "hx", axis=1, tiled=True),
    )
    head_count = q_lat.shape[1]
    q_rope = q_rope.reshape(HYPS, head_count, DR)
    softmax_scale = MSCALE * MSCALE / math.sqrt(DN + DR)
    n_hx = lax.axis_size("hx")
    linear = lax.axis_index("ctx") * n_hx + lax.axis_index("hx")
    ctx_block = cache_latent.shape[1]
    offsets = linear * ctx_block + jnp.arange(ctx_block, dtype=jnp.int32)
    suf_lat = jnp.take(suffix_latent, parents, axis=0)
    suf_rope = jnp.take(suffix_rope, parents, axis=0)
    maxima = []
    totals_list = []
    sums_list = []
    for request in range(REQ):
        hyp_rows = slice(request * BEAMS, (request + 1) * BEAMS)
        is_live = offsets < lengths[request]
        bound_stats = partial(
            request_stats,
            q_lat[hyp_rows],
            q_rope[hyp_rows],
            cache_latent[request],
            cache_rope[request],
            suf_lat[hyp_rows],
            suf_rope[hyp_rows],
            is_live,
            softmax_scale,
        )
        request_sums = bound_stats(True)
        maxima.append(request_sums[0])
        totals_list.append(request_sums[1])
        sums_list.append(request_sums[2])
    row_max = jnp.concatenate(maxima, axis=0)
    weight_sum = jnp.concatenate(totals_list, axis=0)
    weighted = jnp.concatenate(sums_list, axis=0)
    part_max, part_sum, part_acc = (
        lax.all_to_all(row_max[None], "ctx", split_axis=2, concat_axis=0, tiled=True),
        lax.all_to_all(weight_sum[None], "ctx", split_axis=2, concat_axis=0, tiled=True),
        lax.all_to_all(weighted[None], "ctx", split_axis=2, concat_axis=0, tiled=True),
    )
    group_max = jnp.max(part_max, axis=0)
    factor = jnp.exp(part_max - group_max[None])
    group_sum = jnp.sum(part_sum * factor, axis=0)
    group_acc = jnp.sum(part_acc * factor[..., None], axis=0)
    group_max, group_sum, group_acc = merged((group_max, group_sum, group_acc), "hx", merge_pair)
    attention = (group_acc / group_sum[..., None]).astype(jnp.bfloat16)
    columns = w_uv.shape[1]
    head_span = max(1, columns // DV)
    first_head = lax.axis_index("hx") * columns // DV
    chosen = lax.dynamic_slice_in_dim(attention, first_head, head_span, 1)
    value_map = w_uv.reshape(DL, head_span, columns // head_span)
    values = jnp.einsum("bnl,lnc->bnc", chosen, value_map, preferred_element_type=jnp.float32)
    values = values.astype(jnp.bfloat16).reshape(HYPS, columns)
    partial_out = jnp.dot(values, w_o, preferred_element_type=jnp.float32)
    attended = lax.psum(partial_out, ("ctx", "hx")).astype(jnp.bfloat16)
    residual = hidden.astype(jnp.float32) + attended.astype(jnp.float32)
    mean_square = jnp.mean(residual * residual, axis=1, keepdims=True)
    normed = (residual * lax.rsqrt(mean_square + 1e-06) * norm_gain).astype(jnp.bfloat16)
    unit_count = w_gate.shape[0]
    expert_here = linear * unit_count // EFF
    routed = jnp.sum(gate_weights * (expert_ids == expert_here).astype(jnp.float32), axis=1)
    gate_out = lax.dot_general(
        normed, w_gate, (((1,), (1,)), ((), ())), preferred_element_type=jnp.float32
    )
    up_out = lax.dot_general(
        normed, w_up, (((1,), (1,)), ((), ())), preferred_element_type=jnp.float32
    )
    activated = (jax.nn.silu(gate_out) * up_out * routed[:, None]).astype(jnp.bfloat16)
    expert_terms = jnp.dot(activated, w_down, preferred_element_type=jnp.float32)
    moe_share = lax.psum_scatter(expert_terms, ("ctx", "hx"), scatter_dimension=1, tiled=True)
    share_width = moe_share.shape[1]
    residual_share = lax.dynamic_slice_in_dim(residual, linear * share_width, share_width, 1)
    updated = (residual_share + moe_share).astype(jnp.bfloat16)
    return (attended, updated)


def solution(mesh):
    in_specs = (
        P(None, "hx", None),
        P(None, "hx"),
        P(None, ("ctx", "hx"), None),
        P(None, None, ("ctx", "hx")),
        P(None, ("ctx", "hx"), None),
        P(None, None, ("ctx", "hx")),
        P(),
        P(),
        P(None, ("ctx", "hx")),
        P(("ctx", "hx"), None),
        P(),
        P(),
        P(("ctx", "hx"), None),
        P(("ctx", "hx"), None),
        P(("ctx", "hx"), None),
        P(),
        P(),
    )
    out_specs = (P(), P(None, ("ctx", "hx")))
    return jax.shard_map(local, mesh=mesh, in_specs=in_specs, out_specs=out_specs, check_vma=False)
```

profile of v0, /device:TPU:0, one launch (start us, length us, event | category | flops | bytes accessed | tf_op | source)
XLA Modules:
  0.0 433.4 jit_solution(3394055854471211100)
XLA Ops:
  7.2 0.7 all-gather.6.cloned.1.call-update
  7.9 7.4 %all_gather.25 = bf16[16,8192]{1,0:T(8,128)(2,1)S(1)} all-gather(bf16[16,2048]{1,0:T(8,128)(2,1)} %param.20), channel_id=1, replica_groups=mesh['ctx'=8,'hx'=4] {'hx'}, dimensions={1}, use_global_device_ids=true | all-gather | bytes 327680 | tf_op jit(solution)/shard_map/all_gather | solution.py:99
  16.2 0.8 reshape.163
  17.0 0.8 slice.134
  18.0 0.8 slice.126
  19.4 2.0 gather_fusion
  22.1 1.7 fusion.75
  23.8 1.8 fusion.73
  25.6 1.9 broadcast_select_fusion
  27.5 7.4 %all-gather.6.cloned.1.call-done = bf16[16,128,512]{2,1,0:T(8,128)(2,1)} async-done(((bf16[16,32,512]{2,1,0:T(8,128)(2,1)}), bf16[16,128,512]{2,1,0:T(8,128)(2,1)}) %all-gather.6.cloned.1.call-update) | async-done | bytes 2097168 | tf_op jit(solution)/shard_map/all_gather | solution.py:98
  34.9 1.8 fusion.89
  37.6 0.8 copy-done.2
  39.1 1.3 fusion.93
  41.5 1.3 fusion.99
  43.9 1.3 fusion.24
  46.4 1.3 fusion.95
  49.0 1.3 fusion.26
  51.5 1.3 fusion.97
  52.8 1.4 fusion.28
  54.9 0.7 reduce.9
  55.6 0.7 reshape.204
  56.3 5.5 %all-to-all-start = ((f32[8,1,256]{2,1,0:T(1,128)}), f32[8,1,256]{2,1,0:T(1,128)S(1)}, u32[]{:S(2)}, u32[]{:S(2)}) async-start(f32[8,1,256]{2,1,0:T(1,128)} %reshape.204), calls=%async_computation | async-start | bytes 16384 | tf_op jit(solution)/shard_map/all_to_all | solution.py:135
  61.8 1.5 convert_reduce_fusion
  63.4 1.6 convert_reduce_fusion.3
  65.0 1.5 convolution_add_fusion.3
  66.5 1.4 convolution_add_fusion
  68.5 1.4 convolution_add_fusion.1
  70.2 1.4 convolution_add_fusion.2
  71.8 0.7 reduce.11
  72.5 0.7 reshape.206
  73.2 6.0 %all-to-all-start.1 = ((f32[8,1,256]{2,1,0:T(1,128)}), f32[8,1,256]{2,1,0:T(1,128)S(1)}, u32[]{:S(2)}, u32[]{:S(2)}) async-start(f32[8,1,256]{2,1,0:T(1,128)} %reshape.206), calls=%async_computation.1 | async-start | bytes 16384 | tf_op jit(solution)/shard_map/all_to_all | solution.py:136
  79.2 2.5 maximum_bitcast_fusion
  81.7 4.4 %copy.124 = f32[1,16,128,512]{3,1,0,2:T(8,128)} copy(f32[1,16,128,512]{3,2,1,0:T(8,128)S(1)} %maximum_bitcast_fusion) | data formatting | bytes 8388608 | tf_op jit(solution)/shard_map/broadcast_in_dim | solution.py:137
  86.1 6.0 %all-to-all-start.2 = ((f32[1,16,128,512]{3,1,0,2:T(8,128)}), f32[1,16,128,512]{3,1,0,2:T(8,128)}, u32[]{:S(2)}, u32[]{:S(2)}) async-start(f32[1,16,128,512]{3,1,0,2:T(8,128)} %copy.124), calls=%async_computation.2 | async-start | bytes 8388608 | tf_op jit(solution)/shard_map/all_to_all | solution.py:137
  93.7 90.9 %all-to-all-done.2 = f32[1,16,128,512]{3,1,0,2:T(8,128)} async-done(((f32[1,16,128,512]{3,1,0,2:T(8,128)}), f32[1,16,128,512]{3,1,0,2:T(8,128)}, u32[]{:S(2)}, u32[]{:S(2)}) %all-to-all-start.2) | async-done | bytes 4194336 | tf_op jit(solution)/shard_map/all_to_all | solution.py:137
  184.7 2.6 multiply_reduce_fusion
  187.2 1.1 copy.125
  188.6 5.2 %all-gather = f32[64,16]{1,0:T(8,128)S(1)} all-gather(f32[16,16]{1,0:T(8,128)S(1)} %copy.117), channel_id=2, replica_groups=mesh['ctx'=8,'hx'=4] {'hx'}, dimensions={0}, use_global_device_ids=true | all-gather | bytes 5120 | tf_op jit(solution)/shard_map/all_gather | solution.py:24
  193.8 5.2 %all-gather.1 = f32[64,16]{1,0:T(8,128)S(1)} all-gather(f32[16,16]{1,0:T(8,128)S(1)} %copy.119), channel_id=3, replica_groups=mesh['ctx'=8,'hx'=4] {'hx'}, dimensions={0}, use_global_device_ids=true | all-gather | bytes 5120 | tf_op jit(solution)/shard_map/all_gather | solution.py:24
  199.0 10.4 %all-gather.8.cloned.1.call-done = f32[64,16,512]{2,1,0:T(8,128)} async-done(((f32[16,16,512]{2,1,0:T(8,128)}), f32[64,16,512]{2,1,0:T(8,128)}) %all-gather.8.cloned.1.call-update) | async-done | bytes 2097168 | tf_op jit(solution)/shard_map/all_gather | solution.py:24
  209.4 1.2 slice.176
  212.3 4.2 fusion.70
  216.5 45.7 %all-reduce.1 = bf16[16,7168]{1,0:T(8,128)(2,1)S(1)} all-reduce(f32[16,7168]{1,0:T(8,128)S(1)} %fusion.70), channel_id=1, replica_groups=mesh['ctx'=8,'hx'=4] {'ctx','hx'}, use_global_device_ids=true, to_apply=%region_21.22 | all-reduce | flops 114688 | bytes 688128 | tf_op jit(solution)/shard_map/psum | solution.py:153
  262.5 9.1 %fusion.87 = f32[16,1024]{1,0:T(8,128)S(1)} fusion(bf16[1024,7168]{1,0:T(8,128)(2,1)} %param.31, f32[7168]{0:T(1024)S(1)} %copy-done.18, f32[16]{0:T(128)S(1)} %add_rsqrt_fusion, bf16[16,7168]{1,0:T(8,128)(2,1)S(1)} %all-reduce.1, bf16[16,7168]{1,0:T(8,128)(2,1)S(1)} %copy-done.12), kind=kOutput, calls=%fused_computation.156 | convolution fusion | flops 235569152 | bytes 15233088 | tf_op jit(solution)/shard_map/dot_general | solution.py:160
  271.5 15.4 %convolution_bitcast_fusion = f32[7168,16]{1,0:T(8,128)} fusion(bf16[1024,7168]{1,0:T(8,128)(2,1)} %param.33, bf16[1024,7168]{1,0:T(8,128)(2,1)} %param.32, f32[16,1024]{1,0:T(8,128)S(1)} %fusion.87, f32[16]{0:T(128)S(1)} %select_reduce_fusion, f32[7168]{0:T(1024)S(1)} %copy-done.18, f32[16]{0:T(128)S(1)} %add_rsqrt_fusion, ...), kind=kOutput, calls=%fused_computation.10 | convolution fusion | flops 470564864 | bytes 30371968
  286.9 138.3 %reduce-scatter.4.cloned.1.call-done = f32[224,16]{1,0:T(8,128)} async-done(((f32[7168,16]{1,0:T(8,128)}), f32[224,16]{1,0:T(8,128)}) %reduce-scatter.4.cloned.1.call-update) | async-done | bytes 14352
  425.2 1.0 copy.145
  426.2 0.7 add_convert_fusion
  (139 shorter events, 15.4 us)
Async XLA Ops:
  7.2 12.2 %copy-start = (bf16[16,128,512]{2,1,0:T(8,128)(2,1)S(1)}, bf16[16,128,512]{2,1,0:T(8,128)(2,1)}, u32[]{:S(2)}) copy-start(bf16[16,128,512]{2,1,0:T(8,128)(2,1)} %param.23) | copy-start | bytes 6291460
  7.2 11.6 %copy-start.28 = (s32[16]{0:T(128)S(1)}, s32[16]{0:T(128)}, u32[]{:S(2)}) copy-start(s32[16]{0:T(128)} %param.26) | copy-start | bytes 196
  7.2 11.6 %copy-start.17 = (bf16[16,64,128]{2,1,0:T(8,128)(2,1)S(1)}, bf16[16,64,128]{2,1,0:T(8,128)(2,1)}, u32[]{:S(2)}) copy-start(bf16[16,64,128]{2,1,0:T(8,128)(2,1)} %param.24) | copy-start | bytes 786436
  7.2 27.7 %all-gather.6.cloned.1.call-start = ((), (), s32[]{:S(2)}) async-start(), calls=%async_computation.4 | async-start | bytes 2621440 | tf_op jit(solution)/shard_map/all_gather | solution.py:98
  19.4 2.0 copy-start.22
  34.9 2.2 copy-start.3
  36.7 1.7 copy-start.2
  37.1 1.9 copy-start.16
  45.2 0.9 copy-start.15
  45.2 1.2 copy-start.14
  45.2 1.2 copy-start.26
  50.3 0.9 copy-start.13
  50.3 1.2 copy-start.25
  52.8 10.5 %copy-start.21 = (f32[4,128]{1,0:T(4,128)S(1)}, f32[4,128]{1,0:T(4,128)}, u32[]{:S(2)}) copy-start(f32[4,128]{1,0:T(4,128)} %convert_reduce_fusion.4) | copy-start | bytes 6148
  54.2 10.8 %copy-start.4 = (bf16[4,512,512]{2,1,0:T(8,128)(2,1)S(1)}, bf16[4,512,512]{2,1,0:T(8,128)(2,1)}, u32[]{:S(2)}) copy-start(bf16[4,512,512]{2,1,0:T(8,128)(2,1)} %param.21) | copy-start | bytes 6291460
  56.3 16.9 %all-to-all-start = ((f32[8,1,256]{2,1,0:T(1,128)}), f32[8,1,256]{2,1,0:T(1,128)S(1)}, u32[]{:S(2)}, u32[]{:S(2)}) async-start(f32[8,1,256]{2,1,0:T(1,128)} %reshape.204), calls=%async_computation | async-start | bytes 16384 | tf_op jit(solution)/shard_map/all_to_all | solution.py:135
  63.4 3.1 copy-start.5
  66.5 1.4 copy-start.8
  66.5 1.4 copy-start.19
  66.5 1.8 copy-start.20
  66.5 1.9 copy-start.6
  68.0 1.9 copy-start.9
  68.5 1.8 copy-start.7
  70.2 9.0 %copy-start.10 = (f32[4,128,512]{2,1,0:T(8,128)S(1)}, f32[4,128,512]{2,1,0:T(8,128)}, u32[]{:S(2)}) copy-start(f32[4,128,512]{2,1,0:T(8,128)} %convolution_add_fusion.3) | copy-start | bytes 3145732
  73.2 12.9 %all-to-all-start.1 = ((f32[8,1,256]{2,1,0:T(1,128)}), f32[8,1,256]{2,1,0:T(1,128)S(1)}, u32[]{:S(2)}, u32[]{:S(2)}) async-start(f32[8,1,256]{2,1,0:T(1,128)} %reshape.206), calls=%async_computation.1 | async-start | bytes 16384 | tf_op jit(solution)/shard_map/all_to_all | solution.py:136
  86.1 98.5 %all-to-all-start.2 = ((f32[1,16,128,512]{3,1,0,2:T(8,128)}), f32[1,16,128,512]{3,1,0,2:T(8,128)}, u32[]{:S(2)}, u32[]{:S(2)}) async-start(f32[1,16,128,512]{3,1,0,2:T(8,128)} %copy.124), calls=%async_computation.2 | async-start | bytes 8388608 | tf_op jit(solution)/shard_map/all_to_all | solution.py:137
  92.1 117.3 %all-gather.8.cloned.1.call-start = ((), (), s32[]{:S(2)}) async-start(), calls=%async_computation.5 | async-start | bytes 2621440 | tf_op jit(solution)/shard_map/all_gather | solution.py:24
  184.7 3.8 copy-start.23
  184.7 3.8 copy-start.24
  188.4 236.8 %reduce-scatter.4.cloned.1.call-start = ((), (), s32[]{:S(2)}) async-start(), calls=%async_computation.6 | async-start | bytes 3784704
  209.4 1.6 slice-start
  211.0 1.1 copy-start.27
  212.3 50.0 %copy-start.12 = (bf16[16,7168]{1,0:T(8,128)(2,1)S(1)}, bf16[16,7168]{1,0:T(8,128)(2,1)}, u32[]{:S(2)}) copy-start(bf16[16,7168]{1,0:T(8,128)(2,1)} %param.29) | copy-start | bytes 688132
  212.3 50.2 %copy-start.18 = (f32[7168]{0:T(1024)S(1)}, f32[7168]{0:T(1024)}, u32[]{:S(2)}) copy-start(f32[7168]{0:T(1024)} %param.30) | copy-start | bytes 86020
  262.2 9.3 %copy-start.11 = (bf16[16,7168]{1,0:T(8,128)(2,1)}, bf16[16,7168]{1,0:T(8,128)(2,1)S(1)}, u32[]{:S(2)}) copy-start(bf16[16,7168]{1,0:T(8,128)(2,1)S(1)} %all-reduce.1) | copy-start | bytes 688132
  271.5 155.3 %copy-start.1 = (bf16[16,128,512]{2,1,0:T(8,128)(2,1)S(1)}, bf16[16,128,512]{2,1,0:T(8,128)(2,1)}, u32[]{:S(2)}) copy-start(bf16[16,128,512]{2,1,0:T(8,128)(2,1)} %param.23) | copy-start | bytes 6291460
Sparse Core Ops, SparseCore 0:
  9.6 25.2 all-gather.5
  188.5 20.8 all-gather.7
  287.0 138.1 reduce-scatter.3
where the time goes:
time: 434 us; the launch traced here: 433 us
  waiting for transfers between devices  248 us (57%)
  blocking collectives  63.6 us (15%)
  matrix products  48.5 us (11%)
  local copies, waits for them, and re-layouts  21.1 us (5%)
  other arithmetic  20.5 us (5%)
  starting transfers between devices  17.6 us (4%)
  between operations  14.3 us (3%)
    unnamed x4, waiting for transfers between devices  139 us
    all_to_all x1, waiting for transfers between devices, local(): lax.all_to_all(weighted[None], 'ctx', split_axis=2, concat_axis=0, tiled=...  90.9 us
    psum x1, blocking collectives, local(): attended = lax.psum(partial_out, ('ctx', 'hx')).astype(jnp.bfloat16)  45.7 us
    unnamed x1, matrix products  15.4 us
    all_gather x1, waiting for transfers between devices, merged(): pieces = jax.tree.map(lambda part: lax.all_gather(part, axis), value)  10.4 us
    all_gather x2, blocking collectives, merged(): pieces = jax.tree.map(lambda part: lax.all_gather(part, axis), value)  10.4 us
    dot_general x1, matrix products, local(): lax.dot_general(normed, w_gate, (((1,), (1,)), ((), ())), preferred_eleme...  9.05 us
  transfers between devices with their start and end apart: 6, of which 4 were waited for; matrix products, arithmetic and copies ran while one was open for 7% of the time, Pallas kernels for 0%

commit v1 on v0

--- a/solution.py
+++ b/solution.py
@@ -4,6 +4,8 @@
 import jax
 import jax.numpy as jnp
 from jax import lax
+from jax.experimental import pallas as pl
+from jax.experimental.pallas import tpu as pltpu
 from jax.sharding import PartitionSpec as P
 
 DL = 512
@@ -75,7 +77,7 @@
     return (row_max, weight_sum, weighted)
 
 
-def local(
+def general_local(
     query_latent,
     query_rope,
     cache_latent,
@@ -172,25 +174,498 @@
     return (attended, updated)
 
 
+BF = jnp.bfloat16
+F32 = jnp.float32
+AXES = ("z", "x", "y", "core")
+SHAPE = (4, 2, 2, 2)
+HEADS_DEV = 4
+UNITS = 256
+STAT = 16
+LANES = 128
+LENGTHS = 2
+PARENTS = LENGTHS + REQ
+VMEM = pl.BlockSpec(memory_space=pltpu.VMEM)
+SMEM = pl.BlockSpec(memory_space=pltpu.SMEM)
+HBM = pl.BlockSpec(memory_space=pltpu.HBM)
+ANY = pl.BlockSpec(memory_space=pl.ANY)
+NT = (((1,), (1,)), ((), ()))
+
+
+def swap(value, mask, count):
+    return lax.ppermute(value, AXES, [(i, i ^ mask) for i in range(count)])
+
+
+def swaps(values, masks, count):
+    return [swap(value, mask, count) for value, mask in zip(values, masks)]
+
+
+def in_hbm(value):
+    return pltpu.with_memory_space_constraint(value, pltpu.HBM)
+
+
+def column(lane_row):
+    n = lane_row.shape[1]
+    at = lax.broadcasted_iota(jnp.int32, (n, n), 0)
+    to = lax.broadcasted_iota(jnp.int32, (n, n), 1)
+    return jnp.sum(jnp.where(at == to, lane_row, 0.0), axis=1, keepdims=True)
+
+
+def write_stat(stat, row, lse):
+    k, n = lse.shape
+    for i in range(3):
+        part = lse.astype(BF).astype(F32)
+        stat[row:row + k, i * LANES:i * LANES + n] = part
+        lse = lse - part
+
+
+def read_stat(block, n):
+    block = block.astype(F32)
+    return (block[:REQ, :n] + block[:REQ, LANES:LANES + n]) + block[:REQ, 2 * LANES:2 * LANES + n]
+
+
+def joined(lses):
+    top = lses[0]
+    for lse in lses[1:]:
+        top = jnp.maximum(top, lse)
+    weights = [jnp.exp(lse - top) for lse in lses]
+    total = sum(weights[1:], weights[0])
+    return [w / total for w in weights], top + jnp.log(total)
+
+
+def attend_kernel(scale, fetch, info, ql0, ql1, qr0, qr1, cl_hbm, cr_hbm, sl_hbm, sr_hbm,
+                  keep, send, spread, qbuf, rbuf, pbuf, stat, cl, cr, sl, sr, own_q, sems):
+    linear = info[0]
+    core, y, x, z0 = (info[0] >> k & 1 for k in range(4))
+    heads = ql1.shape[1]
+    rows = 2 * heads
+    total_rows = BEAMS * rows
+    half = total_rows // 2
+    targets = keep.shape[0]
+    block = half // targets
+    copies = []
+    for r in range(REQ):
+        beams = pl.ds(r * BEAMS, BEAMS)
+        group = [
+            pltpu.make_async_copy(cl_hbm.at[r], cl.at[r], sems.at[0, r]),
+            pltpu.make_async_copy(cr_hbm.at[r], cr.at[r], sems.at[1, r]),
+            pltpu.make_async_copy(sl_hbm.at[beams], sl.at[beams], sems.at[2, r]),
+            pltpu.make_async_copy(sr_hbm.at[beams], sr.at[beams], sems.at[3, r]),
+        ]
+        if fetch:
+            group.append(pltpu.make_async_copy(ql0.at[beams], own_q.at[beams], sems.at[4, r]))
+        for copy in group:
+            copy.start()
+        copies.append(group)
+    first_q = own_q if fetch else ql0
+
+    out_row = lax.broadcasted_iota(jnp.int32, (total_rows, total_rows), 0)
+    in_row = lax.broadcasted_iota(jnp.int32, (total_rows, total_rows), 1)
+
+    def source_of(row):
+        bit = lambda k: (row >> k) & 1
+        beam, head = (row >> 2) & 3, row & 3
+        target = (bit(6) ^ x) * 4 + (bit(5) ^ y) * 2 + (bit(7) ^ core)
+        return beam * rows + (bit(4) ^ core ^ z0) * heads + target * HEADS_DEV + head
+
+    spread[...] = jnp.where(source_of(out_row) == in_row, 1.0, 0.0).astype(BF)
+    moves = source_of(in_row) == out_row
+    stat[...] = jnp.zeros_like(stat)
+
+    for r in range(REQ):
+        for copy in copies[r]:
+            copy.wait()
+        for j in range(BEAMS):
+            b = r * BEAMS + j
+            qbuf[j * rows:j * rows + heads] = first_q[b]
+            qbuf[j * rows + heads:(j + 1) * rows] = ql1[b]
+            rbuf[j * rows:j * rows + heads] = qr0[b]
+            rbuf[j * rows + heads:(j + 1) * rows] = qr1[b]
+        keys = cl[r]
+        ctx_block = keys.shape[0]
+        pre = lax.dot_general(qbuf[...], keys, NT, preferred_element_type=F32)
+        pre = pre + jnp.dot(rbuf[...], cr[r], preferred_element_type=F32)
+        position = linear * ctx_block + lax.broadcasted_iota(jnp.int32, (1, ctx_block), 1)
+        pre = jnp.where(position < info[LENGTHS + r], pre * scale, NEG)
+        own = [info[PARENTS + r * BEAMS + j] for j in range(BEAMS)]
+        suf = []
+        for j in range(BEAMS):
+            part = slice(j * rows, (j + 1) * rows)
+            s = lax.dot_general(qbuf[part], sl[own[j]], NT, preferred_element_type=F32)
+            s = s + jnp.dot(rbuf[part], sr[own[j]], preferred_element_type=F32)
+            suf.append(s * scale)
+        suf = jnp.concatenate(suf, axis=0)
+        top = jnp.maximum(jnp.max(pre, axis=1, keepdims=True), jnp.max(suf, axis=1, keepdims=True))
+        pre_w = jnp.exp(pre - top).astype(BF)
+        suf_w = jnp.exp(suf - top).astype(BF)
+        total = jnp.sum(pre_w.astype(F32), axis=1, keepdims=True)
+        total = total + jnp.sum(suf_w.astype(F32), axis=1, keepdims=True)
+        acc = jnp.dot(pre_w, keys, preferred_element_type=F32)
+        inv = 1.0 / total
+        for j in range(BEAMS):
+            part = slice(j * rows, (j + 1) * rows)
+            a = acc[part] + jnp.dot(suf_w[part], sl[own[j]], preferred_element_type=F32)
+            pbuf[part] = (a * inv[part]).astype(BF)
+        moved = jnp.dot(spread[...], pbuf[...], preferred_element_type=F32).astype(BF)
+        lse = top + jnp.log(total)
+        lane_lse = jnp.sum(jnp.where(moves, lse, 0.0), axis=0, keepdims=True)
+        for t in range(targets):
+            for i, out in enumerate((keep, send)):
+                at = i * half + t * block
+                out[t, r * block:(r + 1) * block] = moved[at:at + block]
+                write_stat(stat.at[i * targets + t], r, lane_lse[:, at:at + block])
+    for t in range(targets):
+        keep[t, REQ * block:] = stat[t].astype(BF)
+        send[t, REQ * block:] = stat[targets + t].astype(BF)
+
+
+def attend(scale, fetch, info, q_lat, q_rope, caches):
+    heads, width = q_lat[0].shape[1:]
+    rope = q_rope[0].shape[2]
+    total_rows = BEAMS * 2 * heads
+    targets = SHAPE[1] * SHAPE[2]
+    message = jax.ShapeDtypeStruct((targets, REQ * total_rows // (2 * targets) + STAT, width), BF)
+    keys = caches[0].shape[1] + caches[2].shape[1]
+    own_q = q_lat[0].shape if fetch else (8, LANES)
+    return pl.pallas_call(
+        partial(attend_kernel, scale, fetch),
+        in_specs=[SMEM, HBM if fetch else VMEM] + [VMEM] * 3 + [HBM] * 4,
+        out_specs=[VMEM] * 2,
+        out_shape=[message] * 2,
+        scratch_shapes=[
+            pltpu.VMEM((total_rows, total_rows), BF),
+            pltpu.VMEM((total_rows, width), BF),
+            pltpu.VMEM((total_rows, rope), BF),
+            pltpu.VMEM((total_rows, width), BF),
+            pltpu.VMEM((2 * targets, STAT, width), F32),
+        ] + [pltpu.VMEM(c.shape, BF) for c in caches]
+        + [pltpu.VMEM(own_q, BF), pltpu.SemaphoreType.DMA((5, REQ))],
+        compiler_params=pltpu.CompilerParams(vmem_limit_bytes=20 << 20),
+        cost_estimate=pl.CostEstimate(
+            flops=REQ * 2 * total_rows * keys * (2 * width + rope), bytes_accessed=8 << 20,
+            transcendentals=REQ * total_rows * keys),
+        name="attend",
+    )(info, in_hbm(q_lat[0]) if fetch else q_lat[0], q_lat[1], *q_rope, *(in_hbm(c) for c in caches))
+
+
+def pair_kernel(a, b, *rest):
+    outs, stat = rest[:-1], rest[-1]
+    targets, rows, _ = a.shape
+    body = rows - STAT
+    block = body // REQ
+    for t, out in enumerate(outs):
+        weights, lse = joined([read_stat(v[t, body:], block) for v in (a, b)])
+        for r in range(REQ):
+            part = slice(r * block, (r + 1) * block)
+            out[part] = (a[t, part].astype(F32) * column(weights[0][r:r + 1])
+                         + b[t, part].astype(F32) * column(weights[1][r:r + 1])).astype(BF)
+        stat[...] = jnp.zeros_like(stat)
+        write_stat(stat, 0, lse)
+        out[body:] = stat[...].astype(BF)
+
+
+def merge_pair_of(a, b):
+    targets = a.shape[0]
+    return pl.pallas_call(
+        pair_kernel,
+        in_specs=[VMEM] * 2,
+        out_specs=[VMEM] * targets,
+        out_shape=[jax.ShapeDtypeStruct(a.shape[1:], BF)] * targets,
+        scratch_shapes=[pltpu.VMEM((STAT, a.shape[2]), F32)],
+        compiler_params=pltpu.CompilerParams(vmem_limit_bytes=4 << 20),
+        cost_estimate=pl.CostEstimate(flops=4 * a.size, bytes_accessed=6 * a.size, transcendentals=0),
+        name="merge_pair",
+    )(a, b)
+
+
+def plane_kernel(count, info, *refs):
+    near, far = refs[:4], refs[4:8]
+    outs, (stat, held) = refs[8 + count:-2], refs[-2:]
+    body = near[0].shape[0] - STAT
+    block = body // REQ
+    small = block // 2
+    y, z1 = info[0] >> 1 & 1, info[0] >> 4 & 1
+    for other in range(2):
+        sources = [near[2 * x + other] for x in range(2)] + [far[2 * x + 1 - other] for x in range(2)]
+        weights, lse = joined([read_stat(ref[body:], block) for ref in sources])
+        for z0 in range(2):
+            for r in range(REQ):
+                part = slice(r * block + z0 * small, r * block + (z0 + 1) * small)
+                total = None
+                for ref, w in zip(sources, weights):
+                    term = ref[part].astype(F32) * column(w[r:r + 1, z0 * small:(z0 + 1) * small])
+                    total = term if total is None else total + term
+                held[2 * other + z0, r * small:(r + 1) * small] = total.astype(BF)
+            stat[...] = jnp.zeros_like(stat)
+            write_stat(stat, 0, lse[:, z0 * small:(z0 + 1) * small])
+            held[2 * other + z0, REQ * small:] = stat[...].astype(BF)
+    for d, out in enumerate(outs):
+        out[...] = held[2 * ((d >> 1) ^ y ^ z1) + (d & 1)]
+
+
+def merge_plane(info, near, far, needs):
+    rows, width = near[0].shape
+    shape = ((rows - STAT) // 2 + STAT, width)
+    return pl.pallas_call(
+        partial(plane_kernel, len(needs)),
+        in_specs=[SMEM] + [VMEM] * 8 + [ANY] * len(needs),
+        out_specs=[VMEM] * SHAPE[0],
+        out_shape=[jax.ShapeDtypeStruct(shape, BF)] * SHAPE[0],
+        scratch_shapes=[pltpu.VMEM((STAT, width), F32), pltpu.VMEM((SHAPE[0], *shape), BF)],
+        compiler_params=pltpu.CompilerParams(vmem_limit_bytes=4 << 20),
+        cost_estimate=pl.CostEstimate(flops=16 * rows * width, bytes_accessed=24 * rows * width, transcendentals=0),
+        name="merge_plane",
+    )(info, *near, *far, *needs)
+
+
+def sum_kernel(count, split, needs, dtype, *refs):
+    ins, outs = refs[:count], refs[count + needs:]
+    for t, out in enumerate(outs):
+        terms = [(ref[t] if split else ref[...]).astype(F32) for ref in ins]
+        while len(terms) > 1:
+            terms = [terms[i] + terms[i + 1] for i in range(0, len(terms) - 1, 2)] + terms[len(terms) & ~1:]
+        out[...] = terms[0].astype(dtype)
+
+
+def sums(arrays, split=False, needs=()):
+    count = len(arrays)
+    shape = arrays[0].shape
+    outs = shape[0] if split else 1
+    shape = shape[1:] if split else shape
+    return pl.pallas_call(
+        partial(sum_kernel, count, split, len(needs), BF),
+        in_specs=[VMEM] * count + [ANY] * len(needs),
+        out_specs=[VMEM] * outs,
+        out_shape=[jax.ShapeDtypeStruct(shape, BF)] * outs,
+        compiler_params=pltpu.CompilerParams(vmem_limit_bytes=4 << 20),
+        cost_estimate=pl.CostEstimate(flops=count * arrays[0].size, bytes_accessed=4 * count * arrays[0].size,
+                                      transcendentals=0),
+        name="sums",
+    )(*arrays, *needs)
+
+
+def load_kernel(count, parts, which, *refs):
+    sources, dests, sems = refs[:count], refs[count + 1:-1], refs[-1]
+    copies = []
+    for i in range(count):
+        rows = dests[i].shape[0]
+        copies.append(pltpu.make_async_copy(sources[i].at[pl.ds(which * rows, rows)], dests[i], sems.at[i]))
+    for copy in copies:
+        copy.start()
+    for copy in copies:
+        copy.wait()
+
+
+def load(after, *arrays, parts=1, which=0):
+    count = len(arrays)
+    return pl.pallas_call(
+        partial(load_kernel, count, parts, which),
+        in_specs=[HBM] * count + [ANY],
+        out_specs=[VMEM] * count,
+        out_shape=[pltpu.VMEM((a.shape[0] // parts, *a.shape[1:]), a.dtype) for a in arrays],
+        scratch_shapes=[pltpu.SemaphoreType.DMA((count,))],
+        compiler_params=pltpu.CompilerParams(vmem_limit_bytes=1 << 20),
+        cost_estimate=pl.CostEstimate(
+            flops=0, bytes_accessed=sum(2 * a.size for a in arrays) // parts, transcendentals=0),
+        name="load",
+    )(*(in_hbm(a) for a in arrays), after)
+
+
+def project_kernel(info, p0, p1, p2, p3, w_uv, w_o, *rest):
+    keep, send = rest[-2:]
+    parts = (p0, p1, p2, p3)
+    rows, _ = p0.shape
+    body = rows - STAT
+    block = body // REQ
+    weights, _ = joined([read_stat(p[body:], block) for p in parts])
+    sums = []
+    for r in range(REQ):
+        total = None
+        for p, w in zip(parts, weights):
+            term = p[r * block:(r + 1) * block].astype(F32) * column(w[r:r + 1])
+            total = term if total is None else total + term
+        sums.append(total)
+    attention = jnp.concatenate(sums, axis=0).astype(BF)
+    full = jnp.dot(attention, w_uv[...], preferred_element_type=F32)
+    rows, columns = full.shape
+    row = lax.broadcasted_iota(jnp.int32, (rows, columns), 0)
+    lane = lax.broadcasted_iota(jnp.int32, (rows, columns), 1)
+    own = jnp.where((row & (HEADS_DEV - 1)) == lane // DV, full, 0.0).astype(BF)
+    pick_hyp = lax.broadcasted_iota(jnp.int32, (HYPS, rows), 0)
+    pick_row = lax.broadcasted_iota(jnp.int32, (HYPS, rows), 1)
+    pick = jnp.where(pick_row // HEADS_DEV == pick_hyp, 1.0, 0.0).astype(BF)
+    values = jnp.dot(pick, own, preferred_element_type=F32).astype(BF)
+    width = keep.shape[2]
+    plane = info[0] & 7
+    for there, out in enumerate((keep, send)):
+        for t in range(out.shape[0]):
+            at = pl.multiple_of((plane ^ (2 * t + there)) * width, LANES)
+            piece = jnp.dot(values, w_o[:, pl.ds(at, width)], preferred_element_type=F32)
+            out[t] = piece.astype(BF)
+
+
+def project(info, parts, w_uv, w_o, needs):
+    squares = SHAPE[1] * SHAPE[2]
+    out = jax.ShapeDtypeStruct((squares, HYPS, w_o.shape[1] // (2 * squares)), BF)
+    return pl.pallas_call(
+        project_kernel,
+        in_specs=[SMEM] + [VMEM] * 6 + [ANY] * len(needs),
+        out_specs=[VMEM] * 2,
+        out_shape=[out] * 2,
+        compiler_params=pltpu.CompilerParams(vmem_limit_bytes=6 << 20),
+        cost_estimate=pl.CostEstimate(flops=2 * HYPS * w_o.size, bytes_accessed=2 * w_o.size, transcendentals=0),
+        name="project",
+    )(info, *parts, w_uv, w_o, *needs)
+
+
+def experts_kernel(info, *refs):
+    shares = refs[:8]
+    hidden, gain, ids, gates, w_gate, w_up = refs[8:14]
+    w_down, outs = refs[14:-8], refs[-8:]
+    attended, keep, send, residual, x_buf, acc, x_held, held = outs
+    linear = info[0]
+    plane, depth = linear & 7, linear >> 3
+    units = w_gate.shape[0]
+    share = shares[0].shape[1]
+    for d, ref in enumerate(shares):
+        at = pl.multiple_of((plane ^ d) * share, LANES)
+        x_buf[:, pl.ds(at, share)] = ref[...].astype(F32)
+        attended[:, pl.ds(at, share)] = ref[...]
+    x = x_buf[...] + hidden[...].astype(F32)
+    mean_square = jnp.mean(x * x, axis=1, keepdims=True)
+    normed = (x * lax.rsqrt(mean_square + 1e-06) * gain[...]).astype(BF)
+    routed = jnp.sum(jnp.where(ids[...] == info[1], gates[...], 0.0), axis=1, keepdims=True)
+    for k in range(units // UNITS):
+        part = slice(k * UNITS, (k + 1) * UNITS)
+        gate = lax.dot_general(normed, w_gate[part], NT, preferred_element_type=F32)
+        up = lax.dot_general(normed, w_up[part], NT, preferred_element_type=F32)
+        act = (gate / (1.0 + jnp.exp(-gate)) * up * routed).astype(BF)
+        piece, row = divmod(k * UNITS, w_down[0].shape[0])
+        term = jnp.dot(act, w_down[piece][row:row + UNITS], preferred_element_type=F32)
+        if k == 0:
+            acc[...] = term
+        else:
+            acc[...] += term
+    count, _, width = held.shape
+    for d in range(count):
+        x_held[d] = x[:, d * width:(d + 1) * width]
+        held[d] = acc[:, d * width:(d + 1) * width].astype(BF)
+    residual[...] = x_held[linear]
+    for there, out in enumerate((keep, send)):
+        for t in range(out.shape[0]):
+            for z in range(out.shape[1]):
+                out[t, z] = held[((depth ^ z) << 3) + (plane ^ (2 * t + there))]
+
+
+def experts(info, shares, hidden, gain, ids, gates, w_gate, w_up, *w_down):
+    units, width = w_gate.shape
+    squares = SHAPE[1] * SHAPE[2]
+    small = width // (2 * squares * SHAPE[0])
+    terms = jax.ShapeDtypeStruct((squares, SHAPE[0], HYPS, small), BF)
+    return pl.pallas_call(
+        experts_kernel,
+        in_specs=[SMEM] + [VMEM] * (14 + len(w_down)),
+        out_specs=[VMEM] * 4,
+        out_shape=[
+            jax.ShapeDtypeStruct((HYPS, width), BF), terms, terms,
+            jax.ShapeDtypeStruct((HYPS, small), F32),
+        ],
+        scratch_shapes=[pltpu.VMEM((HYPS, width), F32)] * 2 + [
+            pltpu.VMEM((2 * squares * SHAPE[0], HYPS, small), F32),
+            pltpu.VMEM((2 * squares * SHAPE[0], HYPS, small), BF),
+        ],
+        compiler_params=pltpu.CompilerParams(vmem_limit_bytes=6 << 20),
+        cost_estimate=pl.CostEstimate(flops=6 * HYPS * units * width, bytes_accessed=6 * units * width,
+                                      transcendentals=HYPS * units),
+        name="experts",
+    )(info, *shares, hidden, gain, ids, gates, w_gate, w_up, *w_down)
+
+
+def local(
+    query_latent,
+    query_rope,
+    cache_latent,
+    cache_rope,
+    suffix_latent,
+    suffix_rope,
+    lengths,
+    parents,
+    w_uv,
+    w_o,
+    hidden,
+    norm_gain,
+    w_gate,
+    w_up,
+    w_down,
+    expert_ids,
+    gate_weights,
+):
+    count = math.prod(SHAPE)
+    linear = lax.axis_index(AXES)
+    scale = MSCALE * MSCALE / math.sqrt(DN + DR)
+    info = jnp.concatenate([jnp.stack([linear, linear * w_gate.shape[0] // EFF]).astype(jnp.int32), lengths, parents])
+    caches = (cache_latent, cache_rope, suffix_latent, suffix_rope)
+    square, line = (2, 4, 6), (8, 16, 24)
+
+    rope = query_rope.reshape(HYPS, query_latent.shape[1], DR)
+    far_lat, far_rope = swap(query_latent, 2, count), swap(rope, 2, count)
+    near_lat, near_rope = swap(query_latent, 1, count), swap(rope, 1, count)
+    near_keep, near_send = attend(scale, True, info, (query_latent, near_lat), (rope, near_rope), caches)
+    far_lat, far_rope, near_send = lax.optimization_barrier((far_lat, far_rope, near_send))
+    far_lat, far_rope = (far_lat, swap(far_lat, 1, count)), (far_rope, swap(far_rope, 1, count))
+    near = merge_pair_of(near_keep, swap(near_send, 1, count))
+    near = [near[0], *swaps(near[1:], square, count)]
+    far_keep, far_send = attend(scale, False, info, far_lat, far_rope, caches)
+    far = merge_pair_of(far_keep, swap(far_send, 1, count))
+    w_gate, = load(far[0], w_gate)
+    far = [far[0], *swaps(far[1:], square, count)]
+    parts = merge_plane(info, near, far, (w_gate,))
+    w_uv, w_o, w_up = load(parts[0], w_uv, w_o, w_up)
+    parts = [parts[0], *swaps(parts[1:], line, count)]
+    keep, send = project(info, parts, w_uv, w_o, (w_up,))
+
+    pieces = sums([keep, swap(send, 1, count)], split=True)
+    down0, = load(pieces[0], w_down, parts=2, which=0)
+    part, = sums([pieces[0], *swaps(pieces[1:], square, count)], needs=(down0,))
+    down1, = load(part, w_down, parts=2, which=1)
+    share, = sums([part, *swaps([part] * 3, line, count)], needs=(down1,))
+    same_core = [share, *swaps([share] * 3, square, count)]
+    other_core = [swap(v, 1, count) for v in same_core]
+    shares = [v for pair in zip(same_core, other_core) for v in pair]
+    attended, keep, send, residual = experts(
+        info, shares, hidden, norm_gain.reshape(1, -1), expert_ids, gate_weights, w_gate, w_up, down0, down1)
+
+    pieces = sums([keep, swap(send, 1, count)], split=True)
+    parts = sums([pieces[0], *swaps(pieces[1:], square, count)], split=True)
+    total = sum(v.astype(F32) for v in (parts[0], *swaps(parts[1:], line, count)))
+    updated = (residual + total).astype(BF)
+    return (attended, updated)
+
+
 def solution(mesh):
+    if mesh.shape["ctx"] == SHAPE[0] * SHAPE[1] and mesh.shape["hx"] == SHAPE[2] * SHAPE[3]:
+        chosen, names = local, AXES
+        mesh = jax.sharding.Mesh(mesh.devices.reshape(SHAPE), AXES)
+    else:
+        chosen, names = general_local, ("ctx", "hx")
+    all_axes, hx = names, names[len(names) // 2:]
     in_specs = (
-        P(None, "hx", None),
-        P(None, "hx"),
-        P(None, ("ctx", "hx"), None),
-        P(None, None, ("ctx", "hx")),
-        P(None, ("ctx", "hx"), None),
-        P(None, None, ("ctx", "hx")),
+        P(None, hx, None),
+        P(None, hx),
+        P(None, all_axes, None),
+        P(None, None, all_axes),
+        P(None, all_axes, None),
+        P(None, None, all_axes),
         P(),
         P(),
-        P(None, ("ctx", "hx")),
-        P(("ctx", "hx"), None),
+        P(None, all_axes),
+        P(all_axes, None),
         P(),
         P(),
-        P(("ctx", "hx"), None),
-        P(("ctx", "hx"), None),
-        P(("ctx", "hx"), None),
+        P(all_axes, None),
+        P(all_axes, None),
+        P(all_axes, None),
         P(),
         P(),
     )
-    out_specs = (P(), P(None, ("ctx", "hx")))
-    return jax.shard_map(local, mesh=mesh, in_specs=in_specs, out_specs=out_specs, check_vma=False)
+    out_specs = (P(), P(None, all_axes))
+    return jax.shard_map(chosen, mesh=mesh, in_specs=in_specs, out_specs=out_specs, check_vma=False)

time: 434 us -> 142 us (0.33)
  waiting for transfers between devices: 248 us -> 27.1 us
  blocking collectives: 63.6 us -> 0 us
  Pallas kernels: 0 us -> 48.8 us
  matrix products: 48.5 us -> 0 us
  starting transfers between devices: 17.6 us -> 36.9 us
  other arithmetic: 20.5 us -> 1.36 us
  between operations: 14.3 us -> 0.91 us
  local copies, waits for them, and re-layouts: 21.1 us -> 26.8 us
    unnamed x4 -> x0, waiting for transfers between devices: 139 us -> none
    all_to_all x3 -> x0, waiting for transfers between devices: 90.9 us -> none  [the longest x1 90.9 us: local(): lax.all_to_all(weighted[None], 'ctx', split_axis=2, concat_axis=0, tiled=...]
    pallas_call x0 -> x16, Pallas kernels: none -> 48.8 us  [the longest x4 18.8 us: load(): pl.pallas_call(partial(load_kernel, count, parts, which), in_specs=[HBM]...]
    psum x1 -> x0, blocking collectives: 45.7 us -> none  [local(): attended = lax.psum(partial_out, ('ctx', 'hx')).astype(jnp.bfloat16)]
    ppermute x0 -> x38, starting transfers between devices: none -> 36.9 us  [swap(): return lax.ppermute(value, AXES, [(i, i ^ mask) for i in range(count)])]
    dot_general x27 -> x0, matrix products: 33.1 us -> none  [the longest x1 9.05 us: local(): lax.dot_general(normed, w_gate, (((1,), (1,)), ((), ())), preferred_eleme...]
    ppermute x0 -> x38, waiting for transfers between devices: none -> 27.1 us  [swap(): return lax.ppermute(value, AXES, [(i, i ^ mask) for i in range(count)])]
    unnamed x64 -> x26, local copies, waits for them, and re-layouts: 4.86 us -> 25.8 us
  transfers between devices with their start and end apart: 6 -> 38, of which waited for: 4 -> 19; matrix products, arithmetic and copies ran while one was open for 7% -> 1% of each run, Pallas kernels for 0% -> 23%
where the time goes in v1:
time: 142 us
  Pallas kernels  48.8 us (34%)
  starting transfers between devices  36.9 us (26%)
  waiting for transfers between devices  27.1 us (19%)
  local copies, waits for them, and re-layouts  26.8 us (19%)
    ppermute x38, starting transfers between devices, swap(): return lax.ppermute(value, AXES, [(i, i ^ mask) for i in range(count)])  36.9 us
    ppermute x38, waiting for transfers between devices, swap(): return lax.ppermute(value, AXES, [(i, i ^ mask) for i in range(count)])  27.1 us
    unnamed x26, local copies, waits for them, and re-layouts  25.8 us
    pallas_call x4, Pallas kernels, load(): pl.pallas_call(partial(load_kernel, count, parts, which), in_specs=[HBM]...  18.8 us
    pallas_call x2, Pallas kernels, attend(): pl.pallas_call(partial(attend_kernel, scale, fetch), in_specs=[SMEM, HBM...  13.1 us
    pallas_call x1, Pallas kernels, experts(): pl.pallas_call(experts_kernel, in_specs=[SMEM] + [VMEM] * (14 + len(w_dow...  11.6 us
  transfers between devices with their start and end apart: 38, of which 19 were waited for; matrix products, arithmetic and copies ran while one was open for 1% of the time, Pallas kernels for 23%

profile of v1, /device:TPU:0, one launch (start us, length us, event | category | flops | bytes accessed | tf_op | source)
XLA Modules:
  0.0 141.9 jit_solution(3971639459377575220)
XLA Ops:
  1.1 2.6 %collective-permute-start.2 = (bf16[16,32,512]{2,1,0:T(8,128)(2,1)}, bf16[16,32,512]{2,1,0:T(8,128)(2,1)S(1)}, u32[]{:S(2)}, u32[]{:S(2)}) collective-permute-start(bf16[16,32,512]{2,1,0:T(8,128)(2,1)} %ql0.1), channel_id=1, source_target_pairs={{0,2},{1,3},{2,0},{3,1},{4,6},{5,7},{6,4},{7,5},{8,10},{9,11},{10,... | collective-permute-start | bytes 1572872 | tf_op jit(solution)/shard_map/ppermute | solution.py:195
  3.7 1.0 reshape.10.qr0
  5.1 0.7 pad_add_fusion.info
  6.3 6.5 %attend.2 = (bf16[4,144,512]{2,1,0:T(8,128)(2,1)S(1)}, bf16[4,144,512]{2,1,0:T(8,128)(2,1)S(1)}) custom-call(s32[22]{0:T(128)S(1)} %pad_add_fusion.info, bf16[16,32,512]{2,1,0:T(8,128)(2,1)} %ql0.1, bf16[16,32,512]{2,1,0:T(8,128)(2,1)S(1)} %collective-permute-done.ql1, bf16[16,32,64]{2,1,0:T(8,128)(2,1)S(1)} %reshape.10.qr0, ...), custom_call_target="tpu_custom_call" | custom-call | flops 1426063360 | bytes 8388608 | tf_op jit(solution)/shard_map/attend/pallas_call | solution.py:329
  12.8 6.5 %collective-permute-done.3.qr0 = bf16[16,32,64]{2,1,0:T(8,128)(2,1)S(1)} collective-permute-done((bf16[16,32,64]{2,1,0:T(8,128)(2,1)S(1)}, bf16[16,32,64]{2,1,0:T(8,128)(2,1)S(1)}, u32[]{:S(2)}, u32[]{:S(2)}) %collective-permute-start.3) | collective-permute-done | bytes 65568 | tf_op jit(solution)/shard_map/ppermute | solution.py:195
  19.8 1.6 %collective-permute-done.9.qr1 = bf16[16,32,64]{2,1,0:T(8,128)(2,1)S(1)} collective-permute-done((bf16[16,32,64]{2,1,0:T(8,128)(2,1)S(1)}, bf16[16,32,64]{2,1,0:T(8,128)(2,1)S(1)}, u32[]{:S(2)}, u32[]{:S(2)}) %collective-permute-start.9) | collective-permute-done | bytes 65568 | tf_op jit(solution)/shard_map/ppermute | solution.py:195
  21.4 6.5 %attend.3 = (bf16[4,144,512]{2,1,0:T(8,128)(2,1)S(1)}, bf16[4,144,512]{2,1,0:T(8,128)(2,1)S(1)}) custom-call(s32[22]{0:T(128)S(1)} %pad_add_fusion.info, bf16[16,32,512]{2,1,0:T(8,128)(2,1)S(1)} %collective-permute-done.2.ql0, bf16[16,32,512]{2,1,0:T(8,128)(2,1)S(1)} %collective-permute-done.8.ql1, bf16[16,32,64]{2,1,0:T(8,128)(2,1)S(1)} %collective-permute-done.3.qr0, ...), custom_call_target="tpu_custom_call" | custom-call | flops 1426063360 | bytes 8388608 | tf_op jit(solution)/shard_map/attend/pallas_call | solution.py:329
  28.4 1.8 %collective-permute-start.5 = (bf16[144,512]{1,0:T(8,128)(2,1)S(1)}, bf16[144,512]{1,0:T(8,128)(2,1)S(1)}, u32[]{:S(2)}, u32[]{:S(2)}) collective-permute-start(bf16[144,512]{1,0:T(8,128)(2,1)S(1)} %get-tuple-element.46), channel_id=1, source_target_pairs={{0,2},{1,3},{2,0},{3,1},{4,6},{5,7},{6,4},{7,5},{8,10},{9,11},{10,... | collective-permute-start | bytes 442376 | tf_op jit(solution)/shard_map/ppermute | solution.py:195
  30.3 1.5 %collective-permute-start.6 = (bf16[144,512]{1,0:T(8,128)(2,1)S(1)}, bf16[144,512]{1,0:T(8,128)(2,1)S(1)}, u32[]{:S(2)}, u32[]{:S(2)}) collective-permute-start(bf16[144,512]{1,0:T(8,128)(2,1)S(1)} %get-tuple-element.47), channel_id=1, source_target_pairs={{0,4},{1,5},{2,6},{3,7},{4,0},{5,1},{6,2},{7,3},{8,12},{9,13},{10,... | collective-permute-start | bytes 442376 | tf_op jit(solution)/shard_map/ppermute | solution.py:195
  32.3 1.8 %collective-permute-start.11 = (bf16[144,512]{1,0:T(8,128)(2,1)S(1)}, bf16[144,512]{1,0:T(8,128)(2,1)S(1)}, u32[]{:S(2)}, u32[]{:S(2)}) collective-permute-start(bf16[144,512]{1,0:T(8,128)(2,1)S(1)} %get-tuple-element.54), channel_id=1, source_target_pairs={{0,2},{1,3},{2,0},{3,1},{4,6},{5,7},{6,4},{7,5},{8,10},{9,11},{10,... | collective-permute-start | bytes 442376 | tf_op jit(solution)/shard_map/ppermute | solution.py:195
  34.1 1.5 %collective-permute-start.12 = (bf16[144,512]{1,0:T(8,128)(2,1)S(1)}, bf16[144,512]{1,0:T(8,128)(2,1)S(1)}, u32[]{:S(2)}, u32[]{:S(2)}) collective-permute-start(bf16[144,512]{1,0:T(8,128)(2,1)S(1)} %get-tuple-element.55), channel_id=1, source_target_pairs={{0,4},{1,5},{2,6},{3,7},{4,0},{5,1},{6,2},{7,3},{8,12},{9,13},{10,... | collective-permute-start | bytes 442376 | tf_op jit(solution)/shard_map/ppermute | solution.py:195
  35.6 1.7 %collective-permute-start.13 = (bf16[144,512]{1,0:T(8,128)(2,1)S(1)}, bf16[144,512]{1,0:T(8,128)(2,1)S(1)}, u32[]{:S(2)}, u32[]{:S(2)}) collective-permute-start(bf16[144,512]{1,0:T(8,128)(2,1)S(1)} %get-tuple-element.56), channel_id=1, source_target_pairs={{0,6},{1,7},{2,4},{3,5},{4,2},{5,3},{6,0},{7,1},{8,14},{9,15},{10,... | collective-permute-start | bytes 442376 | tf_op jit(solution)/shard_map/ppermute | solution.py:195
  37.4 5.2 %load.4.refs_8_.refs_12_ = bf16[1024,7168]{1,0:T(8,128)(2,1)S(1)} custom-call(bf16[1024,7168]{1,0:T(8,128)(2,1)} %refs_0_.4, bf16[144,512]{1,0:T(8,128)(2,1)S(1)} %get-tuple-element.53.refs_1_.refs_4_), custom_call_target="tpu_custom_call" | custom-call | bytes 14680064 | tf_op jit(solution)/shard_map/load/pallas_call | solution.py:460
  42.6 0.7 collective-permute-done.12.refs_6_
  43.3 2.1 %collective-permute-done.13.refs_7_ = bf16[144,512]{1,0:T(8,128)(2,1)S(1)} collective-permute-done((bf16[144,512]{1,0:T(8,128)(2,1)S(1)}, bf16[144,512]{1,0:T(8,128)(2,1)S(1)}, u32[]{:S(2)}, u32[]{:S(2)}) %collective-permute-start.13) | collective-permute-done | bytes 147488 | tf_op jit(solution)/shard_map/ppermute | solution.py:195
  45.4 2.6 %merge_plane.1 = (bf16[80,512]{1,0:T(8,128)(2,1)S(1)}, bf16[80,512]{1,0:T(8,128)(2,1)S(1)}, bf16[80,512]{1,0:T(8,128)(2,1)S(1)}, bf16[80,512]{1,0:T(8,128)(2,1)S(1)}) custom-call(s32[22]{0:T(128)S(1)} %pad_add_fusion.info, bf16[144,512]{1,0:T(8,128)(2,1)S(1)} %get-tuple-element.45.refs_0_, bf16[144,512]{1,0:T(8,128)(2,1)S(1)} %collective-permute-done.5.refs_1_, ...), custom_call_target="tpu_custom_call" | custom-call | flops 1179648 | bytes 1769472 | tf_op jit(solution)/shard_map/merge_plane/pallas_call | solution.py:408
  48.1 1.8 %collective-permute-start.14 = (bf16[80,512]{1,0:T(8,128)(2,1)S(1)}, bf16[80,512]{1,0:T(8,128)(2,1)S(1)}, u32[]{:S(2)}, u32[]{:S(2)}) collective-permute-start(bf16[80,512]{1,0:T(8,128)(2,1)S(1)} %get-tuple-element.58), channel_id=1, source_target_pairs={{0,8},{1,9},{2,10},{3,11},{4,12},{5,13},{6,14},{7,15},{8,0},{9,1},... | collective-permute-start | bytes 245768 | tf_op jit(solution)/shard_map/ppermute | solution.py:195
  49.8 2.6 %collective-permute-start.15 = (bf16[80,512]{1,0:T(8,128)(2,1)S(1)}, bf16[80,512]{1,0:T(8,128)(2,1)S(1)}, u32[]{:S(2)}, u32[]{:S(2)}) collective-permute-start(bf16[80,512]{1,0:T(8,128)(2,1)S(1)} %get-tuple-element.59), channel_id=1, source_target_pairs={{0,16},{1,17},{2,18},{3,19},{4,20},{5,21},{6,22},{7,23},{8,24},{9,... | collective-permute-start | bytes 245768 | tf_op jit(solution)/shard_map/ppermute | solution.py:195
  52.5 7.5 %load.5 = (bf16[512,512]{1,0:T(8,128)(2,1)S(1)}, bf16[512,7168]{1,0:T(8,128)(2,1)S(1)}, bf16[1024,7168]{1,0:T(8,128)(2,1)S(1)}) custom-call(bf16[512,512]{1,0:T(8,128)(2,1)} %refs_0_.5, bf16[512,7168]{1,0:T(8,128)(2,1)} %refs_1_.1, bf16[1024,7168]{1,0:T(8,128)(2,1)} %refs_2_.1, bf16[80,512]{1,0:T(8,128)(2,1)S(1)} %get-tuple-element.57.refs_3_.p0), custom_call_target="tpu_custom_call" | custom-call | bytes 22544384 | tf_op jit(solution)/shard_map/load/pallas_call | solution.py:460
  60.0 2.0 %project.1 = (bf16[4,16,896]{2,1,0:T(8,128)(2,1)S(1)}, bf16[4,16,896]{2,1,0:T(8,128)(2,1)S(1)}) custom-call(s32[22]{0:T(128)S(1)} %pad_add_fusion.info, bf16[80,512]{1,0:T(8,128)(2,1)S(1)} %get-tuple-element.57.refs_3_.p0, bf16[80,512]{1,0:T(8,128)(2,1)S(1)} %collective-permute-done.14.p1, bf16[80,512]{1,0:T(8,128)(2,1)S(1)} %collective-permute-done.15.p2, ...), custom_call_target="tpu_custom_call" | custom-call | flops 117440512 | bytes 7340032 | tf_op jit(solution)/shard_map/project/pallas_call | solution.py:509
  62.0 3.2 %copy-done.6 = bf16[1024,7168]{1,0:T(8,128)(2,1)} copy-done((bf16[1024,7168]{1,0:T(8,128)(2,1)}, bf16[1024,7168]{1,0:T(8,128)(2,1)S(1)}, u32[]{:S(2)}) %copy-start.6) | copy-done | bytes 14680088
  65.2 1.3 collective-permute-done.17.refs_1_
  66.5 1.7 %collective-permute-start.18 = (bf16[16,896]{1,0:T(8,128)(2,1)S(1)}, bf16[16,896]{1,0:T(8,128)(2,1)S(1)}, u32[]{:S(2)}, u32[]{:S(2)}) collective-permute-start(bf16[16,896]{1,0:T(8,128)(2,1)S(1)} %get-tuple-element.67), channel_id=1, source_target_pairs={{0,2},{1,3},{2,0},{3,1},{4,6},{5,7},{6,4},{7,5},{8,10},{9,11},{10,... | collective-permute-start | bytes 86024 | tf_op jit(solution)/shard_map/ppermute | solution.py:195
  68.3 1.5 %collective-permute-start.19 = (bf16[16,896]{1,0:T(8,128)(2,1)S(1)}, bf16[16,896]{1,0:T(8,128)(2,1)S(1)}, u32[]{:S(2)}, u32[]{:S(2)}) collective-permute-start(bf16[16,896]{1,0:T(8,128)(2,1)S(1)} %get-tuple-element.68), channel_id=1, source_target_pairs={{0,4},{1,5},{2,6},{3,7},{4,0},{5,1},{6,2},{7,3},{8,12},{9,13},{10,... | collective-permute-start | bytes 86024 | tf_op jit(solution)/shard_map/ppermute | solution.py:195
  70.1 3.1 %load.6.refs_4_.refs_14_ = bf16[512,7168]{1,0:T(8,128)(2,1)S(1)} custom-call(bf16[1024,7168]{1,0:T(8,128)(2,1)} %refs_0_.7, bf16[16,896]{1,0:T(8,128)(2,1)S(1)} %get-tuple-element.66.refs_1_.refs_0_), custom_call_target="tpu_custom_call" | custom-call | bytes 7340032 | tf_op jit(solution)/shard_map/load/pallas_call | solution.py:460
  73.2 1.3 collective-permute-done.20.refs_3_
  74.6 3.0 %copy-done.2 = bf16[512,7168]{1,0:T(8,128)(2,1)} copy-done((bf16[512,7168]{1,0:T(8,128)(2,1)}, bf16[512,7168]{1,0:T(8,128)(2,1)S(1)}, u32[]{:S(2)}) %copy-start.2) | copy-done | bytes 7340056
  77.6 3.6 %collective-permute-start.23 = (bf16[16,896]{1,0:T(8,128)(2,1)S(1)}, bf16[16,896]{1,0:T(8,128)(2,1)S(1)}, u32[]{:S(2)}, u32[]{:S(2)}) collective-permute-start(bf16[16,896]{1,0:T(8,128)(2,1)S(1)} %sums.6.refs_1_.refs_0_), channel_id=1, source_target_pairs={{0,24},{1,25},{2,26},{3,27},{4,28},{5,29},{6,30},{7,31},{8,16},{9,... | collective-permute-start | bytes 86024 | tf_op jit(solution)/shard_map/ppermute | solution.py:195
  81.2 0.8 collective-permute-start.21
  82.0 3.1 %load.7.refs_4_.refs_15_ = bf16[512,7168]{1,0:T(8,128)(2,1)S(1)} custom-call(bf16[1024,7168]{1,0:T(8,128)(2,1)} %refs_0_.7, bf16[16,896]{1,0:T(8,128)(2,1)S(1)} %sums.6.refs_1_.refs_0_), custom_call_target="tpu_custom_call" | custom-call | bytes 7340032 | tf_op jit(solution)/shard_map/load/pallas_call | solution.py:460
  85.1 0.8 collective-permute-done.22.refs_2_
  86.0 2.9 %copy-done.4 = bf16[512,7168]{1,0:T(8,128)(2,1)} copy-done((bf16[512,7168]{1,0:T(8,128)(2,1)}, bf16[512,7168]{1,0:T(8,128)(2,1)S(1)}, u32[]{:S(2)}) %copy-start.4) | copy-done | bytes 7340056
  88.9 1.3 collective-permute-start.29
  90.9 1.5 %collective-permute-start.25 = (bf16[16,896]{1,0:T(8,128)(2,1)S(1)}, bf16[16,896]{1,0:T(8,128)(2,1)S(1)}, u32[]{:S(2)}, u32[]{:S(2)}) collective-permute-start(bf16[16,896]{1,0:T(8,128)(2,1)S(1)} %sums.7.refs_0_), channel_id=1, source_target_pairs={{0,2},{1,3},{2,0},{3,1},{4,6},{5,7},{6,4},{7,5},{8,10},{9,11},{10,... | collective-permute-start | bytes 86024 | tf_op jit(solution)/shard_map/ppermute | solution.py:195
  92.4 1.3 collective-permute-done.29.refs_6_
  96.0 5.2 %copy-done.1 = bf16[1024,7168]{1,0:T(8,128)(2,1)S(1)} copy-done((bf16[1024,7168]{1,0:T(8,128)(2,1)S(1)}, bf16[1024,7168]{1,0:T(8,128)(2,1)}, u32[]{:S(2)}) %copy-start.1) | copy-done | bytes 14680088
  101.2 3.1 %copy-done.3 = bf16[512,7168]{1,0:T(8,128)(2,1)S(1)} copy-done((bf16[512,7168]{1,0:T(8,128)(2,1)S(1)}, bf16[512,7168]{1,0:T(8,128)(2,1)}, u32[]{:S(2)}) %copy-start.3) | copy-done | bytes 7340056
  104.2 3.1 %copy-done.5 = bf16[512,7168]{1,0:T(8,128)(2,1)S(1)} copy-done((bf16[512,7168]{1,0:T(8,128)(2,1)S(1)}, bf16[512,7168]{1,0:T(8,128)(2,1)}, u32[]{:S(2)}) %copy-start.5) | copy-done | bytes 7340056
  107.3 5.2 %copy-done.7 = bf16[1024,7168]{1,0:T(8,128)(2,1)S(1)} copy-done((bf16[1024,7168]{1,0:T(8,128)(2,1)S(1)}, bf16[1024,7168]{1,0:T(8,128)(2,1)}, u32[]{:S(2)}) %copy-start.7) | copy-done | bytes 14680088
  112.5 11.6 %experts.1 = (bf16[16,7168]{1,0:T(8,128)(2,1)}, bf16[4,4,16,224]{3,2,1,0:T(8,128)(2,1)S(1)}, bf16[4,4,16,224]{3,2,1,0:T(8,128)(2,1)S(1)}, f32[16,224]{1,0:T(8,128)S(1)}) custom-call(s32[22]{0:T(128)S(1)} %pad_add_fusion.info, bf16[16,896]{1,0:T(8,128)(2,1)S(1)} %sums.7.refs_0_, bf16[16,896]{1,0:T(8,128)(2,1)S(1)} %collective-permute-done.24.refs_1_, ...), custom_call_target="tpu_custom_call" | custom-call | flops 704643072 | bytes 44040192 | tf_op jit(solution)/shard_map/experts/pallas_call | solution.py:564
  124.2 1.2 collective-permute-done.31.refs_1_
  125.4 1.6 %collective-permute-start.32 = (bf16[4,16,224]{2,1,0:T(8,128)(2,1)S(1)}, bf16[4,16,224]{2,1,0:T(8,128)(2,1)S(1)}, u32[]{:S(2)}, u32[]{:S(2)}) collective-permute-start(bf16[4,16,224]{2,1,0:T(8,128)(2,1)S(1)} %get-tuple-element.75), channel_id=1, source_target_pairs={{0,2},{1,3},{2,0},{3,1},{4,6},{5,7},{6,4},{7,5},{8,10},{9,11},{10,... | collective-permute-start | bytes 86024 | tf_op jit(solution)/shard_map/ppermute | solution.py:195
  127.6 1.4 %collective-permute-start.34 = (bf16[4,16,224]{2,1,0:T(8,128)(2,1)S(1)}, bf16[4,16,224]{2,1,0:T(8,128)(2,1)S(1)}, u32[]{:S(2)}, u32[]{:S(2)}) collective-permute-start(bf16[4,16,224]{2,1,0:T(8,128)(2,1)S(1)} %get-tuple-element.77), channel_id=1, source_target_pairs={{0,6},{1,7},{2,4},{3,5},{4,2},{5,3},{6,0},{7,1},{8,14},{9,15},{10,... | collective-permute-start | bytes 86024 | tf_op jit(solution)/shard_map/ppermute | solution.py:195
  129.4 1.8 %collective-permute-done.33.refs_2_ = bf16[4,16,224]{2,1,0:T(8,128)(2,1)S(1)} collective-permute-done((bf16[4,16,224]{2,1,0:T(8,128)(2,1)S(1)}, bf16[4,16,224]{2,1,0:T(8,128)(2,1)S(1)}, u32[]{:S(2)}, u32[]{:S(2)}) %collective-permute-start.33) | collective-permute-done | bytes 28704 | tf_op jit(solution)/shard_map/ppermute | solution.py:195
  131.2 1.2 collective-permute-done.34.refs_3_
  132.9 2.9 %collective-permute-start.36 = (bf16[16,224]{1,0:T(8,128)(2,1)S(1)}, bf16[16,224]{1,0:T(8,128)(2,1)S(1)}, u32[]{:S(2)}, u32[]{:S(2)}) collective-permute-start(bf16[16,224]{1,0:T(8,128)(2,1)S(1)} %get-tuple-element.80), channel_id=1, source_target_pairs={{0,16},{1,17},{2,18},{3,19},{4,20},{5,21},{6,22},{7,23},{8,24},{9,... | collective-permute-start | bytes 21512 | tf_op jit(solution)/shard_map/ppermute | solution.py:195
  135.8 1.0 collective-permute-start.37
  137.4 3.8 %collective-permute-done.37 = bf16[16,224]{1,0:T(8,128)(2,1)S(1)} collective-permute-done((bf16[16,224]{1,0:T(8,128)(2,1)S(1)}, bf16[16,224]{1,0:T(8,128)(2,1)S(1)}, u32[]{:S(2)}, u32[]{:S(2)}) %collective-permute-start.37) | collective-permute-done | bytes 7200 | tf_op jit(solution)/shard_map/ppermute | solution.py:195
  (73 shorter events, 9.2 us)
Async XLA Ops:
  0.6 5.6 %collective-permute-start = (bf16[16,32,512]{2,1,0:T(8,128)(2,1)}, bf16[16,32,512]{2,1,0:T(8,128)(2,1)S(1)}, u32[]{:S(2)}, u32[]{:S(2)}) collective-permute-start(bf16[16,32,512]{2,1,0:T(8,128)(2,1)} %ql0.1), channel_id=1, source_target_pairs={{0,1},{1,0},{2,3},{3,2},{4,5},{5,4},{6,7},{7,6},{8,9},{9,8},{10,11... | collective-permute-start | bytes 1572872 | tf_op jit(solution)/shard_map/ppermute | solution.py:195
  1.1 18.1 %collective-permute-start.2 = (bf16[16,32,512]{2,1,0:T(8,128)(2,1)}, bf16[16,32,512]{2,1,0:T(8,128)(2,1)S(1)}, u32[]{:S(2)}, u32[]{:S(2)}) collective-permute-start(bf16[16,32,512]{2,1,0:T(8,128)(2,1)} %ql0.1), channel_id=1, source_target_pairs={{0,2},{1,3},{2,0},{3,1},{4,6},{5,7},{6,4},{7,5},{8,10},{9,11},{10,... | collective-permute-start | bytes 1572872 | tf_op jit(solution)/shard_map/ppermute | solution.py:195
  4.8 14.5 %collective-permute-start.3 = (bf16[16,32,64]{2,1,0:T(8,128)(2,1)S(1)}, bf16[16,32,64]{2,1,0:T(8,128)(2,1)S(1)}, u32[]{:S(2)}, u32[]{:S(2)}) collective-permute-start(bf16[16,32,64]{2,1,0:T(8,128)(2,1)S(1)} %reshape.10.qr0), channel_id=1, source_target_pairs={{0,2},{1,3},{2,0},{3,1},{4,6},{5,7},{6,4},{7,5},{8,10},{9,11},{10,... | collective-permute-start | bytes 196616 | tf_op jit(solution)/shard_map/ppermute | solution.py:195
  4.9 1.4 collective-permute-start.1
  19.3 2.1 %collective-permute-start.8 = (bf16[16,32,512]{2,1,0:T(8,128)(2,1)S(1)}, bf16[16,32,512]{2,1,0:T(8,128)(2,1)S(1)}, u32[]{:S(2)}, u32[]{:S(2)}) collective-permute-start(bf16[16,32,512]{2,1,0:T(8,128)(2,1)S(1)} %collective-permute-done.2.ql0), channel_id=1, source_target_pairs={{0,1},{1,0},{2,3},{3,2},{4,5},{5,4},{6,7},{7,6},{8,9},{9,8},{10,11... | collective-permute-start | bytes 1572872 | tf_op jit(solution)/shard_map/ppermute | solution.py:195
  19.3 2.1 %collective-permute-start.9 = (bf16[16,32,64]{2,1,0:T(8,128)(2,1)S(1)}, bf16[16,32,64]{2,1,0:T(8,128)(2,1)S(1)}, u32[]{:S(2)}, u32[]{:S(2)}) collective-permute-start(bf16[16,32,64]{2,1,0:T(8,128)(2,1)S(1)} %collective-permute-done.3.qr0), channel_id=1, source_target_pairs={{0,1},{1,0},{2,3},{3,2},{4,5},{5,4},{6,7},{7,6},{8,9},{9,8},{10,11... | collective-permute-start | bytes 196616 | tf_op jit(solution)/shard_map/ppermute | solution.py:195
  19.8 8.3 %collective-permute-start.4 = (bf16[4,144,512]{2,1,0:T(8,128)(2,1)S(1)}, bf16[4,144,512]{2,1,0:T(8,128)(2,1)S(1)}, u32[]{:S(2)}, u32[]{:S(2)}) collective-permute-start(bf16[4,144,512]{2,1,0:T(8,128)(2,1)S(1)} %get-tuple-element.44), channel_id=1, source_target_pairs={{0,1},{1,0},{2,3},{3,2},{4,5},{5,4},{6,7},{7,6},{8,9},{9,8},{10,11... | collective-permute-start | bytes 1769480 | tf_op jit(solution)/shard_map/ppermute | solution.py:195
  27.9 4.1 %collective-permute-start.10 = (bf16[4,144,512]{2,1,0:T(8,128)(2,1)S(1)}, bf16[4,144,512]{2,1,0:T(8,128)(2,1)S(1)}, u32[]{:S(2)}, u32[]{:S(2)}) collective-permute-start(bf16[4,144,512]{2,1,0:T(8,128)(2,1)S(1)} %get-tuple-element.52), channel_id=1, source_target_pairs={{0,1},{1,0},{2,3},{3,2},{4,5},{5,4},{6,7},{7,6},{8,9},{9,8},{10,11... | collective-permute-start | bytes 1769480 | tf_op jit(solution)/shard_map/ppermute | solution.py:195
  28.4 7.2 %collective-permute-start.5 = (bf16[144,512]{1,0:T(8,128)(2,1)S(1)}, bf16[144,512]{1,0:T(8,128)(2,1)S(1)}, u32[]{:S(2)}, u32[]{:S(2)}) collective-permute-start(bf16[144,512]{1,0:T(8,128)(2,1)S(1)} %get-tuple-element.46), channel_id=1, source_target_pairs={{0,2},{1,3},{2,0},{3,1},{4,6},{5,7},{6,4},{7,5},{8,10},{9,11},{10,... | collective-permute-start | bytes 442376 | tf_op jit(solution)/shard_map/ppermute | solution.py:195
  30.3 12.3 %collective-permute-start.6 = (bf16[144,512]{1,0:T(8,128)(2,1)S(1)}, bf16[144,512]{1,0:T(8,128)(2,1)S(1)}, u32[]{:S(2)}, u32[]{:S(2)}) collective-permute-start(bf16[144,512]{1,0:T(8,128)(2,1)S(1)} %get-tuple-element.47), channel_id=1, source_target_pairs={{0,4},{1,5},{2,6},{3,7},{4,0},{5,1},{6,2},{7,3},{8,12},{9,13},{10,... | collective-permute-start | bytes 442376 | tf_op jit(solution)/shard_map/ppermute | solution.py:195
  31.8 10.8 %collective-permute-start.7 = (bf16[144,512]{1,0:T(8,128)(2,1)S(1)}, bf16[144,512]{1,0:T(8,128)(2,1)S(1)}, u32[]{:S(2)}, u32[]{:S(2)}) collective-permute-start(bf16[144,512]{1,0:T(8,128)(2,1)S(1)} %get-tuple-element.48), channel_id=1, source_target_pairs={{0,6},{1,7},{2,4},{3,5},{4,2},{5,3},{6,0},{7,1},{8,14},{9,15},{10,... | collective-permute-start | bytes 442376 | tf_op jit(solution)/shard_map/ppermute | solution.py:195
  32.3 10.3 %collective-permute-start.11 = (bf16[144,512]{1,0:T(8,128)(2,1)S(1)}, bf16[144,512]{1,0:T(8,128)(2,1)S(1)}, u32[]{:S(2)}, u32[]{:S(2)}) collective-permute-start(bf16[144,512]{1,0:T(8,128)(2,1)S(1)} %get-tuple-element.54), channel_id=1, source_target_pairs={{0,2},{1,3},{2,0},{3,1},{4,6},{5,7},{6,4},{7,5},{8,10},{9,11},{10,... | collective-permute-start | bytes 442376 | tf_op jit(solution)/shard_map/ppermute | solution.py:195
  34.1 9.2 %collective-permute-start.12 = (bf16[144,512]{1,0:T(8,128)(2,1)S(1)}, bf16[144,512]{1,0:T(8,128)(2,1)S(1)}, u32[]{:S(2)}, u32[]{:S(2)}) collective-permute-start(bf16[144,512]{1,0:T(8,128)(2,1)S(1)} %get-tuple-element.55), channel_id=1, source_target_pairs={{0,4},{1,5},{2,6},{3,7},{4,0},{5,1},{6,2},{7,3},{8,12},{9,13},{10,... | collective-permute-start | bytes 442376 | tf_op jit(solution)/shard_map/ppermute | solution.py:195
  35.6 9.8 %collective-permute-start.13 = (bf16[144,512]{1,0:T(8,128)(2,1)S(1)}, bf16[144,512]{1,0:T(8,128)(2,1)S(1)}, u32[]{:S(2)}, u32[]{:S(2)}) collective-permute-start(bf16[144,512]{1,0:T(8,128)(2,1)S(1)} %get-tuple-element.56), channel_id=1, source_target_pairs={{0,6},{1,7},{2,4},{3,5},{4,2},{5,3},{6,0},{7,1},{8,14},{9,15},{10,... | collective-permute-start | bytes 442376 | tf_op jit(solution)/shard_map/ppermute | solution.py:195
  42.6 5.5 %copy-start = (bf16[1024,7168]{1,0:T(8,128)(2,1)}, bf16[1024,7168]{1,0:T(8,128)(2,1)S(1)}, u32[]{:S(2)}) copy-start(bf16[1024,7168]{1,0:T(8,128)(2,1)S(1)} %load.4.refs_8_.refs_12_) | copy-start | bytes 44040196
  48.1 11.9 %collective-permute-start.14 = (bf16[80,512]{1,0:T(8,128)(2,1)S(1)}, bf16[80,512]{1,0:T(8,128)(2,1)S(1)}, u32[]{:S(2)}, u32[]{:S(2)}) collective-permute-start(bf16[80,512]{1,0:T(8,128)(2,1)S(1)} %get-tuple-element.58), channel_id=1, source_target_pairs={{0,8},{1,9},{2,10},{3,11},{4,12},{5,13},{6,14},{7,15},{8,0},{9,1},... | collective-permute-start | bytes 245768 | tf_op jit(solution)/shard_map/ppermute | solution.py:195
  49.8 10.2 %collective-permute-start.15 = (bf16[80,512]{1,0:T(8,128)(2,1)S(1)}, bf16[80,512]{1,0:T(8,128)(2,1)S(1)}, u32[]{:S(2)}, u32[]{:S(2)}) collective-permute-start(bf16[80,512]{1,0:T(8,128)(2,1)S(1)} %get-tuple-element.59), channel_id=1, source_target_pairs={{0,16},{1,17},{2,18},{3,19},{4,20},{5,21},{6,22},{7,23},{8,24},{9,... | collective-permute-start | bytes 245768 | tf_op jit(solution)/shard_map/ppermute | solution.py:195
  52.4 7.6 %collective-permute-start.16 = (bf16[80,512]{1,0:T(8,128)(2,1)S(1)}, bf16[80,512]{1,0:T(8,128)(2,1)S(1)}, u32[]{:S(2)}, u32[]{:S(2)}) collective-permute-start(bf16[80,512]{1,0:T(8,128)(2,1)S(1)} %get-tuple-element.60), channel_id=1, source_target_pairs={{0,24},{1,25},{2,26},{3,27},{4,28},{5,29},{6,30},{7,31},{8,16},{9,... | collective-permute-start | bytes 245768 | tf_op jit(solution)/shard_map/ppermute | solution.py:195
  60.0 5.2 %copy-start.6 = (bf16[1024,7168]{1,0:T(8,128)(2,1)}, bf16[1024,7168]{1,0:T(8,128)(2,1)S(1)}, u32[]{:S(2)}) copy-start(bf16[1024,7168]{1,0:T(8,128)(2,1)S(1)} %get-tuple-element.63.rest_0_.refs_13_) | copy-start | bytes 44040196
  65.2 1.3 collective-permute-start.17
  66.5 6.7 %collective-permute-start.18 = (bf16[16,896]{1,0:T(8,128)(2,1)S(1)}, bf16[16,896]{1,0:T(8,128)(2,1)S(1)}, u32[]{:S(2)}, u32[]{:S(2)}) collective-permute-start(bf16[16,896]{1,0:T(8,128)(2,1)S(1)} %get-tuple-element.67), channel_id=1, source_target_pairs={{0,2},{1,3},{2,0},{3,1},{4,6},{5,7},{6,4},{7,5},{8,10},{9,11},{10,... | collective-permute-start | bytes 86024 | tf_op jit(solution)/shard_map/ppermute | solution.py:195
  68.3 4.9 %collective-permute-start.19 = (bf16[16,896]{1,0:T(8,128)(2,1)S(1)}, bf16[16,896]{1,0:T(8,128)(2,1)S(1)}, u32[]{:S(2)}, u32[]{:S(2)}) collective-permute-start(bf16[16,896]{1,0:T(8,128)(2,1)S(1)} %get-tuple-element.68), channel_id=1, source_target_pairs={{0,4},{1,5},{2,6},{3,7},{4,0},{5,1},{6,2},{7,3},{8,12},{9,13},{10,... | collective-permute-start | bytes 86024 | tf_op jit(solution)/shard_map/ppermute | solution.py:195
  69.8 4.8 %collective-permute-start.20 = (bf16[16,896]{1,0:T(8,128)(2,1)S(1)}, bf16[16,896]{1,0:T(8,128)(2,1)S(1)}, u32[]{:S(2)}, u32[]{:S(2)}) collective-permute-start(bf16[16,896]{1,0:T(8,128)(2,1)S(1)} %get-tuple-element.69), channel_id=1, source_target_pairs={{0,6},{1,7},{2,4},{3,5},{4,2},{5,3},{6,0},{7,1},{8,14},{9,15},{10,... | collective-permute-start | bytes 86024 | tf_op jit(solution)/shard_map/ppermute | solution.py:195
  77.6 7.5 %collective-permute-start.23 = (bf16[16,896]{1,0:T(8,128)(2,1)S(1)}, bf16[16,896]{1,0:T(8,128)(2,1)S(1)}, u32[]{:S(2)}, u32[]{:S(2)}) collective-permute-start(bf16[16,896]{1,0:T(8,128)(2,1)S(1)} %sums.6.refs_1_.refs_0_), channel_id=1, source_target_pairs={{0,24},{1,25},{2,26},{3,27},{4,28},{5,29},{6,30},{7,31},{8,16},{9,... | collective-permute-start | bytes 86024 | tf_op jit(solution)/shard_map/ppermute | solution.py:195
  81.2 4.8 %collective-permute-start.22 = (bf16[16,896]{1,0:T(8,128)(2,1)S(1)}, bf16[16,896]{1,0:T(8,128)(2,1)S(1)}, u32[]{:S(2)}, u32[]{:S(2)}) collective-permute-start(bf16[16,896]{1,0:T(8,128)(2,1)S(1)} %sums.6.refs_1_.refs_0_), channel_id=1, source_target_pairs={{0,16},{1,17},{2,18},{3,19},{4,20},{5,21},{6,22},{7,23},{8,24},{9,... | collective-permute-start | bytes 86024 | tf_op jit(solution)/shard_map/ppermute | solution.py:195
  81.2 4.8 %collective-permute-start.21 = (bf16[16,896]{1,0:T(8,128)(2,1)S(1)}, bf16[16,896]{1,0:T(8,128)(2,1)S(1)}, u32[]{:S(2)}, u32[]{:S(2)}) collective-permute-start(bf16[16,896]{1,0:T(8,128)(2,1)S(1)} %sums.6.refs_1_.refs_0_), channel_id=1, source_target_pairs={{0,8},{1,9},{2,10},{3,11},{4,12},{5,13},{6,14},{7,15},{8,0},{9,1},... | collective-permute-start | bytes 86024 | tf_op jit(solution)/shard_map/ppermute | solution.py:195
  85.1 9.7 %copy-start.10 = (s32[16,8]{0,1:T(8,128)S(1)}, s32[16,8]{0,1:T(8,128)}, u32[]{:S(2)}) copy-start(s32[16,8]{0,1:T(8,128)} %param.32) | copy-start | bytes 1540
  85.1 9.8 %copy-start.11 = (f32[16,8]{0,1:T(8,128)S(1)}, f32[16,8]{0,1:T(8,128)}, u32[]{:S(2)}) copy-start(f32[16,8]{0,1:T(8,128)} %param.33) | copy-start | bytes 1540
  85.1 10.9 %copy-start.8 = (bf16[16,7168]{1,0:T(8,128)(2,1)S(1)}, bf16[16,7168]{1,0:T(8,128)(2,1)}, u32[]{:S(2)}) copy-start(bf16[16,7168]{1,0:T(8,128)(2,1)} %refs_8_.1) | copy-start | bytes 688132
  85.1 10.9 %copy-start.9 = (f32[7168]{0:T(1024)S(1)}, f32[7168]{0:T(1024)}, u32[]{:S(2)}) copy-start(f32[7168]{0:T(1024)} %param.28) | copy-start | bytes 86020
  88.9 4.8 %collective-permute-start.29 = (bf16[16,896]{1,0:T(8,128)(2,1)S(1)}, bf16[16,896]{1,0:T(8,128)(2,1)S(1)}, u32[]{:S(2)}, u32[]{:S(2)}) collective-permute-start(bf16[16,896]{1,0:T(8,128)(2,1)S(1)} %sums.7.refs_0_), channel_id=1, source_target_pairs={{0,6},{1,7},{2,4},{3,5},{4,2},{5,3},{6,0},{7,1},{8,14},{9,15},{10,... | collective-permute-start | bytes 86024 | tf_op jit(solution)/shard_map/ppermute | solution.py:195
  90.2 3.9 %collective-permute-start.27 = (bf16[16,896]{1,0:T(8,128)(2,1)S(1)}, bf16[16,896]{1,0:T(8,128)(2,1)S(1)}, u32[]{:S(2)}, u32[]{:S(2)}) collective-permute-start(bf16[16,896]{1,0:T(8,128)(2,1)S(1)} %sums.7.refs_0_), channel_id=1, source_target_pairs={{0,4},{1,5},{2,6},{3,7},{4,0},{5,1},{6,2},{7,3},{8,12},{9,13},{10,... | collective-permute-start | bytes 86024 | tf_op jit(solution)/shard_map/ppermute | solution.py:195
  90.9 3.9 %collective-permute-start.25 = (bf16[16,896]{1,0:T(8,128)(2,1)S(1)}, bf16[16,896]{1,0:T(8,128)(2,1)S(1)}, u32[]{:S(2)}, u32[]{:S(2)}) collective-permute-start(bf16[16,896]{1,0:T(8,128)(2,1)S(1)} %sums.7.refs_0_), channel_id=1, source_target_pairs={{0,2},{1,3},{2,0},{3,1},{4,6},{5,7},{6,4},{7,5},{8,10},{9,11},{10,... | collective-permute-start | bytes 86024 | tf_op jit(solution)/shard_map/ppermute | solution.py:195
  92.4 2.5 %collective-permute-start.24 = (bf16[16,896]{1,0:T(8,128)(2,1)S(1)}, bf16[16,896]{1,0:T(8,128)(2,1)S(1)}, u32[]{:S(2)}, u32[]{:S(2)}) collective-permute-start(bf16[16,896]{1,0:T(8,128)(2,1)S(1)} %sums.7.refs_0_), channel_id=1, source_target_pairs={{0,1},{1,0},{2,3},{3,2},{4,5},{5,4},{6,7},{7,6},{8,9},{9,8},{10,11... | collective-permute-start | bytes 86024 | tf_op jit(solution)/shard_map/ppermute | solution.py:195
  93.7 1.2 collective-permute-start.30
  94.1 1.2 collective-permute-start.28
  94.8 1.2 collective-permute-start.26
  96.0 5.2 %copy-start.1 = (bf16[1024,7168]{1,0:T(8,128)(2,1)S(1)}, bf16[1024,7168]{1,0:T(8,128)(2,1)}, u32[]{:S(2)}) copy-start(bf16[1024,7168]{1,0:T(8,128)(2,1)} %copy-done) | copy-start | bytes 44040196
  101.2 3.1 %copy-start.3 = (bf16[512,7168]{1,0:T(8,128)(2,1)S(1)}, bf16[512,7168]{1,0:T(8,128)(2,1)}, u32[]{:S(2)}) copy-start(bf16[512,7168]{1,0:T(8,128)(2,1)} %copy-done.2) | copy-start | bytes 22020100
  104.2 3.1 %copy-start.5 = (bf16[512,7168]{1,0:T(8,128)(2,1)S(1)}, bf16[512,7168]{1,0:T(8,128)(2,1)}, u32[]{:S(2)}) copy-start(bf16[512,7168]{1,0:T(8,128)(2,1)} %copy-done.4) | copy-start | bytes 22020100
  107.3 5.2 %copy-start.7 = (bf16[1024,7168]{1,0:T(8,128)(2,1)S(1)}, bf16[1024,7168]{1,0:T(8,128)(2,1)}, u32[]{:S(2)}) copy-start(bf16[1024,7168]{1,0:T(8,128)(2,1)} %copy-done.6) | copy-start | bytes 44040196
  124.0 1.3 collective-permute-start.31
  125.4 4.0 %collective-permute-start.32 = (bf16[4,16,224]{2,1,0:T(8,128)(2,1)S(1)}, bf16[4,16,224]{2,1,0:T(8,128)(2,1)S(1)}, u32[]{:S(2)}, u32[]{:S(2)}) collective-permute-start(bf16[4,16,224]{2,1,0:T(8,128)(2,1)S(1)} %get-tuple-element.75), channel_id=1, source_target_pairs={{0,2},{1,3},{2,0},{3,1},{4,6},{5,7},{6,4},{7,5},{8,10},{9,11},{10,... | collective-permute-start | bytes 86024 | tf_op jit(solution)/shard_map/ppermute | solution.py:195
  127.0 4.2 %collective-permute-start.33 = (bf16[4,16,224]{2,1,0:T(8,128)(2,1)S(1)}, bf16[4,16,224]{2,1,0:T(8,128)(2,1)S(1)}, u32[]{:S(2)}, u32[]{:S(2)}) collective-permute-start(bf16[4,16,224]{2,1,0:T(8,128)(2,1)S(1)} %get-tuple-element.76), channel_id=1, source_target_pairs={{0,4},{1,5},{2,6},{3,7},{4,0},{5,1},{6,2},{7,3},{8,12},{9,13},{10,... | collective-permute-start | bytes 86024 | tf_op jit(solution)/shard_map/ppermute | solution.py:195
  127.6 4.8 %collective-permute-start.34 = (bf16[4,16,224]{2,1,0:T(8,128)(2,1)S(1)}, bf16[4,16,224]{2,1,0:T(8,128)(2,1)S(1)}, u32[]{:S(2)}, u32[]{:S(2)}) collective-permute-start(bf16[4,16,224]{2,1,0:T(8,128)(2,1)S(1)} %get-tuple-element.77), channel_id=1, source_target_pairs={{0,6},{1,7},{2,4},{3,5},{4,2},{5,3},{6,0},{7,1},{8,14},{9,15},{10,... | collective-permute-start | bytes 86024 | tf_op jit(solution)/shard_map/ppermute | solution.py:195
  132.4 4.5 %collective-permute-start.35 = (bf16[16,224]{1,0:T(8,128)(2,1)S(1)}, bf16[16,224]{1,0:T(8,128)(2,1)S(1)}, u32[]{:S(2)}, u32[]{:S(2)}) collective-permute-start(bf16[16,224]{1,0:T(8,128)(2,1)S(1)} %get-tuple-element.79), channel_id=1, source_target_pairs={{0,8},{1,9},{2,10},{3,11},{4,12},{5,13},{6,14},{7,15},{8,0},{9,1},... | collective-permute-start | bytes 21512 | tf_op jit(solution)/shard_map/ppermute | solution.py:195
  132.9 4.5 %collective-permute-start.36 = (bf16[16,224]{1,0:T(8,128)(2,1)S(1)}, bf16[16,224]{1,0:T(8,128)(2,1)S(1)}, u32[]{:S(2)}, u32[]{:S(2)}) collective-permute-start(bf16[16,224]{1,0:T(8,128)(2,1)S(1)} %get-tuple-element.80), channel_id=1, source_target_pairs={{0,16},{1,17},{2,18},{3,19},{4,20},{5,21},{6,22},{7,23},{8,24},{9,... | collective-permute-start | bytes 21512 | tf_op jit(solution)/shard_map/ppermute | solution.py:195
  135.8 5.4 %collective-permute-start.37 = (bf16[16,224]{1,0:T(8,128)(2,1)S(1)}, bf16[16,224]{1,0:T(8,128)(2,1)S(1)}, u32[]{:S(2)}, u32[]{:S(2)}) collective-permute-start(bf16[16,224]{1,0:T(8,128)(2,1)S(1)} %get-tuple-element.81), channel_id=1, source_target_pairs={{0,24},{1,25},{2,26},{3,27},{4,28},{5,29},{6,30},{7,31},{8,16},{9,... | collective-permute-start | bytes 21512 | tf_op jit(solution)/shard_map/ppermute | solution.py:195
  (2 other events, 6.0 us)

commit v2 on v1

v2 whole, which is shorter than its diff:
```python
from functools import partial
import math

import jax
import jax.numpy as jnp
from jax import lax
from jax.experimental import pallas as pl
from jax.experimental.pallas import tpu as pltpu
from jax.sharding import PartitionSpec as P

DL = 512
DR = 64
DN = 128
DV = 128
EFF = 2048
REQ = 4
BEAMS = 4
HYPS = 16


MSCALE = 1.0 + 0.1 * math.log(40.0)
NEG = -1e30


def merged(value, axis, join):
    pieces = jax.tree.map(lambda part: lax.all_gather(part, axis), value)
    head = jax.tree.map(lambda part: part[0], pieces)
    tail = jax.tree.map(lambda part: part[1:], pieces)
    subtotal, _ = lax.scan(lambda subtotal, section: (join(subtotal, section), None), head, tail)
    return subtotal


def merge_pair(first_set, second_set):
    max_a, sum_a, acc_a = first_set
    max_b, sum_b, acc_b = second_set
    new_max = jnp.maximum(max_a, max_b)
    factor_a = jnp.exp(max_a - new_max)
    factor_b = jnp.exp(max_b - new_max)
    return (
        new_max,
        sum_a * factor_a + sum_b * factor_b,
        acc_a * factor_a[..., None] + acc_b * factor_b[..., None],
    )


def request_stats(
    q_lat, q_rope, pre_lat, pre_rope, suf_lat, suf_rope, is_live, softmax_scale, with_prefix
):
    suf_scores = jnp.einsum("bhl,bsl->bhs", q_lat, suf_lat, preferred_element_type=jnp.float32)
    suf_scores = (
        suf_scores
        + jnp.einsum("bhr,brs->bhs", q_rope, suf_rope, preferred_element_type=jnp.float32)
    ) * softmax_scale
    row_max = jnp.max(suf_scores, axis=2)
    beam_count, head_count, lat_width = q_lat.shape
    flat_lat = q_lat.reshape(beam_count * head_count, lat_width)
    flat_rope = q_rope.reshape(beam_count * head_count, q_rope.shape[2])
    pre_scores = lax.dot_general(
        flat_lat, pre_lat, (((1,), (1,)), ((), ())), preferred_element_type=jnp.float32
    )
    pre_scores = pre_scores + jnp.dot(flat_rope, pre_rope, preferred_element_type=jnp.float32)
    pre_scores = jnp.where(is_live[None, :], pre_scores * softmax_scale, NEG).reshape(
        beam_count, head_count, -1
    )
    row_max = jnp.maximum(row_max, jnp.max(pre_scores, axis=2))
    suf_weights = jnp.exp(suf_scores - row_max[..., None]).astype(jnp.bfloat16)
    weight_sum = jnp.sum(suf_weights.astype(jnp.float32), axis=2)
    weighted = jnp.einsum("bhs,bsl->bhl", suf_weights, suf_lat, preferred_element_type=jnp.float32)
    pre_weights = jnp.exp(pre_scores - row_max[..., None]).astype(jnp.bfloat16)
    weight_sum = weight_sum + jnp.sum(pre_weights.astype(jnp.float32), axis=2)
    prefix_part = jnp.dot(
        pre_weights.reshape(beam_count * head_count, -1),
        pre_lat,
        preferred_element_type=jnp.float32,
    )
    weighted = weighted + prefix_part.reshape(beam_count, head_count, lat_width)
    return (row_max, weight_sum, weighted)


def general_local(
    query_latent,
    query_rope,
    cache_latent,
    cache_rope,
    suffix_latent,
    suffix_rope,
    lengths,
    parents,
    w_uv,
    w_o,
    hidden,
    norm_gain,
    w_gate,
    w_up,
    w_down,
    expert_ids,
    gate_weights,
):
    q_lat, q_rope = (
        lax.all_gather(query_latent, "hx", axis=1, tiled=True),
        lax.all_gather(query_rope, "hx", axis=1, tiled=True),
    )
    head_count = q_lat.shape[1]
    q_rope = q_rope.reshape(HYPS, head_count, DR)
    softmax_scale = MSCALE * MSCALE / math.sqrt(DN + DR)
    n_hx = lax.axis_size("hx")
    linear = lax.axis_index("ctx") * n_hx + lax.axis_index("hx")
    ctx_block = cache_latent.shape[1]
    offsets = linear * ctx_block + jnp.arange(ctx_block, dtype=jnp.int32)
    suf_lat = jnp.take(suffix_latent, parents, axis=0)
    suf_rope = jnp.take(suffix_rope, parents, axis=0)
    maxima = []
    totals_list = []
    sums_list = []
    for request in range(REQ):
        hyp_rows = slice(request * BEAMS, (request + 1) * BEAMS)
        is_live = offsets < lengths[request]
        bound_stats = partial(
            request_stats,
            q_lat[hyp_rows],
            q_rope[hyp_rows],
            cache_latent[request],
            cache_rope[request],
            suf_lat[hyp_rows],
            suf_rope[hyp_rows],
            is_live,
            softmax_scale,
        )
        request_sums = bound_stats(True)
        maxima.append(request_sums[0])
        totals_list.append(request_sums[1])
        sums_list.append(request_sums[2])
    row_max = jnp.concatenate(maxima, axis=0)
    weight_sum = jnp.concatenate(totals_list, axis=0)
    weighted = jnp.concatenate(sums_list, axis=0)
    part_max, part_sum, part_acc = (
        lax.all_to_all(row_max[None], "ctx", split_axis=2, concat_axis=0, tiled=True),
        lax.all_to_all(weight_sum[None], "ctx", split_axis=2, concat_axis=0, tiled=True),
        lax.all_to_all(weighted[None], "ctx", split_axis=2, concat_axis=0, tiled=True),
    )
    group_max = jnp.max(part_max, axis=0)
    factor = jnp.exp(part_max - group_max[None])
    group_sum = jnp.sum(part_sum * factor, axis=0)
    group_acc = jnp.sum(part_acc * factor[..., None], axis=0)
    group_max, group_sum, group_acc = merged((group_max, group_sum, group_acc), "hx", merge_pair)
    attention = (group_acc / group_sum[..., None]).astype(jnp.bfloat16)
    columns = w_uv.shape[1]
    head_span = max(1, columns // DV)
    first_head = lax.axis_index("hx") * columns // DV
    chosen = lax.dynamic_slice_in_dim(attention, first_head, head_span, 1)
    value_map = w_uv.reshape(DL, head_span, columns // head_span)
    values = jnp.einsum("bnl,lnc->bnc", chosen, value_map, preferred_element_type=jnp.float32)
    values = values.astype(jnp.bfloat16).reshape(HYPS, columns)
    partial_out = jnp.dot(values, w_o, preferred_element_type=jnp.float32)
    attended = lax.psum(partial_out, ("ctx", "hx")).astype(jnp.bfloat16)
    residual = hidden.astype(jnp.float32) + attended.astype(jnp.float32)
    mean_square = jnp.mean(residual * residual, axis=1, keepdims=True)
    normed = (residual * lax.rsqrt(mean_square + 1e-06) * norm_gain).astype(jnp.bfloat16)
    unit_count = w_gate.shape[0]
    expert_here = linear * unit_count // EFF
    routed = jnp.sum(gate_weights * (expert_ids == expert_here).astype(jnp.float32), axis=1)
    gate_out = lax.dot_general(
        normed, w_gate, (((1,), (1,)), ((), ())), preferred_element_type=jnp.float32
    )
    up_out = lax.dot_general(
        normed, w_up, (((1,), (1,)), ((), ())), preferred_element_type=jnp.float32
    )
    activated = (jax.nn.silu(gate_out) * up_out * routed[:, None]).astype(jnp.bfloat16)
    expert_terms = jnp.dot(activated, w_down, preferred_element_type=jnp.float32)
    moe_share = lax.psum_scatter(expert_terms, ("ctx", "hx"), scatter_dimension=1, tiled=True)
    share_width = moe_share.shape[1]
    residual_share = lax.dynamic_slice_in_dim(residual, linear * share_width, share_width, 1)
    updated = (residual_share + moe_share).astype(jnp.bfloat16)
    return (attended, updated)


BF = jnp.bfloat16
F32 = jnp.float32
AXES = ("z", "x", "y", "core")
SHAPE = (4, 2, 2, 2)
CORE, Y, X, Z0, Z1 = 1, 2, 4, 8, 16
HEADS_DEV = 4
UNITS = 256
STAT = 16
LANES = 128
PARENTS = REQ
VMEM = pl.BlockSpec(memory_space=pltpu.VMEM)
SMEM = pl.BlockSpec(memory_space=pltpu.SMEM)
HBM = pl.BlockSpec(memory_space=pltpu.HBM)
NT = (((1,), (1,)), ((), ()))


def swap(value, mask):
    return lax.ppermute(value, AXES, [(i, i ^ mask) for i in range(math.prod(SHAPE))])


def in_hbm(value):
    return pltpu.with_memory_space_constraint(value, pltpu.HBM)


def bits(linear):
    return [linear >> k & 1 for k in range(5)]


def column(lane_row):
    n = lane_row.shape[1]
    at = lax.broadcasted_iota(jnp.int32, (n, n), 0)
    to = lax.broadcasted_iota(jnp.int32, (n, n), 1)
    return jnp.sum(jnp.where(at == to, lane_row, 0.0), axis=1, keepdims=True)


def stat_rows(lse):
    parts = []
    for _ in range(3):
        part = lse.astype(BF).astype(F32)
        parts.append(part)
        lse = lse - part
    return parts


def write_stat(out, body, parts, stat):
    stat[...] = jnp.zeros_like(stat)
    for i, part in enumerate(parts):
        stat[0:1, i * LANES:i * LANES + part.shape[1]] = part
    out[body:] = stat[...].astype(BF)


def read_stat(block, n):
    block = block.astype(F32)
    return (block[:1, :n] + block[:1, LANES:LANES + n]) + block[:1, 2 * LANES:2 * LANES + n]


def joined(lses):
    top = lses[0]
    for lse in lses[1:]:
        top = jnp.maximum(top, lse)
    weights = [jnp.exp(lse - top) for lse in lses]
    total = sum(weights[1:], weights[0])
    return [w / total for w in weights], top + jnp.log(total)


def attend_kernel(scale, first, count, fetch, later, info, ql0, ql1, qr0, qr1, cl_hbm, cr_hbm, sl_hbm, sr_hbm, *rest):
    earlier, rest = rest[:2 if later else 0], rest[-15:]
    keep, send, spread, qbuf, rbuf, pbuf, wide, lse_buf, stat, cl, cr, sl, sr, own_q, sems = rest
    linear = lax.axis_index(AXES)
    core, y, x, z0, _ = bits(linear)
    heads = ql1.shape[1]
    rows = 2 * heads
    total_rows = BEAMS * rows
    half = total_rows // 2
    targets = keep.shape[0]
    body = keep.shape[1] - STAT
    small = body // (2 * REQ)
    copies = []
    for k in range(count):
        beams = pl.ds((first + k) * BEAMS, BEAMS)
        here = pl.ds(k * BEAMS, BEAMS)
        group = [
            pltpu.make_async_copy(cl_hbm.at[first + k], cl.at[k], sems.at[0, k]),
            pltpu.make_async_copy(cr_hbm.at[first + k], cr.at[k], sems.at[1, k]),
            pltpu.make_async_copy(sl_hbm.at[beams], sl.at[here], sems.at[2, k]),
            pltpu.make_async_copy(sr_hbm.at[beams], sr.at[here], sems.at[3, k]),
        ]
        if fetch:
            group.append(pltpu.make_async_copy(ql0.at[here], own_q.at[here], sems.at[4, k]))
        for copy in group:
            copy.start()
        copies.append(group)
    first_q = own_q if fetch else ql0

    out_row = lax.broadcasted_iota(jnp.int32, (total_rows, total_rows), 0)
    in_row = lax.broadcasted_iota(jnp.int32, (total_rows, total_rows), 1)

    def source_of(row):
        bit = lambda k: (row >> k) & 1
        beam, head = (row >> 2) & 3, row & 3
        target = (bit(6) ^ x) * 4 + (bit(5) ^ y) * 2 + (bit(7) ^ core)
        return beam * rows + (bit(4) ^ core ^ z0) * heads + target * HEADS_DEV + head

    spread[...] = jnp.where(source_of(out_row) == in_row, 1.0, 0.0).astype(BF)
    moves = source_of(in_row) == out_row
    for i, out in enumerate((keep, send)):
        for t in range(targets):
            if later:
                out[t] = earlier[i][t]
                lse_buf[i * targets + t:i * targets + t + 1] = read_stat(earlier[i][t, body:], body)
            else:
                lse_buf[i * targets + t:i * targets + t + 1] = jnp.zeros((1, body), F32)
    wide[0] = qr0[...].astype(F32)
    wide[1] = qr1[...].astype(F32)
    per_group = LANES // DR
    head_row = lax.broadcasted_iota(jnp.int32, (heads, LANES), 0)
    own_lanes = lax.broadcasted_iota(jnp.int32, (heads, LANES), 1) // DR == head_row % per_group

    for k in range(count):
        r = first + k
        for copy in copies[k]:
            copy.wait()
        for j in range(BEAMS):
            for piece, q in enumerate((first_q, ql1)):
                part = slice(j * rows + piece * heads, j * rows + (piece + 1) * heads)
                qbuf[part] = q[k * BEAMS + j]
                b = r * BEAMS + j
                unfolded = jnp.zeros((heads, LANES), F32)
                for g in range(heads // per_group):
                    lanes = wide[piece, b:b + 1, g * LANES:(g + 1) * LANES]
                    unfolded = jnp.where(head_row // per_group == g, lanes, unfolded)
                rbuf[part] = jnp.where(own_lanes, unfolded, 0.0).astype(BF)
        keys = cl[k]
        ctx_block = keys.shape[0]
        pre = lax.dot_general(qbuf[...], keys, NT, preferred_element_type=F32)
        pre = pre + jnp.dot(rbuf[...], jnp.concatenate([cr[k]] * per_group, axis=0), preferred_element_type=F32)
        position = linear * ctx_block + lax.broadcasted_iota(jnp.int32, (1, ctx_block), 1)
        pre = jnp.where(position < info[r], pre * scale, NEG)
        own = [info[PARENTS + r * BEAMS + j] - first * BEAMS for j in range(BEAMS)]
        suf = []
        for j in range(BEAMS):
            part = slice(j * rows, (j + 1) * rows)
            s = lax.dot_general(qbuf[part], sl[own[j]], NT, preferred_element_type=F32)
            s = s + jnp.dot(rbuf[part], jnp.concatenate([sr[own[j]]] * per_group, axis=0),
                            preferred_element_type=F32)
            suf.append(s * scale)
        suf = jnp.concatenate(suf, axis=0)
        top = jnp.maximum(jnp.max(pre, axis=1, keepdims=True), jnp.max(suf, axis=1, keepdims=True))
        pre_w = jnp.exp(pre - top).astype(BF)
        suf_w = jnp.exp(suf - top).astype(BF)
        total = jnp.sum(pre_w.astype(F32), axis=1, keepdims=True)
        total = total + jnp.sum(suf_w.astype(F32), axis=1, keepdims=True)
        acc = jnp.dot(pre_w, keys, preferred_element_type=F32)
        inv = 1.0 / total
        for j in range(BEAMS):
            part = slice(j * rows, (j + 1) * rows)
            a = acc[part] + jnp.dot(suf_w[part], sl[own[j]], preferred_element_type=F32)
            pbuf[part] = (a * inv[part]).astype(BF)
        moved = jnp.dot(spread[...], pbuf[...], preferred_element_type=F32).astype(BF)
        lse = top + jnp.log(total)
        lane_lse = jnp.sum(jnp.where(moves, lse, 0.0), axis=0, keepdims=True)
        for i, out in enumerate((keep, send)):
            for t in range(targets):
                for zz in range(2):
                    at = i * half + (2 * t + zz) * small
                    to = (zz * REQ + r) * small
                    out[t, to:to + small] = moved[at:at + small]
                    lse_buf[i * targets + t:i * targets + t + 1, to:to + small] = lane_lse[:, at:at + small]
    parts = stat_rows(lse_buf[...])
    for i, out in enumerate((keep, send)):
        for t in range(targets):
            n = i * targets + t
            write_stat(out.at[t], body, [p[n:n + 1] for p in parts], stat)


def attend(scale, first, count, info, q_lat, q_rope, caches, earlier=()):
    fetch = first == 0 and count == REQ
    heads, width = q_lat[0].shape[1:]
    total_rows = BEAMS * 2 * heads
    targets = SHAPE[1] * SHAPE[2]
    body = REQ * total_rows // (2 * targets)
    message = jax.ShapeDtypeStruct((targets, body + STAT, width), BF)
    keys = caches[0].shape[1] + caches[2].shape[1]
    own_q = q_lat[0].shape if fetch else (8, LANES)
    return pl.pallas_call(
        partial(attend_kernel, scale, first, count, fetch, bool(earlier)),
        in_specs=[SMEM, HBM if fetch else VMEM] + [VMEM] * 3 + [HBM] * 4 + [VMEM] * len(earlier),
        out_specs=[VMEM] * 2,
        out_shape=[message] * 2,
        scratch_shapes=[
            pltpu.VMEM((total_rows, total_rows), BF),
            pltpu.VMEM((total_rows, width), BF),
            pltpu.VMEM((total_rows, LANES), BF),
            pltpu.VMEM((total_rows, width), BF),
            pltpu.VMEM((2, *q_rope[0].shape), F32),
            pltpu.VMEM((2 * targets, body), F32),
            pltpu.VMEM((STAT, width), F32),
        ] + [pltpu.VMEM((c.shape[0] * count // REQ, *c.shape[1:]), BF) for c in caches]
        + [pltpu.VMEM(own_q, BF), pltpu.SemaphoreType.DMA((5, count))],
        compiler_params=pltpu.CompilerParams(vmem_limit_bytes=14 << 20),
        cost_estimate=pl.CostEstimate(
            flops=count * 2 * total_rows * keys * (2 * width + DR), bytes_accessed=2 * count << 20,
            transcendentals=count * total_rows * keys),
        name="attend",
    )(info, in_hbm(q_lat[0]) if fetch else q_lat[0], q_lat[1], *q_rope, *(in_hbm(c) for c in caches), *earlier)


def pair_kernel(a, b, *rest):
    outs, stat = rest[:-1], rest[-1]
    targets, rows, _ = a.shape
    body = rows - STAT
    each = targets // len(outs)
    for t in range(targets):
        weights, lse = joined([read_stat(v[t, body:], body) for v in (a, b)])
        out = outs[t // each].at[t % each]
        out[:body] = (a[t, :body].astype(F32) * column(weights[0])
                      + b[t, :body].astype(F32) * column(weights[1])).astype(BF)
        write_stat(out, body, stat_rows(lse), stat)


def merge_pair_of(a, b, parts):
    return pl.pallas_call(
        pair_kernel,
        in_specs=[VMEM] * 2,
        out_specs=[VMEM] * parts,
        out_shape=[jax.ShapeDtypeStruct((a.shape[0] // parts, *a.shape[1:]), BF)] * parts,
        scratch_shapes=[pltpu.VMEM((STAT, a.shape[2]), F32)],
        compiler_params=pltpu.CompilerParams(vmem_limit_bytes=4 << 20),
        cost_estimate=pl.CostEstimate(flops=4 * a.size, bytes_accessed=6 * a.size, transcendentals=0),
        name="merge_pair",
    )(a, b)


def plane_kernel(count, *refs):
    groups = refs[:count], refs[count:2 * count]
    outs, (stat, held) = refs[2 * count:-2], refs[-2:]
    body = refs[0].shape[1] - STAT
    small = body // 2
    _, y, _, _, z1 = bits(lax.axis_index(AXES))
    for other, sources in enumerate(groups):
        weights, lse = joined([read_stat(ref[0, body:], body) for ref in sources])
        parts = stat_rows(lse)
        columns = [column(w) for w in weights]
        for z0 in range(2):
            part = slice(z0 * small, (z0 + 1) * small)
            total = None
            for ref, w in zip(sources, columns):
                term = ref[0, part].astype(F32) * w[part]
                total = term if total is None else total + term
            held[2 * other + z0, :small] = total.astype(BF)
            write_stat(held.at[2 * other + z0], small, [p[:, part] for p in parts], stat)
    for d, out in enumerate(outs):
        out[...] = held[2 * ((d >> 1) ^ y ^ z1) + (d & 1)]


def merge_plane(same, other):
    _, rows, width = same[0].shape
    shape = ((rows - STAT) // 2 + STAT, width)
    return pl.pallas_call(
        partial(plane_kernel, len(same)),
        in_specs=[VMEM] * 2 * len(same),
        out_specs=[VMEM] * SHAPE[0],
        out_shape=[jax.ShapeDtypeStruct(shape, BF)] * SHAPE[0],
        scratch_shapes=[pltpu.VMEM((STAT, width), F32), pltpu.VMEM((SHAPE[0], *shape), BF)],
        compiler_params=pltpu.CompilerParams(vmem_limit_bytes=4 << 20),
        cost_estimate=pl.CostEstimate(flops=16 * rows * width, bytes_accessed=24 * rows * width, transcendentals=0),
        name="merge_plane",
    )(*same, *other)


def sum_kernel(a, b, *outs):
    each = a.shape[0] // len(outs)
    for i, out in enumerate(outs):
        part = slice(i * each, (i + 1) * each)
        out[...] = (a[part].astype(F32) + b[part].astype(F32)).astype(out.dtype)


def stack_kernel(a, b, out):
    out[:a.shape[0]] = a[...]
    out[a.shape[0]:] = b[...]


def small_call(kernel, name, a, b, outs):
    return pl.pallas_call(
        kernel,
        in_specs=[VMEM] * 2,
        out_specs=[VMEM] * len(outs),
        out_shape=[jax.ShapeDtypeStruct(shape, BF) for shape in outs],
        compiler_params=pltpu.CompilerParams(vmem_limit_bytes=4 << 20),
        cost_estimate=pl.CostEstimate(flops=a.size, bytes_accessed=6 * a.size, transcendentals=0),
        name=name,
    )(a, b)


def halves(a, b):
    return small_call(sum_kernel, "halves", a, b, [(a.shape[0] // 2, *a.shape[1:])] * 2)


def plus(a, b):
    return small_call(sum_kernel, "plus", a, b, [a.shape])[0]


def cut_line(a, b):
    _, n, *tail = a.shape
    return halves(a.reshape(n, *tail), b.reshape(n, *tail))


def stacked(a, b):
    return small_call(stack_kernel, "stacked", a, b, [(2 * a.shape[0], *a.shape[1:])])[0]


def project_kernel(p0, p1, p2, p3, w_uv, w_o, keep, send):
    parts = (p0, p1, p2, p3)
    rows, _ = p0.shape
    body = rows - STAT
    weights, _ = joined([read_stat(p[body:], body) for p in parts])
    total = None
    for p, w in zip(parts, weights):
        term = p[:body].astype(F32) * column(w)
        total = term if total is None else total + term
    full = jnp.dot(total.astype(BF), w_uv[...], preferred_element_type=F32)
    rows, columns = full.shape
    row = lax.broadcasted_iota(jnp.int32, (rows, columns), 0)
    lane = lax.broadcasted_iota(jnp.int32, (rows, columns), 1)
    own = jnp.where((row & (HEADS_DEV - 1)) == lane // DV, full, 0.0).astype(BF)
    pick_hyp = lax.broadcasted_iota(jnp.int32, (HYPS, rows), 0)
    pick_row = lax.broadcasted_iota(jnp.int32, (HYPS, rows), 1)
    pick = jnp.where(pick_row // HEADS_DEV == pick_hyp, 1.0, 0.0).astype(BF)
    values = jnp.dot(pick, own, preferred_element_type=F32).astype(BF)
    width = keep.shape[2]
    plane = lax.axis_index(AXES) & 7
    for there, out in enumerate((keep, send)):
        for t in range(out.shape[0]):
            at = pl.multiple_of((plane ^ (2 * t + there)) * width, LANES)
            piece = jnp.dot(values, w_o[:, pl.ds(at, width)], preferred_element_type=F32)
            out[t] = piece.astype(BF)


def project(parts, w_uv, w_o):
    squares = SHAPE[1] * SHAPE[2]
    out = jax.ShapeDtypeStruct((squares, HYPS, w_o.shape[1] // (2 * squares)), BF)
    return pl.pallas_call(
        project_kernel,
        in_specs=[VMEM] * 6,
        out_specs=[VMEM] * 2,
        out_shape=[out] * 2,
        compiler_params=pltpu.CompilerParams(vmem_limit_bytes=4 << 20),
        cost_estimate=pl.CostEstimate(flops=2 * HYPS * w_o.size, bytes_accessed=2 * w_o.size, transcendentals=0),
        name="project",
    )(*parts, w_uv, w_o)


def experts_kernel(here, there, hidden, gain, ids, gates, w_gate, up_hbm, down_hbm,
                   attended, keep, send, residual, x_buf, acc, x_held, held, w_up, w_down, sems):
    units = w_gate.shape[0]
    chunks = units // UNITS
    copies = []
    for i, (source, dest) in enumerate(((up_hbm, w_up), (down_hbm, w_down))):
        for k in range(chunks):
            part = pl.ds(k * UNITS, UNITS)
            copy = pltpu.make_async_copy(source.at[part], dest.at[part], sems.at[i, k])
            copy.start()
            copies.append(copy)
    linear = lax.axis_index(AXES)
    plane, depth = linear & 7, linear >> 3
    share = here.shape[2]
    for core, shares in enumerate((here, there)):
        for t in range(shares.shape[0]):
            at = pl.multiple_of((plane ^ (2 * t + core)) * share, LANES)
            x_buf[:, pl.ds(at, share)] = shares[t].astype(F32)
            attended[:, pl.ds(at, share)] = shares[t]
    x = x_buf[...] + hidden[...].astype(F32)
    mean_square = jnp.mean(x * x, axis=1, keepdims=True)
    normed = (x * lax.rsqrt(mean_square + 1e-06) * gain[...]).astype(BF)
    expert = linear * units // EFF
    routed = column(jnp.sum(jnp.where(ids[...] == expert, gates[...], 0.0), axis=0, keepdims=True))
    parts = [slice(k * UNITS, (k + 1) * UNITS) for k in range(chunks)]
    gate = [lax.dot_general(normed, w_gate[part], NT, preferred_element_type=F32) for part in parts]
    gate = [g / (1.0 + jnp.exp(-g)) * routed for g in gate]
    act = []
    for k, part in enumerate(parts):
        copies[k].wait()
        up = lax.dot_general(normed, w_up[part], NT, preferred_element_type=F32)
        act.append((gate[k] * up).astype(BF))
    for k, part in enumerate(parts):
        copies[chunks + k].wait()
        term = jnp.dot(act[k], w_down[part], preferred_element_type=F32)
        if k == 0:
            acc[...] = term
        else:
            acc[...] += term
    count, _, width = held.shape
    for d in range(count):
        x_held[d] = x[:, d * width:(d + 1) * width]
        held[d] = acc[:, d * width:(d + 1) * width].astype(BF)
    residual[...] = x_held[linear]
    for core, out in enumerate((keep, send)):
        for t in range(out.shape[0]):
            for z in range(out.shape[1]):
                out[t, z] = held[((depth ^ z) << 3) + (plane ^ (2 * t + core))]


def experts(here, there, hidden, gain, ids, gates, w_gate, w_up, w_down):
    units, width = w_gate.shape
    squares = SHAPE[1] * SHAPE[2]
    small = width // (2 * squares * SHAPE[0])
    terms = jax.ShapeDtypeStruct((squares, SHAPE[0], HYPS, small), BF)
    return pl.pallas_call(
        experts_kernel,
        in_specs=[VMEM] * 7 + [HBM] * 2,
        out_specs=[VMEM] * 4,
        out_shape=[
            jax.ShapeDtypeStruct((HYPS, width), BF), terms, terms,
            jax.ShapeDtypeStruct((HYPS, small), F32),
        ],
        scratch_shapes=[pltpu.VMEM((HYPS, width), F32)] * 2 + [
            pltpu.VMEM((2 * squares * SHAPE[0], HYPS, small), F32),
            pltpu.VMEM((2 * squares * SHAPE[0], HYPS, small), BF),
        ] + [pltpu.VMEM((units, width), BF)] * 2 + [pltpu.SemaphoreType.DMA((2, units // UNITS))],
        compiler_params=pltpu.CompilerParams(vmem_limit_bytes=36 << 20),
        cost_estimate=pl.CostEstimate(flops=6 * HYPS * units * width, bytes_accessed=6 * units * width,
                                      transcendentals=HYPS * units),
        name="experts",
    )(here, there, hidden, gain, ids, gates, w_gate, in_hbm(w_up), in_hbm(w_down))


def local(
    query_latent,
    query_rope,
    cache_latent,
    cache_rope,
    suffix_latent,
    suffix_rope,
    lengths,
    parents,
    w_uv,
    w_o,
    hidden,
    norm_gain,
    w_gate,
    w_up,
    w_down,
    expert_ids,
    gate_weights,
):
    scale = MSCALE * MSCALE / math.sqrt(DN + DR)
    info = jnp.concatenate([lengths, parents])
    caches = (cache_latent, cache_rope, suffix_latent, suffix_rope)
    cut = HYPS // 2
    tied = lax.optimization_barrier

    near_lat, near_rope = swap(query_latent, CORE), swap(query_rope, CORE)
    lat_a = swap(query_latent[:cut], Y)
    far_rope = swap(query_rope, Y)
    lat_b = swap(query_latent[cut:], Y)
    keep, send = attend(scale, 0, REQ, info, (query_latent, near_lat), (query_rope, near_rope), caches)
    lat_a, far_rope, send = tied((lat_a, far_rope, send))
    far_rope = far_rope, swap(far_rope, CORE)
    near = merge_pair_of(keep, swap(send, CORE), 2)
    keep, send = attend(scale, 0, REQ // 2, info, (lat_a, swap(lat_a, CORE)), far_rope, caches)
    lat_b, send = tied((lat_b, send))
    near = merge_pair_of(near[0], swap(near[1], X), 2)
    keep, send = attend(scale, REQ // 2, REQ // 2, info, (lat_b, swap(lat_b, CORE)), far_rope, caches, (keep, send))
    far = merge_pair_of(keep, swap(send, CORE), SHAPE[1] * SHAPE[2])
    far_y, far_x, far_xy = (swap(v, mask) for v, mask in zip(far[1:], (Y, X, X ^ Y)))
    parts = merge_plane((near[0], far_y, far_xy), (swap(near[1], Y), far[0], far_x))
    parts = [parts[0], *(swap(v, mask) for v, mask in zip(parts[1:], (Z0, Z1, Z0 ^ Z1)))]
    keep, send = project(parts, w_uv, w_o)

    keep, send = halves(keep, swap(send, CORE))
    keep, send = halves(keep, swap(send, X))
    share = plus(keep, swap(send, Y))
    share = plus(share, swap(share, Z0))
    share = plus(share, swap(share, Z1))
    shares = stacked(share, swap(share, Y))
    shares = stacked(shares, swap(shares, X))
    attended, keep, send, residual = experts(
        shares, swap(shares, CORE), hidden, norm_gain.reshape(1, -1), expert_ids.T, gate_weights.T, w_gate, w_up, w_down)

    keep, send = halves(keep, swap(send, CORE))
    keep, send = halves(keep, swap(send, X))
    keep, send = cut_line(keep, swap(send, Y))
    keep, send = halves(keep, swap(send, Z1))
    total = keep.astype(F32) + swap(send, Z0).astype(F32)
    updated = (residual + total[0]).astype(BF)
    return (attended, updated)


def solution(mesh):
    if mesh.shape["ctx"] == SHAPE[0] * SHAPE[1] and mesh.shape["hx"] == SHAPE[2] * SHAPE[3]:
        chosen, names = local, AXES
        mesh = jax.sharding.Mesh(mesh.devices.reshape(SHAPE), AXES)
    else:
        chosen, names = general_local, ("ctx", "hx")
    all_axes, hx = names, names[len(names) // 2:]
    in_specs = (
        P(None, hx, None),
        P(None, hx),
        P(None, all_axes, None),
        P(None, None, all_axes),
        P(None, all_axes, None),
        P(None, None, all_axes),
        P(),
        P(),
        P(None, all_axes),
        P(all_axes, None),
        P(),
        P(),
        P(all_axes, None),
        P(all_axes, None),
        P(all_axes, None),
        P(),
        P(),
    )
    out_specs = (P(), P(None, all_axes))
    return jax.shard_map(chosen, mesh=mesh, in_specs=in_specs, out_specs=out_specs, check_vma=False)
```

time: 142 us -> 125 us (0.88)
  waiting for transfers between devices: 27.1 us -> 56.5 us
  local copies, waits for them, and re-layouts: 26.8 us -> 2.36 us
  Pallas kernels: 48.8 us -> 32.6 us
  starting transfers between devices: 36.9 us -> 31.1 us
    ppermute x38 -> x31, waiting for transfers between devices: 27.1 us -> 56.5 us  [swap(): lax.ppermute(value, AXES, [(i, i ^ mask) for i in range(math.prod(SHAPE))])]
    unnamed x26 -> x24, local copies, waits for them, and re-layouts: 25.8 us -> 1.03 us
    pallas_call x16 -> x20, Pallas kernels: 48.8 us -> 32.6 us  [the longest x3 15.5 us: attend(): pl.pallas_call(partial(attend_kernel, scale, first, count, fetch, bool(ea...]
    ppermute x38 -> x31, starting transfers between devices: 36.9 us -> 31.1 us  [swap(): lax.ppermute(value, AXES, [(i, i ^ mask) for i in range(math.prod(SHAPE))])]
  transfers between devices with their start and end apart: 38 -> 31, of which waited for: 19 -> 22; matrix products, arithmetic and copies ran while one was open for 1% -> 2% of each run, Pallas kernels for 23% -> 13%
where the time goes in v2:
time: 125 us
  waiting for transfers between devices  56.5 us (45%)
  Pallas kernels  32.6 us (26%)
  starting transfers between devices  31.1 us (25%)
  local copies, waits for them, and re-layouts  2.36 us (2%)
  other arithmetic  1.35 us (1%)
    ppermute x31, waiting for transfers between devices, swap(): lax.ppermute(value, AXES, [(i, i ^ mask) for i in range(math.prod(SHAPE))])  56.5 us
    ppermute x31, starting transfers between devices, swap(): lax.ppermute(value, AXES, [(i, i ^ mask) for i in range(math.prod(SHAPE))])  31.1 us
    pallas_call x3, Pallas kernels, attend(): pl.pallas_call(partial(attend_kernel, scale, first, count, fetch, bool(ea...  15.5 us
    pallas_call x1, Pallas kernels, experts(): pl.pallas_call(experts_kernel, in_specs=[VMEM] * 7 + [HBM] * 2, out_specs...  14.3 us
  transfers between devices with their start and end apart: 31, of which 22 were waited for; matrix products, arithmetic and copies ran while one was open for 2% of the time, Pallas kernels for 13%

profile of v2, /device:TPU:0, one launch (start us, length us, event | category | flops | bytes accessed | tf_op | source)
XLA Modules:
  0.0 124.8 jit_solution(10940337772577771296)
XLA Ops:
  1.2 1.3 %fusion.1 = (bf16[8,32,512]{2,1,0:T(8,128)(2,1)S(1)}, bf16[8,32,512]{2,1,0:T(8,128)(2,1)S(1)}) fusion(bf16[16,32,512]{2,1,0:T(8,128)(2,1)} %ql0.1), kind=kLoop, calls=%fused_computation.3 | loop fusion | bytes 1048576 | tf_op jit(solution)/shard_map/slice | solution.py:631
  2.5 2.5 %collective-permute-start.2 = (bf16[8,32,512]{2,1,0:T(8,128)(2,1)S(1)}, bf16[8,32,512]{2,1,0:T(8,128)(2,1)S(1)}, u32[]{:S(2)}, u32[]{:S(2)}) collective-permute-start(bf16[8,32,512]{2,1,0:T(8,128)(2,1)S(1)} %get-tuple-element.85), channel_id=1, source_target_pairs={{0,2},{1,3},{2,0},{3,1},{4,6},{5,7},{6,4},{7,5},{8,10},{9,11},{10,... | collective-permute-start | bytes 786440 | tf_op jit(solution)/shard_map/ppermute | solution.py:194
  5.8 0.7 pad_add_fusion.info
  6.6 1.0 copy-done.2
  7.5 6.7 %attend.3 = (bf16[4,144,512]{2,1,0:T(8,128)(2,1)S(1)}, bf16[4,144,512]{2,1,0:T(8,128)(2,1)S(1)}) custom-call(s32[20]{0:T(128)S(1)} %pad_add_fusion.info, bf16[16,32,512]{2,1,0:T(8,128)(2,1)} %ql0.1, bf16[16,32,512]{2,1,0:T(8,128)(2,1)S(1)} %collective-permute-done.ql1, bf16[16,2048]{1,0:T(8,128)(2,1)S(1)} %copy-done.2, ...), custom_call_target="tpu_custom_call" | custom-call | flops 1426063360 | bytes 8388608 | tf_op jit(solution)/shard_map/attend/pallas_call | solution.py:361
  14.3 0.5 collective-permute-start.7
  14.9 1.3 %collective-permute-start.6 = (bf16[8,32,512]{2,1,0:T(8,128)(2,1)S(1)}, bf16[8,32,512]{2,1,0:T(8,128)(2,1)S(1)}, u32[]{:S(2)}, u32[]{:S(2)}) collective-permute-start(bf16[8,32,512]{2,1,0:T(8,128)(2,1)S(1)} %get-tuple-element.84), channel_id=1, source_target_pairs={{0,2},{1,3},{2,0},{3,1},{4,6},{5,7},{6,4},{7,5},{8,10},{9,11},{10,... | collective-permute-start | bytes 786440 | tf_op jit(solution)/shard_map/ppermute | solution.py:194
  16.3 1.1 collective-permute-done.8.qr1
  17.4 4.2 %attend.4 = (bf16[4,144,512]{2,1,0:T(8,128)(2,1)S(1)}, bf16[4,144,512]{2,1,0:T(8,128)(2,1)S(1)}) custom-call(s32[20]{0:T(128)S(1)} %pad_add_fusion.info, bf16[8,32,512]{2,1,0:T(8,128)(2,1)S(1)} %collective-permute-done.2.ql0, bf16[8,32,512]{2,1,0:T(8,128)(2,1)S(1)} %collective-permute-done.7.ql1, bf16[16,2048]{1,0:T(8,128)(2,1)S(1)} %collective-permute-done.3.qr0, ...), custom_call_target="tpu_custom_call" | custom-call | flops 713031680 | bytes 4194304 | tf_op jit(solution)/shard_map/attend/pallas_call | solution.py:361
  21.7 1.5 %collective-permute-done.6.ql0 = bf16[8,32,512]{2,1,0:T(8,128)(2,1)S(1)} collective-permute-done((bf16[8,32,512]{2,1,0:T(8,128)(2,1)S(1)}, bf16[8,32,512]{2,1,0:T(8,128)(2,1)S(1)}, u32[]{:S(2)}, u32[]{:S(2)}) %collective-permute-start.6) | collective-permute-done | bytes 262176 | tf_op jit(solution)/shard_map/ppermute | solution.py:194
  23.7 1.0 collective-permute-done.9.ql1
  24.7 4.5 %attend.5 = (bf16[4,144,512]{2,1,0:T(8,128)(2,1)S(1)}, bf16[4,144,512]{2,1,0:T(8,128)(2,1)S(1)}) custom-call(s32[20]{0:T(128)S(1)} %pad_add_fusion.info, bf16[8,32,512]{2,1,0:T(8,128)(2,1)S(1)} %collective-permute-done.6.ql0, bf16[8,32,512]{2,1,0:T(8,128)(2,1)S(1)} %collective-permute-done.9.ql1, bf16[16,2048]{1,0:T(8,128)(2,1)S(1)} %collective-permute-done.3.qr0, ...), custom_call_target="tpu_custom_call" | custom-call | flops 713031680 | bytes 4194304 | tf_op jit(solution)/shard_map/attend/pallas_call | solution.py:361
  29.8 1.7 %collective-permute-start.5 = (bf16[2,144,512]{2,1,0:T(8,128)(2,1)S(1)}, bf16[2,144,512]{2,1,0:T(8,128)(2,1)S(1)}, u32[]{:S(2)}, u32[]{:S(2)}) collective-permute-start(bf16[2,144,512]{2,1,0:T(8,128)(2,1)S(1)} %get-tuple-element.47), channel_id=1, source_target_pairs={{0,4},{1,5},{2,6},{3,7},{4,0},{5,1},{6,2},{7,3},{8,12},{9,13},{10,... | collective-permute-start | bytes 884744 | tf_op jit(solution)/shard_map/ppermute | solution.py:194
  31.4 7.7 %collective-permute-done.5.b = bf16[2,144,512]{2,1,0:T(8,128)(2,1)S(1)} collective-permute-done((bf16[2,144,512]{2,1,0:T(8,128)(2,1)S(1)}, bf16[2,144,512]{2,1,0:T(8,128)(2,1)S(1)}, u32[]{:S(2)}, u32[]{:S(2)}) %collective-permute-start.5) | collective-permute-done | bytes 294944 | tf_op jit(solution)/shard_map/ppermute | solution.py:194
  39.3 1.7 %collective-permute-start.13 = (bf16[1,144,512]{2,1,0:T(8,128)(2,1)S(1)}, bf16[1,144,512]{2,1,0:T(8,128)(2,1)S(1)}, u32[]{:S(2)}, u32[]{:S(2)}) collective-permute-start(bf16[1,144,512]{2,1,0:T(8,128)(2,1)S(1)} %get-tuple-element.59), channel_id=1, source_target_pairs={{0,2},{1,3},{2,0},{3,1},{4,6},{5,7},{6,4},{7,5},{8,10},{9,11},{10,... | collective-permute-start | bytes 442376 | tf_op jit(solution)/shard_map/ppermute | solution.py:194
  41.8 2.5 %collective-permute-start.12 = (bf16[1,144,512]{2,1,0:T(8,128)(2,1)S(1)}, bf16[1,144,512]{2,1,0:T(8,128)(2,1)S(1)}, u32[]{:S(2)}, u32[]{:S(2)}) collective-permute-start(bf16[1,144,512]{2,1,0:T(8,128)(2,1)S(1)} %get-tuple-element.58), channel_id=1, source_target_pairs={{0,6},{1,7},{2,4},{3,5},{4,2},{5,3},{6,0},{7,1},{8,14},{9,15},{10,... | collective-permute-start | bytes 442376 | tf_op jit(solution)/shard_map/ppermute | solution.py:194
  44.4 0.5 collective-permute-start.14
  44.9 4.4 %collective-permute-done.13.refs_3_ = bf16[1,144,512]{2,1,0:T(8,128)(2,1)S(1)} collective-permute-done((bf16[1,144,512]{2,1,0:T(8,128)(2,1)S(1)}, bf16[1,144,512]{2,1,0:T(8,128)(2,1)S(1)}, u32[]{:S(2)}, u32[]{:S(2)}) %collective-permute-start.13) | collective-permute-done | bytes 147488 | tf_op jit(solution)/shard_map/ppermute | solution.py:194
  49.3 1.7 %collective-permute-done.11.refs_1_ = bf16[1,144,512]{2,1,0:T(8,128)(2,1)S(1)} collective-permute-done((bf16[1,144,512]{2,1,0:T(8,128)(2,1)S(1)}, bf16[1,144,512]{2,1,0:T(8,128)(2,1)S(1)}, u32[]{:S(2)}, u32[]{:S(2)}) %collective-permute-start.11) | collective-permute-done | bytes 147488 | tf_op jit(solution)/shard_map/ppermute | solution.py:194
  51.4 1.7 %collective-permute-start.15 = (bf16[80,512]{1,0:T(8,128)(2,1)S(1)}, bf16[80,512]{1,0:T(8,128)(2,1)S(1)}, u32[]{:S(2)}, u32[]{:S(2)}) collective-permute-start(bf16[80,512]{1,0:T(8,128)(2,1)S(1)} %get-tuple-element.63), channel_id=1, source_target_pairs={{0,8},{1,9},{2,10},{3,11},{4,12},{5,13},{6,14},{7,15},{8,0},{9,1},... | collective-permute-start | bytes 245768 | tf_op jit(solution)/shard_map/ppermute | solution.py:194
  53.1 2.6 %collective-permute-start.16 = (bf16[80,512]{1,0:T(8,128)(2,1)S(1)}, bf16[80,512]{1,0:T(8,128)(2,1)S(1)}, u32[]{:S(2)}, u32[]{:S(2)}) collective-permute-start(bf16[80,512]{1,0:T(8,128)(2,1)S(1)} %get-tuple-element.64), channel_id=1, source_target_pairs={{0,16},{1,17},{2,18},{3,19},{4,20},{5,21},{6,22},{7,23},{8,24},{9,... | collective-permute-start | bytes 245768 | tf_op jit(solution)/shard_map/ppermute | solution.py:194
  55.8 0.8 collective-permute-done.15.p1
  56.6 3.6 %collective-permute-done.16.p2 = bf16[80,512]{1,0:T(8,128)(2,1)S(1)} collective-permute-done((bf16[80,512]{1,0:T(8,128)(2,1)S(1)}, bf16[80,512]{1,0:T(8,128)(2,1)S(1)}, u32[]{:S(2)}, u32[]{:S(2)}) %collective-permute-start.16) | collective-permute-done | bytes 81952 | tf_op jit(solution)/shard_map/ppermute | solution.py:194
  60.2 1.8 %collective-permute-done.17.p3 = bf16[80,512]{1,0:T(8,128)(2,1)S(1)} collective-permute-done((bf16[80,512]{1,0:T(8,128)(2,1)S(1)}, bf16[80,512]{1,0:T(8,128)(2,1)S(1)}, u32[]{:S(2)}, u32[]{:S(2)}) %collective-permute-start.17) | collective-permute-done | bytes 81952 | tf_op jit(solution)/shard_map/ppermute | solution.py:194
  62.0 1.4 %project.1 = (bf16[4,16,896]{2,1,0:T(8,128)(2,1)S(1)}, bf16[4,16,896]{2,1,0:T(8,128)(2,1)S(1)}) custom-call(bf16[80,512]{1,0:T(8,128)(2,1)S(1)} %get-tuple-element.62.p0, bf16[80,512]{1,0:T(8,128)(2,1)S(1)} %collective-permute-done.15.p1, bf16[80,512]{1,0:T(8,128)(2,1)S(1)} %collective-permute-done.16.p2, bf16[80,512]{1,0:T(8,128)(2,1)S(1)} %collective-permute-done.17.p3, ...), custom_call_target="tpu_custom_call" | custom-call | flops 117440512 | bytes 7340032 | tf_op jit(solution)/shard_map/project/pallas_call | solution.py:518
  63.5 1.3 %collective-permute-done.18.b = bf16[4,16,896]{2,1,0:T(8,128)(2,1)S(1)} collective-permute-done((bf16[4,16,896]{2,1,0:T(8,128)(2,1)S(1)}, bf16[4,16,896]{2,1,0:T(8,128)(2,1)S(1)}, u32[]{:S(2)}, u32[]{:S(2)}) %collective-permute-start.18) | collective-permute-done | bytes 114720 | tf_op jit(solution)/shard_map/ppermute | solution.py:194
  64.9 1.5 %collective-permute-start.19 = (bf16[2,16,896]{2,1,0:T(8,128)(2,1)S(1)}, bf16[2,16,896]{2,1,0:T(8,128)(2,1)S(1)}, u32[]{:S(2)}, u32[]{:S(2)}) collective-permute-start(bf16[2,16,896]{2,1,0:T(8,128)(2,1)S(1)} %get-tuple-element.69), channel_id=1, source_target_pairs={{0,4},{1,5},{2,6},{3,7},{4,0},{5,1},{6,2},{7,3},{8,12},{9,13},{10,... | collective-permute-start | bytes 172040 | tf_op jit(solution)/shard_map/ppermute | solution.py:194
  66.4 2.7 %collective-permute-done.19.b = bf16[2,16,896]{2,1,0:T(8,128)(2,1)S(1)} collective-permute-done((bf16[2,16,896]{2,1,0:T(8,128)(2,1)S(1)}, bf16[2,16,896]{2,1,0:T(8,128)(2,1)S(1)}, u32[]{:S(2)}, u32[]{:S(2)}) %collective-permute-start.19) | collective-permute-done | bytes 57376 | tf_op jit(solution)/shard_map/ppermute | solution.py:194
  69.1 1.6 %collective-permute-start.20 = (bf16[1,16,896]{2,1,0:T(8,128)(2,1)S(1)}, bf16[1,16,896]{2,1,0:T(8,128)(2,1)S(1)}, u32[]{:S(2)}, u32[]{:S(2)}) collective-permute-start(bf16[1,16,896]{2,1,0:T(8,128)(2,1)S(1)} %get-tuple-element.71), channel_id=1, source_target_pairs={{0,2},{1,3},{2,0},{3,1},{4,6},{5,7},{6,4},{7,5},{8,10},{9,11},{10,... | collective-permute-start | bytes 86024 | tf_op jit(solution)/shard_map/ppermute | solution.py:194
  70.7 2.4 %collective-permute-done.20.b = bf16[1,16,896]{2,1,0:T(8,128)(2,1)S(1)} collective-permute-done((bf16[1,16,896]{2,1,0:T(8,128)(2,1)S(1)}, bf16[1,16,896]{2,1,0:T(8,128)(2,1)S(1)}, u32[]{:S(2)}, u32[]{:S(2)}) %collective-permute-start.20) | collective-permute-done | bytes 28704 | tf_op jit(solution)/shard_map/ppermute | solution.py:194
  73.2 3.9 %collective-permute-done.21.b = bf16[1,16,896]{2,1,0:T(8,128)(2,1)S(1)} collective-permute-done((bf16[1,16,896]{2,1,0:T(8,128)(2,1)S(1)}, bf16[1,16,896]{2,1,0:T(8,128)(2,1)S(1)}, u32[]{:S(2)}, u32[]{:S(2)}) %collective-permute-start.21) | collective-permute-done | bytes 28704 | tf_op jit(solution)/shard_map/ppermute | solution.py:194
  77.0 1.7 %collective-permute-start.22 = (bf16[1,16,896]{2,1,0:T(8,128)(2,1)S(1)}, bf16[1,16,896]{2,1,0:T(8,128)(2,1)S(1)}, u32[]{:S(2)}, u32[]{:S(2)}) collective-permute-start(bf16[1,16,896]{2,1,0:T(8,128)(2,1)S(1)} %plus.4.a), channel_id=1, source_target_pairs={{0,16},{1,17},{2,18},{3,19},{4,20},{5,21},{6,22},{7,23},{8,24},{9,... | collective-permute-start | bytes 86024 | tf_op jit(solution)/shard_map/ppermute | solution.py:194
  78.7 3.2 %collective-permute-done.22.b = bf16[1,16,896]{2,1,0:T(8,128)(2,1)S(1)} collective-permute-done((bf16[1,16,896]{2,1,0:T(8,128)(2,1)S(1)}, bf16[1,16,896]{2,1,0:T(8,128)(2,1)S(1)}, u32[]{:S(2)}, u32[]{:S(2)}) %collective-permute-start.22) | collective-permute-done | bytes 28704 | tf_op jit(solution)/shard_map/ppermute | solution.py:194
  81.9 1.6 %collective-permute-start.23 = (bf16[1,16,896]{2,1,0:T(8,128)(2,1)S(1)}, bf16[1,16,896]{2,1,0:T(8,128)(2,1)S(1)}, u32[]{:S(2)}, u32[]{:S(2)}) collective-permute-start(bf16[1,16,896]{2,1,0:T(8,128)(2,1)S(1)} %plus.5.a), channel_id=1, source_target_pairs={{0,2},{1,3},{2,0},{3,1},{4,6},{5,7},{6,4},{7,5},{8,10},{9,11},{10,... | collective-permute-start | bytes 86024 | tf_op jit(solution)/shard_map/ppermute | solution.py:194
  83.5 2.4 %collective-permute-done.23.b = bf16[1,16,896]{2,1,0:T(8,128)(2,1)S(1)} collective-permute-done((bf16[1,16,896]{2,1,0:T(8,128)(2,1)S(1)}, bf16[1,16,896]{2,1,0:T(8,128)(2,1)S(1)}, u32[]{:S(2)}, u32[]{:S(2)}) %collective-permute-start.23) | collective-permute-done | bytes 28704 | tf_op jit(solution)/shard_map/ppermute | solution.py:194
  85.8 1.5 %collective-permute-start.24 = (bf16[2,16,896]{2,1,0:T(8,128)(2,1)S(1)}, bf16[2,16,896]{2,1,0:T(8,128)(2,1)S(1)}, u32[]{:S(2)}, u32[]{:S(2)}) collective-permute-start(bf16[2,16,896]{2,1,0:T(8,128)(2,1)S(1)} %stacked.2.a), channel_id=1, source_target_pairs={{0,4},{1,5},{2,6},{3,7},{4,0},{5,1},{6,2},{7,3},{8,12},{9,13},{10,... | collective-permute-start | bytes 172040 | tf_op jit(solution)/shard_map/ppermute | solution.py:194
  87.3 2.7 %collective-permute-done.24.b = bf16[2,16,896]{2,1,0:T(8,128)(2,1)S(1)} collective-permute-done((bf16[2,16,896]{2,1,0:T(8,128)(2,1)S(1)}, bf16[2,16,896]{2,1,0:T(8,128)(2,1)S(1)}, u32[]{:S(2)}, u32[]{:S(2)}) %collective-permute-start.24) | collective-permute-done | bytes 57376 | tf_op jit(solution)/shard_map/ppermute | solution.py:194
  90.3 1.3 %collective-permute-done.25.there = bf16[4,16,896]{2,1,0:T(8,128)(2,1)S(1)} collective-permute-done((bf16[4,16,896]{2,1,0:T(8,128)(2,1)S(1)}, bf16[4,16,896]{2,1,0:T(8,128)(2,1)S(1)}, u32[]{:S(2)}, u32[]{:S(2)}) %collective-permute-start.25) | collective-permute-done | bytes 114720 | tf_op jit(solution)/shard_map/ppermute | solution.py:194
  91.7 14.3 %experts.1 = (bf16[16,7168]{1,0:T(8,128)(2,1)}, bf16[4,4,16,224]{3,2,1,0:T(8,128)(2,1)S(1)}, bf16[4,4,16,224]{3,2,1,0:T(8,128)(2,1)S(1)}, f32[16,224]{1,0:T(8,128)S(1)}) custom-call(bf16[4,16,896]{2,1,0:T(8,128)(2,1)S(1)} %stacked.3.here, bf16[4,16,896]{2,1,0:T(8,128)(2,1)S(1)} %collective-permute-done.25.there, bf16[16,7168]{1,0:T(8,128)(2,1)S(1)} %copy-done.1, ...), custom_call_target="tpu_custom_call" | custom-call | flops 704643072 | bytes 44040192 | tf_op jit(solution)/shard_map/experts/pallas_call | solution.py:584
  106.2 1.2 collective-permute-done.26.b
  107.4 1.5 %collective-permute-start.27 = (bf16[2,4,16,224]{3,2,1,0:T(8,128)(2,1)S(1)}, bf16[2,4,16,224]{3,2,1,0:T(8,128)(2,1)S(1)}, u32[]{:S(2)}, u32[]{:S(2)}) collective-permute-start(bf16[2,4,16,224]{3,2,1,0:T(8,128)(2,1)S(1)} %get-tuple-element.77), channel_id=1, source_target_pairs={{0,4},{1,5},{2,6},{3,7},{4,0},{5,1},{6,2},{7,3},{8,12},{9,13},{10,... | collective-permute-start | bytes 172040 | tf_op jit(solution)/shard_map/ppermute | solution.py:194
  109.0 2.8 %collective-permute-done.27.b = bf16[2,4,16,224]{3,2,1,0:T(8,128)(2,1)S(1)} collective-permute-done((bf16[2,4,16,224]{3,2,1,0:T(8,128)(2,1)S(1)}, bf16[2,4,16,224]{3,2,1,0:T(8,128)(2,1)S(1)}, u32[]{:S(2)}, u32[]{:S(2)}) %collective-permute-start.27) | collective-permute-done | bytes 57376 | tf_op jit(solution)/shard_map/ppermute | solution.py:194
  111.8 1.6 %collective-permute-start.28 = (bf16[1,4,16,224]{3,2,1,0:T(8,128)(2,1)S(1)}, bf16[1,4,16,224]{3,2,1,0:T(8,128)(2,1)S(1)}, u32[]{:S(2)}, u32[]{:S(2)}) collective-permute-start(bf16[1,4,16,224]{3,2,1,0:T(8,128)(2,1)S(1)} %get-tuple-element.79), channel_id=1, source_target_pairs={{0,2},{1,3},{2,0},{3,1},{4,6},{5,7},{6,4},{7,5},{8,10},{9,11},{10,... | collective-permute-start | bytes 86024 | tf_op jit(solution)/shard_map/ppermute | solution.py:194
  113.4 2.4 %collective-permute-done.28 = bf16[1,4,16,224]{3,2,1,0:T(8,128)(2,1)S(1)} collective-permute-done((bf16[1,4,16,224]{3,2,1,0:T(8,128)(2,1)S(1)}, bf16[1,4,16,224]{3,2,1,0:T(8,128)(2,1)S(1)}, u32[]{:S(2)}, u32[]{:S(2)}) %collective-permute-start.28) | collective-permute-done | bytes 28704 | tf_op jit(solution)/shard_map/ppermute | solution.py:194
  115.8 1.7 %collective-permute-start.29 = (bf16[2,16,224]{2,1,0:T(8,128)(2,1)S(1)}, bf16[2,16,224]{2,1,0:T(8,128)(2,1)S(1)}, u32[]{:S(2)}, u32[]{:S(2)}) collective-permute-start(bf16[2,16,224]{2,1,0:T(8,128)(2,1)S(1)} %get-tuple-element.81), channel_id=1, source_target_pairs={{0,16},{1,17},{2,18},{3,19},{4,20},{5,21},{6,22},{7,23},{8,24},{9,... | collective-permute-start | bytes 43016 | tf_op jit(solution)/shard_map/ppermute | solution.py:194
  117.5 3.0 %collective-permute-done.29.b = bf16[2,16,224]{2,1,0:T(8,128)(2,1)S(1)} collective-permute-done((bf16[2,16,224]{2,1,0:T(8,128)(2,1)S(1)}, bf16[2,16,224]{2,1,0:T(8,128)(2,1)S(1)}, u32[]{:S(2)}, u32[]{:S(2)}) %collective-permute-start.29) | collective-permute-done | bytes 14368 | tf_op jit(solution)/shard_map/ppermute | solution.py:194
  120.6 3.6 %collective-permute-done.30 = bf16[1,16,224]{2,1,0:T(8,128)(2,1)S(1)} collective-permute-done((bf16[1,16,224]{2,1,0:T(8,128)(2,1)S(1)}, bf16[1,16,224]{2,1,0:T(8,128)(2,1)S(1)}, u32[]{:S(2)}, u32[]{:S(2)}) %collective-permute-start.30) | collective-permute-done | bytes 7200 | tf_op jit(solution)/shard_map/ppermute | solution.py:194
  124.2 0.6 fusion
  (63 shorter events, 4.9 us)
Async XLA Ops:
  0.6 61.4 %slice-start.4 = ((s8[7340032]{0:T(1024)(128)(4,1)}), s8[4194304]{0:T(1024)(128)(4,1)S(1)}, s32[]{:S(2)}) async-start(s8[7340032]{0:T(1024)(128)(4,1)} %bitcast.11), calls=%async_computation.4 | async-start | bytes 8388608
  0.6 61.3 %copy-start = (bf16[512,512]{1,0:T(8,128)(2,1)S(1)}, bf16[512,512]{1,0:T(8,128)(2,1)}, u32[]{:S(2)}) copy-start(bf16[512,512]{1,0:T(8,128)(2,1)} %w_uv.1) | copy-start | bytes 1572868
  0.7 5.9 %collective-permute-start = (bf16[16,32,512]{2,1,0:T(8,128)(2,1)}, bf16[16,32,512]{2,1,0:T(8,128)(2,1)S(1)}, u32[]{:S(2)}, u32[]{:S(2)}) collective-permute-start(bf16[16,32,512]{2,1,0:T(8,128)(2,1)} %ql0.1), channel_id=1, source_target_pairs={{0,1},{1,0},{2,3},{3,2},{4,5},{5,4},{6,7},{7,6},{8,9},{9,8},{10,11... | collective-permute-start | bytes 1572872 | tf_op jit(solution)/shard_map/ppermute | solution.py:194
  2.5 11.8 %collective-permute-start.2 = (bf16[8,32,512]{2,1,0:T(8,128)(2,1)S(1)}, bf16[8,32,512]{2,1,0:T(8,128)(2,1)S(1)}, u32[]{:S(2)}, u32[]{:S(2)}) collective-permute-start(bf16[8,32,512]{2,1,0:T(8,128)(2,1)S(1)} %get-tuple-element.85), channel_id=1, source_target_pairs={{0,2},{1,3},{2,0},{3,1},{4,6},{5,7},{6,4},{7,5},{8,10},{9,11},{10,... | collective-permute-start | bytes 786440 | tf_op jit(solution)/shard_map/ppermute | solution.py:194
  5.0 1.5 %collective-permute-start.1 = (bf16[16,2048]{1,0:T(8,128)(2,1)}, bf16[16,2048]{1,0:T(8,128)(2,1)S(1)}, u32[]{:S(2)}, u32[]{:S(2)}) collective-permute-start(bf16[16,2048]{1,0:T(8,128)(2,1)} %qr0.1), channel_id=1, source_target_pairs={{0,1},{1,0},{2,3},{3,2},{4,5},{5,4},{6,7},{7,6},{8,9},{9,8},{10,11... | collective-permute-start | bytes 196616 | tf_op jit(solution)/shard_map/ppermute | solution.py:194
  5.4 8.9 %collective-permute-start.3 = (bf16[16,2048]{1,0:T(8,128)(2,1)}, bf16[16,2048]{1,0:T(8,128)(2,1)S(1)}, u32[]{:S(2)}, u32[]{:S(2)}) collective-permute-start(bf16[16,2048]{1,0:T(8,128)(2,1)} %qr0.1), channel_id=1, source_target_pairs={{0,2},{1,3},{2,0},{3,1},{4,6},{5,7},{6,4},{7,5},{8,10},{9,11},{10,... | collective-permute-start | bytes 196616 | tf_op jit(solution)/shard_map/ppermute | solution.py:194
  6.5 85.1 %slice-start = ((s8[14680064]{0:T(1024)(128)(4,1)}), s8[4194304]{0:T(1024)(128)(4,1)S(1)}, s32[]{:S(2)}) async-start(s8[14680064]{0:T(1024)(128)(4,1)} %bitcast.9), calls=%async_computation | async-start | bytes 8388608
  6.5 85.1 %copy-start.1 = (bf16[16,7168]{1,0:T(8,128)(2,1)S(1)}, bf16[16,7168]{1,0:T(8,128)(2,1)}, u32[]{:S(2)}) copy-start(bf16[16,7168]{1,0:T(8,128)(2,1)} %hidden.1) | copy-start | bytes 688132
  6.5 1.0 copy-start.2
  7.5 84.1 %copy-start.3 = (f32[7168]{0:T(1024)S(1)}, f32[7168]{0:T(1024)}, u32[]{:S(2)}) copy-start(f32[7168]{0:T(1024)} %param.28) | copy-start | bytes 86020
  7.5 84.1 %copy-start.4 = (s32[16,8]{0,1:T(8,128)S(1)}, s32[16,8]{0,1:T(8,128)}, u32[]{:S(2)}) copy-start(s32[16,8]{0,1:T(8,128)} %param.32) | copy-start | bytes 1540
  7.5 84.1 %copy-start.5 = (f32[16,8]{0,1:T(8,128)S(1)}, f32[16,8]{0,1:T(8,128)}, u32[]{:S(2)}) copy-start(f32[16,8]{0,1:T(8,128)} %param.33) | copy-start | bytes 1540
  14.3 3.1 %collective-permute-start.7 = (bf16[8,32,512]{2,1,0:T(8,128)(2,1)S(1)}, bf16[8,32,512]{2,1,0:T(8,128)(2,1)S(1)}, u32[]{:S(2)}, u32[]{:S(2)}) collective-permute-start(bf16[8,32,512]{2,1,0:T(8,128)(2,1)S(1)} %collective-permute-done.2.ql0), channel_id=1, source_target_pairs={{0,1},{1,0},{2,3},{3,2},{4,5},{5,4},{6,7},{7,6},{8,9},{9,8},{10,11... | collective-permute-start | bytes 786440 | tf_op jit(solution)/shard_map/ppermute | solution.py:194
  14.9 47.1 %slice-start.5 = ((s8[7340032]{0:T(1024)(128)(4,1)}), s8[3145728]{0:T(1024)(128)(4,1)S(1)}, s32[]{:S(2)}) async-start(s8[7340032]{0:T(1024)(128)(4,1)} %bitcast.11), calls=%async_computation.5 | async-start | bytes 6291456
  14.9 76.8 %slice-start.1 = ((s8[14680064]{0:T(1024)(128)(4,1)}), s8[4194304]{0:T(1024)(128)(4,1)S(1)}, s32[]{:S(2)}) async-start(s8[14680064]{0:T(1024)(128)(4,1)} %bitcast.9), calls=%async_computation.1 | async-start | bytes 8388608
  14.9 8.3 %collective-permute-start.6 = (bf16[8,32,512]{2,1,0:T(8,128)(2,1)S(1)}, bf16[8,32,512]{2,1,0:T(8,128)(2,1)S(1)}, u32[]{:S(2)}, u32[]{:S(2)}) collective-permute-start(bf16[8,32,512]{2,1,0:T(8,128)(2,1)S(1)} %get-tuple-element.84), channel_id=1, source_target_pairs={{0,2},{1,3},{2,0},{3,1},{4,6},{5,7},{6,4},{7,5},{8,10},{9,11},{10,... | collective-permute-start | bytes 786440 | tf_op jit(solution)/shard_map/ppermute | solution.py:194
  16.1 1.3 %collective-permute-start.8 = (bf16[16,2048]{1,0:T(8,128)(2,1)S(1)}, bf16[16,2048]{1,0:T(8,128)(2,1)S(1)}, u32[]{:S(2)}, u32[]{:S(2)}) collective-permute-start(bf16[16,2048]{1,0:T(8,128)(2,1)S(1)} %collective-permute-done.3.qr0), channel_id=1, source_target_pairs={{0,1},{1,0},{2,3},{3,2},{4,5},{5,4},{6,7},{7,6},{8,9},{9,8},{10,11... | collective-permute-start | bytes 196616 | tf_op jit(solution)/shard_map/ppermute | solution.py:194
  23.2 1.5 %collective-permute-start.9 = (bf16[8,32,512]{2,1,0:T(8,128)(2,1)S(1)}, bf16[8,32,512]{2,1,0:T(8,128)(2,1)S(1)}, u32[]{:S(2)}, u32[]{:S(2)}) collective-permute-start(bf16[8,32,512]{2,1,0:T(8,128)(2,1)S(1)} %collective-permute-done.6.ql0), channel_id=1, source_target_pairs={{0,1},{1,0},{2,3},{3,2},{4,5},{5,4},{6,7},{7,6},{8,9},{9,8},{10,11... | collective-permute-start | bytes 786440 | tf_op jit(solution)/shard_map/ppermute | solution.py:194
  23.2 6.3 %collective-permute-start.4 = (bf16[4,144,512]{2,1,0:T(8,128)(2,1)S(1)}, bf16[4,144,512]{2,1,0:T(8,128)(2,1)S(1)}, u32[]{:S(2)}, u32[]{:S(2)}) collective-permute-start(bf16[4,144,512]{2,1,0:T(8,128)(2,1)S(1)} %get-tuple-element.45), channel_id=1, source_target_pairs={{0,1},{1,0},{2,3},{3,2},{4,5},{5,4},{6,7},{7,6},{8,9},{9,8},{10,11... | collective-permute-start | bytes 1769480 | tf_op jit(solution)/shard_map/ppermute | solution.py:194
  24.7 66.9 %slice-start.2 = ((s8[14680064]{0:T(1024)(128)(4,1)}), s8[4194304]{0:T(1024)(128)(4,1)S(1)}, s32[]{:S(2)}) async-start(s8[14680064]{0:T(1024)(128)(4,1)} %bitcast.9), calls=%async_computation.2 | async-start | bytes 8388608
  29.2 11.8 %collective-permute-start.10 = (bf16[4,144,512]{2,1,0:T(8,128)(2,1)S(1)}, bf16[4,144,512]{2,1,0:T(8,128)(2,1)S(1)}, u32[]{:S(2)}, u32[]{:S(2)}) collective-permute-start(bf16[4,144,512]{2,1,0:T(8,128)(2,1)S(1)} %get-tuple-element.56), channel_id=1, source_target_pairs={{0,1},{1,0},{2,3},{3,2},{4,5},{5,4},{6,7},{7,6},{8,9},{9,8},{10,11... | collective-permute-start | bytes 1769480 | tf_op jit(solution)/shard_map/ppermute | solution.py:194
  29.8 9.4 %collective-permute-start.5 = (bf16[2,144,512]{2,1,0:T(8,128)(2,1)S(1)}, bf16[2,144,512]{2,1,0:T(8,128)(2,1)S(1)}, u32[]{:S(2)}, u32[]{:S(2)}) collective-permute-start(bf16[2,144,512]{2,1,0:T(8,128)(2,1)S(1)} %get-tuple-element.47), channel_id=1, source_target_pairs={{0,4},{1,5},{2,6},{3,7},{4,0},{5,1},{6,2},{7,3},{8,12},{9,13},{10,... | collective-permute-start | bytes 884744 | tf_op jit(solution)/shard_map/ppermute | solution.py:194
  39.3 10.0 %collective-permute-start.13 = (bf16[1,144,512]{2,1,0:T(8,128)(2,1)S(1)}, bf16[1,144,512]{2,1,0:T(8,128)(2,1)S(1)}, u32[]{:S(2)}, u32[]{:S(2)}) collective-permute-start(bf16[1,144,512]{2,1,0:T(8,128)(2,1)S(1)} %get-tuple-element.59), channel_id=1, source_target_pairs={{0,2},{1,3},{2,0},{3,1},{4,6},{5,7},{6,4},{7,5},{8,10},{9,11},{10,... | collective-permute-start | bytes 442376 | tf_op jit(solution)/shard_map/ppermute | solution.py:194
  41.3 9.7 %collective-permute-start.11 = (bf16[1,144,512]{2,1,0:T(8,128)(2,1)S(1)}, bf16[1,144,512]{2,1,0:T(8,128)(2,1)S(1)}, u32[]{:S(2)}, u32[]{:S(2)}) collective-permute-start(bf16[1,144,512]{2,1,0:T(8,128)(2,1)S(1)} %get-tuple-element.57), channel_id=1, source_target_pairs={{0,2},{1,3},{2,0},{3,1},{4,6},{5,7},{6,4},{7,5},{8,10},{9,11},{10,... | collective-permute-start | bytes 442376 | tf_op jit(solution)/shard_map/ppermute | solution.py:194
  41.8 9.2 %collective-permute-start.12 = (bf16[1,144,512]{2,1,0:T(8,128)(2,1)S(1)}, bf16[1,144,512]{2,1,0:T(8,128)(2,1)S(1)}, u32[]{:S(2)}, u32[]{:S(2)}) collective-permute-start(bf16[1,144,512]{2,1,0:T(8,128)(2,1)S(1)} %get-tuple-element.58), channel_id=1, source_target_pairs={{0,6},{1,7},{2,4},{3,5},{4,2},{5,3},{6,0},{7,1},{8,14},{9,15},{10,... | collective-permute-start | bytes 442376 | tf_op jit(solution)/shard_map/ppermute | solution.py:194
  44.4 6.7 %collective-permute-start.14 = (bf16[1,144,512]{2,1,0:T(8,128)(2,1)S(1)}, bf16[1,144,512]{2,1,0:T(8,128)(2,1)S(1)}, u32[]{:S(2)}, u32[]{:S(2)}) collective-permute-start(bf16[1,144,512]{2,1,0:T(8,128)(2,1)S(1)} %get-tuple-element.61), channel_id=1, source_target_pairs={{0,4},{1,5},{2,6},{3,7},{4,0},{5,1},{6,2},{7,3},{8,12},{9,13},{10,... | collective-permute-start | bytes 442376 | tf_op jit(solution)/shard_map/ppermute | solution.py:194
  51.4 5.3 %collective-permute-start.15 = (bf16[80,512]{1,0:T(8,128)(2,1)S(1)}, bf16[80,512]{1,0:T(8,128)(2,1)S(1)}, u32[]{:S(2)}, u32[]{:S(2)}) collective-permute-start(bf16[80,512]{1,0:T(8,128)(2,1)S(1)} %get-tuple-element.63), channel_id=1, source_target_pairs={{0,8},{1,9},{2,10},{3,11},{4,12},{5,13},{6,14},{7,15},{8,0},{9,1},... | collective-permute-start | bytes 245768 | tf_op jit(solution)/shard_map/ppermute | solution.py:194
  53.1 7.1 %collective-permute-start.16 = (bf16[80,512]{1,0:T(8,128)(2,1)S(1)}, bf16[80,512]{1,0:T(8,128)(2,1)S(1)}, u32[]{:S(2)}, u32[]{:S(2)}) collective-permute-start(bf16[80,512]{1,0:T(8,128)(2,1)S(1)} %get-tuple-element.64), channel_id=1, source_target_pairs={{0,16},{1,17},{2,18},{3,19},{4,20},{5,21},{6,22},{7,23},{8,24},{9,... | collective-permute-start | bytes 245768 | tf_op jit(solution)/shard_map/ppermute | solution.py:194
  55.7 6.3 %collective-permute-start.17 = (bf16[80,512]{1,0:T(8,128)(2,1)S(1)}, bf16[80,512]{1,0:T(8,128)(2,1)S(1)}, u32[]{:S(2)}, u32[]{:S(2)}) collective-permute-start(bf16[80,512]{1,0:T(8,128)(2,1)S(1)} %get-tuple-element.65), channel_id=1, source_target_pairs={{0,24},{1,25},{2,26},{3,27},{4,28},{5,29},{6,30},{7,31},{8,16},{9,... | collective-permute-start | bytes 245768 | tf_op jit(solution)/shard_map/ppermute | solution.py:194
  62.0 29.6 %slice-start.3 = ((s8[14680064]{0:T(1024)(128)(4,1)}), s8[2097152]{0:T(1024)(128)(4,1)S(1)}, s32[]{:S(2)}) async-start(s8[14680064]{0:T(1024)(128)(4,1)} %bitcast.9), calls=%async_computation.3 | async-start | bytes 4194304
  63.5 1.4 %collective-permute-start.18 = (bf16[4,16,896]{2,1,0:T(8,128)(2,1)S(1)}, bf16[4,16,896]{2,1,0:T(8,128)(2,1)S(1)}, u32[]{:S(2)}, u32[]{:S(2)}) collective-permute-start(bf16[4,16,896]{2,1,0:T(8,128)(2,1)S(1)} %get-tuple-element.67), channel_id=1, source_target_pairs={{0,1},{1,0},{2,3},{3,2},{4,5},{5,4},{6,7},{7,6},{8,9},{9,8},{10,11... | collective-permute-start | bytes 344072 | tf_op jit(solution)/shard_map/ppermute | solution.py:194
  64.9 4.2 %collective-permute-start.19 = (bf16[2,16,896]{2,1,0:T(8,128)(2,1)S(1)}, bf16[2,16,896]{2,1,0:T(8,128)(2,1)S(1)}, u32[]{:S(2)}, u32[]{:S(2)}) collective-permute-start(bf16[2,16,896]{2,1,0:T(8,128)(2,1)S(1)} %get-tuple-element.69), channel_id=1, source_target_pairs={{0,4},{1,5},{2,6},{3,7},{4,0},{5,1},{6,2},{7,3},{8,12},{9,13},{10,... | collective-permute-start | bytes 172040 | tf_op jit(solution)/shard_map/ppermute | solution.py:194
  69.1 3.9 %collective-permute-start.20 = (bf16[1,16,896]{2,1,0:T(8,128)(2,1)S(1)}, bf16[1,16,896]{2,1,0:T(8,128)(2,1)S(1)}, u32[]{:S(2)}, u32[]{:S(2)}) collective-permute-start(bf16[1,16,896]{2,1,0:T(8,128)(2,1)S(1)} %get-tuple-element.71), channel_id=1, source_target_pairs={{0,2},{1,3},{2,0},{3,1},{4,6},{5,7},{6,4},{7,5},{8,10},{9,11},{10,... | collective-permute-start | bytes 86024 | tf_op jit(solution)/shard_map/ppermute | solution.py:194
  73.1 3.9 %collective-permute-start.21 = (bf16[1,16,896]{2,1,0:T(8,128)(2,1)S(1)}, bf16[1,16,896]{2,1,0:T(8,128)(2,1)S(1)}, u32[]{:S(2)}, u32[]{:S(2)}) collective-permute-start(bf16[1,16,896]{2,1,0:T(8,128)(2,1)S(1)} %plus.3.a), channel_id=1, source_target_pairs={{0,8},{1,9},{2,10},{3,11},{4,12},{5,13},{6,14},{7,15},{8,0},{9,1},... | collective-permute-start | bytes 86024 | tf_op jit(solution)/shard_map/ppermute | solution.py:194
  77.0 4.8 %collective-permute-start.22 = (bf16[1,16,896]{2,1,0:T(8,128)(2,1)S(1)}, bf16[1,16,896]{2,1,0:T(8,128)(2,1)S(1)}, u32[]{:S(2)}, u32[]{:S(2)}) collective-permute-start(bf16[1,16,896]{2,1,0:T(8,128)(2,1)S(1)} %plus.4.a), channel_id=1, source_target_pairs={{0,16},{1,17},{2,18},{3,19},{4,20},{5,21},{6,22},{7,23},{8,24},{9,... | collective-permute-start | bytes 86024 | tf_op jit(solution)/shard_map/ppermute | solution.py:194
  81.9 3.9 %collective-permute-start.23 = (bf16[1,16,896]{2,1,0:T(8,128)(2,1)S(1)}, bf16[1,16,896]{2,1,0:T(8,128)(2,1)S(1)}, u32[]{:S(2)}, u32[]{:S(2)}) collective-permute-start(bf16[1,16,896]{2,1,0:T(8,128)(2,1)S(1)} %plus.5.a), channel_id=1, source_target_pairs={{0,2},{1,3},{2,0},{3,1},{4,6},{5,7},{6,4},{7,5},{8,10},{9,11},{10,... | collective-permute-start | bytes 86024 | tf_op jit(solution)/shard_map/ppermute | solution.py:194
  85.8 4.2 %collective-permute-start.24 = (bf16[2,16,896]{2,1,0:T(8,128)(2,1)S(1)}, bf16[2,16,896]{2,1,0:T(8,128)(2,1)S(1)}, u32[]{:S(2)}, u32[]{:S(2)}) collective-permute-start(bf16[2,16,896]{2,1,0:T(8,128)(2,1)S(1)} %stacked.2.a), channel_id=1, source_target_pairs={{0,4},{1,5},{2,6},{3,7},{4,0},{5,1},{6,2},{7,3},{8,12},{9,13},{10,... | collective-permute-start | bytes 172040 | tf_op jit(solution)/shard_map/ppermute | solution.py:194
  90.0 1.6 %collective-permute-start.25 = (bf16[4,16,896]{2,1,0:T(8,128)(2,1)S(1)}, bf16[4,16,896]{2,1,0:T(8,128)(2,1)S(1)}, u32[]{:S(2)}, u32[]{:S(2)}) collective-permute-start(bf16[4,16,896]{2,1,0:T(8,128)(2,1)S(1)} %stacked.3.here), channel_id=1, source_target_pairs={{0,1},{1,0},{2,3},{3,2},{4,5},{5,4},{6,7},{7,6},{8,9},{9,8},{10,11... | collective-permute-start | bytes 344072 | tf_op jit(solution)/shard_map/ppermute | solution.py:194
  106.0 1.4 %collective-permute-start.26 = (bf16[4,4,16,224]{3,2,1,0:T(8,128)(2,1)S(1)}, bf16[4,4,16,224]{3,2,1,0:T(8,128)(2,1)S(1)}, u32[]{:S(2)}, u32[]{:S(2)}) collective-permute-start(bf16[4,4,16,224]{3,2,1,0:T(8,128)(2,1)S(1)} %get-tuple-element.75), channel_id=1, source_target_pairs={{0,1},{1,0},{2,3},{3,2},{4,5},{5,4},{6,7},{7,6},{8,9},{9,8},{10,11... | collective-permute-start | bytes 344072 | tf_op jit(solution)/shard_map/ppermute | solution.py:194
  107.4 4.3 %collective-permute-start.27 = (bf16[2,4,16,224]{3,2,1,0:T(8,128)(2,1)S(1)}, bf16[2,4,16,224]{3,2,1,0:T(8,128)(2,1)S(1)}, u32[]{:S(2)}, u32[]{:S(2)}) collective-permute-start(bf16[2,4,16,224]{3,2,1,0:T(8,128)(2,1)S(1)} %get-tuple-element.77), channel_id=1, source_target_pairs={{0,4},{1,5},{2,6},{3,7},{4,0},{5,1},{6,2},{7,3},{8,12},{9,13},{10,... | collective-permute-start | bytes 172040 | tf_op jit(solution)/shard_map/ppermute | solution.py:194
  111.8 4.0 %collective-permute-start.28 = (bf16[1,4,16,224]{3,2,1,0:T(8,128)(2,1)S(1)}, bf16[1,4,16,224]{3,2,1,0:T(8,128)(2,1)S(1)}, u32[]{:S(2)}, u32[]{:S(2)}) collective-permute-start(bf16[1,4,16,224]{3,2,1,0:T(8,128)(2,1)S(1)} %get-tuple-element.79), channel_id=1, source_target_pairs={{0,2},{1,3},{2,0},{3,1},{4,6},{5,7},{6,4},{7,5},{8,10},{9,11},{10,... | collective-permute-start | bytes 86024 | tf_op jit(solution)/shard_map/ppermute | solution.py:194
  115.8 4.7 %collective-permute-start.29 = (bf16[2,16,224]{2,1,0:T(8,128)(2,1)S(1)}, bf16[2,16,224]{2,1,0:T(8,128)(2,1)S(1)}, u32[]{:S(2)}, u32[]{:S(2)}) collective-permute-start(bf16[2,16,224]{2,1,0:T(8,128)(2,1)S(1)} %get-tuple-element.81), channel_id=1, source_target_pairs={{0,16},{1,17},{2,18},{3,19},{4,20},{5,21},{6,22},{7,23},{8,24},{9,... | collective-permute-start | bytes 43016 | tf_op jit(solution)/shard_map/ppermute | solution.py:194
  120.5 3.7 %collective-permute-start.30 = (bf16[1,16,224]{2,1,0:T(8,128)(2,1)S(1)}, bf16[1,16,224]{2,1,0:T(8,128)(2,1)S(1)}, u32[]{:S(2)}, u32[]{:S(2)}) collective-permute-start(bf16[1,16,224]{2,1,0:T(8,128)(2,1)S(1)} %get-tuple-element.83), channel_id=1, source_target_pairs={{0,8},{1,9},{2,10},{3,11},{4,12},{5,13},{6,14},{7,15},{8,0},{9,1},... | collective-permute-start | bytes 21512 | tf_op jit(solution)/shard_map/ppermute | solution.py:194

commit v3 on v2

--- a/solution.py
+++ b/solution.py
@@ -184,10 +184,12 @@
 STAT = 16
 LANES = 128
 PARENTS = REQ
+LOG2E = math.log2(math.e)
 VMEM = pl.BlockSpec(memory_space=pltpu.VMEM)
 SMEM = pl.BlockSpec(memory_space=pltpu.SMEM)
 HBM = pl.BlockSpec(memory_space=pltpu.HBM)
 NT = (((1,), (1,)), ((), ()))
+EXCHANGE = pl.CostEstimate(flops=0, bytes_accessed=12 << 20, transcendentals=0)
 
 
 def swap(value, mask):
@@ -239,34 +241,35 @@
     return [w / total for w in weights], top + jnp.log(total)
 
 
-def attend_kernel(scale, first, count, fetch, later, info, ql0, ql1, qr0, qr1, cl_hbm, cr_hbm, sl_hbm, sr_hbm, *rest):
-    earlier, rest = rest[:2 if later else 0], rest[-15:]
-    keep, send, spread, qbuf, rbuf, pbuf, wide, lse_buf, stat, cl, cr, sl, sr, own_q, sems = rest
+def attend_kernel(scale, fetch, info, ql0, ql1, qr0, qr1, cl_hbm, cr_hbm, sl_hbm, sr_hbm, keep, send0, send1,
+                  spread, qbuf, rbuf, pbuf, wide, lse_buf, stat, cl, cr, sl, sr, own_q, own_r, sems):
     linear = lax.axis_index(AXES)
     core, y, x, z0, _ = bits(linear)
     heads = ql1.shape[1]
     rows = 2 * heads
     total_rows = BEAMS * rows
-    half = total_rows // 2
     targets = keep.shape[0]
     body = keep.shape[1] - STAT
     small = body // (2 * REQ)
+    query_copies = []
+    if fetch:
+        query_copies = [pltpu.make_async_copy(qr0, own_r, sems.at[4, 0]),
+                        pltpu.make_async_copy(ql0, own_q, sems.at[4, 1])]
+        for copy in query_copies:
+            copy.start()
     copies = []
-    for k in range(count):
-        beams = pl.ds((first + k) * BEAMS, BEAMS)
-        here = pl.ds(k * BEAMS, BEAMS)
+    for r in range(REQ):
+        beams = pl.ds(r * BEAMS, BEAMS)
         group = [
-            pltpu.make_async_copy(cl_hbm.at[first + k], cl.at[k], sems.at[0, k]),
-            pltpu.make_async_copy(cr_hbm.at[first + k], cr.at[k], sems.at[1, k]),
-            pltpu.make_async_copy(sl_hbm.at[beams], sl.at[here], sems.at[2, k]),
-            pltpu.make_async_copy(sr_hbm.at[beams], sr.at[here], sems.at[3, k]),
+            pltpu.make_async_copy(cl_hbm.at[r], cl.at[r], sems.at[0, r]),
+            pltpu.make_async_copy(cr_hbm.at[r], cr.at[r], sems.at[1, r]),
+            pltpu.make_async_copy(sl_hbm.at[beams], sl.at[beams], sems.at[2, r]),
+            pltpu.make_async_copy(sr_hbm.at[beams], sr.at[beams], sems.at[3, r]),
         ]
-        if fetch:
-            group.append(pltpu.make_async_copy(ql0.at[here], own_q.at[here], sems.at[4, k]))
         for copy in group:
             copy.start()
         copies.append(group)
-    first_q = own_q if fetch else ql0
+    first_q, first_r = (own_q, own_r) if fetch else (ql0, qr0)
 
     out_row = lax.broadcasted_iota(jnp.int32, (total_rows, total_rows), 0)
     in_row = lax.broadcasted_iota(jnp.int32, (total_rows, total_rows), 1)
@@ -279,132 +282,146 @@
 
     spread[...] = jnp.where(source_of(out_row) == in_row, 1.0, 0.0).astype(BF)
     moves = source_of(in_row) == out_row
-    for i, out in enumerate((keep, send)):
-        for t in range(targets):
-            if later:
-                out[t] = earlier[i][t]
-                lse_buf[i * targets + t:i * targets + t + 1] = read_stat(earlier[i][t, body:], body)
-            else:
-                lse_buf[i * targets + t:i * targets + t + 1] = jnp.zeros((1, body), F32)
-    wide[0] = qr0[...].astype(F32)
+    messages = [keep.at[t] for t in range(targets)]
+    messages += [send.at[t] for send in (send0, send1) for t in range(targets // 2)]
+    lse_buf[...] = jnp.zeros_like(lse_buf)
+    for copy in query_copies:
+        copy.wait()
+    wide[0] = first_r[...].astype(F32)
     wide[1] = qr1[...].astype(F32)
     per_group = LANES // DR
     head_row = lax.broadcasted_iota(jnp.int32, (heads, LANES), 0)
     own_lanes = lax.broadcasted_iota(jnp.int32, (heads, LANES), 1) // DR == head_row % per_group
 
-    for k in range(count):
-        r = first + k
-        for copy in copies[k]:
-            copy.wait()
+    for r in range(REQ):
         for j in range(BEAMS):
             for piece, q in enumerate((first_q, ql1)):
                 part = slice(j * rows + piece * heads, j * rows + (piece + 1) * heads)
-                qbuf[part] = q[k * BEAMS + j]
                 b = r * BEAMS + j
+                qbuf[r, part] = q[b]
                 unfolded = jnp.zeros((heads, LANES), F32)
                 for g in range(heads // per_group):
                     lanes = wide[piece, b:b + 1, g * LANES:(g + 1) * LANES]
                     unfolded = jnp.where(head_row // per_group == g, lanes, unfolded)
-                rbuf[part] = jnp.where(own_lanes, unfolded, 0.0).astype(BF)
-        keys = cl[k]
+                rbuf[r, part] = jnp.where(own_lanes, unfolded, 0.0).astype(BF)
+
+    def scores(r):
+        for copy in copies[r]:
+            copy.wait()
+        keys = cl[r]
         ctx_block = keys.shape[0]
-        pre = lax.dot_general(qbuf[...], keys, NT, preferred_element_type=F32)
-        pre = pre + jnp.dot(rbuf[...], jnp.concatenate([cr[k]] * per_group, axis=0), preferred_element_type=F32)
+        pre = lax.dot_general(qbuf[r], keys, NT, preferred_element_type=F32)
+        pre = pre + jnp.dot(rbuf[r], jnp.concatenate([cr[r]] * per_group, axis=0), preferred_element_type=F32)
         position = linear * ctx_block + lax.broadcasted_iota(jnp.int32, (1, ctx_block), 1)
-        pre = jnp.where(position < info[r], pre * scale, NEG)
-        own = [info[PARENTS + r * BEAMS + j] - first * BEAMS for j in range(BEAMS)]
+        pre = jnp.where(position < info[r], pre, NEG)
+        own = [info[PARENTS + r * BEAMS + j] for j in range(BEAMS)]
         suf = []
-        for j in range(BEAMS):
-            part = slice(j * rows, (j + 1) * rows)
-            s = lax.dot_general(qbuf[part], sl[own[j]], NT, preferred_element_type=F32)
-            s = s + jnp.dot(rbuf[part], jnp.concatenate([sr[own[j]]] * per_group, axis=0),
+        suf_keys = []
+        for j in range(0, BEAMS, 2):
+            part = slice(j * rows, (j + 2) * rows)
+            pair_keys = jnp.concatenate([sl[own[j]], sl[own[j + 1]]], axis=0)
+            pair_rope = jnp.concatenate([sr[own[j]], sr[own[j + 1]]], axis=1)
+            s = lax.dot_general(qbuf[r, part], pair_keys, NT, preferred_element_type=F32)
+            s = s + jnp.dot(rbuf[r, part], jnp.concatenate([pair_rope] * per_group, axis=0),
                             preferred_element_type=F32)
-            suf.append(s * scale)
-        suf = jnp.concatenate(suf, axis=0)
+            n = s.shape[1] // 2
+            suf += [s[:rows, :n], s[rows:, n:]]
+            suf_keys.append(pair_keys)
+        return pre, jnp.concatenate(suf, axis=0), suf_keys
+
+    def finish(r, pre, suf, suf_keys):
         top = jnp.maximum(jnp.max(pre, axis=1, keepdims=True), jnp.max(suf, axis=1, keepdims=True))
-        pre_w = jnp.exp(pre - top).astype(BF)
-        suf_w = jnp.exp(suf - top).astype(BF)
-        total = jnp.sum(pre_w.astype(F32), axis=1, keepdims=True)
-        total = total + jnp.sum(suf_w.astype(F32), axis=1, keepdims=True)
-        acc = jnp.dot(pre_w, keys, preferred_element_type=F32)
+        pre_w = jnp.exp2((pre - top) * (scale * LOG2E))
+        suf_w = jnp.exp2((suf - top) * (scale * LOG2E))
+        total = jnp.sum(pre_w, axis=1, keepdims=True) + jnp.sum(suf_w, axis=1, keepdims=True)
+        pre_w, suf_w = pre_w.astype(BF), suf_w.astype(BF)
+        acc = jnp.dot(pre_w, cl[r], preferred_element_type=F32)
         inv = 1.0 / total
-        for j in range(BEAMS):
-            part = slice(j * rows, (j + 1) * rows)
-            a = acc[part] + jnp.dot(suf_w[part], sl[own[j]], preferred_element_type=F32)
-            pbuf[part] = (a * inv[part]).astype(BF)
-        moved = jnp.dot(spread[...], pbuf[...], preferred_element_type=F32).astype(BF)
-        lse = top + jnp.log(total)
+        for j in range(0, BEAMS, 2):
+            part = slice(j * rows, (j + 2) * rows)
+            first, second = suf_w[j * rows:(j + 1) * rows], suf_w[(j + 1) * rows:(j + 2) * rows]
+            none = jnp.zeros_like(first)
+            spread_w = jnp.concatenate([jnp.concatenate([first, none], axis=1),
+                                        jnp.concatenate([none, second], axis=1)], axis=0)
+            a = acc[part] + jnp.dot(spread_w, suf_keys[j // 2], preferred_element_type=F32)
+            pbuf[r, part] = (a * inv[part]).astype(BF)
+        moved = jnp.dot(spread[...], pbuf[r], preferred_element_type=F32).astype(BF)
+        lse = scale * top + jnp.log(total)
         lane_lse = jnp.sum(jnp.where(moves, lse, 0.0), axis=0, keepdims=True)
-        for i, out in enumerate((keep, send)):
-            for t in range(targets):
-                for zz in range(2):
-                    at = i * half + (2 * t + zz) * small
-                    to = (zz * REQ + r) * small
-                    out[t, to:to + small] = moved[at:at + small]
-                    lse_buf[i * targets + t:i * targets + t + 1, to:to + small] = lane_lse[:, at:at + small]
+        for n, message in enumerate(messages):
+            for zz in range(2):
+                at = (2 * n + zz) * small
+                to = (zz * REQ + r) * small
+                message[to:to + small] = moved[at:at + small]
+                lse_buf[n:n + 1, to:to + small] = lane_lse[:, at:at + small]
+
+    now = scores(0)
+    for r in range(REQ):
+        later = scores(r + 1) if r + 1 < REQ else None
+        finish(r, *now)
+        now = later
     parts = stat_rows(lse_buf[...])
-    for i, out in enumerate((keep, send)):
-        for t in range(targets):
-            n = i * targets + t
-            write_stat(out.at[t], body, [p[n:n + 1] for p in parts], stat)
-
-
-def attend(scale, first, count, info, q_lat, q_rope, caches, earlier=()):
-    fetch = first == 0 and count == REQ
+    for n, message in enumerate(messages):
+        write_stat(message, body, [p[n:n + 1] for p in parts], stat)
+
+
+def attend(scale, fetch, info, q_lat, q_rope, caches):
     heads, width = q_lat[0].shape[1:]
     total_rows = BEAMS * 2 * heads
     targets = SHAPE[1] * SHAPE[2]
     body = REQ * total_rows // (2 * targets)
-    message = jax.ShapeDtypeStruct((targets, body + STAT, width), BF)
+    message = lambda n: jax.ShapeDtypeStruct((n, body + STAT, width), BF)
     keys = caches[0].shape[1] + caches[2].shape[1]
-    own_q = q_lat[0].shape if fetch else (8, LANES)
+    own = [v.shape if fetch else (STAT, LANES) for v in (q_lat[0], q_rope[0])]
+    first = [in_hbm(v) if fetch else v for v in (q_lat[0], q_rope[0])]
+    spec = HBM if fetch else VMEM
     return pl.pallas_call(
-        partial(attend_kernel, scale, first, count, fetch, bool(earlier)),
-        in_specs=[SMEM, HBM if fetch else VMEM] + [VMEM] * 3 + [HBM] * 4 + [VMEM] * len(earlier),
-        out_specs=[VMEM] * 2,
-        out_shape=[message] * 2,
+        partial(attend_kernel, scale, fetch),
+        in_specs=[SMEM, spec, VMEM, spec, VMEM] + [HBM] * 4,
+        out_specs=[VMEM] * 3,
+        out_shape=[message(targets), message(targets // 2), message(targets // 2)],
         scratch_shapes=[
             pltpu.VMEM((total_rows, total_rows), BF),
-            pltpu.VMEM((total_rows, width), BF),
-            pltpu.VMEM((total_rows, LANES), BF),
-            pltpu.VMEM((total_rows, width), BF),
+            pltpu.VMEM((REQ, total_rows, width), BF),
+            pltpu.VMEM((REQ, total_rows, LANES), BF),
+            pltpu.VMEM((REQ, total_rows, width), BF),
             pltpu.VMEM((2, *q_rope[0].shape), F32),
             pltpu.VMEM((2 * targets, body), F32),
             pltpu.VMEM((STAT, width), F32),
-        ] + [pltpu.VMEM((c.shape[0] * count // REQ, *c.shape[1:]), BF) for c in caches]
-        + [pltpu.VMEM(own_q, BF), pltpu.SemaphoreType.DMA((5, count))],
+        ] + [pltpu.VMEM(c.shape, BF) for c in caches]
+        + [pltpu.VMEM(shape, BF) for shape in own] + [pltpu.SemaphoreType.DMA((5, REQ))],
         compiler_params=pltpu.CompilerParams(vmem_limit_bytes=14 << 20),
         cost_estimate=pl.CostEstimate(
-            flops=count * 2 * total_rows * keys * (2 * width + DR), bytes_accessed=2 * count << 20,
-            transcendentals=count * total_rows * keys),
+            flops=REQ * 2 * total_rows * keys * (2 * width + DR), bytes_accessed=8 << 20,
+            transcendentals=REQ * total_rows * keys),
         name="attend",
-    )(info, in_hbm(q_lat[0]) if fetch else q_lat[0], q_lat[1], *q_rope, *(in_hbm(c) for c in caches), *earlier)
-
-
-def pair_kernel(a, b, *rest):
-    outs, stat = rest[:-1], rest[-1]
+    )(info, first[0], q_lat[1], first[1], q_rope[1], *(in_hbm(c) for c in caches))
+
+
+def pair_kernel(count, a, *refs):
+    got, outs, stat = refs[:count], refs[count:-1], refs[-1]
     targets, rows, _ = a.shape
     body = rows - STAT
-    each = targets // len(outs)
     for t in range(targets):
-        weights, lse = joined([read_stat(v[t, body:], body) for v in (a, b)])
-        out = outs[t // each].at[t % each]
-        out[:body] = (a[t, :body].astype(F32) * column(weights[0])
-                      + b[t, :body].astype(F32) * column(weights[1])).astype(BF)
+        ours, theirs = a.at[t], got[t // (targets // count)].at[t % (targets // count)]
+        out = outs[t // (targets // len(outs))].at[t % (targets // len(outs))]
+        weights, lse = joined([read_stat(v[body:], body) for v in (ours, theirs)])
+        out[:body] = (ours[:body].astype(F32) * column(weights[0])
+                      + theirs[:body].astype(F32) * column(weights[1])).astype(BF)
         write_stat(out, body, stat_rows(lse), stat)
 
 
-def merge_pair_of(a, b, parts):
+def merge_pairs(a, got, parts):
     return pl.pallas_call(
-        pair_kernel,
-        in_specs=[VMEM] * 2,
+        partial(pair_kernel, len(got)),
+        in_specs=[VMEM] * (1 + len(got)),
         out_specs=[VMEM] * parts,
         out_shape=[jax.ShapeDtypeStruct((a.shape[0] // parts, *a.shape[1:]), BF)] * parts,
         scratch_shapes=[pltpu.VMEM((STAT, a.shape[2]), F32)],
         compiler_params=pltpu.CompilerParams(vmem_limit_bytes=4 << 20),
         cost_estimate=pl.CostEstimate(flops=4 * a.size, bytes_accessed=6 * a.size, transcendentals=0),
-        name="merge_pair",
-    )(a, b)
+        name="merge_pairs",
+    )(a, *got)
 
 
 def plane_kernel(count, *refs):
@@ -444,45 +461,27 @@
     )(*same, *other)
 
 
-def sum_kernel(a, b, *outs):
-    each = a.shape[0] // len(outs)
+def sum_kernel(count, *refs):
+    ins, outs = refs[:count], refs[count:]
     for i, out in enumerate(outs):
-        part = slice(i * each, (i + 1) * each)
-        out[...] = (a[part].astype(F32) + b[part].astype(F32)).astype(out.dtype)
-
-
-def stack_kernel(a, b, out):
-    out[:a.shape[0]] = a[...]
-    out[a.shape[0]:] = b[...]
-
-
-def small_call(kernel, name, a, b, outs):
+        terms = [(ref[...] if len(outs) == 1 else ref[i]).astype(F32) for ref in ins]
+        while len(terms) > 1:
+            terms = [a + b for a, b in zip(terms[::2], terms[1::2])]
+        out[...] = terms[0].astype(BF)
+
+
+def sums(arrays, split):
+    count, shape = len(arrays), arrays[0].shape
+    outs = [shape[1:]] * shape[0] if split else [shape]
     return pl.pallas_call(
-        kernel,
-        in_specs=[VMEM] * 2,
+        partial(sum_kernel, count),
+        in_specs=[VMEM] * count,
         out_specs=[VMEM] * len(outs),
-        out_shape=[jax.ShapeDtypeStruct(shape, BF) for shape in outs],
+        out_shape=[jax.ShapeDtypeStruct(out, BF) for out in outs],
         compiler_params=pltpu.CompilerParams(vmem_limit_bytes=4 << 20),
-        cost_estimate=pl.CostEstimate(flops=a.size, bytes_accessed=6 * a.size, transcendentals=0),
-        name=name,
-    )(a, b)
-
-
-def halves(a, b):
-    return small_call(sum_kernel, "halves", a, b, [(a.shape[0] // 2, *a.shape[1:])] * 2)
-
-
-def plus(a, b):
-    return small_call(sum_kernel, "plus", a, b, [a.shape])[0]
-
-
-def cut_line(a, b):
-    _, n, *tail = a.shape
-    return halves(a.reshape(n, *tail), b.reshape(n, *tail))
-
-
-def stacked(a, b):
-    return small_call(stack_kernel, "stacked", a, b, [(2 * a.shape[0], *a.shape[1:])])[0]
+        cost_estimate=EXCHANGE,
+        name="sums",
+    )(*arrays)
 
 
 def project_kernel(p0, p1, p2, p3, w_uv, w_o, keep, send):
@@ -526,78 +525,121 @@
     )(*parts, w_uv, w_o)
 
 
-def experts_kernel(here, there, hidden, gain, ids, gates, w_gate, up_hbm, down_hbm,
-                   attended, keep, send, residual, x_buf, acc, x_held, held, w_up, w_down, sems):
+def core_sum_kernel(a, b, out):
+    chip = lax.axis_index(AXES) >> 1
+    square, depth = chip & 3, chip >> 2
+    for t in range(a.shape[0]):
+        for z in range(a.shape[1]):
+            out[(depth ^ z) * a.shape[0] + (square ^ t)] = (a[t, z].astype(F32) + b[t, z].astype(F32)).astype(BF)
+
+
+def core_sum(a, b):
+    squares, depth, *tail = a.shape
+    return pl.pallas_call(
+        core_sum_kernel,
+        in_specs=[VMEM] * 2,
+        out_specs=VMEM,
+        out_shape=jax.ShapeDtypeStruct((squares * depth, *tail), BF),
+        compiler_params=pltpu.CompilerParams(vmem_limit_bytes=4 << 20),
+        cost_estimate=EXCHANGE,
+        name="core_sum",
+    )(a, b)
+
+
+def load_kernel(count, *refs):
+    sources, dests, sems = refs[:count], refs[count + 1:-1], refs[-1]
+    copies = [pltpu.make_async_copy(sources[i], dests[i], sems.at[i]) for i in range(count)]
+    for copy in copies:
+        copy.start()
+    for copy in copies:
+        copy.wait()
+
+
+def load(after, *arrays):
+    count = len(arrays)
+    return pl.pallas_call(
+        partial(load_kernel, count),
+        in_specs=[HBM] * count + [pl.BlockSpec(memory_space=pl.ANY)],
+        out_specs=[VMEM] * count,
+        out_shape=[pltpu.VMEM(a.shape, a.dtype) for a in arrays],
+        scratch_shapes=[pltpu.SemaphoreType.DMA((count,))],
+        compiler_params=pltpu.CompilerParams(vmem_limit_bytes=1 << 20),
+        cost_estimate=pl.CostEstimate(
+            flops=0, bytes_accessed=sum(2 * a.size for a in arrays), transcendentals=0),
+        name="load",
+    )(*(in_hbm(a) for a in arrays), after)
+
+
+def experts_kernel(*refs):
+    shares, (hidden, gain, ids, gates, w_gate, w_up, down_hbm) = refs[:8], refs[8:15]
+    attended, keep, send, residual, x_buf, acc, x_held, w_down, sems = refs[15:]
     units = w_gate.shape[0]
     chunks = units // UNITS
-    copies = []
-    for i, (source, dest) in enumerate(((up_hbm, w_up), (down_hbm, w_down))):
-        for k in range(chunks):
-            part = pl.ds(k * UNITS, UNITS)
-            copy = pltpu.make_async_copy(source.at[part], dest.at[part], sems.at[i, k])
-            copy.start()
-            copies.append(copy)
+    parts = [slice(k * UNITS, (k + 1) * UNITS) for k in range(chunks)]
+    downs = [pltpu.make_async_copy(down_hbm.at[pl.ds(k * UNITS, UNITS)], w_down.at[pl.ds(k * UNITS, UNITS)],
+                                   sems.at[k]) for k in range(chunks)]
+    for copy in downs:
+        copy.start()
     linear = lax.axis_index(AXES)
     plane, depth = linear & 7, linear >> 3
-    share = here.shape[2]
-    for core, shares in enumerate((here, there)):
-        for t in range(shares.shape[0]):
-            at = pl.multiple_of((plane ^ (2 * t + core)) * share, LANES)
-            x_buf[:, pl.ds(at, share)] = shares[t].astype(F32)
-            attended[:, pl.ds(at, share)] = shares[t]
+    share = shares[0].shape[1]
+    for d, ref in enumerate(shares):
+        at = pl.multiple_of((plane ^ d) * share, LANES)
+        x_buf[:, pl.ds(at, share)] = ref[...].astype(F32)
+        attended[:, pl.ds(at, share)] = ref[...]
     x = x_buf[...] + hidden[...].astype(F32)
     mean_square = jnp.mean(x * x, axis=1, keepdims=True)
     normed = (x * lax.rsqrt(mean_square + 1e-06) * gain[...]).astype(BF)
     expert = linear * units // EFF
     routed = column(jnp.sum(jnp.where(ids[...] == expert, gates[...], 0.0), axis=0, keepdims=True))
-    parts = [slice(k * UNITS, (k + 1) * UNITS) for k in range(chunks)]
+    count, _, width = x_held.shape
+    for d in range(count):
+        x_held[d] = x[:, d * width:(d + 1) * width]
+    residual[...] = x_held[linear]
     gate = [lax.dot_general(normed, w_gate[part], NT, preferred_element_type=F32) for part in parts]
     gate = [g / (1.0 + jnp.exp(-g)) * routed for g in gate]
     act = []
     for k, part in enumerate(parts):
-        copies[k].wait()
         up = lax.dot_general(normed, w_up[part], NT, preferred_element_type=F32)
         act.append((gate[k] * up).astype(BF))
     for k, part in enumerate(parts):
-        copies[chunks + k].wait()
+        downs[k].wait()
         term = jnp.dot(act[k], w_down[part], preferred_element_type=F32)
         if k == 0:
             acc[...] = term
         else:
             acc[...] += term
-    count, _, width = held.shape
-    for d in range(count):
-        x_held[d] = x[:, d * width:(d + 1) * width]
-        held[d] = acc[:, d * width:(d + 1) * width].astype(BF)
-    residual[...] = x_held[linear]
-    for core, out in enumerate((keep, send)):
-        for t in range(out.shape[0]):
-            for z in range(out.shape[1]):
-                out[t, z] = held[((depth ^ z) << 3) + (plane ^ (2 * t + core))]
-
-
-def experts(here, there, hidden, gain, ids, gates, w_gate, w_up, w_down):
+    core = linear & CORE
+    for d in range(0, count, 2):
+        pair = [acc[:, (d + i) * width:(d + i + 1) * width].astype(BF) for i in range(2)]
+        at = ((d >> 1) ^ (linear >> 1)) & 3, depth ^ (d >> 3)
+        keep[at] = jnp.where(core == 1, pair[1], pair[0])
+        send[at] = jnp.where(core == 1, pair[0], pair[1])
+
+
+def experts(shares, hidden, gain, ids, gates, w_gate, w_up, w_down):
     units, width = w_gate.shape
-    squares = SHAPE[1] * SHAPE[2]
-    small = width // (2 * squares * SHAPE[0])
-    terms = jax.ShapeDtypeStruct((squares, SHAPE[0], HYPS, small), BF)
+    count = math.prod(SHAPE)
+    small = width // count
+    terms = jax.ShapeDtypeStruct((SHAPE[1] * SHAPE[2], SHAPE[0], HYPS, small), BF)
     return pl.pallas_call(
         experts_kernel,
-        in_specs=[VMEM] * 7 + [HBM] * 2,
+        in_specs=[VMEM] * 14 + [HBM],
         out_specs=[VMEM] * 4,
         out_shape=[
             jax.ShapeDtypeStruct((HYPS, width), BF), terms, terms,
             jax.ShapeDtypeStruct((HYPS, small), F32),
         ],
         scratch_shapes=[pltpu.VMEM((HYPS, width), F32)] * 2 + [
-            pltpu.VMEM((2 * squares * SHAPE[0], HYPS, small), F32),
-            pltpu.VMEM((2 * squares * SHAPE[0], HYPS, small), BF),
-        ] + [pltpu.VMEM((units, width), BF)] * 2 + [pltpu.SemaphoreType.DMA((2, units // UNITS))],
-        compiler_params=pltpu.CompilerParams(vmem_limit_bytes=36 << 20),
+            pltpu.VMEM((count, HYPS, small), F32),
+            pltpu.VMEM((units, width), BF),
+            pltpu.SemaphoreType.DMA((units // UNITS,)),
+        ],
+        compiler_params=pltpu.CompilerParams(vmem_limit_bytes=18 << 20),
         cost_estimate=pl.CostEstimate(flops=6 * HYPS * units * width, bytes_accessed=6 * units * width,
                                       transcendentals=HYPS * units),
         name="experts",
-    )(here, there, hidden, gain, ids, gates, w_gate, in_hbm(w_up), in_hbm(w_down))
+    )(*shares, hidden, gain, ids, gates, w_gate, w_up, in_hbm(w_down))
 
 
 def local(
@@ -622,43 +664,38 @@
     scale = MSCALE * MSCALE / math.sqrt(DN + DR)
     info = jnp.concatenate([lengths, parents])
     caches = (cache_latent, cache_rope, suffix_latent, suffix_rope)
-    cut = HYPS // 2
     tied = lax.optimization_barrier
+    square, line = (Y, X, X ^ Y), (Z0 ^ Z1, Z1, Z0)
 
     near_lat, near_rope = swap(query_latent, CORE), swap(query_rope, CORE)
-    lat_a = swap(query_latent[:cut], Y)
-    far_rope = swap(query_rope, Y)
-    lat_b = swap(query_latent[cut:], Y)
-    keep, send = attend(scale, 0, REQ, info, (query_latent, near_lat), (query_rope, near_rope), caches)
-    lat_a, far_rope, send = tied((lat_a, far_rope, send))
-    far_rope = far_rope, swap(far_rope, CORE)
-    near = merge_pair_of(keep, swap(send, CORE), 2)
-    keep, send = attend(scale, 0, REQ // 2, info, (lat_a, swap(lat_a, CORE)), far_rope, caches)
-    lat_b, send = tied((lat_b, send))
-    near = merge_pair_of(near[0], swap(near[1], X), 2)
-    keep, send = attend(scale, REQ // 2, REQ // 2, info, (lat_b, swap(lat_b, CORE)), far_rope, caches, (keep, send))
-    far = merge_pair_of(keep, swap(send, CORE), SHAPE[1] * SHAPE[2])
-    far_y, far_x, far_xy = (swap(v, mask) for v, mask in zip(far[1:], (Y, X, X ^ Y)))
-    parts = merge_plane((near[0], far_y, far_xy), (swap(near[1], Y), far[0], far_x))
-    parts = [parts[0], *(swap(v, mask) for v, mask in zip(parts[1:], (Z0, Z1, Z0 ^ Z1)))]
+    far_lat, far_rope = swap(query_latent, Y), swap(query_rope, Y)
+    keep, *send = attend(scale, True, info, (query_latent, near_lat), (query_rope, near_rope), caches)
+    near = merge_pairs(keep, [swap(v, CORE) for v in send], 2)
+    far_lat, far_rope, near = tied((far_lat, far_rope, near))
+    near_x = swap(near[1], X)
+    far_lat, far_rope = (far_lat, swap(far_lat, CORE)), (far_rope, swap(far_rope, CORE))
+    keep, *send = attend(scale, False, info, far_lat, far_rope, caches)
+    keep, send, near_x = tied((keep, send, near_x))
+    near = merge_pairs(near[0], [near_x], 2)
+    near_y = swap(near[1], Y)
+    far = merge_pairs(keep, [swap(v, CORE) for v in send], len(square) + 1)
+    far_xy, far_x, far_y = swap(far[3], X ^ Y), swap(far[2], X), swap(far[1], Y)
+    parts = merge_plane((near[0], far_y, far_xy), (near_y, far[0], far_x))
+    w_uv, w_o = load(parts[0], w_uv, w_o)
+    parts = [parts[0], *(swap(v, mask) for v, mask in zip(parts[:0:-1], line))]
     keep, send = project(parts, w_uv, w_o)
 
-    keep, send = halves(keep, swap(send, CORE))
-    keep, send = halves(keep, swap(send, X))
-    share = plus(keep, swap(send, Y))
-    share = plus(share, swap(share, Z0))
-    share = plus(share, swap(share, Z1))
-    shares = stacked(share, swap(share, Y))
-    shares = stacked(shares, swap(shares, X))
+    pieces = sums([keep, swap(send, CORE)], True)
+    share, = sums([pieces[0], *(swap(v, mask) for v, mask in zip(pieces[1:], square))], False)
+    share, = sums([share, *(swap(share, mask) for mask in line[::-1])], False)
+    shares = [share, *(swap(share, mask) for mask in square)]
+    shares = [v for pair in zip(shares, [swap(v, CORE) for v in shares]) for v in pair]
     attended, keep, send, residual = experts(
-        shares, swap(shares, CORE), hidden, norm_gain.reshape(1, -1), expert_ids.T, gate_weights.T, w_gate, w_up, w_down)
-
-    keep, send = halves(keep, swap(send, CORE))
-    keep, send = halves(keep, swap(send, X))
-    keep, send = cut_line(keep, swap(send, Y))
-    keep, send = halves(keep, swap(send, Z1))
-    total = keep.astype(F32) + swap(send, Z0).astype(F32)
-    updated = (residual + total[0]).astype(BF)
+        shares, hidden, norm_gain.reshape(1, -1), expert_ids.T, gate_weights.T, w_gate, w_up, w_down)
+
+    total = core_sum(keep, swap(send, CORE))
+    total = lax.all_to_all(total, AXES[:3], split_axis=0, concat_axis=0, tiled=True)
+    updated = (residual + jnp.sum(total.astype(F32), axis=0)).astype(BF)
     return (attended, updated)
 
 

time: 125 us -> 101 us (0.81)
  waiting for transfers between devices: 56.5 us -> 28.2 us
  blocking collectives: 0 us -> 12 us
  Pallas kernels: 32.6 us -> 29.3 us
  local copies, waits for them, and re-layouts: 2.36 us -> 0.04 us
  starting transfers between devices: 31.1 us -> 29.3 us
    ppermute x31 -> x33, waiting for transfers between devices: 56.5 us -> 28.2 us  [swap(): lax.ppermute(value, AXES, [(i, i ^ mask) for i in range(math.prod(SHAPE))])]
    all_to_all x0 -> x1, blocking collectives: none -> 12 us  [local(): lax.all_to_all(total, AXES[:3], split_axis=0, concat_axis=0, tiled=True)]
    pallas_call x18 -> x11, Pallas kernels: 30.8 us -> 27.5 us  [the longest x2 12.3 us: attend(): pl.pallas_call(partial(attend_kernel, scale, fetch), in_specs=[SMEM, spec...]
    ppermute x31 -> x33, starting transfers between devices: 31.1 us -> 29.3 us  [swap(): lax.ppermute(value, AXES, [(i, i ^ mask) for i in range(math.prod(SHAPE))])]
    slice x1 -> x0, local copies, waits for them, and re-layouts: 1.32 us -> none  [local(): lat_b = swap(query_latent[cut:], Y)]
  transfers between devices with their start and end apart: 31 -> 33, of which waited for: 22 -> 21; matrix products, arithmetic and copies ran while one was open for 2% -> 1% of each run, Pallas kernels for 13% -> 16%
where the time goes in v3:
time: 101 us
  starting transfers between devices  29.3 us (29%)
  Pallas kernels  29.3 us (29%)
  waiting for transfers between devices  28.2 us (28%)
  blocking collectives  12 us (12%)
  other arithmetic  1.38 us (1%)
    ppermute x33, starting transfers between devices, swap(): lax.ppermute(value, AXES, [(i, i ^ mask) for i in range(math.prod(SHAPE))])  29.3 us
    ppermute x33, waiting for transfers between devices, swap(): lax.ppermute(value, AXES, [(i, i ^ mask) for i in range(math.prod(SHAPE))])  28.2 us
    pallas_call x2, Pallas kernels, attend(): pl.pallas_call(partial(attend_kernel, scale, fetch), in_specs=[SMEM, spec...  12.3 us
    all_to_all x1, blocking collectives, local(): lax.all_to_all(total, AXES[:3], split_axis=0, concat_axis=0, tiled=True)  12 us
    pallas_call x1, Pallas kernels, experts(): pl.pallas_call(experts_kernel, in_specs=[VMEM] * 14 + [HBM], out_specs=[V...  10.9 us
    pallas_call x1, Pallas kernels, load(): pl.pallas_call(partial(load_kernel, count), in_specs=[HBM] * count + [pl....  3.41 us
  transfers between devices with their start and end apart: 33, of which 21 were waited for; matrix products, arithmetic and copies ran while one was open for 1% of the time, Pallas kernels for 16%

profile of v3, /device:TPU:0, one launch (start us, length us, event | category | flops | bytes accessed | tf_op | source)
XLA Modules:
  0.0 101.0 jit_solution(5665618300744713508)
XLA Ops:
  0.6 0.5 collective-permute-start.2
  1.1 2.6 %collective-permute-start = (bf16[16,32,512]{2,1,0:T(8,128)(2,1)}, bf16[16,32,512]{2,1,0:T(8,128)(2,1)S(1)}, u32[]{:S(2)}, u32[]{:S(2)}) collective-permute-start(bf16[16,32,512]{2,1,0:T(8,128)(2,1)} %ql0.1), channel_id=1, source_target_pairs={{0,2},{1,3},{2,0},{3,1},{4,6},{5,7},{6,4},{7,5},{8,10},{9,11},{10,... | collective-permute-start | bytes 1572872 | tf_op jit(solution)/shard_map/ppermute | solution.py:196
  3.9 0.7 pad_add_fusion.info
  4.7 0.6 collective-permute-done.3.qr1
  5.2 6.4 %attend.2 = (bf16[4,144,512]{2,1,0:T(8,128)(2,1)S(1)}, bf16[2,144,512]{2,1,0:T(8,128)(2,1)S(1)}, bf16[2,144,512]{2,1,0:T(8,128)(2,1)S(1)}) custom-call(s32[20]{0:T(128)S(1)} %pad_add_fusion.info, bf16[16,32,512]{2,1,0:T(8,128)(2,1)} %ql0.1, bf16[16,32,512]{2,1,0:T(8,128)(2,1)S(1)} %collective-permute-done.2.ql1, bf16[16,2048]{1,0:T(8,128)(2,1)} %qr0.1, ...), custom_call_target="tpu_custom_call" | custom-call | flops 1426063360 | bytes 8388608 | tf_op jit(solution)/shard_map/attend/pallas_call | solution.py:378
  11.8 0.4 collective-permute-start.5
  12.2 0.7 collective-permute-start.1
  12.8 0.4 collective-permute-done.4.refs_0_
  13.2 0.4 collective-permute-done.5.refs_1_
  14.0 3.9 %collective-permute-done.1.qr0 = bf16[16,2048]{1,0:T(8,128)(2,1)S(1)} collective-permute-done((bf16[16,2048]{1,0:T(8,128)(2,1)}, bf16[16,2048]{1,0:T(8,128)(2,1)S(1)}, u32[]{:S(2)}, u32[]{:S(2)}) %collective-permute-start.1) | collective-permute-done | bytes 65568 | tf_op jit(solution)/shard_map/ppermute | solution.py:196
  17.9 1.8 %collective-permute-start.8 = (bf16[2,144,512]{2,1,0:T(8,128)(2,1)S(1)}, bf16[2,144,512]{2,1,0:T(8,128)(2,1)S(1)}, u32[]{:S(2)}, u32[]{:S(2)}) collective-permute-start(bf16[2,144,512]{2,1,0:T(8,128)(2,1)S(1)} %get-tuple-element.51), channel_id=1, source_target_pairs={{0,4},{1,5},{2,6},{3,7},{4,0},{5,1},{6,2},{7,3},{8,12},{9,13},{10,... | collective-permute-start | bytes 884744 | tf_op jit(solution)/shard_map/ppermute | solution.py:196
  19.8 1.1 %collective-permute-done.7.qr1 = bf16[16,2048]{1,0:T(8,128)(2,1)S(1)} collective-permute-done((bf16[16,2048]{1,0:T(8,128)(2,1)S(1)}, bf16[16,2048]{1,0:T(8,128)(2,1)S(1)}, u32[]{:S(2)}, u32[]{:S(2)}) %collective-permute-start.7) | collective-permute-done | bytes 65568 | tf_op jit(solution)/shard_map/ppermute | solution.py:196
  20.9 6.0 %attend.3 = (bf16[4,144,512]{2,1,0:T(8,128)(2,1)S(1)}, bf16[2,144,512]{2,1,0:T(8,128)(2,1)S(1)}, bf16[2,144,512]{2,1,0:T(8,128)(2,1)S(1)}) custom-call(s32[20]{0:T(128)S(1)} %pad_add_fusion.info, bf16[16,32,512]{2,1,0:T(8,128)(2,1)S(1)} %collective-permute-done.ql0, bf16[16,32,512]{2,1,0:T(8,128)(2,1)S(1)} %collective-permute-done.6.ql1, ...), custom_call_target="tpu_custom_call" | custom-call | flops 1426063360 | bytes 8388608 | tf_op jit(solution)/shard_map/attend/pallas_call | solution.py:378
  26.9 0.4 collective-permute-done.8.refs_0_
  27.3 0.5 collective-permute-start.10
  28.0 1.8 %collective-permute-start.13 = (bf16[1,144,512]{2,1,0:T(8,128)(2,1)S(1)}, bf16[1,144,512]{2,1,0:T(8,128)(2,1)S(1)}, u32[]{:S(2)}, u32[]{:S(2)}) collective-permute-start(bf16[1,144,512]{2,1,0:T(8,128)(2,1)S(1)} %get-tuple-element.59), channel_id=1, source_target_pairs={{0,2},{1,3},{2,0},{3,1},{4,6},{5,7},{6,4},{7,5},{8,10},{9,11},{10,... | collective-permute-start | bytes 442376 | tf_op jit(solution)/shard_map/ppermute | solution.py:196
  30.2 1.3 %collective-permute-start.11 = (bf16[1,144,512]{2,1,0:T(8,128)(2,1)S(1)}, bf16[1,144,512]{2,1,0:T(8,128)(2,1)S(1)}, u32[]{:S(2)}, u32[]{:S(2)}) collective-permute-start(bf16[1,144,512]{2,1,0:T(8,128)(2,1)S(1)} %get-tuple-element.57), channel_id=1, source_target_pairs={{0,2},{1,3},{2,0},{3,1},{4,6},{5,7},{6,4},{7,5},{8,10},{9,11},{10,... | collective-permute-start | bytes 442376 | tf_op jit(solution)/shard_map/ppermute | solution.py:196
  31.5 1.7 %collective-permute-start.12 = (bf16[1,144,512]{2,1,0:T(8,128)(2,1)S(1)}, bf16[1,144,512]{2,1,0:T(8,128)(2,1)S(1)}, u32[]{:S(2)}, u32[]{:S(2)}) collective-permute-start(bf16[1,144,512]{2,1,0:T(8,128)(2,1)S(1)} %get-tuple-element.58), channel_id=1, source_target_pairs={{0,6},{1,7},{2,4},{3,5},{4,2},{5,3},{6,0},{7,1},{8,14},{9,15},{10,... | collective-permute-start | bytes 442376 | tf_op jit(solution)/shard_map/ppermute | solution.py:196
  33.2 0.5 collective-permute-start.14
  33.7 2.8 %collective-permute-done.13.refs_3_ = bf16[1,144,512]{2,1,0:T(8,128)(2,1)S(1)} collective-permute-done((bf16[1,144,512]{2,1,0:T(8,128)(2,1)S(1)}, bf16[1,144,512]{2,1,0:T(8,128)(2,1)S(1)}, u32[]{:S(2)}, u32[]{:S(2)}) %collective-permute-start.13) | collective-permute-done | bytes 147488 | tf_op jit(solution)/shard_map/ppermute | solution.py:196
  36.5 3.7 %collective-permute-done.11.refs_1_ = bf16[1,144,512]{2,1,0:T(8,128)(2,1)S(1)} collective-permute-done((bf16[1,144,512]{2,1,0:T(8,128)(2,1)S(1)}, bf16[1,144,512]{2,1,0:T(8,128)(2,1)S(1)}, u32[]{:S(2)}, u32[]{:S(2)}) %collective-permute-start.11) | collective-permute-done | bytes 147488 | tf_op jit(solution)/shard_map/ppermute | solution.py:196
  40.5 3.9 %collective-permute-start.15 = (bf16[80,512]{1,0:T(8,128)(2,1)S(1)}, bf16[80,512]{1,0:T(8,128)(2,1)S(1)}, u32[]{:S(2)}, u32[]{:S(2)}) collective-permute-start(bf16[80,512]{1,0:T(8,128)(2,1)S(1)} %get-tuple-element.63), channel_id=1, source_target_pairs={{0,24},{1,25},{2,26},{3,27},{4,28},{5,29},{6,30},{7,31},{8,16},{9,... | collective-permute-start | bytes 245768 | tf_op jit(solution)/shard_map/ppermute | solution.py:196
  44.4 0.6 collective-permute-start.17
  45.1 3.4 %load.1 = (bf16[512,512]{1,0:T(8,128)(2,1)S(1)}, bf16[512,7168]{1,0:T(8,128)(2,1)S(1)}) custom-call(bf16[512,512]{1,0:T(8,128)(2,1)} %refs_0_.1, bf16[512,7168]{1,0:T(8,128)(2,1)} %refs_1_.1, bf16[80,512]{1,0:T(8,128)(2,1)S(1)} %get-tuple-element.62.refs_2_.p0), custom_call_target="tpu_custom_call" | custom-call | bytes 7864320 | tf_op jit(solution)/shard_map/load/pallas_call | solution.py:560
  48.5 2.1 %collective-permute-done.16.p2 = bf16[80,512]{1,0:T(8,128)(2,1)S(1)} collective-permute-done((bf16[80,512]{1,0:T(8,128)(2,1)S(1)}, bf16[80,512]{1,0:T(8,128)(2,1)S(1)}, u32[]{:S(2)}, u32[]{:S(2)}) %collective-permute-start.16) | collective-permute-done | bytes 81952 | tf_op jit(solution)/shard_map/ppermute | solution.py:196
  50.6 1.4 %project.1 = (bf16[4,16,896]{2,1,0:T(8,128)(2,1)S(1)}, bf16[4,16,896]{2,1,0:T(8,128)(2,1)S(1)}) custom-call(bf16[80,512]{1,0:T(8,128)(2,1)S(1)} %get-tuple-element.62.refs_2_.p0, bf16[80,512]{1,0:T(8,128)(2,1)S(1)} %collective-permute-done.15.p1, bf16[80,512]{1,0:T(8,128)(2,1)S(1)} %collective-permute-done.16.p2, ...), custom_call_target="tpu_custom_call" | custom-call | flops 117440512 | bytes 7340032 | tf_op jit(solution)/shard_map/project/pallas_call | solution.py:517
  52.2 1.3 %collective-permute-done.18.refs_1_ = bf16[4,16,896]{2,1,0:T(8,128)(2,1)S(1)} collective-permute-done((bf16[4,16,896]{2,1,0:T(8,128)(2,1)S(1)}, bf16[4,16,896]{2,1,0:T(8,128)(2,1)S(1)}, u32[]{:S(2)}, u32[]{:S(2)}) %collective-permute-start.18) | collective-permute-done | bytes 114720 | tf_op jit(solution)/shard_map/ppermute | solution.py:196
  53.5 1.6 %collective-permute-start.19 = (bf16[16,896]{1,0:T(8,128)(2,1)S(1)}, bf16[16,896]{1,0:T(8,128)(2,1)S(1)}, u32[]{:S(2)}, u32[]{:S(2)}) collective-permute-start(bf16[16,896]{1,0:T(8,128)(2,1)S(1)} %get-tuple-element.71), channel_id=1, source_target_pairs={{0,2},{1,3},{2,0},{3,1},{4,6},{5,7},{6,4},{7,5},{8,10},{9,11},{10,... | collective-permute-start | bytes 86024 | tf_op jit(solution)/shard_map/ppermute | solution.py:196
  55.1 1.5 %collective-permute-start.20 = (bf16[16,896]{1,0:T(8,128)(2,1)S(1)}, bf16[16,896]{1,0:T(8,128)(2,1)S(1)}, u32[]{:S(2)}, u32[]{:S(2)}) collective-permute-start(bf16[16,896]{1,0:T(8,128)(2,1)S(1)} %get-tuple-element.72), channel_id=1, source_target_pairs={{0,4},{1,5},{2,6},{3,7},{4,0},{5,1},{6,2},{7,3},{8,12},{9,13},{10,... | collective-permute-start | bytes 86024 | tf_op jit(solution)/shard_map/ppermute | solution.py:196
  56.6 0.5 collective-permute-start.21
  57.1 0.4 collective-permute-done.19.refs_1_
  57.4 1.8 %collective-permute-done.20.refs_2_ = bf16[16,896]{1,0:T(8,128)(2,1)S(1)} collective-permute-done((bf16[16,896]{1,0:T(8,128)(2,1)S(1)}, bf16[16,896]{1,0:T(8,128)(2,1)S(1)}, u32[]{:S(2)}, u32[]{:S(2)}) %collective-permute-start.20) | collective-permute-done | bytes 28704 | tf_op jit(solution)/shard_map/ppermute | solution.py:196
  59.2 2.1 %collective-permute-done.21.refs_3_ = bf16[16,896]{1,0:T(8,128)(2,1)S(1)} collective-permute-done((bf16[16,896]{1,0:T(8,128)(2,1)S(1)}, bf16[16,896]{1,0:T(8,128)(2,1)S(1)}, u32[]{:S(2)}, u32[]{:S(2)}) %collective-permute-start.21) | collective-permute-done | bytes 28704 | tf_op jit(solution)/shard_map/ppermute | solution.py:196
  61.4 2.7 %collective-permute-start.24 = (bf16[16,896]{1,0:T(8,128)(2,1)S(1)}, bf16[16,896]{1,0:T(8,128)(2,1)S(1)}, u32[]{:S(2)}, u32[]{:S(2)}) collective-permute-start(bf16[16,896]{1,0:T(8,128)(2,1)S(1)} %sums.4.refs_0_), channel_id=1, source_target_pairs={{0,24},{1,25},{2,26},{3,27},{4,28},{5,29},{6,30},{7,31},{8,16},{9,... | collective-permute-start | bytes 86024 | tf_op jit(solution)/shard_map/ppermute | solution.py:196
  64.1 1.8 %collective-permute-start.22 = (bf16[16,896]{1,0:T(8,128)(2,1)S(1)}, bf16[16,896]{1,0:T(8,128)(2,1)S(1)}, u32[]{:S(2)}, u32[]{:S(2)}) collective-permute-start(bf16[16,896]{1,0:T(8,128)(2,1)S(1)} %sums.4.refs_0_), channel_id=1, source_target_pairs={{0,8},{1,9},{2,10},{3,11},{4,12},{5,13},{6,14},{7,15},{8,0},{9,1},... | collective-permute-start | bytes 86024 | tf_op jit(solution)/shard_map/ppermute | solution.py:196
  65.8 1.5 %collective-permute-done.24.refs_3_ = bf16[16,896]{1,0:T(8,128)(2,1)S(1)} collective-permute-done((bf16[16,896]{1,0:T(8,128)(2,1)S(1)}, bf16[16,896]{1,0:T(8,128)(2,1)S(1)}, u32[]{:S(2)}, u32[]{:S(2)}) %collective-permute-start.24) | collective-permute-done | bytes 28704 | tf_op jit(solution)/shard_map/ppermute | solution.py:196
  67.3 1.5 %collective-permute-done.23.refs_2_ = bf16[16,896]{1,0:T(8,128)(2,1)S(1)} collective-permute-done((bf16[16,896]{1,0:T(8,128)(2,1)S(1)}, bf16[16,896]{1,0:T(8,128)(2,1)S(1)}, u32[]{:S(2)}, u32[]{:S(2)}) %collective-permute-start.23) | collective-permute-done | bytes 28704 | tf_op jit(solution)/shard_map/ppermute | solution.py:196
  68.9 0.5 collective-permute-start.30
  69.4 1.5 %collective-permute-start.28 = (bf16[16,896]{1,0:T(8,128)(2,1)S(1)}, bf16[16,896]{1,0:T(8,128)(2,1)S(1)}, u32[]{:S(2)}, u32[]{:S(2)}) collective-permute-start(bf16[16,896]{1,0:T(8,128)(2,1)S(1)} %sums.5.refs_0_), channel_id=1, source_target_pairs={{0,4},{1,5},{2,6},{3,7},{4,0},{5,1},{6,2},{7,3},{8,12},{9,13},{10,... | collective-permute-start | bytes 86024 | tf_op jit(solution)/shard_map/ppermute | solution.py:196
  70.9 1.5 %collective-permute-start.26 = (bf16[16,896]{1,0:T(8,128)(2,1)S(1)}, bf16[16,896]{1,0:T(8,128)(2,1)S(1)}, u32[]{:S(2)}, u32[]{:S(2)}) collective-permute-start(bf16[16,896]{1,0:T(8,128)(2,1)S(1)} %sums.5.refs_0_), channel_id=1, source_target_pairs={{0,2},{1,3},{2,0},{3,1},{4,6},{5,7},{6,4},{7,5},{8,10},{9,11},{10,... | collective-permute-start | bytes 86024 | tf_op jit(solution)/shard_map/ppermute | solution.py:196
  72.4 1.3 %collective-permute-done.30.refs_6_ = bf16[16,896]{1,0:T(8,128)(2,1)S(1)} collective-permute-done((bf16[16,896]{1,0:T(8,128)(2,1)S(1)}, bf16[16,896]{1,0:T(8,128)(2,1)S(1)}, u32[]{:S(2)}, u32[]{:S(2)}) %collective-permute-start.30) | collective-permute-done | bytes 28704 | tf_op jit(solution)/shard_map/ppermute | solution.py:196
  73.7 0.5 collective-permute-start.29
  74.2 0.6 collective-permute-done.26.refs_2_
  75.1 0.9 collective-permute-done.27.refs_3_
  76.0 10.9 %experts.1 = (bf16[16,7168]{1,0:T(8,128)(2,1)}, bf16[4,4,16,224]{3,2,1,0:T(8,128)(2,1)S(1)}, bf16[4,4,16,224]{3,2,1,0:T(8,128)(2,1)S(1)}, f32[16,224]{1,0:T(8,128)S(1)}) custom-call(bf16[16,896]{1,0:T(8,128)(2,1)S(1)} %sums.5.refs_0_, bf16[16,896]{1,0:T(8,128)(2,1)S(1)} %collective-permute-done.25.refs_1_, ...), custom_call_target="tpu_custom_call" | custom-call | flops 704643072 | bytes 44040192 | tf_op jit(solution)/shard_map/experts/pallas_call | solution.py:625
  87.1 1.2 %collective-permute-done.32.b = bf16[4,4,16,224]{3,2,1,0:T(8,128)(2,1)S(1)} collective-permute-done((bf16[4,4,16,224]{3,2,1,0:T(8,128)(2,1)S(1)}, bf16[4,4,16,224]{3,2,1,0:T(8,128)(2,1)S(1)}, u32[]{:S(2)}, u32[]{:S(2)}) %collective-permute-start.32) | collective-permute-done | bytes 114720 | tf_op jit(solution)/shard_map/ppermute | solution.py:196
  88.4 12.0 %all_to_all.5 = bf16[16,16,224]{2,1,0:T(8,128)(2,1)S(1)} all-to-all(bf16[16,16,224]{2,1,0:T(8,128)(2,1)S(1)} %core_sum.1), channel_id=1, replica_groups=mesh['z'=4,'x'=2,'y'=2,'core'=2] {'z','x','y'}, dimensions={0} | all-to-all | bytes 229376 | tf_op jit(solution)/shard_map/all_to_all | solution.py:697
  100.4 0.6 add_convert_fusion
  (54 shorter events, 2.5 us)
Async XLA Ops:
  0.6 4.6 %collective-permute-start.2 = (bf16[16,32,512]{2,1,0:T(8,128)(2,1)}, bf16[16,32,512]{2,1,0:T(8,128)(2,1)S(1)}, u32[]{:S(2)}, u32[]{:S(2)}) collective-permute-start(bf16[16,32,512]{2,1,0:T(8,128)(2,1)} %ql0.1), channel_id=1, source_target_pairs={{0,1},{1,0},{2,3},{3,2},{4,5},{5,4},{6,7},{7,6},{8,9},{9,8},{10,11... | collective-permute-start | bytes 1572872 | tf_op jit(solution)/shard_map/ppermute | solution.py:196
  1.1 16.7 %collective-permute-start = (bf16[16,32,512]{2,1,0:T(8,128)(2,1)}, bf16[16,32,512]{2,1,0:T(8,128)(2,1)S(1)}, u32[]{:S(2)}, u32[]{:S(2)}) collective-permute-start(bf16[16,32,512]{2,1,0:T(8,128)(2,1)} %ql0.1), channel_id=1, source_target_pairs={{0,2},{1,3},{2,0},{3,1},{4,6},{5,7},{6,4},{7,5},{8,10},{9,11},{10,... | collective-permute-start | bytes 1572872 | tf_op jit(solution)/shard_map/ppermute | solution.py:196
  3.7 1.5 %collective-permute-start.3 = (bf16[16,2048]{1,0:T(8,128)(2,1)}, bf16[16,2048]{1,0:T(8,128)(2,1)S(1)}, u32[]{:S(2)}, u32[]{:S(2)}) collective-permute-start(bf16[16,2048]{1,0:T(8,128)(2,1)} %qr0.1), channel_id=1, source_target_pairs={{0,1},{1,0},{2,3},{3,2},{4,5},{5,4},{6,7},{7,6},{8,9},{9,8},{10,11... | collective-permute-start | bytes 196616 | tf_op jit(solution)/shard_map/ppermute | solution.py:196
  5.2 70.8 %copy-start = (bf16[1024,7168]{1,0:T(8,128)(2,1)S(1)}, bf16[1024,7168]{1,0:T(8,128)(2,1)}, u32[]{:S(2)}) copy-start(bf16[1024,7168]{1,0:T(8,128)(2,1)} %refs_13_.1) | copy-start | bytes 44040196
  11.6 1.6 %collective-permute-start.4 = (bf16[2,144,512]{2,1,0:T(8,128)(2,1)S(1)}, bf16[2,144,512]{2,1,0:T(8,128)(2,1)S(1)}, u32[]{:S(2)}, u32[]{:S(2)}) collective-permute-start(bf16[2,144,512]{2,1,0:T(8,128)(2,1)S(1)} %get-tuple-element.41), channel_id=1, source_target_pairs={{0,1},{1,0},{2,3},{3,2},{4,5},{5,4},{6,7},{7,6},{8,9},{9,8},{10,11... | collective-permute-start | bytes 884744 | tf_op jit(solution)/shard_map/ppermute | solution.py:196
  11.8 1.9 %collective-permute-start.5 = (bf16[2,144,512]{2,1,0:T(8,128)(2,1)S(1)}, bf16[2,144,512]{2,1,0:T(8,128)(2,1)S(1)}, u32[]{:S(2)}, u32[]{:S(2)}) collective-permute-start(bf16[2,144,512]{2,1,0:T(8,128)(2,1)S(1)} %get-tuple-element.42), channel_id=1, source_target_pairs={{0,1},{1,0},{2,3},{3,2},{4,5},{5,4},{6,7},{7,6},{8,9},{9,8},{10,11... | collective-permute-start | bytes 884744 | tf_op jit(solution)/shard_map/ppermute | solution.py:196
  12.2 5.7 %collective-permute-start.1 = (bf16[16,2048]{1,0:T(8,128)(2,1)}, bf16[16,2048]{1,0:T(8,128)(2,1)S(1)}, u32[]{:S(2)}, u32[]{:S(2)}) collective-permute-start(bf16[16,2048]{1,0:T(8,128)(2,1)} %qr0.1), channel_id=1, source_target_pairs={{0,2},{1,3},{2,0},{3,1},{4,6},{5,7},{6,4},{7,5},{8,10},{9,11},{10,... | collective-permute-start | bytes 196616 | tf_op jit(solution)/shard_map/ppermute | solution.py:196
  13.7 62.3 %slice-start = ((s8[14680064]{0:T(1024)(128)(4,1)}), s8[4194304]{0:T(1024)(128)(4,1)S(1)}, s32[]{:S(2)}) async-start(s8[14680064]{0:T(1024)(128)(4,1)} %bitcast.3), calls=%async_computation.1 | async-start | bytes 8388608
  17.9 58.1 %slice-start.1 = ((s8[14680064]{0:T(1024)(128)(4,1)}), s8[4194304]{0:T(1024)(128)(4,1)S(1)}, s32[]{:S(2)}) async-start(s8[14680064]{0:T(1024)(128)(4,1)} %bitcast.3), calls=%async_computation.2 | async-start | bytes 8388608
  17.9 3.1 %collective-permute-start.6 = (bf16[16,32,512]{2,1,0:T(8,128)(2,1)S(1)}, bf16[16,32,512]{2,1,0:T(8,128)(2,1)S(1)}, u32[]{:S(2)}, u32[]{:S(2)}) collective-permute-start(bf16[16,32,512]{2,1,0:T(8,128)(2,1)S(1)} %collective-permute-done.ql0), channel_id=1, source_target_pairs={{0,1},{1,0},{2,3},{3,2},{4,5},{5,4},{6,7},{7,6},{8,9},{9,8},{10,11... | collective-permute-start | bytes 1572872 | tf_op jit(solution)/shard_map/ppermute | solution.py:196
  17.9 9.4 %collective-permute-start.8 = (bf16[2,144,512]{2,1,0:T(8,128)(2,1)S(1)}, bf16[2,144,512]{2,1,0:T(8,128)(2,1)S(1)}, u32[]{:S(2)}, u32[]{:S(2)}) collective-permute-start(bf16[2,144,512]{2,1,0:T(8,128)(2,1)S(1)} %get-tuple-element.51), channel_id=1, source_target_pairs={{0,4},{1,5},{2,6},{3,7},{4,0},{5,1},{6,2},{7,3},{8,12},{9,13},{10,... | collective-permute-start | bytes 884744 | tf_op jit(solution)/shard_map/ppermute | solution.py:196
  19.7 1.3 %collective-permute-start.7 = (bf16[16,2048]{1,0:T(8,128)(2,1)S(1)}, bf16[16,2048]{1,0:T(8,128)(2,1)S(1)}, u32[]{:S(2)}, u32[]{:S(2)}) collective-permute-start(bf16[16,2048]{1,0:T(8,128)(2,1)S(1)} %collective-permute-done.1.qr0), channel_id=1, source_target_pairs={{0,1},{1,0},{2,3},{3,2},{4,5},{5,4},{6,7},{7,6},{8,9},{9,8},{10,11... | collective-permute-start | bytes 196616 | tf_op jit(solution)/shard_map/ppermute | solution.py:196
  27.3 2.5 %collective-permute-start.9 = (bf16[2,144,512]{2,1,0:T(8,128)(2,1)S(1)}, bf16[2,144,512]{2,1,0:T(8,128)(2,1)S(1)}, u32[]{:S(2)}, u32[]{:S(2)}) collective-permute-start(bf16[2,144,512]{2,1,0:T(8,128)(2,1)S(1)} %get-tuple-element.55), channel_id=1, source_target_pairs={{0,1},{1,0},{2,3},{3,2},{4,5},{5,4},{6,7},{7,6},{8,9},{9,8},{10,11... | collective-permute-start | bytes 884744 | tf_op jit(solution)/shard_map/ppermute | solution.py:196
  27.3 2.5 %collective-permute-start.10 = (bf16[2,144,512]{2,1,0:T(8,128)(2,1)S(1)}, bf16[2,144,512]{2,1,0:T(8,128)(2,1)S(1)}, u32[]{:S(2)}, u32[]{:S(2)}) collective-permute-start(bf16[2,144,512]{2,1,0:T(8,128)(2,1)S(1)} %get-tuple-element.56), channel_id=1, source_target_pairs={{0,1},{1,0},{2,3},{3,2},{4,5},{5,4},{6,7},{7,6},{8,9},{9,8},{10,11... | collective-permute-start | bytes 884744 | tf_op jit(solution)/shard_map/ppermute | solution.py:196
  28.0 8.5 %collective-permute-start.13 = (bf16[1,144,512]{2,1,0:T(8,128)(2,1)S(1)}, bf16[1,144,512]{2,1,0:T(8,128)(2,1)S(1)}, u32[]{:S(2)}, u32[]{:S(2)}) collective-permute-start(bf16[1,144,512]{2,1,0:T(8,128)(2,1)S(1)} %get-tuple-element.59), channel_id=1, source_target_pairs={{0,2},{1,3},{2,0},{3,1},{4,6},{5,7},{6,4},{7,5},{8,10},{9,11},{10,... | collective-permute-start | bytes 442376 | tf_op jit(solution)/shard_map/ppermute | solution.py:196
  30.2 10.0 %collective-permute-start.11 = (bf16[1,144,512]{2,1,0:T(8,128)(2,1)S(1)}, bf16[1,144,512]{2,1,0:T(8,128)(2,1)S(1)}, u32[]{:S(2)}, u32[]{:S(2)}) collective-permute-start(bf16[1,144,512]{2,1,0:T(8,128)(2,1)S(1)} %get-tuple-element.57), channel_id=1, source_target_pairs={{0,2},{1,3},{2,0},{3,1},{4,6},{5,7},{6,4},{7,5},{8,10},{9,11},{10,... | collective-permute-start | bytes 442376 | tf_op jit(solution)/shard_map/ppermute | solution.py:196
  31.5 8.7 %collective-permute-start.12 = (bf16[1,144,512]{2,1,0:T(8,128)(2,1)S(1)}, bf16[1,144,512]{2,1,0:T(8,128)(2,1)S(1)}, u32[]{:S(2)}, u32[]{:S(2)}) collective-permute-start(bf16[1,144,512]{2,1,0:T(8,128)(2,1)S(1)} %get-tuple-element.58), channel_id=1, source_target_pairs={{0,6},{1,7},{2,4},{3,5},{4,2},{5,3},{6,0},{7,1},{8,14},{9,15},{10,... | collective-permute-start | bytes 442376 | tf_op jit(solution)/shard_map/ppermute | solution.py:196
  33.2 7.0 %collective-permute-start.14 = (bf16[1,144,512]{2,1,0:T(8,128)(2,1)S(1)}, bf16[1,144,512]{2,1,0:T(8,128)(2,1)S(1)}, u32[]{:S(2)}, u32[]{:S(2)}) collective-permute-start(bf16[1,144,512]{2,1,0:T(8,128)(2,1)S(1)} %get-tuple-element.61), channel_id=1, source_target_pairs={{0,4},{1,5},{2,6},{3,7},{4,0},{5,1},{6,2},{7,3},{8,12},{9,13},{10,... | collective-permute-start | bytes 442376 | tf_op jit(solution)/shard_map/ppermute | solution.py:196
  40.5 8.0 %collective-permute-start.15 = (bf16[80,512]{1,0:T(8,128)(2,1)S(1)}, bf16[80,512]{1,0:T(8,128)(2,1)S(1)}, u32[]{:S(2)}, u32[]{:S(2)}) collective-permute-start(bf16[80,512]{1,0:T(8,128)(2,1)S(1)} %get-tuple-element.63), channel_id=1, source_target_pairs={{0,24},{1,25},{2,26},{3,27},{4,28},{5,29},{6,30},{7,31},{8,16},{9,... | collective-permute-start | bytes 245768 | tf_op jit(solution)/shard_map/ppermute | solution.py:196
  44.4 6.2 %collective-permute-start.16 = (bf16[80,512]{1,0:T(8,128)(2,1)S(1)}, bf16[80,512]{1,0:T(8,128)(2,1)S(1)}, u32[]{:S(2)}, u32[]{:S(2)}) collective-permute-start(bf16[80,512]{1,0:T(8,128)(2,1)S(1)} %get-tuple-element.64), channel_id=1, source_target_pairs={{0,16},{1,17},{2,18},{3,19},{4,20},{5,21},{6,22},{7,23},{8,24},{9,... | collective-permute-start | bytes 245768 | tf_op jit(solution)/shard_map/ppermute | solution.py:196
  44.4 6.2 %collective-permute-start.17 = (bf16[80,512]{1,0:T(8,128)(2,1)S(1)}, bf16[80,512]{1,0:T(8,128)(2,1)S(1)}, u32[]{:S(2)}, u32[]{:S(2)}) collective-permute-start(bf16[80,512]{1,0:T(8,128)(2,1)S(1)} %get-tuple-element.65), channel_id=1, source_target_pairs={{0,8},{1,9},{2,10},{3,11},{4,12},{5,13},{6,14},{7,15},{8,0},{9,1},... | collective-permute-start | bytes 245768 | tf_op jit(solution)/shard_map/ppermute | solution.py:196
  45.0 30.9 %slice-start.2 = ((s8[14680064]{0:T(1024)(128)(4,1)}), s8[4194304]{0:T(1024)(128)(4,1)S(1)}, s32[]{:S(2)}) async-start(s8[14680064]{0:T(1024)(128)(4,1)} %bitcast.3), calls=%async_computation.3 | async-start | bytes 8388608
  45.0 30.9 %copy-start.1 = (bf16[16,7168]{1,0:T(8,128)(2,1)S(1)}, bf16[16,7168]{1,0:T(8,128)(2,1)}, u32[]{:S(2)}) copy-start(bf16[16,7168]{1,0:T(8,128)(2,1)} %refs_8_.1) | copy-start | bytes 688132
  45.0 30.9 %copy-start.2 = (f32[7168]{0:T(1024)S(1)}, f32[7168]{0:T(1024)}, u32[]{:S(2)}) copy-start(f32[7168]{0:T(1024)} %param.28) | copy-start | bytes 86020
  45.1 31.0 %copy-start.3 = (s32[16,8]{0,1:T(8,128)S(1)}, s32[16,8]{0,1:T(8,128)}, u32[]{:S(2)}) copy-start(s32[16,8]{0,1:T(8,128)} %param.32) | copy-start | bytes 1540
  45.1 31.0 %copy-start.4 = (f32[16,8]{0,1:T(8,128)S(1)}, f32[16,8]{0,1:T(8,128)}, u32[]{:S(2)}) copy-start(f32[16,8]{0,1:T(8,128)} %param.33) | copy-start | bytes 1540
  50.6 25.4 %slice-start.3 = ((s8[14680064]{0:T(1024)(128)(4,1)}), s8[2097152]{0:T(1024)(128)(4,1)S(1)}, s32[]{:S(2)}) async-start(s8[14680064]{0:T(1024)(128)(4,1)} %bitcast.3), calls=%async_computation.4 | async-start | bytes 4194304
  52.1 1.4 %collective-permute-start.18 = (bf16[4,16,896]{2,1,0:T(8,128)(2,1)S(1)}, bf16[4,16,896]{2,1,0:T(8,128)(2,1)S(1)}, u32[]{:S(2)}, u32[]{:S(2)}) collective-permute-start(bf16[4,16,896]{2,1,0:T(8,128)(2,1)S(1)} %get-tuple-element.69), channel_id=1, source_target_pairs={{0,1},{1,0},{2,3},{3,2},{4,5},{5,4},{6,7},{7,6},{8,9},{9,8},{10,11... | collective-permute-start | bytes 344072 | tf_op jit(solution)/shard_map/ppermute | solution.py:196
  53.5 3.9 %collective-permute-start.19 = (bf16[16,896]{1,0:T(8,128)(2,1)S(1)}, bf16[16,896]{1,0:T(8,128)(2,1)S(1)}, u32[]{:S(2)}, u32[]{:S(2)}) collective-permute-start(bf16[16,896]{1,0:T(8,128)(2,1)S(1)} %get-tuple-element.71), channel_id=1, source_target_pairs={{0,2},{1,3},{2,0},{3,1},{4,6},{5,7},{6,4},{7,5},{8,10},{9,11},{10,... | collective-permute-start | bytes 86024 | tf_op jit(solution)/shard_map/ppermute | solution.py:196
  55.1 4.1 %collective-permute-start.20 = (bf16[16,896]{1,0:T(8,128)(2,1)S(1)}, bf16[16,896]{1,0:T(8,128)(2,1)S(1)}, u32[]{:S(2)}, u32[]{:S(2)}) collective-permute-start(bf16[16,896]{1,0:T(8,128)(2,1)S(1)} %get-tuple-element.72), channel_id=1, source_target_pairs={{0,4},{1,5},{2,6},{3,7},{4,0},{5,1},{6,2},{7,3},{8,12},{9,13},{10,... | collective-permute-start | bytes 86024 | tf_op jit(solution)/shard_map/ppermute | solution.py:196
  56.6 4.8 %collective-permute-start.21 = (bf16[16,896]{1,0:T(8,128)(2,1)S(1)}, bf16[16,896]{1,0:T(8,128)(2,1)S(1)}, u32[]{:S(2)}, u32[]{:S(2)}) collective-permute-start(bf16[16,896]{1,0:T(8,128)(2,1)S(1)} %get-tuple-element.73), channel_id=1, source_target_pairs={{0,6},{1,7},{2,4},{3,5},{4,2},{5,3},{6,0},{7,1},{8,14},{9,15},{10,... | collective-permute-start | bytes 86024 | tf_op jit(solution)/shard_map/ppermute | solution.py:196
  61.4 5.9 %collective-permute-start.24 = (bf16[16,896]{1,0:T(8,128)(2,1)S(1)}, bf16[16,896]{1,0:T(8,128)(2,1)S(1)}, u32[]{:S(2)}, u32[]{:S(2)}) collective-permute-start(bf16[16,896]{1,0:T(8,128)(2,1)S(1)} %sums.4.refs_0_), channel_id=1, source_target_pairs={{0,24},{1,25},{2,26},{3,27},{4,28},{5,29},{6,30},{7,31},{8,16},{9,... | collective-permute-start | bytes 86024 | tf_op jit(solution)/shard_map/ppermute | solution.py:196
  64.1 4.8 %collective-permute-start.23 = (bf16[16,896]{1,0:T(8,128)(2,1)S(1)}, bf16[16,896]{1,0:T(8,128)(2,1)S(1)}, u32[]{:S(2)}, u32[]{:S(2)}) collective-permute-start(bf16[16,896]{1,0:T(8,128)(2,1)S(1)} %sums.4.refs_0_), channel_id=1, source_target_pairs={{0,16},{1,17},{2,18},{3,19},{4,20},{5,21},{6,22},{7,23},{8,24},{9,... | collective-permute-start | bytes 86024 | tf_op jit(solution)/shard_map/ppermute | solution.py:196
  64.1 4.8 %collective-permute-start.22 = (bf16[16,896]{1,0:T(8,128)(2,1)S(1)}, bf16[16,896]{1,0:T(8,128)(2,1)S(1)}, u32[]{:S(2)}, u32[]{:S(2)}) collective-permute-start(bf16[16,896]{1,0:T(8,128)(2,1)S(1)} %sums.4.refs_0_), channel_id=1, source_target_pairs={{0,8},{1,9},{2,10},{3,11},{4,12},{5,13},{6,14},{7,15},{8,0},{9,1},... | collective-permute-start | bytes 86024 | tf_op jit(solution)/shard_map/ppermute | solution.py:196
  68.9 4.8 %collective-permute-start.30 = (bf16[16,896]{1,0:T(8,128)(2,1)S(1)}, bf16[16,896]{1,0:T(8,128)(2,1)S(1)}, u32[]{:S(2)}, u32[]{:S(2)}) collective-permute-start(bf16[16,896]{1,0:T(8,128)(2,1)S(1)} %sums.5.refs_0_), channel_id=1, source_target_pairs={{0,6},{1,7},{2,4},{3,5},{4,2},{5,3},{6,0},{7,1},{8,14},{9,15},{10,... | collective-permute-start | bytes 86024 | tf_op jit(solution)/shard_map/ppermute | solution.py:196
  69.4 4.3 %collective-permute-start.28 = (bf16[16,896]{1,0:T(8,128)(2,1)S(1)}, bf16[16,896]{1,0:T(8,128)(2,1)S(1)}, u32[]{:S(2)}, u32[]{:S(2)}) collective-permute-start(bf16[16,896]{1,0:T(8,128)(2,1)S(1)} %sums.5.refs_0_), channel_id=1, source_target_pairs={{0,4},{1,5},{2,6},{3,7},{4,0},{5,1},{6,2},{7,3},{8,12},{9,13},{10,... | collective-permute-start | bytes 86024 | tf_op jit(solution)/shard_map/ppermute | solution.py:196
  70.9 3.9 %collective-permute-start.26 = (bf16[16,896]{1,0:T(8,128)(2,1)S(1)}, bf16[16,896]{1,0:T(8,128)(2,1)S(1)}, u32[]{:S(2)}, u32[]{:S(2)}) collective-permute-start(bf16[16,896]{1,0:T(8,128)(2,1)S(1)} %sums.5.refs_0_), channel_id=1, source_target_pairs={{0,2},{1,3},{2,0},{3,1},{4,6},{5,7},{6,4},{7,5},{8,10},{9,11},{10,... | collective-permute-start | bytes 86024 | tf_op jit(solution)/shard_map/ppermute | solution.py:196
  72.4 2.4 %collective-permute-start.25 = (bf16[16,896]{1,0:T(8,128)(2,1)S(1)}, bf16[16,896]{1,0:T(8,128)(2,1)S(1)}, u32[]{:S(2)}, u32[]{:S(2)}) collective-permute-start(bf16[16,896]{1,0:T(8,128)(2,1)S(1)} %sums.5.refs_0_), channel_id=1, source_target_pairs={{0,1},{1,0},{2,3},{3,2},{4,5},{5,4},{6,7},{7,6},{8,9},{9,8},{10,11... | collective-permute-start | bytes 86024 | tf_op jit(solution)/shard_map/ppermute | solution.py:196
  73.7 1.2 %collective-permute-start.31 = (bf16[16,896]{1,0:T(8,128)(2,1)S(1)}, bf16[16,896]{1,0:T(8,128)(2,1)S(1)}, u32[]{:S(2)}, u32[]{:S(2)}) collective-permute-start(bf16[16,896]{1,0:T(8,128)(2,1)S(1)} %collective-permute-done.30.refs_6_), channel_id=1, source_target_pairs={{0,1},{1,0},{2,3},{3,2},{4,5},{5,4},{6,7},{7,6},{8,9},{9,8},{10,11... | collective-permute-start | bytes 86024 | tf_op jit(solution)/shard_map/ppermute | solution.py:196
  73.7 1.4 %collective-permute-start.29 = (bf16[16,896]{1,0:T(8,128)(2,1)S(1)}, bf16[16,896]{1,0:T(8,128)(2,1)S(1)}, u32[]{:S(2)}, u32[]{:S(2)}) collective-permute-start(bf16[16,896]{1,0:T(8,128)(2,1)S(1)} %collective-permute-done.28.refs_4_), channel_id=1, source_target_pairs={{0,1},{1,0},{2,3},{3,2},{4,5},{5,4},{6,7},{7,6},{8,9},{9,8},{10,11... | collective-permute-start | bytes 86024 | tf_op jit(solution)/shard_map/ppermute | solution.py:196
  74.8 1.2 %collective-permute-start.27 = (bf16[16,896]{1,0:T(8,128)(2,1)S(1)}, bf16[16,896]{1,0:T(8,128)(2,1)S(1)}, u32[]{:S(2)}, u32[]{:S(2)}) collective-permute-start(bf16[16,896]{1,0:T(8,128)(2,1)S(1)} %collective-permute-done.26.refs_2_), channel_id=1, source_target_pairs={{0,1},{1,0},{2,3},{3,2},{4,5},{5,4},{6,7},{7,6},{8,9},{9,8},{10,11... | collective-permute-start | bytes 86024 | tf_op jit(solution)/shard_map/ppermute | solution.py:196
  86.9 1.4 %collective-permute-start.32 = (bf16[4,4,16,224]{3,2,1,0:T(8,128)(2,1)S(1)}, bf16[4,4,16,224]{3,2,1,0:T(8,128)(2,1)S(1)}, u32[]{:S(2)}, u32[]{:S(2)}) collective-permute-start(bf16[4,4,16,224]{3,2,1,0:T(8,128)(2,1)S(1)} %get-tuple-element.77), channel_id=1, source_target_pairs={{0,1},{1,0},{2,3},{3,2},{4,5},{5,4},{6,7},{7,6},{8,9},{9,8},{10,11... | collective-permute-start | bytes 344072 | tf_op jit(solution)/shard_map/ppermute | solution.py:196

commit v4 on v3

--- a/solution.py
+++ b/solution.py
@@ -181,9 +181,10 @@
 CORE, Y, X, Z0, Z1 = 1, 2, 4, 8, 16
 HEADS_DEV = 4
 UNITS = 256
-STAT = 16
+STAT = 8
 LANES = 128
 PARENTS = REQ
+AHEAD = 2
 LOG2E = math.log2(math.e)
 VMEM = pl.BlockSpec(memory_space=pltpu.VMEM)
 SMEM = pl.BlockSpec(memory_space=pltpu.SMEM)
@@ -266,9 +267,10 @@
             pltpu.make_async_copy(sl_hbm.at[beams], sl.at[beams], sems.at[2, r]),
             pltpu.make_async_copy(sr_hbm.at[beams], sr.at[beams], sems.at[3, r]),
         ]
-        for copy in group:
-            copy.start()
         copies.append(group)
+        if r < AHEAD:
+            for copy in group:
+                copy.start()
     first_q, first_r = (own_q, own_r) if fetch else (ql0, qr0)
 
     out_row = lax.broadcasted_iota(jnp.int32, (total_rows, total_rows), 0)
@@ -308,6 +310,9 @@
     def scores(r):
         for copy in copies[r]:
             copy.wait()
+        if r + AHEAD < REQ:
+            for copy in copies[r + AHEAD]:
+                copy.start()
         keys = cl[r]
         ctx_block = keys.shape[0]
         pre = lax.dot_general(qbuf[r], keys, NT, preferred_element_type=F32)
@@ -372,7 +377,7 @@
     body = REQ * total_rows // (2 * targets)
     message = lambda n: jax.ShapeDtypeStruct((n, body + STAT, width), BF)
     keys = caches[0].shape[1] + caches[2].shape[1]
-    own = [v.shape if fetch else (STAT, LANES) for v in (q_lat[0], q_rope[0])]
+    own = [v.shape if fetch else (16, LANES) for v in (q_lat[0], q_rope[0])]
     first = [in_hbm(v) if fetch else v for v in (q_lat[0], q_rope[0])]
     spec = HBM if fetch else VMEM
     return pl.pallas_call(
@@ -686,7 +691,7 @@
     keep, send = project(parts, w_uv, w_o)
 
     pieces = sums([keep, swap(send, CORE)], True)
-    share, = sums([pieces[0], *(swap(v, mask) for v, mask in zip(pieces[1:], square))], False)
+    share, = sums([pieces[0], *(swap(v, mask) for v, mask in zip(pieces[:0:-1], square[::-1]))], False)
     share, = sums([share, *(swap(share, mask) for mask in line[::-1])], False)
     shares = [share, *(swap(share, mask) for mask in square)]
     shares = [v for pair in zip(shares, [swap(v, CORE) for v in shares]) for v in pair]

time: 101 us -> 99.7 us (0.987)
  waiting for transfers between devices: 28.2 us -> 26.3 us
    ppermute x33, waiting for transfers between devices: 28.2 us -> 26.3 us  [swap(): lax.ppermute(value, AXES, [(i, i ^ mask) for i in range(math.prod(SHAPE))])]
  transfers between devices with their start and end apart: 33 -> 33, of which waited for: 21 -> 21; matrix products, arithmetic and copies ran while one was open for 1% -> 1% of each run, Pallas kernels for 16% -> 17%
where the time goes in v4:
time: 99.7 us; the launch traced here: 99.5 us
  Pallas kernels  29.3 us (29%)
  starting transfers between devices  28.7 us (29%)
  waiting for transfers between devices  26.3 us (26%)
  blocking collectives  12.9 us (13%)
  other arithmetic  1.38 us (1%)
    ppermute x33, starting transfers between devices, swap(): lax.ppermute(value, AXES, [(i, i ^ mask) for i in range(math.prod(SHAPE))])  28.7 us
    ppermute x33, waiting for transfers between devices, swap(): lax.ppermute(value, AXES, [(i, i ^ mask) for i in range(math.prod(SHAPE))])  26.3 us
    all_to_all x1, blocking collectives, local(): lax.all_to_all(total, AXES[:3], split_axis=0, concat_axis=0, tiled=True)  12.9 us
    pallas_call x2, Pallas kernels, attend(): pl.pallas_call(partial(attend_kernel, scale, fetch), in_specs=[SMEM, spec...  12.4 us
    pallas_call x1, Pallas kernels, experts(): pl.pallas_call(experts_kernel, in_specs=[VMEM] * 14 + [HBM], out_specs=[V...  10.9 us
    pallas_call x1, Pallas kernels, load(): pl.pallas_call(partial(load_kernel, count), in_specs=[HBM] * count + [pl....  3.41 us
  transfers between devices with their start and end apart: 33, of which 21 were waited for; matrix products, arithmetic and copies ran while one was open for 1% of the time, Pallas kernels for 17%

profile of v4, /device:TPU:0, one launch (start us, length us, event | category | flops | bytes accessed | tf_op | source)
XLA Modules:
  0.0 99.5 jit_solution(9035819493278591528)
XLA Ops:
  0.6 0.5 collective-permute-start.2
  1.1 2.6 %collective-permute-start = (bf16[16,32,512]{2,1,0:T(8,128)(2,1)}, bf16[16,32,512]{2,1,0:T(8,128)(2,1)S(1)}, u32[]{:S(2)}, u32[]{:S(2)}) collective-permute-start(bf16[16,32,512]{2,1,0:T(8,128)(2,1)} %ql0.1), channel_id=1, source_target_pairs={{0,2},{1,3},{2,0},{3,1},{4,6},{5,7},{6,4},{7,5},{8,10},{9,11},{10,... | collective-permute-start | bytes 1572872 | tf_op jit(solution)/shard_map/ppermute | solution.py:197
  3.9 0.7 pad_add_fusion.info
  4.7 0.6 collective-permute-done.3.qr1
  5.2 6.4 %attend.2 = (bf16[4,136,512]{2,1,0:T(8,128)(2,1)S(1)}, bf16[2,136,512]{2,1,0:T(8,128)(2,1)S(1)}, bf16[2,136,512]{2,1,0:T(8,128)(2,1)S(1)}) custom-call(s32[20]{0:T(128)S(1)} %pad_add_fusion.info, bf16[16,32,512]{2,1,0:T(8,128)(2,1)} %ql0.1, bf16[16,32,512]{2,1,0:T(8,128)(2,1)S(1)} %collective-permute-done.2.ql1, bf16[16,2048]{1,0:T(8,128)(2,1)} %qr0.1, ...), custom_call_target="tpu_custom_call" | custom-call | flops 1426063360 | bytes 8388608 | tf_op jit(solution)/shard_map/attend/pallas_call | solution.py:383
  11.9 0.3 collective-permute-start.5
  12.2 0.7 collective-permute-start.1
  12.9 0.4 collective-permute-done.4.refs_0_
  13.2 0.4 collective-permute-done.5.refs_1_
  14.0 3.9 %collective-permute-done.1.qr0 = bf16[16,2048]{1,0:T(8,128)(2,1)S(1)} collective-permute-done((bf16[16,2048]{1,0:T(8,128)(2,1)}, bf16[16,2048]{1,0:T(8,128)(2,1)S(1)}, u32[]{:S(2)}, u32[]{:S(2)}) %collective-permute-start.1) | collective-permute-done | bytes 65568 | tf_op jit(solution)/shard_map/ppermute | solution.py:197
  17.9 1.8 %collective-permute-start.8 = (bf16[2,136,512]{2,1,0:T(8,128)(2,1)S(1)}, bf16[2,136,512]{2,1,0:T(8,128)(2,1)S(1)}, u32[]{:S(2)}, u32[]{:S(2)}) collective-permute-start(bf16[2,136,512]{2,1,0:T(8,128)(2,1)S(1)} %get-tuple-element.51), channel_id=1, source_target_pairs={{0,4},{1,5},{2,6},{3,7},{4,0},{5,1},{6,2},{7,3},{8,12},{9,13},{10,... | collective-permute-start | bytes 835592 | tf_op jit(solution)/shard_map/ppermute | solution.py:197
  19.8 1.1 %collective-permute-done.7.qr1 = bf16[16,2048]{1,0:T(8,128)(2,1)S(1)} collective-permute-done((bf16[16,2048]{1,0:T(8,128)(2,1)S(1)}, bf16[16,2048]{1,0:T(8,128)(2,1)S(1)}, u32[]{:S(2)}, u32[]{:S(2)}) %collective-permute-start.7) | collective-permute-done | bytes 65568 | tf_op jit(solution)/shard_map/ppermute | solution.py:197
  20.9 6.0 %attend.3 = (bf16[4,136,512]{2,1,0:T(8,128)(2,1)S(1)}, bf16[2,136,512]{2,1,0:T(8,128)(2,1)S(1)}, bf16[2,136,512]{2,1,0:T(8,128)(2,1)S(1)}) custom-call(s32[20]{0:T(128)S(1)} %pad_add_fusion.info, bf16[16,32,512]{2,1,0:T(8,128)(2,1)S(1)} %collective-permute-done.ql0, bf16[16,32,512]{2,1,0:T(8,128)(2,1)S(1)} %collective-permute-done.6.ql1, ...), custom_call_target="tpu_custom_call" | custom-call | flops 1426063360 | bytes 8388608 | tf_op jit(solution)/shard_map/attend/pallas_call | solution.py:383
  27.1 0.3 collective-permute-start.10
  27.7 1.8 %collective-permute-start.13 = (bf16[1,136,512]{2,1,0:T(8,128)(2,1)S(1)}, bf16[1,136,512]{2,1,0:T(8,128)(2,1)S(1)}, u32[]{:S(2)}, u32[]{:S(2)}) collective-permute-start(bf16[1,136,512]{2,1,0:T(8,128)(2,1)S(1)} %get-tuple-element.59), channel_id=1, source_target_pairs={{0,2},{1,3},{2,0},{3,1},{4,6},{5,7},{6,4},{7,5},{8,10},{9,11},{10,... | collective-permute-start | bytes 417800 | tf_op jit(solution)/shard_map/ppermute | solution.py:197
  29.8 1.2 %collective-permute-start.11 = (bf16[1,136,512]{2,1,0:T(8,128)(2,1)S(1)}, bf16[1,136,512]{2,1,0:T(8,128)(2,1)S(1)}, u32[]{:S(2)}, u32[]{:S(2)}) collective-permute-start(bf16[1,136,512]{2,1,0:T(8,128)(2,1)S(1)} %get-tuple-element.57), channel_id=1, source_target_pairs={{0,2},{1,3},{2,0},{3,1},{4,6},{5,7},{6,4},{7,5},{8,10},{9,11},{10,... | collective-permute-start | bytes 417800 | tf_op jit(solution)/shard_map/ppermute | solution.py:197
  31.1 1.8 %collective-permute-start.12 = (bf16[1,136,512]{2,1,0:T(8,128)(2,1)S(1)}, bf16[1,136,512]{2,1,0:T(8,128)(2,1)S(1)}, u32[]{:S(2)}, u32[]{:S(2)}) collective-permute-start(bf16[1,136,512]{2,1,0:T(8,128)(2,1)S(1)} %get-tuple-element.58), channel_id=1, source_target_pairs={{0,6},{1,7},{2,4},{3,5},{4,2},{5,3},{6,0},{7,1},{8,14},{9,15},{10,... | collective-permute-start | bytes 417800 | tf_op jit(solution)/shard_map/ppermute | solution.py:197
  32.8 0.5 collective-permute-start.14
  33.4 2.2 %collective-permute-done.13.refs_3_ = bf16[1,136,512]{2,1,0:T(8,128)(2,1)S(1)} collective-permute-done((bf16[1,136,512]{2,1,0:T(8,128)(2,1)S(1)}, bf16[1,136,512]{2,1,0:T(8,128)(2,1)S(1)}, u32[]{:S(2)}, u32[]{:S(2)}) %collective-permute-start.13) | collective-permute-done | bytes 139296 | tf_op jit(solution)/shard_map/ppermute | solution.py:197
  35.6 3.8 %collective-permute-done.11.refs_1_ = bf16[1,136,512]{2,1,0:T(8,128)(2,1)S(1)} collective-permute-done((bf16[1,136,512]{2,1,0:T(8,128)(2,1)S(1)}, bf16[1,136,512]{2,1,0:T(8,128)(2,1)S(1)}, u32[]{:S(2)}, u32[]{:S(2)}) %collective-permute-start.11) | collective-permute-done | bytes 139296 | tf_op jit(solution)/shard_map/ppermute | solution.py:197
  39.8 3.7 %collective-permute-start.15 = (bf16[72,512]{1,0:T(8,128)(2,1)S(1)}, bf16[72,512]{1,0:T(8,128)(2,1)S(1)}, u32[]{:S(2)}, u32[]{:S(2)}) collective-permute-start(bf16[72,512]{1,0:T(8,128)(2,1)S(1)} %get-tuple-element.63), channel_id=1, source_target_pairs={{0,24},{1,25},{2,26},{3,27},{4,28},{5,29},{6,30},{7,31},{8,16},{9,... | collective-permute-start | bytes 221192 | tf_op jit(solution)/shard_map/ppermute | solution.py:197
  43.5 0.7 collective-permute-start.17
  44.3 3.4 %load.1 = (bf16[512,512]{1,0:T(8,128)(2,1)S(1)}, bf16[512,7168]{1,0:T(8,128)(2,1)S(1)}) custom-call(bf16[512,512]{1,0:T(8,128)(2,1)} %refs_0_.1, bf16[512,7168]{1,0:T(8,128)(2,1)} %refs_1_.1, bf16[72,512]{1,0:T(8,128)(2,1)S(1)} %get-tuple-element.62.refs_2_.p0), custom_call_target="tpu_custom_call" | custom-call | bytes 7864320 | tf_op jit(solution)/shard_map/load/pallas_call | solution.py:565
  47.7 1.6 %collective-permute-done.16.p2 = bf16[72,512]{1,0:T(8,128)(2,1)S(1)} collective-permute-done((bf16[72,512]{1,0:T(8,128)(2,1)S(1)}, bf16[72,512]{1,0:T(8,128)(2,1)S(1)}, u32[]{:S(2)}, u32[]{:S(2)}) %collective-permute-start.16) | collective-permute-done | bytes 73760 | tf_op jit(solution)/shard_map/ppermute | solution.py:197
  49.3 1.4 %project.1 = (bf16[4,16,896]{2,1,0:T(8,128)(2,1)S(1)}, bf16[4,16,896]{2,1,0:T(8,128)(2,1)S(1)}) custom-call(bf16[72,512]{1,0:T(8,128)(2,1)S(1)} %get-tuple-element.62.refs_2_.p0, bf16[72,512]{1,0:T(8,128)(2,1)S(1)} %collective-permute-done.15.p1, bf16[72,512]{1,0:T(8,128)(2,1)S(1)} %collective-permute-done.16.p2, ...), custom_call_target="tpu_custom_call" | custom-call | flops 117440512 | bytes 7340032 | tf_op jit(solution)/shard_map/project/pallas_call | solution.py:522
  50.8 1.3 %collective-permute-done.18.refs_1_ = bf16[4,16,896]{2,1,0:T(8,128)(2,1)S(1)} collective-permute-done((bf16[4,16,896]{2,1,0:T(8,128)(2,1)S(1)}, bf16[4,16,896]{2,1,0:T(8,128)(2,1)S(1)}, u32[]{:S(2)}, u32[]{:S(2)}) %collective-permute-start.18) | collective-permute-done | bytes 114720 | tf_op jit(solution)/shard_map/ppermute | solution.py:197
  52.1 2.5 %collective-permute-start.19 = (bf16[16,896]{1,0:T(8,128)(2,1)S(1)}, bf16[16,896]{1,0:T(8,128)(2,1)S(1)}, u32[]{:S(2)}, u32[]{:S(2)}) collective-permute-start(bf16[16,896]{1,0:T(8,128)(2,1)S(1)} %get-tuple-element.71), channel_id=1, source_target_pairs={{0,6},{1,7},{2,4},{3,5},{4,2},{5,3},{6,0},{7,1},{8,14},{9,15},{10,... | collective-permute-start | bytes 86024 | tf_op jit(solution)/shard_map/ppermute | solution.py:197
  54.6 0.5 collective-permute-start.20
  55.2 0.5 collective-permute-start.21
  55.7 1.3 %collective-permute-done.19.refs_1_ = bf16[16,896]{1,0:T(8,128)(2,1)S(1)} collective-permute-done((bf16[16,896]{1,0:T(8,128)(2,1)S(1)}, bf16[16,896]{1,0:T(8,128)(2,1)S(1)}, u32[]{:S(2)}, u32[]{:S(2)}) %collective-permute-start.19) | collective-permute-done | bytes 28704 | tf_op jit(solution)/shard_map/ppermute | solution.py:197
  57.0 1.5 %collective-permute-done.20.refs_2_ = bf16[16,896]{1,0:T(8,128)(2,1)S(1)} collective-permute-done((bf16[16,896]{1,0:T(8,128)(2,1)S(1)}, bf16[16,896]{1,0:T(8,128)(2,1)S(1)}, u32[]{:S(2)}, u32[]{:S(2)}) %collective-permute-start.20) | collective-permute-done | bytes 28704 | tf_op jit(solution)/shard_map/ppermute | solution.py:197
  58.5 0.5 collective-permute-done.21.refs_3_
  59.1 2.6 %collective-permute-start.24 = (bf16[16,896]{1,0:T(8,128)(2,1)S(1)}, bf16[16,896]{1,0:T(8,128)(2,1)S(1)}, u32[]{:S(2)}, u32[]{:S(2)}) collective-permute-start(bf16[16,896]{1,0:T(8,128)(2,1)S(1)} %sums.4.refs_0_), channel_id=1, source_target_pairs={{0,24},{1,25},{2,26},{3,27},{4,28},{5,29},{6,30},{7,31},{8,16},{9,... | collective-permute-start | bytes 86024 | tf_op jit(solution)/shard_map/ppermute | solution.py:197
  61.6 1.9 %collective-permute-start.22 = (bf16[16,896]{1,0:T(8,128)(2,1)S(1)}, bf16[16,896]{1,0:T(8,128)(2,1)S(1)}, u32[]{:S(2)}, u32[]{:S(2)}) collective-permute-start(bf16[16,896]{1,0:T(8,128)(2,1)S(1)} %sums.4.refs_0_), channel_id=1, source_target_pairs={{0,8},{1,9},{2,10},{3,11},{4,12},{5,13},{6,14},{7,15},{8,0},{9,1},... | collective-permute-start | bytes 86024 | tf_op jit(solution)/shard_map/ppermute | solution.py:197
  63.5 1.6 %collective-permute-done.24.refs_3_ = bf16[16,896]{1,0:T(8,128)(2,1)S(1)} collective-permute-done((bf16[16,896]{1,0:T(8,128)(2,1)S(1)}, bf16[16,896]{1,0:T(8,128)(2,1)S(1)}, u32[]{:S(2)}, u32[]{:S(2)}) %collective-permute-start.24) | collective-permute-done | bytes 28704 | tf_op jit(solution)/shard_map/ppermute | solution.py:197
  65.1 1.3 %collective-permute-done.23.refs_2_ = bf16[16,896]{1,0:T(8,128)(2,1)S(1)} collective-permute-done((bf16[16,896]{1,0:T(8,128)(2,1)S(1)}, bf16[16,896]{1,0:T(8,128)(2,1)S(1)}, u32[]{:S(2)}, u32[]{:S(2)}) %collective-permute-start.23) | collective-permute-done | bytes 28704 | tf_op jit(solution)/shard_map/ppermute | solution.py:197
  66.4 1.5 %collective-permute-start.30 = (bf16[16,896]{1,0:T(8,128)(2,1)S(1)}, bf16[16,896]{1,0:T(8,128)(2,1)S(1)}, u32[]{:S(2)}, u32[]{:S(2)}) collective-permute-start(bf16[16,896]{1,0:T(8,128)(2,1)S(1)} %sums.5.refs_0_), channel_id=1, source_target_pairs={{0,6},{1,7},{2,4},{3,5},{4,2},{5,3},{6,0},{7,1},{8,14},{9,15},{10,... | collective-permute-start | bytes 86024 | tf_op jit(solution)/shard_map/ppermute | solution.py:197
  67.9 0.5 collective-permute-start.28
  68.5 1.5 %collective-permute-start.26 = (bf16[16,896]{1,0:T(8,128)(2,1)S(1)}, bf16[16,896]{1,0:T(8,128)(2,1)S(1)}, u32[]{:S(2)}, u32[]{:S(2)}) collective-permute-start(bf16[16,896]{1,0:T(8,128)(2,1)S(1)} %sums.5.refs_0_), channel_id=1, source_target_pairs={{0,2},{1,3},{2,0},{3,1},{4,6},{5,7},{6,4},{7,5},{8,10},{9,11},{10,... | collective-permute-start | bytes 86024 | tf_op jit(solution)/shard_map/ppermute | solution.py:197
  70.0 1.3 %collective-permute-done.30.refs_6_ = bf16[16,896]{1,0:T(8,128)(2,1)S(1)} collective-permute-done((bf16[16,896]{1,0:T(8,128)(2,1)S(1)}, bf16[16,896]{1,0:T(8,128)(2,1)S(1)}, u32[]{:S(2)}, u32[]{:S(2)}) %collective-permute-start.30) | collective-permute-done | bytes 28704 | tf_op jit(solution)/shard_map/ppermute | solution.py:197
  71.3 0.5 collective-permute-done.28.refs_4_
  71.8 0.5 collective-permute-done.26.refs_2_
  72.5 0.5 collective-permute-done.29.refs_5_
  73.0 0.5 collective-permute-done.27.refs_3_
  73.6 10.9 %experts.1 = (bf16[16,7168]{1,0:T(8,128)(2,1)}, bf16[4,4,16,224]{3,2,1,0:T(8,128)(2,1)S(1)}, bf16[4,4,16,224]{3,2,1,0:T(8,128)(2,1)S(1)}, f32[16,224]{1,0:T(8,128)S(1)}) custom-call(bf16[16,896]{1,0:T(8,128)(2,1)S(1)} %sums.5.refs_0_, bf16[16,896]{1,0:T(8,128)(2,1)S(1)} %collective-permute-done.25.refs_1_, ...), custom_call_target="tpu_custom_call" | custom-call | flops 704643072 | bytes 44040192 | tf_op jit(solution)/shard_map/experts/pallas_call | solution.py:630
  84.7 1.2 %collective-permute-done.32.b = bf16[4,4,16,224]{3,2,1,0:T(8,128)(2,1)S(1)} collective-permute-done((bf16[4,4,16,224]{3,2,1,0:T(8,128)(2,1)S(1)}, bf16[4,4,16,224]{3,2,1,0:T(8,128)(2,1)S(1)}, u32[]{:S(2)}, u32[]{:S(2)}) %collective-permute-start.32) | collective-permute-done | bytes 114720 | tf_op jit(solution)/shard_map/ppermute | solution.py:197
  85.9 12.9 %all_to_all.5 = bf16[16,16,224]{2,1,0:T(8,128)(2,1)S(1)} all-to-all(bf16[16,16,224]{2,1,0:T(8,128)(2,1)S(1)} %core_sum.1), channel_id=1, replica_groups=mesh['z'=4,'x'=2,'y'=2,'core'=2] {'z','x','y'}, dimensions={0} | all-to-all | bytes 229376 | tf_op jit(solution)/shard_map/all_to_all | solution.py:702
  98.9 0.6 add_convert_fusion
  (54 shorter events, 2.6 us)
Async XLA Ops:
  0.6 4.6 %collective-permute-start.2 = (bf16[16,32,512]{2,1,0:T(8,128)(2,1)}, bf16[16,32,512]{2,1,0:T(8,128)(2,1)S(1)}, u32[]{:S(2)}, u32[]{:S(2)}) collective-permute-start(bf16[16,32,512]{2,1,0:T(8,128)(2,1)} %ql0.1), channel_id=1, source_target_pairs={{0,1},{1,0},{2,3},{3,2},{4,5},{5,4},{6,7},{7,6},{8,9},{9,8},{10,11... | collective-permute-start | bytes 1572872 | tf_op jit(solution)/shard_map/ppermute | solution.py:197
  1.1 16.7 %collective-permute-start = (bf16[16,32,512]{2,1,0:T(8,128)(2,1)}, bf16[16,32,512]{2,1,0:T(8,128)(2,1)S(1)}, u32[]{:S(2)}, u32[]{:S(2)}) collective-permute-start(bf16[16,32,512]{2,1,0:T(8,128)(2,1)} %ql0.1), channel_id=1, source_target_pairs={{0,2},{1,3},{2,0},{3,1},{4,6},{5,7},{6,4},{7,5},{8,10},{9,11},{10,... | collective-permute-start | bytes 1572872 | tf_op jit(solution)/shard_map/ppermute | solution.py:197
  3.7 1.5 %collective-permute-start.3 = (bf16[16,2048]{1,0:T(8,128)(2,1)}, bf16[16,2048]{1,0:T(8,128)(2,1)S(1)}, u32[]{:S(2)}, u32[]{:S(2)}) collective-permute-start(bf16[16,2048]{1,0:T(8,128)(2,1)} %qr0.1), channel_id=1, source_target_pairs={{0,1},{1,0},{2,3},{3,2},{4,5},{5,4},{6,7},{7,6},{8,9},{9,8},{10,11... | collective-permute-start | bytes 196616 | tf_op jit(solution)/shard_map/ppermute | solution.py:197
  5.2 68.3 %slice-start = ((s8[14680064]{0:T(1024)(128)(4,1)}), s8[4194304]{0:T(1024)(128)(4,1)S(1)}, s32[]{:S(2)}) async-start(s8[14680064]{0:T(1024)(128)(4,1)} %bitcast.3), calls=%async_computation.1 | async-start | bytes 8388608
  11.6 1.6 %collective-permute-start.4 = (bf16[2,136,512]{2,1,0:T(8,128)(2,1)S(1)}, bf16[2,136,512]{2,1,0:T(8,128)(2,1)S(1)}, u32[]{:S(2)}, u32[]{:S(2)}) collective-permute-start(bf16[2,136,512]{2,1,0:T(8,128)(2,1)S(1)} %get-tuple-element.41), channel_id=1, source_target_pairs={{0,1},{1,0},{2,3},{3,2},{4,5},{5,4},{6,7},{7,6},{8,9},{9,8},{10,11... | collective-permute-start | bytes 835592 | tf_op jit(solution)/shard_map/ppermute | solution.py:197
  11.9 1.8 %collective-permute-start.5 = (bf16[2,136,512]{2,1,0:T(8,128)(2,1)S(1)}, bf16[2,136,512]{2,1,0:T(8,128)(2,1)S(1)}, u32[]{:S(2)}, u32[]{:S(2)}) collective-permute-start(bf16[2,136,512]{2,1,0:T(8,128)(2,1)S(1)} %get-tuple-element.42), channel_id=1, source_target_pairs={{0,1},{1,0},{2,3},{3,2},{4,5},{5,4},{6,7},{7,6},{8,9},{9,8},{10,11... | collective-permute-start | bytes 835592 | tf_op jit(solution)/shard_map/ppermute | solution.py:197
  12.2 5.7 %collective-permute-start.1 = (bf16[16,2048]{1,0:T(8,128)(2,1)}, bf16[16,2048]{1,0:T(8,128)(2,1)S(1)}, u32[]{:S(2)}, u32[]{:S(2)}) collective-permute-start(bf16[16,2048]{1,0:T(8,128)(2,1)} %qr0.1), channel_id=1, source_target_pairs={{0,2},{1,3},{2,0},{3,1},{4,6},{5,7},{6,4},{7,5},{8,10},{9,11},{10,... | collective-permute-start | bytes 196616 | tf_op jit(solution)/shard_map/ppermute | solution.py:197
  13.6 59.9 %copy-start = (bf16[1024,7168]{1,0:T(8,128)(2,1)S(1)}, bf16[1024,7168]{1,0:T(8,128)(2,1)}, u32[]{:S(2)}) copy-start(bf16[1024,7168]{1,0:T(8,128)(2,1)} %refs_13_.1) | copy-start | bytes 44040196
  17.9 55.7 %slice-start.1 = ((s8[14680064]{0:T(1024)(128)(4,1)}), s8[4194304]{0:T(1024)(128)(4,1)S(1)}, s32[]{:S(2)}) async-start(s8[14680064]{0:T(1024)(128)(4,1)} %bitcast.3), calls=%async_computation.2 | async-start | bytes 8388608
  17.9 3.1 %collective-permute-start.6 = (bf16[16,32,512]{2,1,0:T(8,128)(2,1)S(1)}, bf16[16,32,512]{2,1,0:T(8,128)(2,1)S(1)}, u32[]{:S(2)}, u32[]{:S(2)}) collective-permute-start(bf16[16,32,512]{2,1,0:T(8,128)(2,1)S(1)} %collective-permute-done.ql0), channel_id=1, source_target_pairs={{0,1},{1,0},{2,3},{3,2},{4,5},{5,4},{6,7},{7,6},{8,9},{9,8},{10,11... | collective-permute-start | bytes 1572872 | tf_op jit(solution)/shard_map/ppermute | solution.py:197
  17.9 9.1 %collective-permute-start.8 = (bf16[2,136,512]{2,1,0:T(8,128)(2,1)S(1)}, bf16[2,136,512]{2,1,0:T(8,128)(2,1)S(1)}, u32[]{:S(2)}, u32[]{:S(2)}) collective-permute-start(bf16[2,136,512]{2,1,0:T(8,128)(2,1)S(1)} %get-tuple-element.51), channel_id=1, source_target_pairs={{0,4},{1,5},{2,6},{3,7},{4,0},{5,1},{6,2},{7,3},{8,12},{9,13},{10,... | collective-permute-start | bytes 835592 | tf_op jit(solution)/shard_map/ppermute | solution.py:197
  19.7 1.3 %collective-permute-start.7 = (bf16[16,2048]{1,0:T(8,128)(2,1)S(1)}, bf16[16,2048]{1,0:T(8,128)(2,1)S(1)}, u32[]{:S(2)}, u32[]{:S(2)}) collective-permute-start(bf16[16,2048]{1,0:T(8,128)(2,1)S(1)} %collective-permute-done.1.qr0), channel_id=1, source_target_pairs={{0,1},{1,0},{2,3},{3,2},{4,5},{5,4},{6,7},{7,6},{8,9},{9,8},{10,11... | collective-permute-start | bytes 196616 | tf_op jit(solution)/shard_map/ppermute | solution.py:197
  27.0 2.5 %collective-permute-start.9 = (bf16[2,136,512]{2,1,0:T(8,128)(2,1)S(1)}, bf16[2,136,512]{2,1,0:T(8,128)(2,1)S(1)}, u32[]{:S(2)}, u32[]{:S(2)}) collective-permute-start(bf16[2,136,512]{2,1,0:T(8,128)(2,1)S(1)} %get-tuple-element.55), channel_id=1, source_target_pairs={{0,1},{1,0},{2,3},{3,2},{4,5},{5,4},{6,7},{7,6},{8,9},{9,8},{10,11... | collective-permute-start | bytes 835592 | tf_op jit(solution)/shard_map/ppermute | solution.py:197
  27.1 2.4 %collective-permute-start.10 = (bf16[2,136,512]{2,1,0:T(8,128)(2,1)S(1)}, bf16[2,136,512]{2,1,0:T(8,128)(2,1)S(1)}, u32[]{:S(2)}, u32[]{:S(2)}) collective-permute-start(bf16[2,136,512]{2,1,0:T(8,128)(2,1)S(1)} %get-tuple-element.56), channel_id=1, source_target_pairs={{0,1},{1,0},{2,3},{3,2},{4,5},{5,4},{6,7},{7,6},{8,9},{9,8},{10,11... | collective-permute-start | bytes 835592 | tf_op jit(solution)/shard_map/ppermute | solution.py:197
  27.7 7.9 %collective-permute-start.13 = (bf16[1,136,512]{2,1,0:T(8,128)(2,1)S(1)}, bf16[1,136,512]{2,1,0:T(8,128)(2,1)S(1)}, u32[]{:S(2)}, u32[]{:S(2)}) collective-permute-start(bf16[1,136,512]{2,1,0:T(8,128)(2,1)S(1)} %get-tuple-element.59), channel_id=1, source_target_pairs={{0,2},{1,3},{2,0},{3,1},{4,6},{5,7},{6,4},{7,5},{8,10},{9,11},{10,... | collective-permute-start | bytes 417800 | tf_op jit(solution)/shard_map/ppermute | solution.py:197
  29.8 9.6 %collective-permute-start.11 = (bf16[1,136,512]{2,1,0:T(8,128)(2,1)S(1)}, bf16[1,136,512]{2,1,0:T(8,128)(2,1)S(1)}, u32[]{:S(2)}, u32[]{:S(2)}) collective-permute-start(bf16[1,136,512]{2,1,0:T(8,128)(2,1)S(1)} %get-tuple-element.57), channel_id=1, source_target_pairs={{0,2},{1,3},{2,0},{3,1},{4,6},{5,7},{6,4},{7,5},{8,10},{9,11},{10,... | collective-permute-start | bytes 417800 | tf_op jit(solution)/shard_map/ppermute | solution.py:197
  31.1 8.4 %collective-permute-start.12 = (bf16[1,136,512]{2,1,0:T(8,128)(2,1)S(1)}, bf16[1,136,512]{2,1,0:T(8,128)(2,1)S(1)}, u32[]{:S(2)}, u32[]{:S(2)}) collective-permute-start(bf16[1,136,512]{2,1,0:T(8,128)(2,1)S(1)} %get-tuple-element.58), channel_id=1, source_target_pairs={{0,6},{1,7},{2,4},{3,5},{4,2},{5,3},{6,0},{7,1},{8,14},{9,15},{10,... | collective-permute-start | bytes 417800 | tf_op jit(solution)/shard_map/ppermute | solution.py:197
  32.8 6.6 %collective-permute-start.14 = (bf16[1,136,512]{2,1,0:T(8,128)(2,1)S(1)}, bf16[1,136,512]{2,1,0:T(8,128)(2,1)S(1)}, u32[]{:S(2)}, u32[]{:S(2)}) collective-permute-start(bf16[1,136,512]{2,1,0:T(8,128)(2,1)S(1)} %get-tuple-element.61), channel_id=1, source_target_pairs={{0,4},{1,5},{2,6},{3,7},{4,0},{5,1},{6,2},{7,3},{8,12},{9,13},{10,... | collective-permute-start | bytes 417800 | tf_op jit(solution)/shard_map/ppermute | solution.py:197
  39.8 7.9 %collective-permute-start.15 = (bf16[72,512]{1,0:T(8,128)(2,1)S(1)}, bf16[72,512]{1,0:T(8,128)(2,1)S(1)}, u32[]{:S(2)}, u32[]{:S(2)}) collective-permute-start(bf16[72,512]{1,0:T(8,128)(2,1)S(1)} %get-tuple-element.63), channel_id=1, source_target_pairs={{0,24},{1,25},{2,26},{3,27},{4,28},{5,29},{6,30},{7,31},{8,16},{9,... | collective-permute-start | bytes 221192 | tf_op jit(solution)/shard_map/ppermute | solution.py:197
  43.5 5.7 %collective-permute-start.16 = (bf16[72,512]{1,0:T(8,128)(2,1)S(1)}, bf16[72,512]{1,0:T(8,128)(2,1)S(1)}, u32[]{:S(2)}, u32[]{:S(2)}) collective-permute-start(bf16[72,512]{1,0:T(8,128)(2,1)S(1)} %get-tuple-element.64), channel_id=1, source_target_pairs={{0,16},{1,17},{2,18},{3,19},{4,20},{5,21},{6,22},{7,23},{8,24},{9,... | collective-permute-start | bytes 221192 | tf_op jit(solution)/shard_map/ppermute | solution.py:197
  43.5 5.7 %collective-permute-start.17 = (bf16[72,512]{1,0:T(8,128)(2,1)S(1)}, bf16[72,512]{1,0:T(8,128)(2,1)S(1)}, u32[]{:S(2)}, u32[]{:S(2)}) collective-permute-start(bf16[72,512]{1,0:T(8,128)(2,1)S(1)} %get-tuple-element.65), channel_id=1, source_target_pairs={{0,8},{1,9},{2,10},{3,11},{4,12},{5,13},{6,14},{7,15},{8,0},{9,1},... | collective-permute-start | bytes 221192 | tf_op jit(solution)/shard_map/ppermute | solution.py:197
  44.3 29.3 %slice-start.2 = ((s8[14680064]{0:T(1024)(128)(4,1)}), s8[4194304]{0:T(1024)(128)(4,1)S(1)}, s32[]{:S(2)}) async-start(s8[14680064]{0:T(1024)(128)(4,1)} %bitcast.3), calls=%async_computation.3 | async-start | bytes 8388608
  44.3 29.3 %copy-start.1 = (bf16[16,7168]{1,0:T(8,128)(2,1)S(1)}, bf16[16,7168]{1,0:T(8,128)(2,1)}, u32[]{:S(2)}) copy-start(bf16[16,7168]{1,0:T(8,128)(2,1)} %refs_8_.1) | copy-start | bytes 688132
  44.3 29.3 %copy-start.2 = (f32[7168]{0:T(1024)S(1)}, f32[7168]{0:T(1024)}, u32[]{:S(2)}) copy-start(f32[7168]{0:T(1024)} %param.28) | copy-start | bytes 86020
  44.3 29.3 %copy-start.3 = (s32[16,8]{0,1:T(8,128)S(1)}, s32[16,8]{0,1:T(8,128)}, u32[]{:S(2)}) copy-start(s32[16,8]{0,1:T(8,128)} %param.32) | copy-start | bytes 1540
  44.3 29.3 %copy-start.4 = (f32[16,8]{0,1:T(8,128)S(1)}, f32[16,8]{0,1:T(8,128)}, u32[]{:S(2)}) copy-start(f32[16,8]{0,1:T(8,128)} %param.33) | copy-start | bytes 1540
  49.3 24.3 %slice-start.3 = ((s8[14680064]{0:T(1024)(128)(4,1)}), s8[2097152]{0:T(1024)(128)(4,1)S(1)}, s32[]{:S(2)}) async-start(s8[14680064]{0:T(1024)(128)(4,1)} %bitcast.3), calls=%async_computation.4 | async-start | bytes 4194304
  50.7 1.4 %collective-permute-start.18 = (bf16[4,16,896]{2,1,0:T(8,128)(2,1)S(1)}, bf16[4,16,896]{2,1,0:T(8,128)(2,1)S(1)}, u32[]{:S(2)}, u32[]{:S(2)}) collective-permute-start(bf16[4,16,896]{2,1,0:T(8,128)(2,1)S(1)} %get-tuple-element.69), channel_id=1, source_target_pairs={{0,1},{1,0},{2,3},{3,2},{4,5},{5,4},{6,7},{7,6},{8,9},{9,8},{10,11... | collective-permute-start | bytes 344072 | tf_op jit(solution)/shard_map/ppermute | solution.py:197
  52.1 4.8 %collective-permute-start.19 = (bf16[16,896]{1,0:T(8,128)(2,1)S(1)}, bf16[16,896]{1,0:T(8,128)(2,1)S(1)}, u32[]{:S(2)}, u32[]{:S(2)}) collective-permute-start(bf16[16,896]{1,0:T(8,128)(2,1)S(1)} %get-tuple-element.71), channel_id=1, source_target_pairs={{0,6},{1,7},{2,4},{3,5},{4,2},{5,3},{6,0},{7,1},{8,14},{9,15},{10,... | collective-permute-start | bytes 86024 | tf_op jit(solution)/shard_map/ppermute | solution.py:197
  54.6 3.9 %collective-permute-start.20 = (bf16[16,896]{1,0:T(8,128)(2,1)S(1)}, bf16[16,896]{1,0:T(8,128)(2,1)S(1)}, u32[]{:S(2)}, u32[]{:S(2)}) collective-permute-start(bf16[16,896]{1,0:T(8,128)(2,1)S(1)} %get-tuple-element.72), channel_id=1, source_target_pairs={{0,4},{1,5},{2,6},{3,7},{4,0},{5,1},{6,2},{7,3},{8,12},{9,13},{10,... | collective-permute-start | bytes 86024 | tf_op jit(solution)/shard_map/ppermute | solution.py:197
  55.2 3.9 %collective-permute-start.21 = (bf16[16,896]{1,0:T(8,128)(2,1)S(1)}, bf16[16,896]{1,0:T(8,128)(2,1)S(1)}, u32[]{:S(2)}, u32[]{:S(2)}) collective-permute-start(bf16[16,896]{1,0:T(8,128)(2,1)S(1)} %get-tuple-element.73), channel_id=1, source_target_pairs={{0,2},{1,3},{2,0},{3,1},{4,6},{5,7},{6,4},{7,5},{8,10},{9,11},{10,... | collective-permute-start | bytes 86024 | tf_op jit(solution)/shard_map/ppermute | solution.py:197
  59.1 6.0 %collective-permute-start.24 = (bf16[16,896]{1,0:T(8,128)(2,1)S(1)}, bf16[16,896]{1,0:T(8,128)(2,1)S(1)}, u32[]{:S(2)}, u32[]{:S(2)}) collective-permute-start(bf16[16,896]{1,0:T(8,128)(2,1)S(1)} %sums.4.refs_0_), channel_id=1, source_target_pairs={{0,24},{1,25},{2,26},{3,27},{4,28},{5,29},{6,30},{7,31},{8,16},{9,... | collective-permute-start | bytes 86024 | tf_op jit(solution)/shard_map/ppermute | solution.py:197
  61.6 4.8 %collective-permute-start.23 = (bf16[16,896]{1,0:T(8,128)(2,1)S(1)}, bf16[16,896]{1,0:T(8,128)(2,1)S(1)}, u32[]{:S(2)}, u32[]{:S(2)}) collective-permute-start(bf16[16,896]{1,0:T(8,128)(2,1)S(1)} %sums.4.refs_0_), channel_id=1, source_target_pairs={{0,16},{1,17},{2,18},{3,19},{4,20},{5,21},{6,22},{7,23},{8,24},{9,... | collective-permute-start | bytes 86024 | tf_op jit(solution)/shard_map/ppermute | solution.py:197
  61.6 4.8 %collective-permute-start.22 = (bf16[16,896]{1,0:T(8,128)(2,1)S(1)}, bf16[16,896]{1,0:T(8,128)(2,1)S(1)}, u32[]{:S(2)}, u32[]{:S(2)}) collective-permute-start(bf16[16,896]{1,0:T(8,128)(2,1)S(1)} %sums.4.refs_0_), channel_id=1, source_target_pairs={{0,8},{1,9},{2,10},{3,11},{4,12},{5,13},{6,14},{7,15},{8,0},{9,1},... | collective-permute-start | bytes 86024 | tf_op jit(solution)/shard_map/ppermute | solution.py:197
  66.4 4.8 %collective-permute-start.30 = (bf16[16,896]{1,0:T(8,128)(2,1)S(1)}, bf16[16,896]{1,0:T(8,128)(2,1)S(1)}, u32[]{:S(2)}, u32[]{:S(2)}) collective-permute-start(bf16[16,896]{1,0:T(8,128)(2,1)S(1)} %sums.5.refs_0_), channel_id=1, source_target_pairs={{0,6},{1,7},{2,4},{3,5},{4,2},{5,3},{6,0},{7,1},{8,14},{9,15},{10,... | collective-permute-start | bytes 86024 | tf_op jit(solution)/shard_map/ppermute | solution.py:197
  67.9 3.9 %collective-permute-start.28 = (bf16[16,896]{1,0:T(8,128)(2,1)S(1)}, bf16[16,896]{1,0:T(8,128)(2,1)S(1)}, u32[]{:S(2)}, u32[]{:S(2)}) collective-permute-start(bf16[16,896]{1,0:T(8,128)(2,1)S(1)} %sums.5.refs_0_), channel_id=1, source_target_pairs={{0,4},{1,5},{2,6},{3,7},{4,0},{5,1},{6,2},{7,3},{8,12},{9,13},{10,... | collective-permute-start | bytes 86024 | tf_op jit(solution)/shard_map/ppermute | solution.py:197
  68.5 3.9 %collective-permute-start.26 = (bf16[16,896]{1,0:T(8,128)(2,1)S(1)}, bf16[16,896]{1,0:T(8,128)(2,1)S(1)}, u32[]{:S(2)}, u32[]{:S(2)}) collective-permute-start(bf16[16,896]{1,0:T(8,128)(2,1)S(1)} %sums.5.refs_0_), channel_id=1, source_target_pairs={{0,2},{1,3},{2,0},{3,1},{4,6},{5,7},{6,4},{7,5},{8,10},{9,11},{10,... | collective-permute-start | bytes 86024 | tf_op jit(solution)/shard_map/ppermute | solution.py:197
  70.0 2.4 %collective-permute-start.25 = (bf16[16,896]{1,0:T(8,128)(2,1)S(1)}, bf16[16,896]{1,0:T(8,128)(2,1)S(1)}, u32[]{:S(2)}, u32[]{:S(2)}) collective-permute-start(bf16[16,896]{1,0:T(8,128)(2,1)S(1)} %sums.5.refs_0_), channel_id=1, source_target_pairs={{0,1},{1,0},{2,3},{3,2},{4,5},{5,4},{6,7},{7,6},{8,9},{9,8},{10,11... | collective-permute-start | bytes 86024 | tf_op jit(solution)/shard_map/ppermute | solution.py:197
  71.3 1.2 %collective-permute-start.31 = (bf16[16,896]{1,0:T(8,128)(2,1)S(1)}, bf16[16,896]{1,0:T(8,128)(2,1)S(1)}, u32[]{:S(2)}, u32[]{:S(2)}) collective-permute-start(bf16[16,896]{1,0:T(8,128)(2,1)S(1)} %collective-permute-done.30.refs_6_), channel_id=1, source_target_pairs={{0,1},{1,0},{2,3},{3,2},{4,5},{5,4},{6,7},{7,6},{8,9},{9,8},{10,11... | collective-permute-start | bytes 86024 | tf_op jit(solution)/shard_map/ppermute | solution.py:197
  71.8 1.2 %collective-permute-start.29 = (bf16[16,896]{1,0:T(8,128)(2,1)S(1)}, bf16[16,896]{1,0:T(8,128)(2,1)S(1)}, u32[]{:S(2)}, u32[]{:S(2)}) collective-permute-start(bf16[16,896]{1,0:T(8,128)(2,1)S(1)} %collective-permute-done.28.refs_4_), channel_id=1, source_target_pairs={{0,1},{1,0},{2,3},{3,2},{4,5},{5,4},{6,7},{7,6},{8,9},{9,8},{10,11... | collective-permute-start | bytes 86024 | tf_op jit(solution)/shard_map/ppermute | solution.py:197
  72.3 1.2 %collective-permute-start.27 = (bf16[16,896]{1,0:T(8,128)(2,1)S(1)}, bf16[16,896]{1,0:T(8,128)(2,1)S(1)}, u32[]{:S(2)}, u32[]{:S(2)}) collective-permute-start(bf16[16,896]{1,0:T(8,128)(2,1)S(1)} %collective-permute-done.26.refs_2_), channel_id=1, source_target_pairs={{0,1},{1,0},{2,3},{3,2},{4,5},{5,4},{6,7},{7,6},{8,9},{9,8},{10,11... | collective-permute-start | bytes 86024 | tf_op jit(solution)/shard_map/ppermute | solution.py:197
  84.5 1.4 %collective-permute-start.32 = (bf16[4,4,16,224]{3,2,1,0:T(8,128)(2,1)S(1)}, bf16[4,4,16,224]{3,2,1,0:T(8,128)(2,1)S(1)}, u32[]{:S(2)}, u32[]{:S(2)}) collective-permute-start(bf16[4,4,16,224]{3,2,1,0:T(8,128)(2,1)S(1)} %get-tuple-element.77), channel_id=1, source_target_pairs={{0,1},{1,0},{2,3},{3,2},{4,5},{5,4},{6,7},{7,6},{8,9},{9,8},{10,11... | collective-permute-start | bytes 344072 | tf_op jit(solution)/shard_map/ppermute | solution.py:197

commit v5 on v4

--- a/solution.py
+++ b/solution.py
@@ -180,7 +180,7 @@
 SHAPE = (4, 2, 2, 2)
 CORE, Y, X, Z0, Z1 = 1, 2, 4, 8, 16
 HEADS_DEV = 4
-UNITS = 256
+UNITS = 512
 STAT = 8
 LANES = 128
 PARENTS = REQ
@@ -273,8 +273,8 @@
                 copy.start()
     first_q, first_r = (own_q, own_r) if fetch else (ql0, qr0)
 
-    out_row = lax.broadcasted_iota(jnp.int32, (total_rows, total_rows), 0)
-    in_row = lax.broadcasted_iota(jnp.int32, (total_rows, total_rows), 1)
+    down = lax.broadcasted_iota(jnp.int32, (total_rows, 1), 0)
+    along = lax.broadcasted_iota(jnp.int32, (1, total_rows), 1)
 
     def source_of(row):
         bit = lambda k: (row >> k) & 1
@@ -282,8 +282,8 @@
         target = (bit(6) ^ x) * 4 + (bit(5) ^ y) * 2 + (bit(7) ^ core)
         return beam * rows + (bit(4) ^ core ^ z0) * heads + target * HEADS_DEV + head
 
-    spread[...] = jnp.where(source_of(out_row) == in_row, 1.0, 0.0).astype(BF)
-    moves = source_of(in_row) == out_row
+    spread[...] = jnp.where(source_of(down) == along, 1.0, 0.0).astype(BF)
+    moves = source_of(along) == down
     messages = [keep.at[t] for t in range(targets)]
     messages += [send.at[t] for send in (send0, send1) for t in range(targets // 2)]
     lse_buf[...] = jnp.zeros_like(lse_buf)
@@ -292,20 +292,23 @@
     wide[0] = first_r[...].astype(F32)
     wide[1] = qr1[...].astype(F32)
     per_group = LANES // DR
-    head_row = lax.broadcasted_iota(jnp.int32, (heads, LANES), 0)
-    own_lanes = lax.broadcasted_iota(jnp.int32, (heads, LANES), 1) // DR == head_row % per_group
-
+    block = 8
+    row8 = lax.broadcasted_iota(jnp.int32, (block, LANES), 0)
+    own_lanes = lax.broadcasted_iota(jnp.int32, (block, LANES), 1) // DR == row8 % per_group
     for r in range(REQ):
         for j in range(BEAMS):
             for piece, q in enumerate((first_q, ql1)):
                 part = slice(j * rows + piece * heads, j * rows + (piece + 1) * heads)
                 b = r * BEAMS + j
                 qbuf[r, part] = q[b]
-                unfolded = jnp.zeros((heads, LANES), F32)
-                for g in range(heads // per_group):
-                    lanes = wide[piece, b:b + 1, g * LANES:(g + 1) * LANES]
-                    unfolded = jnp.where(head_row // per_group == g, lanes, unfolded)
-                rbuf[r, part] = jnp.where(own_lanes, unfolded, 0.0).astype(BF)
+                unfolded = []
+                for top in range(0, heads, block):
+                    rows8 = jnp.zeros((block, LANES), F32)
+                    for g in range(block // per_group):
+                        at = (top // per_group + g) * LANES
+                        rows8 = jnp.where(row8 // per_group == g, wide[piece, b:b + 1, at:at + LANES], rows8)
+                    unfolded.append(jnp.where(own_lanes, rows8, 0.0))
+                rbuf[r, part] = jnp.concatenate(unfolded, axis=0).astype(BF)
 
     def scores(r):
         for copy in copies[r]:

time: 99.7 us -> 102 us (1.023)
  Pallas kernels: 29.3 us -> 31.3 us
    pallas_call x1, Pallas kernels: 10.9 us -> 12.8 us  [experts(): pl.pallas_call(experts_kernel, in_specs=[VMEM] * 14 + [HBM], out_specs=[V...]
  transfers between devices with their start and end apart: 33 -> 33, of which waited for: 21 -> 22; matrix products, arithmetic and copies ran while one was open for 1% -> 1% of each run, Pallas kernels for 17% -> 16%
where the time goes in v5:
time: 102 us; the launch traced here: 101 us
  Pallas kernels  31.3 us (31%)
  starting transfers between devices  28.7 us (28%)
  waiting for transfers between devices  26.4 us (26%)
  blocking collectives  12.9 us (13%)
  other arithmetic  1.38 us (1%)
    ppermute x33, starting transfers between devices, swap(): lax.ppermute(value, AXES, [(i, i ^ mask) for i in range(math.prod(SHAPE))])  28.7 us
    ppermute x33, waiting for transfers between devices, swap(): lax.ppermute(value, AXES, [(i, i ^ mask) for i in range(math.prod(SHAPE))])  26.4 us
    all_to_all x1, blocking collectives, local(): lax.all_to_all(total, AXES[:3], split_axis=0, concat_axis=0, tiled=True)  12.9 us
    pallas_call x1, Pallas kernels, experts(): pl.pallas_call(experts_kernel, in_specs=[VMEM] * 14 + [HBM], out_specs=[V...  12.8 us
    pallas_call x2, Pallas kernels, attend(): pl.pallas_call(partial(attend_kernel, scale, fetch), in_specs=[SMEM, spec...  12.3 us
    pallas_call x1, Pallas kernels, load(): pl.pallas_call(partial(load_kernel, count), in_specs=[HBM] * count + [pl....  3.41 us
  transfers between devices with their start and end apart: 33, of which 22 were waited for; matrix products, arithmetic and copies ran while one was open for 1% of the time, Pallas kernels for 16%

profile of v5, /device:TPU:0, one launch (start us, length us, event | category | flops | bytes accessed | tf_op | source)
XLA Modules:
  0.0 101.4 jit_solution(10447680744312822931)
XLA Ops:
  0.6 0.5 collective-permute-start.2
  1.1 2.6 %collective-permute-start = (bf16[16,32,512]{2,1,0:T(8,128)(2,1)}, bf16[16,32,512]{2,1,0:T(8,128)(2,1)S(1)}, u32[]{:S(2)}, u32[]{:S(2)}) collective-permute-start(bf16[16,32,512]{2,1,0:T(8,128)(2,1)} %ql0.1), channel_id=1, source_target_pairs={{0,2},{1,3},{2,0},{3,1},{4,6},{5,7},{6,4},{7,5},{8,10},{9,11},{10,... | collective-permute-start | bytes 1572872 | tf_op jit(solution)/shard_map/ppermute | solution.py:197
  3.9 0.7 pad_add_fusion.info
  4.7 0.6 collective-permute-done.3.qr1
  5.2 6.4 %attend.2 = (bf16[4,136,512]{2,1,0:T(8,128)(2,1)S(1)}, bf16[2,136,512]{2,1,0:T(8,128)(2,1)S(1)}, bf16[2,136,512]{2,1,0:T(8,128)(2,1)S(1)}) custom-call(s32[20]{0:T(128)S(1)} %pad_add_fusion.info, bf16[16,32,512]{2,1,0:T(8,128)(2,1)} %ql0.1, bf16[16,32,512]{2,1,0:T(8,128)(2,1)S(1)} %collective-permute-done.2.ql1, bf16[16,2048]{1,0:T(8,128)(2,1)} %qr0.1, ...), custom_call_target="tpu_custom_call" | custom-call | flops 1426063360 | bytes 8388608 | tf_op jit(solution)/shard_map/attend/pallas_call | solution.py:386
  11.8 0.3 collective-permute-start.5
  12.2 0.7 collective-permute-start.1
  12.9 0.4 collective-permute-done.4.refs_0_
  13.2 0.4 collective-permute-done.5.refs_1_
  14.0 3.9 %collective-permute-done.1.qr0 = bf16[16,2048]{1,0:T(8,128)(2,1)S(1)} collective-permute-done((bf16[16,2048]{1,0:T(8,128)(2,1)}, bf16[16,2048]{1,0:T(8,128)(2,1)S(1)}, u32[]{:S(2)}, u32[]{:S(2)}) %collective-permute-start.1) | collective-permute-done | bytes 65568 | tf_op jit(solution)/shard_map/ppermute | solution.py:197
  17.9 1.8 %collective-permute-start.8 = (bf16[2,136,512]{2,1,0:T(8,128)(2,1)S(1)}, bf16[2,136,512]{2,1,0:T(8,128)(2,1)S(1)}, u32[]{:S(2)}, u32[]{:S(2)}) collective-permute-start(bf16[2,136,512]{2,1,0:T(8,128)(2,1)S(1)} %get-tuple-element.51), channel_id=1, source_target_pairs={{0,4},{1,5},{2,6},{3,7},{4,0},{5,1},{6,2},{7,3},{8,12},{9,13},{10,... | collective-permute-start | bytes 835592 | tf_op jit(solution)/shard_map/ppermute | solution.py:197
  19.8 1.1 %collective-permute-done.7.qr1 = bf16[16,2048]{1,0:T(8,128)(2,1)S(1)} collective-permute-done((bf16[16,2048]{1,0:T(8,128)(2,1)S(1)}, bf16[16,2048]{1,0:T(8,128)(2,1)S(1)}, u32[]{:S(2)}, u32[]{:S(2)}) %collective-permute-start.7) | collective-permute-done | bytes 65568 | tf_op jit(solution)/shard_map/ppermute | solution.py:197
  20.9 5.9 %attend.3 = (bf16[4,136,512]{2,1,0:T(8,128)(2,1)S(1)}, bf16[2,136,512]{2,1,0:T(8,128)(2,1)S(1)}, bf16[2,136,512]{2,1,0:T(8,128)(2,1)S(1)}) custom-call(s32[20]{0:T(128)S(1)} %pad_add_fusion.info, bf16[16,32,512]{2,1,0:T(8,128)(2,1)S(1)} %collective-permute-done.ql0, bf16[16,32,512]{2,1,0:T(8,128)(2,1)S(1)} %collective-permute-done.6.ql1, ...), custom_call_target="tpu_custom_call" | custom-call | flops 1426063360 | bytes 8388608 | tf_op jit(solution)/shard_map/attend/pallas_call | solution.py:386
  27.1 0.3 collective-permute-start.10
  27.7 1.8 %collective-permute-start.13 = (bf16[1,136,512]{2,1,0:T(8,128)(2,1)S(1)}, bf16[1,136,512]{2,1,0:T(8,128)(2,1)S(1)}, u32[]{:S(2)}, u32[]{:S(2)}) collective-permute-start(bf16[1,136,512]{2,1,0:T(8,128)(2,1)S(1)} %get-tuple-element.59), channel_id=1, source_target_pairs={{0,2},{1,3},{2,0},{3,1},{4,6},{5,7},{6,4},{7,5},{8,10},{9,11},{10,... | collective-permute-start | bytes 417800 | tf_op jit(solution)/shard_map/ppermute | solution.py:197
  29.8 1.2 %collective-permute-start.11 = (bf16[1,136,512]{2,1,0:T(8,128)(2,1)S(1)}, bf16[1,136,512]{2,1,0:T(8,128)(2,1)S(1)}, u32[]{:S(2)}, u32[]{:S(2)}) collective-permute-start(bf16[1,136,512]{2,1,0:T(8,128)(2,1)S(1)} %get-tuple-element.57), channel_id=1, source_target_pairs={{0,2},{1,3},{2,0},{3,1},{4,6},{5,7},{6,4},{7,5},{8,10},{9,11},{10,... | collective-permute-start | bytes 417800 | tf_op jit(solution)/shard_map/ppermute | solution.py:197
  31.1 1.8 %collective-permute-start.12 = (bf16[1,136,512]{2,1,0:T(8,128)(2,1)S(1)}, bf16[1,136,512]{2,1,0:T(8,128)(2,1)S(1)}, u32[]{:S(2)}, u32[]{:S(2)}) collective-permute-start(bf16[1,136,512]{2,1,0:T(8,128)(2,1)S(1)} %get-tuple-element.58), channel_id=1, source_target_pairs={{0,6},{1,7},{2,4},{3,5},{4,2},{5,3},{6,0},{7,1},{8,14},{9,15},{10,... | collective-permute-start | bytes 417800 | tf_op jit(solution)/shard_map/ppermute | solution.py:197
  32.8 0.5 collective-permute-start.14
  33.4 2.2 %collective-permute-done.13.refs_3_ = bf16[1,136,512]{2,1,0:T(8,128)(2,1)S(1)} collective-permute-done((bf16[1,136,512]{2,1,0:T(8,128)(2,1)S(1)}, bf16[1,136,512]{2,1,0:T(8,128)(2,1)S(1)}, u32[]{:S(2)}, u32[]{:S(2)}) %collective-permute-start.13) | collective-permute-done | bytes 139296 | tf_op jit(solution)/shard_map/ppermute | solution.py:197
  35.6 3.8 %collective-permute-done.11.refs_1_ = bf16[1,136,512]{2,1,0:T(8,128)(2,1)S(1)} collective-permute-done((bf16[1,136,512]{2,1,0:T(8,128)(2,1)S(1)}, bf16[1,136,512]{2,1,0:T(8,128)(2,1)S(1)}, u32[]{:S(2)}, u32[]{:S(2)}) %collective-permute-start.11) | collective-permute-done | bytes 139296 | tf_op jit(solution)/shard_map/ppermute | solution.py:197
  39.8 3.7 %collective-permute-start.15 = (bf16[72,512]{1,0:T(8,128)(2,1)S(1)}, bf16[72,512]{1,0:T(8,128)(2,1)S(1)}, u32[]{:S(2)}, u32[]{:S(2)}) collective-permute-start(bf16[72,512]{1,0:T(8,128)(2,1)S(1)} %get-tuple-element.63), channel_id=1, source_target_pairs={{0,24},{1,25},{2,26},{3,27},{4,28},{5,29},{6,30},{7,31},{8,16},{9,... | collective-permute-start | bytes 221192 | tf_op jit(solution)/shard_map/ppermute | solution.py:197
  43.5 0.7 collective-permute-start.17
  44.3 3.4 %load.1 = (bf16[512,512]{1,0:T(8,128)(2,1)S(1)}, bf16[512,7168]{1,0:T(8,128)(2,1)S(1)}) custom-call(bf16[512,512]{1,0:T(8,128)(2,1)} %refs_0_.1, bf16[512,7168]{1,0:T(8,128)(2,1)} %refs_1_.1, bf16[72,512]{1,0:T(8,128)(2,1)S(1)} %get-tuple-element.62.refs_2_.p0), custom_call_target="tpu_custom_call" | custom-call | bytes 7864320 | tf_op jit(solution)/shard_map/load/pallas_call | solution.py:568
  47.7 1.6 %collective-permute-done.16.p2 = bf16[72,512]{1,0:T(8,128)(2,1)S(1)} collective-permute-done((bf16[72,512]{1,0:T(8,128)(2,1)S(1)}, bf16[72,512]{1,0:T(8,128)(2,1)S(1)}, u32[]{:S(2)}, u32[]{:S(2)}) %collective-permute-start.16) | collective-permute-done | bytes 73760 | tf_op jit(solution)/shard_map/ppermute | solution.py:197
  49.3 1.4 %project.1 = (bf16[4,16,896]{2,1,0:T(8,128)(2,1)S(1)}, bf16[4,16,896]{2,1,0:T(8,128)(2,1)S(1)}) custom-call(bf16[72,512]{1,0:T(8,128)(2,1)S(1)} %get-tuple-element.62.refs_2_.p0, bf16[72,512]{1,0:T(8,128)(2,1)S(1)} %collective-permute-done.15.p1, bf16[72,512]{1,0:T(8,128)(2,1)S(1)} %collective-permute-done.16.p2, ...), custom_call_target="tpu_custom_call" | custom-call | flops 117440512 | bytes 7340032 | tf_op jit(solution)/shard_map/project/pallas_call | solution.py:525
  50.8 1.3 %collective-permute-done.18.refs_1_ = bf16[4,16,896]{2,1,0:T(8,128)(2,1)S(1)} collective-permute-done((bf16[4,16,896]{2,1,0:T(8,128)(2,1)S(1)}, bf16[4,16,896]{2,1,0:T(8,128)(2,1)S(1)}, u32[]{:S(2)}, u32[]{:S(2)}) %collective-permute-start.18) | collective-permute-done | bytes 114720 | tf_op jit(solution)/shard_map/ppermute | solution.py:197
  52.1 2.5 %collective-permute-start.19 = (bf16[16,896]{1,0:T(8,128)(2,1)S(1)}, bf16[16,896]{1,0:T(8,128)(2,1)S(1)}, u32[]{:S(2)}, u32[]{:S(2)}) collective-permute-start(bf16[16,896]{1,0:T(8,128)(2,1)S(1)} %get-tuple-element.71), channel_id=1, source_target_pairs={{0,6},{1,7},{2,4},{3,5},{4,2},{5,3},{6,0},{7,1},{8,14},{9,15},{10,... | collective-permute-start | bytes 86024 | tf_op jit(solution)/shard_map/ppermute | solution.py:197
  54.6 0.5 collective-permute-start.20
  55.2 0.5 collective-permute-start.21
  55.7 1.3 %collective-permute-done.19.refs_1_ = bf16[16,896]{1,0:T(8,128)(2,1)S(1)} collective-permute-done((bf16[16,896]{1,0:T(8,128)(2,1)S(1)}, bf16[16,896]{1,0:T(8,128)(2,1)S(1)}, u32[]{:S(2)}, u32[]{:S(2)}) %collective-permute-start.19) | collective-permute-done | bytes 28704 | tf_op jit(solution)/shard_map/ppermute | solution.py:197
  57.0 1.5 %collective-permute-done.20.refs_2_ = bf16[16,896]{1,0:T(8,128)(2,1)S(1)} collective-permute-done((bf16[16,896]{1,0:T(8,128)(2,1)S(1)}, bf16[16,896]{1,0:T(8,128)(2,1)S(1)}, u32[]{:S(2)}, u32[]{:S(2)}) %collective-permute-start.20) | collective-permute-done | bytes 28704 | tf_op jit(solution)/shard_map/ppermute | solution.py:197
  58.5 0.5 collective-permute-done.21.refs_3_
  59.1 2.6 %collective-permute-start.24 = (bf16[16,896]{1,0:T(8,128)(2,1)S(1)}, bf16[16,896]{1,0:T(8,128)(2,1)S(1)}, u32[]{:S(2)}, u32[]{:S(2)}) collective-permute-start(bf16[16,896]{1,0:T(8,128)(2,1)S(1)} %sums.4.refs_0_), channel_id=1, source_target_pairs={{0,24},{1,25},{2,26},{3,27},{4,28},{5,29},{6,30},{7,31},{8,16},{9,... | collective-permute-start | bytes 86024 | tf_op jit(solution)/shard_map/ppermute | solution.py:197
  61.6 1.9 %collective-permute-start.22 = (bf16[16,896]{1,0:T(8,128)(2,1)S(1)}, bf16[16,896]{1,0:T(8,128)(2,1)S(1)}, u32[]{:S(2)}, u32[]{:S(2)}) collective-permute-start(bf16[16,896]{1,0:T(8,128)(2,1)S(1)} %sums.4.refs_0_), channel_id=1, source_target_pairs={{0,8},{1,9},{2,10},{3,11},{4,12},{5,13},{6,14},{7,15},{8,0},{9,1},... | collective-permute-start | bytes 86024 | tf_op jit(solution)/shard_map/ppermute | solution.py:197
  63.5 1.6 %collective-permute-done.24.refs_3_ = bf16[16,896]{1,0:T(8,128)(2,1)S(1)} collective-permute-done((bf16[16,896]{1,0:T(8,128)(2,1)S(1)}, bf16[16,896]{1,0:T(8,128)(2,1)S(1)}, u32[]{:S(2)}, u32[]{:S(2)}) %collective-permute-start.24) | collective-permute-done | bytes 28704 | tf_op jit(solution)/shard_map/ppermute | solution.py:197
  65.1 1.3 %collective-permute-done.23.refs_2_ = bf16[16,896]{1,0:T(8,128)(2,1)S(1)} collective-permute-done((bf16[16,896]{1,0:T(8,128)(2,1)S(1)}, bf16[16,896]{1,0:T(8,128)(2,1)S(1)}, u32[]{:S(2)}, u32[]{:S(2)}) %collective-permute-start.23) | collective-permute-done | bytes 28704 | tf_op jit(solution)/shard_map/ppermute | solution.py:197
  66.4 1.5 %collective-permute-start.30 = (bf16[16,896]{1,0:T(8,128)(2,1)S(1)}, bf16[16,896]{1,0:T(8,128)(2,1)S(1)}, u32[]{:S(2)}, u32[]{:S(2)}) collective-permute-start(bf16[16,896]{1,0:T(8,128)(2,1)S(1)} %sums.5.refs_0_), channel_id=1, source_target_pairs={{0,6},{1,7},{2,4},{3,5},{4,2},{5,3},{6,0},{7,1},{8,14},{9,15},{10,... | collective-permute-start | bytes 86024 | tf_op jit(solution)/shard_map/ppermute | solution.py:197
  67.9 0.6 collective-permute-start.28
  68.5 1.5 %collective-permute-start.26 = (bf16[16,896]{1,0:T(8,128)(2,1)S(1)}, bf16[16,896]{1,0:T(8,128)(2,1)S(1)}, u32[]{:S(2)}, u32[]{:S(2)}) collective-permute-start(bf16[16,896]{1,0:T(8,128)(2,1)S(1)} %sums.5.refs_0_), channel_id=1, source_target_pairs={{0,2},{1,3},{2,0},{3,1},{4,6},{5,7},{6,4},{7,5},{8,10},{9,11},{10,... | collective-permute-start | bytes 86024 | tf_op jit(solution)/shard_map/ppermute | solution.py:197
  70.0 1.3 %collective-permute-done.30.refs_6_ = bf16[16,896]{1,0:T(8,128)(2,1)S(1)} collective-permute-done((bf16[16,896]{1,0:T(8,128)(2,1)S(1)}, bf16[16,896]{1,0:T(8,128)(2,1)S(1)}, u32[]{:S(2)}, u32[]{:S(2)}) %collective-permute-start.30) | collective-permute-done | bytes 28704 | tf_op jit(solution)/shard_map/ppermute | solution.py:197
  71.3 0.5 collective-permute-done.28.refs_4_
  71.8 0.6 collective-permute-done.26.refs_2_
  72.5 0.5 collective-permute-done.29.refs_5_
  73.0 0.6 collective-permute-done.27.refs_3_
  73.6 12.8 %experts.1 = (bf16[16,7168]{1,0:T(8,128)(2,1)}, bf16[4,4,16,224]{3,2,1,0:T(8,128)(2,1)S(1)}, bf16[4,4,16,224]{3,2,1,0:T(8,128)(2,1)S(1)}, f32[16,224]{1,0:T(8,128)S(1)}) custom-call(bf16[16,896]{1,0:T(8,128)(2,1)S(1)} %sums.5.refs_0_, bf16[16,896]{1,0:T(8,128)(2,1)S(1)} %collective-permute-done.25.refs_1_, ...), custom_call_target="tpu_custom_call" | custom-call | flops 704643072 | bytes 44040192 | tf_op jit(solution)/shard_map/experts/pallas_call | solution.py:633
  86.7 1.2 %collective-permute-done.32.b = bf16[4,4,16,224]{3,2,1,0:T(8,128)(2,1)S(1)} collective-permute-done((bf16[4,4,16,224]{3,2,1,0:T(8,128)(2,1)S(1)}, bf16[4,4,16,224]{3,2,1,0:T(8,128)(2,1)S(1)}, u32[]{:S(2)}, u32[]{:S(2)}) %collective-permute-start.32) | collective-permute-done | bytes 114720 | tf_op jit(solution)/shard_map/ppermute | solution.py:197
  87.9 12.9 %all_to_all.5 = bf16[16,16,224]{2,1,0:T(8,128)(2,1)S(1)} all-to-all(bf16[16,16,224]{2,1,0:T(8,128)(2,1)S(1)} %core_sum.1), channel_id=1, replica_groups=mesh['z'=4,'x'=2,'y'=2,'core'=2] {'z','x','y'}, dimensions={0} | all-to-all | bytes 229376 | tf_op jit(solution)/shard_map/all_to_all | solution.py:705
  100.8 0.6 add_convert_fusion
  (54 shorter events, 2.6 us)
Async XLA Ops:
  0.6 4.6 %collective-permute-start.2 = (bf16[16,32,512]{2,1,0:T(8,128)(2,1)}, bf16[16,32,512]{2,1,0:T(8,128)(2,1)S(1)}, u32[]{:S(2)}, u32[]{:S(2)}) collective-permute-start(bf16[16,32,512]{2,1,0:T(8,128)(2,1)} %ql0.1), channel_id=1, source_target_pairs={{0,1},{1,0},{2,3},{3,2},{4,5},{5,4},{6,7},{7,6},{8,9},{9,8},{10,11... | collective-permute-start | bytes 1572872 | tf_op jit(solution)/shard_map/ppermute | solution.py:197
  1.1 16.7 %collective-permute-start = (bf16[16,32,512]{2,1,0:T(8,128)(2,1)}, bf16[16,32,512]{2,1,0:T(8,128)(2,1)S(1)}, u32[]{:S(2)}, u32[]{:S(2)}) collective-permute-start(bf16[16,32,512]{2,1,0:T(8,128)(2,1)} %ql0.1), channel_id=1, source_target_pairs={{0,2},{1,3},{2,0},{3,1},{4,6},{5,7},{6,4},{7,5},{8,10},{9,11},{10,... | collective-permute-start | bytes 1572872 | tf_op jit(solution)/shard_map/ppermute | solution.py:197
  3.7 1.5 %collective-permute-start.3 = (bf16[16,2048]{1,0:T(8,128)(2,1)}, bf16[16,2048]{1,0:T(8,128)(2,1)S(1)}, u32[]{:S(2)}, u32[]{:S(2)}) collective-permute-start(bf16[16,2048]{1,0:T(8,128)(2,1)} %qr0.1), channel_id=1, source_target_pairs={{0,1},{1,0},{2,3},{3,2},{4,5},{5,4},{6,7},{7,6},{8,9},{9,8},{10,11... | collective-permute-start | bytes 196616 | tf_op jit(solution)/shard_map/ppermute | solution.py:197
  5.2 68.4 %slice-start = ((s8[14680064]{0:T(1024)(128)(4,1)}), s8[4194304]{0:T(1024)(128)(4,1)S(1)}, s32[]{:S(2)}) async-start(s8[14680064]{0:T(1024)(128)(4,1)} %bitcast.3), calls=%async_computation.1 | async-start | bytes 8388608
  11.6 1.6 %collective-permute-start.4 = (bf16[2,136,512]{2,1,0:T(8,128)(2,1)S(1)}, bf16[2,136,512]{2,1,0:T(8,128)(2,1)S(1)}, u32[]{:S(2)}, u32[]{:S(2)}) collective-permute-start(bf16[2,136,512]{2,1,0:T(8,128)(2,1)S(1)} %get-tuple-element.41), channel_id=1, source_target_pairs={{0,1},{1,0},{2,3},{3,2},{4,5},{5,4},{6,7},{7,6},{8,9},{9,8},{10,11... | collective-permute-start | bytes 835592 | tf_op jit(solution)/shard_map/ppermute | solution.py:197
  11.8 1.8 %collective-permute-start.5 = (bf16[2,136,512]{2,1,0:T(8,128)(2,1)S(1)}, bf16[2,136,512]{2,1,0:T(8,128)(2,1)S(1)}, u32[]{:S(2)}, u32[]{:S(2)}) collective-permute-start(bf16[2,136,512]{2,1,0:T(8,128)(2,1)S(1)} %get-tuple-element.42), channel_id=1, source_target_pairs={{0,1},{1,0},{2,3},{3,2},{4,5},{5,4},{6,7},{7,6},{8,9},{9,8},{10,11... | collective-permute-start | bytes 835592 | tf_op jit(solution)/shard_map/ppermute | solution.py:197
  12.2 5.7 %collective-permute-start.1 = (bf16[16,2048]{1,0:T(8,128)(2,1)}, bf16[16,2048]{1,0:T(8,128)(2,1)S(1)}, u32[]{:S(2)}, u32[]{:S(2)}) collective-permute-start(bf16[16,2048]{1,0:T(8,128)(2,1)} %qr0.1), channel_id=1, source_target_pairs={{0,2},{1,3},{2,0},{3,1},{4,6},{5,7},{6,4},{7,5},{8,10},{9,11},{10,... | collective-permute-start | bytes 196616 | tf_op jit(solution)/shard_map/ppermute | solution.py:197
  13.6 59.9 %copy-start = (bf16[1024,7168]{1,0:T(8,128)(2,1)S(1)}, bf16[1024,7168]{1,0:T(8,128)(2,1)}, u32[]{:S(2)}) copy-start(bf16[1024,7168]{1,0:T(8,128)(2,1)} %refs_13_.1) | copy-start | bytes 44040196
  17.9 55.7 %slice-start.1 = ((s8[14680064]{0:T(1024)(128)(4,1)}), s8[4194304]{0:T(1024)(128)(4,1)S(1)}, s32[]{:S(2)}) async-start(s8[14680064]{0:T(1024)(128)(4,1)} %bitcast.3), calls=%async_computation.2 | async-start | bytes 8388608
  17.9 3.1 %collective-permute-start.6 = (bf16[16,32,512]{2,1,0:T(8,128)(2,1)S(1)}, bf16[16,32,512]{2,1,0:T(8,128)(2,1)S(1)}, u32[]{:S(2)}, u32[]{:S(2)}) collective-permute-start(bf16[16,32,512]{2,1,0:T(8,128)(2,1)S(1)} %collective-permute-done.ql0), channel_id=1, source_target_pairs={{0,1},{1,0},{2,3},{3,2},{4,5},{5,4},{6,7},{7,6},{8,9},{9,8},{10,11... | collective-permute-start | bytes 1572872 | tf_op jit(solution)/shard_map/ppermute | solution.py:197
  17.9 9.1 %collective-permute-start.8 = (bf16[2,136,512]{2,1,0:T(8,128)(2,1)S(1)}, bf16[2,136,512]{2,1,0:T(8,128)(2,1)S(1)}, u32[]{:S(2)}, u32[]{:S(2)}) collective-permute-start(bf16[2,136,512]{2,1,0:T(8,128)(2,1)S(1)} %get-tuple-element.51), channel_id=1, source_target_pairs={{0,4},{1,5},{2,6},{3,7},{4,0},{5,1},{6,2},{7,3},{8,12},{9,13},{10,... | collective-permute-start | bytes 835592 | tf_op jit(solution)/shard_map/ppermute | solution.py:197
  19.7 1.3 %collective-permute-start.7 = (bf16[16,2048]{1,0:T(8,128)(2,1)S(1)}, bf16[16,2048]{1,0:T(8,128)(2,1)S(1)}, u32[]{:S(2)}, u32[]{:S(2)}) collective-permute-start(bf16[16,2048]{1,0:T(8,128)(2,1)S(1)} %collective-permute-done.1.qr0), channel_id=1, source_target_pairs={{0,1},{1,0},{2,3},{3,2},{4,5},{5,4},{6,7},{7,6},{8,9},{9,8},{10,11... | collective-permute-start | bytes 196616 | tf_op jit(solution)/shard_map/ppermute | solution.py:197
  27.0 2.5 %collective-permute-start.9 = (bf16[2,136,512]{2,1,0:T(8,128)(2,1)S(1)}, bf16[2,136,512]{2,1,0:T(8,128)(2,1)S(1)}, u32[]{:S(2)}, u32[]{:S(2)}) collective-permute-start(bf16[2,136,512]{2,1,0:T(8,128)(2,1)S(1)} %get-tuple-element.55), channel_id=1, source_target_pairs={{0,1},{1,0},{2,3},{3,2},{4,5},{5,4},{6,7},{7,6},{8,9},{9,8},{10,11... | collective-permute-start | bytes 835592 | tf_op jit(solution)/shard_map/ppermute | solution.py:197
  27.1 2.4 %collective-permute-start.10 = (bf16[2,136,512]{2,1,0:T(8,128)(2,1)S(1)}, bf16[2,136,512]{2,1,0:T(8,128)(2,1)S(1)}, u32[]{:S(2)}, u32[]{:S(2)}) collective-permute-start(bf16[2,136,512]{2,1,0:T(8,128)(2,1)S(1)} %get-tuple-element.56), channel_id=1, source_target_pairs={{0,1},{1,0},{2,3},{3,2},{4,5},{5,4},{6,7},{7,6},{8,9},{9,8},{10,11... | collective-permute-start | bytes 835592 | tf_op jit(solution)/shard_map/ppermute | solution.py:197
  27.7 7.9 %collective-permute-start.13 = (bf16[1,136,512]{2,1,0:T(8,128)(2,1)S(1)}, bf16[1,136,512]{2,1,0:T(8,128)(2,1)S(1)}, u32[]{:S(2)}, u32[]{:S(2)}) collective-permute-start(bf16[1,136,512]{2,1,0:T(8,128)(2,1)S(1)} %get-tuple-element.59), channel_id=1, source_target_pairs={{0,2},{1,3},{2,0},{3,1},{4,6},{5,7},{6,4},{7,5},{8,10},{9,11},{10,... | collective-permute-start | bytes 417800 | tf_op jit(solution)/shard_map/ppermute | solution.py:197
  29.8 9.6 %collective-permute-start.11 = (bf16[1,136,512]{2,1,0:T(8,128)(2,1)S(1)}, bf16[1,136,512]{2,1,0:T(8,128)(2,1)S(1)}, u32[]{:S(2)}, u32[]{:S(2)}) collective-permute-start(bf16[1,136,512]{2,1,0:T(8,128)(2,1)S(1)} %get-tuple-element.57), channel_id=1, source_target_pairs={{0,2},{1,3},{2,0},{3,1},{4,6},{5,7},{6,4},{7,5},{8,10},{9,11},{10,... | collective-permute-start | bytes 417800 | tf_op jit(solution)/shard_map/ppermute | solution.py:197
  31.1 8.4 %collective-permute-start.12 = (bf16[1,136,512]{2,1,0:T(8,128)(2,1)S(1)}, bf16[1,136,512]{2,1,0:T(8,128)(2,1)S(1)}, u32[]{:S(2)}, u32[]{:S(2)}) collective-permute-start(bf16[1,136,512]{2,1,0:T(8,128)(2,1)S(1)} %get-tuple-element.58), channel_id=1, source_target_pairs={{0,6},{1,7},{2,4},{3,5},{4,2},{5,3},{6,0},{7,1},{8,14},{9,15},{10,... | collective-permute-start | bytes 417800 | tf_op jit(solution)/shard_map/ppermute | solution.py:197
  32.8 6.6 %collective-permute-start.14 = (bf16[1,136,512]{2,1,0:T(8,128)(2,1)S(1)}, bf16[1,136,512]{2,1,0:T(8,128)(2,1)S(1)}, u32[]{:S(2)}, u32[]{:S(2)}) collective-permute-start(bf16[1,136,512]{2,1,0:T(8,128)(2,1)S(1)} %get-tuple-element.61), channel_id=1, source_target_pairs={{0,4},{1,5},{2,6},{3,7},{4,0},{5,1},{6,2},{7,3},{8,12},{9,13},{10,... | collective-permute-start | bytes 417800 | tf_op jit(solution)/shard_map/ppermute | solution.py:197
  39.8 7.9 %collective-permute-start.15 = (bf16[72,512]{1,0:T(8,128)(2,1)S(1)}, bf16[72,512]{1,0:T(8,128)(2,1)S(1)}, u32[]{:S(2)}, u32[]{:S(2)}) collective-permute-start(bf16[72,512]{1,0:T(8,128)(2,1)S(1)} %get-tuple-element.63), channel_id=1, source_target_pairs={{0,24},{1,25},{2,26},{3,27},{4,28},{5,29},{6,30},{7,31},{8,16},{9,... | collective-permute-start | bytes 221192 | tf_op jit(solution)/shard_map/ppermute | solution.py:197
  43.5 5.7 %collective-permute-start.16 = (bf16[72,512]{1,0:T(8,128)(2,1)S(1)}, bf16[72,512]{1,0:T(8,128)(2,1)S(1)}, u32[]{:S(2)}, u32[]{:S(2)}) collective-permute-start(bf16[72,512]{1,0:T(8,128)(2,1)S(1)} %get-tuple-element.64), channel_id=1, source_target_pairs={{0,16},{1,17},{2,18},{3,19},{4,20},{5,21},{6,22},{7,23},{8,24},{9,... | collective-permute-start | bytes 221192 | tf_op jit(solution)/shard_map/ppermute | solution.py:197
  43.5 5.7 %collective-permute-start.17 = (bf16[72,512]{1,0:T(8,128)(2,1)S(1)}, bf16[72,512]{1,0:T(8,128)(2,1)S(1)}, u32[]{:S(2)}, u32[]{:S(2)}) collective-permute-start(bf16[72,512]{1,0:T(8,128)(2,1)S(1)} %get-tuple-element.65), channel_id=1, source_target_pairs={{0,8},{1,9},{2,10},{3,11},{4,12},{5,13},{6,14},{7,15},{8,0},{9,1},... | collective-permute-start | bytes 221192 | tf_op jit(solution)/shard_map/ppermute | solution.py:197
  44.3 29.3 %slice-start.2 = ((s8[14680064]{0:T(1024)(128)(4,1)}), s8[4194304]{0:T(1024)(128)(4,1)S(1)}, s32[]{:S(2)}) async-start(s8[14680064]{0:T(1024)(128)(4,1)} %bitcast.3), calls=%async_computation.3 | async-start | bytes 8388608
  44.3 29.3 %copy-start.1 = (bf16[16,7168]{1,0:T(8,128)(2,1)S(1)}, bf16[16,7168]{1,0:T(8,128)(2,1)}, u32[]{:S(2)}) copy-start(bf16[16,7168]{1,0:T(8,128)(2,1)} %refs_8_.1) | copy-start | bytes 688132
  44.3 29.3 %copy-start.2 = (f32[7168]{0:T(1024)S(1)}, f32[7168]{0:T(1024)}, u32[]{:S(2)}) copy-start(f32[7168]{0:T(1024)} %param.28) | copy-start | bytes 86020
  44.3 29.3 %copy-start.3 = (s32[16,8]{0,1:T(8,128)S(1)}, s32[16,8]{0,1:T(8,128)}, u32[]{:S(2)}) copy-start(s32[16,8]{0,1:T(8,128)} %param.32) | copy-start | bytes 1540
  44.3 29.3 %copy-start.4 = (f32[16,8]{0,1:T(8,128)S(1)}, f32[16,8]{0,1:T(8,128)}, u32[]{:S(2)}) copy-start(f32[16,8]{0,1:T(8,128)} %param.33) | copy-start | bytes 1540
  49.3 24.4 %slice-start.3 = ((s8[14680064]{0:T(1024)(128)(4,1)}), s8[2097152]{0:T(1024)(128)(4,1)S(1)}, s32[]{:S(2)}) async-start(s8[14680064]{0:T(1024)(128)(4,1)} %bitcast.3), calls=%async_computation.4 | async-start | bytes 4194304
  50.7 1.4 %collective-permute-start.18 = (bf16[4,16,896]{2,1,0:T(8,128)(2,1)S(1)}, bf16[4,16,896]{2,1,0:T(8,128)(2,1)S(1)}, u32[]{:S(2)}, u32[]{:S(2)}) collective-permute-start(bf16[4,16,896]{2,1,0:T(8,128)(2,1)S(1)} %get-tuple-element.69), channel_id=1, source_target_pairs={{0,1},{1,0},{2,3},{3,2},{4,5},{5,4},{6,7},{7,6},{8,9},{9,8},{10,11... | collective-permute-start | bytes 344072 | tf_op jit(solution)/shard_map/ppermute | solution.py:197
  52.1 4.8 %collective-permute-start.19 = (bf16[16,896]{1,0:T(8,128)(2,1)S(1)}, bf16[16,896]{1,0:T(8,128)(2,1)S(1)}, u32[]{:S(2)}, u32[]{:S(2)}) collective-permute-start(bf16[16,896]{1,0:T(8,128)(2,1)S(1)} %get-tuple-element.71), channel_id=1, source_target_pairs={{0,6},{1,7},{2,4},{3,5},{4,2},{5,3},{6,0},{7,1},{8,14},{9,15},{10,... | collective-permute-start | bytes 86024 | tf_op jit(solution)/shard_map/ppermute | solution.py:197
  54.6 3.9 %collective-permute-start.20 = (bf16[16,896]{1,0:T(8,128)(2,1)S(1)}, bf16[16,896]{1,0:T(8,128)(2,1)S(1)}, u32[]{:S(2)}, u32[]{:S(2)}) collective-permute-start(bf16[16,896]{1,0:T(8,128)(2,1)S(1)} %get-tuple-element.72), channel_id=1, source_target_pairs={{0,4},{1,5},{2,6},{3,7},{4,0},{5,1},{6,2},{7,3},{8,12},{9,13},{10,... | collective-permute-start | bytes 86024 | tf_op jit(solution)/shard_map/ppermute | solution.py:197
  55.2 3.9 %collective-permute-start.21 = (bf16[16,896]{1,0:T(8,128)(2,1)S(1)}, bf16[16,896]{1,0:T(8,128)(2,1)S(1)}, u32[]{:S(2)}, u32[]{:S(2)}) collective-permute-start(bf16[16,896]{1,0:T(8,128)(2,1)S(1)} %get-tuple-element.73), channel_id=1, source_target_pairs={{0,2},{1,3},{2,0},{3,1},{4,6},{5,7},{6,4},{7,5},{8,10},{9,11},{10,... | collective-permute-start | bytes 86024 | tf_op jit(solution)/shard_map/ppermute | solution.py:197
  59.1 6.0 %collective-permute-start.24 = (bf16[16,896]{1,0:T(8,128)(2,1)S(1)}, bf16[16,896]{1,0:T(8,128)(2,1)S(1)}, u32[]{:S(2)}, u32[]{:S(2)}) collective-permute-start(bf16[16,896]{1,0:T(8,128)(2,1)S(1)} %sums.4.refs_0_), channel_id=1, source_target_pairs={{0,24},{1,25},{2,26},{3,27},{4,28},{5,29},{6,30},{7,31},{8,16},{9,... | collective-permute-start | bytes 86024 | tf_op jit(solution)/shard_map/ppermute | solution.py:197
  61.6 4.8 %collective-permute-start.23 = (bf16[16,896]{1,0:T(8,128)(2,1)S(1)}, bf16[16,896]{1,0:T(8,128)(2,1)S(1)}, u32[]{:S(2)}, u32[]{:S(2)}) collective-permute-start(bf16[16,896]{1,0:T(8,128)(2,1)S(1)} %sums.4.refs_0_), channel_id=1, source_target_pairs={{0,16},{1,17},{2,18},{3,19},{4,20},{5,21},{6,22},{7,23},{8,24},{9,... | collective-permute-start | bytes 86024 | tf_op jit(solution)/shard_map/ppermute | solution.py:197
  61.6 4.8 %collective-permute-start.22 = (bf16[16,896]{1,0:T(8,128)(2,1)S(1)}, bf16[16,896]{1,0:T(8,128)(2,1)S(1)}, u32[]{:S(2)}, u32[]{:S(2)}) collective-permute-start(bf16[16,896]{1,0:T(8,128)(2,1)S(1)} %sums.4.refs_0_), channel_id=1, source_target_pairs={{0,8},{1,9},{2,10},{3,11},{4,12},{5,13},{6,14},{7,15},{8,0},{9,1},... | collective-permute-start | bytes 86024 | tf_op jit(solution)/shard_map/ppermute | solution.py:197
  66.4 4.8 %collective-permute-start.30 = (bf16[16,896]{1,0:T(8,128)(2,1)S(1)}, bf16[16,896]{1,0:T(8,128)(2,1)S(1)}, u32[]{:S(2)}, u32[]{:S(2)}) collective-permute-start(bf16[16,896]{1,0:T(8,128)(2,1)S(1)} %sums.5.refs_0_), channel_id=1, source_target_pairs={{0,6},{1,7},{2,4},{3,5},{4,2},{5,3},{6,0},{7,1},{8,14},{9,15},{10,... | collective-permute-start | bytes 86024 | tf_op jit(solution)/shard_map/ppermute | solution.py:197
  67.9 3.9 %collective-permute-start.28 = (bf16[16,896]{1,0:T(8,128)(2,1)S(1)}, bf16[16,896]{1,0:T(8,128)(2,1)S(1)}, u32[]{:S(2)}, u32[]{:S(2)}) collective-permute-start(bf16[16,896]{1,0:T(8,128)(2,1)S(1)} %sums.5.refs_0_), channel_id=1, source_target_pairs={{0,4},{1,5},{2,6},{3,7},{4,0},{5,1},{6,2},{7,3},{8,12},{9,13},{10,... | collective-permute-start | bytes 86024 | tf_op jit(solution)/shard_map/ppermute | solution.py:197
  68.5 3.9 %collective-permute-start.26 = (bf16[16,896]{1,0:T(8,128)(2,1)S(1)}, bf16[16,896]{1,0:T(8,128)(2,1)S(1)}, u32[]{:S(2)}, u32[]{:S(2)}) collective-permute-start(bf16[16,896]{1,0:T(8,128)(2,1)S(1)} %sums.5.refs_0_), channel_id=1, source_target_pairs={{0,2},{1,3},{2,0},{3,1},{4,6},{5,7},{6,4},{7,5},{8,10},{9,11},{10,... | collective-permute-start | bytes 86024 | tf_op jit(solution)/shard_map/ppermute | solution.py:197
  70.0 2.4 %collective-permute-start.25 = (bf16[16,896]{1,0:T(8,128)(2,1)S(1)}, bf16[16,896]{1,0:T(8,128)(2,1)S(1)}, u32[]{:S(2)}, u32[]{:S(2)}) collective-permute-start(bf16[16,896]{1,0:T(8,128)(2,1)S(1)} %sums.5.refs_0_), channel_id=1, source_target_pairs={{0,1},{1,0},{2,3},{3,2},{4,5},{5,4},{6,7},{7,6},{8,9},{9,8},{10,11... | collective-permute-start | bytes 86024 | tf_op jit(solution)/shard_map/ppermute | solution.py:197
  71.3 1.2 %collective-permute-start.31 = (bf16[16,896]{1,0:T(8,128)(2,1)S(1)}, bf16[16,896]{1,0:T(8,128)(2,1)S(1)}, u32[]{:S(2)}, u32[]{:S(2)}) collective-permute-start(bf16[16,896]{1,0:T(8,128)(2,1)S(1)} %collective-permute-done.30.refs_6_), channel_id=1, source_target_pairs={{0,1},{1,0},{2,3},{3,2},{4,5},{5,4},{6,7},{7,6},{8,9},{9,8},{10,11... | collective-permute-start | bytes 86024 | tf_op jit(solution)/shard_map/ppermute | solution.py:197
  71.8 1.2 %collective-permute-start.29 = (bf16[16,896]{1,0:T(8,128)(2,1)S(1)}, bf16[16,896]{1,0:T(8,128)(2,1)S(1)}, u32[]{:S(2)}, u32[]{:S(2)}) collective-permute-start(bf16[16,896]{1,0:T(8,128)(2,1)S(1)} %collective-permute-done.28.refs_4_), channel_id=1, source_target_pairs={{0,1},{1,0},{2,3},{3,2},{4,5},{5,4},{6,7},{7,6},{8,9},{9,8},{10,11... | collective-permute-start | bytes 86024 | tf_op jit(solution)/shard_map/ppermute | solution.py:197
  72.4 1.2 %collective-permute-start.27 = (bf16[16,896]{1,0:T(8,128)(2,1)S(1)}, bf16[16,896]{1,0:T(8,128)(2,1)S(1)}, u32[]{:S(2)}, u32[]{:S(2)}) collective-permute-start(bf16[16,896]{1,0:T(8,128)(2,1)S(1)} %collective-permute-done.26.refs_2_), channel_id=1, source_target_pairs={{0,1},{1,0},{2,3},{3,2},{4,5},{5,4},{6,7},{7,6},{8,9},{9,8},{10,11... | collective-permute-start | bytes 86024 | tf_op jit(solution)/shard_map/ppermute | solution.py:197
  86.5 1.4 %collective-permute-start.32 = (bf16[4,4,16,224]{3,2,1,0:T(8,128)(2,1)S(1)}, bf16[4,4,16,224]{3,2,1,0:T(8,128)(2,1)S(1)}, u32[]{:S(2)}, u32[]{:S(2)}) collective-permute-start(bf16[4,4,16,224]{3,2,1,0:T(8,128)(2,1)S(1)} %get-tuple-element.77), channel_id=1, source_target_pairs={{0,1},{1,0},{2,3},{3,2},{4,5},{5,4},{6,7},{7,6},{8,9},{9,8},{10,11... | collective-permute-start | bytes 344072 | tf_op jit(solution)/shard_map/ppermute | solution.py:197

commit v6 on v5

--- a/solution.py
+++ b/solution.py
@@ -180,7 +180,8 @@
 SHAPE = (4, 2, 2, 2)
 CORE, Y, X, Z0, Z1 = 1, 2, 4, 8, 16
 HEADS_DEV = 4
-UNITS = 512
+UNITS = 256
+DOT_UNITS = 128
 STAT = 8
 LANES = 128
 PARENTS = REQ
@@ -604,15 +605,17 @@
     for d in range(count):
         x_held[d] = x[:, d * width:(d + 1) * width]
     residual[...] = x_held[linear]
-    gate = [lax.dot_general(normed, w_gate[part], NT, preferred_element_type=F32) for part in parts]
+    dots = [slice(u, u + DOT_UNITS) for u in range(0, units, DOT_UNITS)]
+    gate = [lax.dot_general(normed, w_gate[part], NT, preferred_element_type=F32) for part in dots]
     gate = [g / (1.0 + jnp.exp(-g)) * routed for g in gate]
     act = []
-    for k, part in enumerate(parts):
+    for g, part in zip(gate, dots):
         up = lax.dot_general(normed, w_up[part], NT, preferred_element_type=F32)
-        act.append((gate[k] * up).astype(BF))
+        act.append((g * up).astype(BF))
+    act = jnp.concatenate(act, axis=1)
     for k, part in enumerate(parts):
         downs[k].wait()
-        term = jnp.dot(act[k], w_down[part], preferred_element_type=F32)
+        term = jnp.dot(act[:, part], w_down[part], preferred_element_type=F32)
         if k == 0:
             acc[...] = term
         else:

time: 102 us -> 102 us (level)
  no operation moved by 1% of the time
where the time goes in v6:
time: 102 us
  Pallas kernels  32 us (31%)
  starting transfers between devices  28.7 us (28%)
  waiting for transfers between devices  26.4 us (26%)
  blocking collectives  12.9 us (13%)
  other arithmetic  1.38 us (1%)
    ppermute x33, starting transfers between devices, swap(): lax.ppermute(value, AXES, [(i, i ^ mask) for i in range(math.prod(SHAPE))])  28.7 us
    ppermute x33, waiting for transfers between devices, swap(): lax.ppermute(value, AXES, [(i, i ^ mask) for i in range(math.prod(SHAPE))])  26.4 us
    pallas_call x1, Pallas kernels, experts(): pl.pallas_call(experts_kernel, in_specs=[VMEM] * 14 + [HBM], out_specs=[V...  13.6 us
    all_to_all x1, blocking collectives, local(): lax.all_to_all(total, AXES[:3], split_axis=0, concat_axis=0, tiled=True)  12.9 us
    pallas_call x2, Pallas kernels, attend(): pl.pallas_call(partial(attend_kernel, scale, fetch), in_specs=[SMEM, spec...  12.3 us
    pallas_call x1, Pallas kernels, load(): pl.pallas_call(partial(load_kernel, count), in_specs=[HBM] * count + [pl....  3.41 us
  transfers between devices with their start and end apart: 33, of which 22 were waited for; matrix products, arithmetic and copies ran while one was open for 1% of the time, Pallas kernels for 16%

profile of v6, /device:TPU:0, one launch (start us, length us, event | category | flops | bytes accessed | tf_op | source)
XLA Modules:
  0.0 102.2 jit_solution(15261388667154442877)
XLA Ops:
  0.6 0.5 collective-permute-start.2
  1.1 2.6 %collective-permute-start = (bf16[16,32,512]{2,1,0:T(8,128)(2,1)}, bf16[16,32,512]{2,1,0:T(8,128)(2,1)S(1)}, u32[]{:S(2)}, u32[]{:S(2)}) collective-permute-start(bf16[16,32,512]{2,1,0:T(8,128)(2,1)} %ql0.1), channel_id=1, source_target_pairs={{0,2},{1,3},{2,0},{3,1},{4,6},{5,7},{6,4},{7,5},{8,10},{9,11},{10,... | collective-permute-start | bytes 1572872 | tf_op jit(solution)/shard_map/ppermute | solution.py:198
  3.9 0.7 pad_add_fusion.info
  4.7 0.6 collective-permute-done.3.qr1
  5.2 6.4 %attend.2 = (bf16[4,136,512]{2,1,0:T(8,128)(2,1)S(1)}, bf16[2,136,512]{2,1,0:T(8,128)(2,1)S(1)}, bf16[2,136,512]{2,1,0:T(8,128)(2,1)S(1)}) custom-call(s32[20]{0:T(128)S(1)} %pad_add_fusion.info, bf16[16,32,512]{2,1,0:T(8,128)(2,1)} %ql0.1, bf16[16,32,512]{2,1,0:T(8,128)(2,1)S(1)} %collective-permute-done.2.ql1, bf16[16,2048]{1,0:T(8,128)(2,1)} %qr0.1, ...), custom_call_target="tpu_custom_call" | custom-call | flops 1426063360 | bytes 8388608 | tf_op jit(solution)/shard_map/attend/pallas_call | solution.py:387
  11.8 0.3 collective-permute-start.5
  12.2 0.7 collective-permute-start.1
  12.9 0.4 collective-permute-done.4.refs_0_
  13.2 0.4 collective-permute-done.5.refs_1_
  14.0 3.9 %collective-permute-done.1.qr0 = bf16[16,2048]{1,0:T(8,128)(2,1)S(1)} collective-permute-done((bf16[16,2048]{1,0:T(8,128)(2,1)}, bf16[16,2048]{1,0:T(8,128)(2,1)S(1)}, u32[]{:S(2)}, u32[]{:S(2)}) %collective-permute-start.1) | collective-permute-done | bytes 65568 | tf_op jit(solution)/shard_map/ppermute | solution.py:198
  17.9 1.8 %collective-permute-start.8 = (bf16[2,136,512]{2,1,0:T(8,128)(2,1)S(1)}, bf16[2,136,512]{2,1,0:T(8,128)(2,1)S(1)}, u32[]{:S(2)}, u32[]{:S(2)}) collective-permute-start(bf16[2,136,512]{2,1,0:T(8,128)(2,1)S(1)} %get-tuple-element.51), channel_id=1, source_target_pairs={{0,4},{1,5},{2,6},{3,7},{4,0},{5,1},{6,2},{7,3},{8,12},{9,13},{10,... | collective-permute-start | bytes 835592 | tf_op jit(solution)/shard_map/ppermute | solution.py:198
  19.8 1.1 %collective-permute-done.7.qr1 = bf16[16,2048]{1,0:T(8,128)(2,1)S(1)} collective-permute-done((bf16[16,2048]{1,0:T(8,128)(2,1)S(1)}, bf16[16,2048]{1,0:T(8,128)(2,1)S(1)}, u32[]{:S(2)}, u32[]{:S(2)}) %collective-permute-start.7) | collective-permute-done | bytes 65568 | tf_op jit(solution)/shard_map/ppermute | solution.py:198
  20.9 5.9 %attend.3 = (bf16[4,136,512]{2,1,0:T(8,128)(2,1)S(1)}, bf16[2,136,512]{2,1,0:T(8,128)(2,1)S(1)}, bf16[2,136,512]{2,1,0:T(8,128)(2,1)S(1)}) custom-call(s32[20]{0:T(128)S(1)} %pad_add_fusion.info, bf16[16,32,512]{2,1,0:T(8,128)(2,1)S(1)} %collective-permute-done.ql0, bf16[16,32,512]{2,1,0:T(8,128)(2,1)S(1)} %collective-permute-done.6.ql1, ...), custom_call_target="tpu_custom_call" | custom-call | flops 1426063360 | bytes 8388608 | tf_op jit(solution)/shard_map/attend/pallas_call | solution.py:387
  27.1 0.3 collective-permute-start.10
  27.7 1.8 %collective-permute-start.13 = (bf16[1,136,512]{2,1,0:T(8,128)(2,1)S(1)}, bf16[1,136,512]{2,1,0:T(8,128)(2,1)S(1)}, u32[]{:S(2)}, u32[]{:S(2)}) collective-permute-start(bf16[1,136,512]{2,1,0:T(8,128)(2,1)S(1)} %get-tuple-element.59), channel_id=1, source_target_pairs={{0,2},{1,3},{2,0},{3,1},{4,6},{5,7},{6,4},{7,5},{8,10},{9,11},{10,... | collective-permute-start | bytes 417800 | tf_op jit(solution)/shard_map/ppermute | solution.py:198
  29.8 1.2 %collective-permute-start.11 = (bf16[1,136,512]{2,1,0:T(8,128)(2,1)S(1)}, bf16[1,136,512]{2,1,0:T(8,128)(2,1)S(1)}, u32[]{:S(2)}, u32[]{:S(2)}) collective-permute-start(bf16[1,136,512]{2,1,0:T(8,128)(2,1)S(1)} %get-tuple-element.57), channel_id=1, source_target_pairs={{0,2},{1,3},{2,0},{3,1},{4,6},{5,7},{6,4},{7,5},{8,10},{9,11},{10,... | collective-permute-start | bytes 417800 | tf_op jit(solution)/shard_map/ppermute | solution.py:198
  31.1 1.8 %collective-permute-start.12 = (bf16[1,136,512]{2,1,0:T(8,128)(2,1)S(1)}, bf16[1,136,512]{2,1,0:T(8,128)(2,1)S(1)}, u32[]{:S(2)}, u32[]{:S(2)}) collective-permute-start(bf16[1,136,512]{2,1,0:T(8,128)(2,1)S(1)} %get-tuple-element.58), channel_id=1, source_target_pairs={{0,6},{1,7},{2,4},{3,5},{4,2},{5,3},{6,0},{7,1},{8,14},{9,15},{10,... | collective-permute-start | bytes 417800 | tf_op jit(solution)/shard_map/ppermute | solution.py:198
  32.8 0.5 collective-permute-start.14
  33.4 2.2 %collective-permute-done.13.refs_3_ = bf16[1,136,512]{2,1,0:T(8,128)(2,1)S(1)} collective-permute-done((bf16[1,136,512]{2,1,0:T(8,128)(2,1)S(1)}, bf16[1,136,512]{2,1,0:T(8,128)(2,1)S(1)}, u32[]{:S(2)}, u32[]{:S(2)}) %collective-permute-start.13) | collective-permute-done | bytes 139296 | tf_op jit(solution)/shard_map/ppermute | solution.py:198
  35.6 3.8 %collective-permute-done.11.refs_1_ = bf16[1,136,512]{2,1,0:T(8,128)(2,1)S(1)} collective-permute-done((bf16[1,136,512]{2,1,0:T(8,128)(2,1)S(1)}, bf16[1,136,512]{2,1,0:T(8,128)(2,1)S(1)}, u32[]{:S(2)}, u32[]{:S(2)}) %collective-permute-start.11) | collective-permute-done | bytes 139296 | tf_op jit(solution)/shard_map/ppermute | solution.py:198
  39.8 3.7 %collective-permute-start.15 = (bf16[72,512]{1,0:T(8,128)(2,1)S(1)}, bf16[72,512]{1,0:T(8,128)(2,1)S(1)}, u32[]{:S(2)}, u32[]{:S(2)}) collective-permute-start(bf16[72,512]{1,0:T(8,128)(2,1)S(1)} %get-tuple-element.63), channel_id=1, source_target_pairs={{0,24},{1,25},{2,26},{3,27},{4,28},{5,29},{6,30},{7,31},{8,16},{9,... | collective-permute-start | bytes 221192 | tf_op jit(solution)/shard_map/ppermute | solution.py:198
  43.5 0.7 collective-permute-start.17
  44.3 3.4 %load.1 = (bf16[512,512]{1,0:T(8,128)(2,1)S(1)}, bf16[512,7168]{1,0:T(8,128)(2,1)S(1)}) custom-call(bf16[512,512]{1,0:T(8,128)(2,1)} %refs_0_.1, bf16[512,7168]{1,0:T(8,128)(2,1)} %refs_1_.1, bf16[72,512]{1,0:T(8,128)(2,1)S(1)} %get-tuple-element.62.refs_2_.p0), custom_call_target="tpu_custom_call" | custom-call | bytes 7864320 | tf_op jit(solution)/shard_map/load/pallas_call | solution.py:569
  47.7 1.6 %collective-permute-done.16.p2 = bf16[72,512]{1,0:T(8,128)(2,1)S(1)} collective-permute-done((bf16[72,512]{1,0:T(8,128)(2,1)S(1)}, bf16[72,512]{1,0:T(8,128)(2,1)S(1)}, u32[]{:S(2)}, u32[]{:S(2)}) %collective-permute-start.16) | collective-permute-done | bytes 73760 | tf_op jit(solution)/shard_map/ppermute | solution.py:198
  49.3 1.4 %project.1 = (bf16[4,16,896]{2,1,0:T(8,128)(2,1)S(1)}, bf16[4,16,896]{2,1,0:T(8,128)(2,1)S(1)}) custom-call(bf16[72,512]{1,0:T(8,128)(2,1)S(1)} %get-tuple-element.62.refs_2_.p0, bf16[72,512]{1,0:T(8,128)(2,1)S(1)} %collective-permute-done.15.p1, bf16[72,512]{1,0:T(8,128)(2,1)S(1)} %collective-permute-done.16.p2, ...), custom_call_target="tpu_custom_call" | custom-call | flops 117440512 | bytes 7340032 | tf_op jit(solution)/shard_map/project/pallas_call | solution.py:526
  50.8 1.3 %collective-permute-done.18.refs_1_ = bf16[4,16,896]{2,1,0:T(8,128)(2,1)S(1)} collective-permute-done((bf16[4,16,896]{2,1,0:T(8,128)(2,1)S(1)}, bf16[4,16,896]{2,1,0:T(8,128)(2,1)S(1)}, u32[]{:S(2)}, u32[]{:S(2)}) %collective-permute-start.18) | collective-permute-done | bytes 114720 | tf_op jit(solution)/shard_map/ppermute | solution.py:198
  52.1 2.5 %collective-permute-start.19 = (bf16[16,896]{1,0:T(8,128)(2,1)S(1)}, bf16[16,896]{1,0:T(8,128)(2,1)S(1)}, u32[]{:S(2)}, u32[]{:S(2)}) collective-permute-start(bf16[16,896]{1,0:T(8,128)(2,1)S(1)} %get-tuple-element.71), channel_id=1, source_target_pairs={{0,6},{1,7},{2,4},{3,5},{4,2},{5,3},{6,0},{7,1},{8,14},{9,15},{10,... | collective-permute-start | bytes 86024 | tf_op jit(solution)/shard_map/ppermute | solution.py:198
  54.6 0.5 collective-permute-start.20
  55.2 0.5 collective-permute-start.21
  55.7 1.3 %collective-permute-done.19.refs_1_ = bf16[16,896]{1,0:T(8,128)(2,1)S(1)} collective-permute-done((bf16[16,896]{1,0:T(8,128)(2,1)S(1)}, bf16[16,896]{1,0:T(8,128)(2,1)S(1)}, u32[]{:S(2)}, u32[]{:S(2)}) %collective-permute-start.19) | collective-permute-done | bytes 28704 | tf_op jit(solution)/shard_map/ppermute | solution.py:198
  57.0 1.5 %collective-permute-done.20.refs_2_ = bf16[16,896]{1,0:T(8,128)(2,1)S(1)} collective-permute-done((bf16[16,896]{1,0:T(8,128)(2,1)S(1)}, bf16[16,896]{1,0:T(8,128)(2,1)S(1)}, u32[]{:S(2)}, u32[]{:S(2)}) %collective-permute-start.20) | collective-permute-done | bytes 28704 | tf_op jit(solution)/shard_map/ppermute | solution.py:198
  58.5 0.5 collective-permute-done.21.refs_3_
  59.1 2.6 %collective-permute-start.24 = (bf16[16,896]{1,0:T(8,128)(2,1)S(1)}, bf16[16,896]{1,0:T(8,128)(2,1)S(1)}, u32[]{:S(2)}, u32[]{:S(2)}) collective-permute-start(bf16[16,896]{1,0:T(8,128)(2,1)S(1)} %sums.4.refs_0_), channel_id=1, source_target_pairs={{0,24},{1,25},{2,26},{3,27},{4,28},{5,29},{6,30},{7,31},{8,16},{9,... | collective-permute-start | bytes 86024 | tf_op jit(solution)/shard_map/ppermute | solution.py:198
  61.6 1.9 %collective-permute-start.22 = (bf16[16,896]{1,0:T(8,128)(2,1)S(1)}, bf16[16,896]{1,0:T(8,128)(2,1)S(1)}, u32[]{:S(2)}, u32[]{:S(2)}) collective-permute-start(bf16[16,896]{1,0:T(8,128)(2,1)S(1)} %sums.4.refs_0_), channel_id=1, source_target_pairs={{0,8},{1,9},{2,10},{3,11},{4,12},{5,13},{6,14},{7,15},{8,0},{9,1},... | collective-permute-start | bytes 86024 | tf_op jit(solution)/shard_map/ppermute | solution.py:198
  63.5 1.6 %collective-permute-done.24.refs_3_ = bf16[16,896]{1,0:T(8,128)(2,1)S(1)} collective-permute-done((bf16[16,896]{1,0:T(8,128)(2,1)S(1)}, bf16[16,896]{1,0:T(8,128)(2,1)S(1)}, u32[]{:S(2)}, u32[]{:S(2)}) %collective-permute-start.24) | collective-permute-done | bytes 28704 | tf_op jit(solution)/shard_map/ppermute | solution.py:198
  65.1 1.3 %collective-permute-done.23.refs_2_ = bf16[16,896]{1,0:T(8,128)(2,1)S(1)} collective-permute-done((bf16[16,896]{1,0:T(8,128)(2,1)S(1)}, bf16[16,896]{1,0:T(8,128)(2,1)S(1)}, u32[]{:S(2)}, u32[]{:S(2)}) %collective-permute-start.23) | collective-permute-done | bytes 28704 | tf_op jit(solution)/shard_map/ppermute | solution.py:198
  66.4 1.5 %collective-permute-start.30 = (bf16[16,896]{1,0:T(8,128)(2,1)S(1)}, bf16[16,896]{1,0:T(8,128)(2,1)S(1)}, u32[]{:S(2)}, u32[]{:S(2)}) collective-permute-start(bf16[16,896]{1,0:T(8,128)(2,1)S(1)} %sums.5.refs_0_), channel_id=1, source_target_pairs={{0,6},{1,7},{2,4},{3,5},{4,2},{5,3},{6,0},{7,1},{8,14},{9,15},{10,... | collective-permute-start | bytes 86024 | tf_op jit(solution)/shard_map/ppermute | solution.py:198
  67.9 0.6 collective-permute-start.28
  68.5 1.5 %collective-permute-start.26 = (bf16[16,896]{1,0:T(8,128)(2,1)S(1)}, bf16[16,896]{1,0:T(8,128)(2,1)S(1)}, u32[]{:S(2)}, u32[]{:S(2)}) collective-permute-start(bf16[16,896]{1,0:T(8,128)(2,1)S(1)} %sums.5.refs_0_), channel_id=1, source_target_pairs={{0,2},{1,3},{2,0},{3,1},{4,6},{5,7},{6,4},{7,5},{8,10},{9,11},{10,... | collective-permute-start | bytes 86024 | tf_op jit(solution)/shard_map/ppermute | solution.py:198
  70.0 1.3 %collective-permute-done.30.refs_6_ = bf16[16,896]{1,0:T(8,128)(2,1)S(1)} collective-permute-done((bf16[16,896]{1,0:T(8,128)(2,1)S(1)}, bf16[16,896]{1,0:T(8,128)(2,1)S(1)}, u32[]{:S(2)}, u32[]{:S(2)}) %collective-permute-start.30) | collective-permute-done | bytes 28704 | tf_op jit(solution)/shard_map/ppermute | solution.py:198
  71.3 0.5 collective-permute-done.28.refs_4_
  71.8 0.6 collective-permute-done.26.refs_2_
  72.5 0.5 collective-permute-done.29.refs_5_
  73.0 0.6 collective-permute-done.27.refs_3_
  73.6 13.6 %experts.1 = (bf16[16,7168]{1,0:T(8,128)(2,1)}, bf16[4,4,16,224]{3,2,1,0:T(8,128)(2,1)S(1)}, bf16[4,4,16,224]{3,2,1,0:T(8,128)(2,1)S(1)}, f32[16,224]{1,0:T(8,128)S(1)}) custom-call(bf16[16,896]{1,0:T(8,128)(2,1)S(1)} %sums.5.refs_0_, bf16[16,896]{1,0:T(8,128)(2,1)S(1)} %collective-permute-done.25.refs_1_, ...), custom_call_target="tpu_custom_call" | custom-call | flops 704643072 | bytes 44040192 | tf_op jit(solution)/shard_map/experts/pallas_call | solution.py:636
  87.4 1.2 %collective-permute-done.32.b = bf16[4,4,16,224]{3,2,1,0:T(8,128)(2,1)S(1)} collective-permute-done((bf16[4,4,16,224]{3,2,1,0:T(8,128)(2,1)S(1)}, bf16[4,4,16,224]{3,2,1,0:T(8,128)(2,1)S(1)}, u32[]{:S(2)}, u32[]{:S(2)}) %collective-permute-start.32) | collective-permute-done | bytes 114720 | tf_op jit(solution)/shard_map/ppermute | solution.py:198
  88.7 12.9 %all_to_all.5 = bf16[16,16,224]{2,1,0:T(8,128)(2,1)S(1)} all-to-all(bf16[16,16,224]{2,1,0:T(8,128)(2,1)S(1)} %core_sum.1), channel_id=1, replica_groups=mesh['z'=4,'x'=2,'y'=2,'core'=2] {'z','x','y'}, dimensions={0} | all-to-all | bytes 229376 | tf_op jit(solution)/shard_map/all_to_all | solution.py:708
  101.5 0.6 add_convert_fusion
  (54 shorter events, 2.6 us)
Async XLA Ops:
  0.6 4.6 %collective-permute-start.2 = (bf16[16,32,512]{2,1,0:T(8,128)(2,1)}, bf16[16,32,512]{2,1,0:T(8,128)(2,1)S(1)}, u32[]{:S(2)}, u32[]{:S(2)}) collective-permute-start(bf16[16,32,512]{2,1,0:T(8,128)(2,1)} %ql0.1), channel_id=1, source_target_pairs={{0,1},{1,0},{2,3},{3,2},{4,5},{5,4},{6,7},{7,6},{8,9},{9,8},{10,11... | collective-permute-start | bytes 1572872 | tf_op jit(solution)/shard_map/ppermute | solution.py:198
  1.1 16.7 %collective-permute-start = (bf16[16,32,512]{2,1,0:T(8,128)(2,1)}, bf16[16,32,512]{2,1,0:T(8,128)(2,1)S(1)}, u32[]{:S(2)}, u32[]{:S(2)}) collective-permute-start(bf16[16,32,512]{2,1,0:T(8,128)(2,1)} %ql0.1), channel_id=1, source_target_pairs={{0,2},{1,3},{2,0},{3,1},{4,6},{5,7},{6,4},{7,5},{8,10},{9,11},{10,... | collective-permute-start | bytes 1572872 | tf_op jit(solution)/shard_map/ppermute | solution.py:198
  3.7 1.5 %collective-permute-start.3 = (bf16[16,2048]{1,0:T(8,128)(2,1)}, bf16[16,2048]{1,0:T(8,128)(2,1)S(1)}, u32[]{:S(2)}, u32[]{:S(2)}) collective-permute-start(bf16[16,2048]{1,0:T(8,128)(2,1)} %qr0.1), channel_id=1, source_target_pairs={{0,1},{1,0},{2,3},{3,2},{4,5},{5,4},{6,7},{7,6},{8,9},{9,8},{10,11... | collective-permute-start | bytes 196616 | tf_op jit(solution)/shard_map/ppermute | solution.py:198
  5.2 68.4 %slice-start = ((s8[14680064]{0:T(1024)(128)(4,1)}), s8[4194304]{0:T(1024)(128)(4,1)S(1)}, s32[]{:S(2)}) async-start(s8[14680064]{0:T(1024)(128)(4,1)} %bitcast.3), calls=%async_computation.1 | async-start | bytes 8388608
  11.6 1.6 %collective-permute-start.4 = (bf16[2,136,512]{2,1,0:T(8,128)(2,1)S(1)}, bf16[2,136,512]{2,1,0:T(8,128)(2,1)S(1)}, u32[]{:S(2)}, u32[]{:S(2)}) collective-permute-start(bf16[2,136,512]{2,1,0:T(8,128)(2,1)S(1)} %get-tuple-element.41), channel_id=1, source_target_pairs={{0,1},{1,0},{2,3},{3,2},{4,5},{5,4},{6,7},{7,6},{8,9},{9,8},{10,11... | collective-permute-start | bytes 835592 | tf_op jit(solution)/shard_map/ppermute | solution.py:198
  11.8 1.8 %collective-permute-start.5 = (bf16[2,136,512]{2,1,0:T(8,128)(2,1)S(1)}, bf16[2,136,512]{2,1,0:T(8,128)(2,1)S(1)}, u32[]{:S(2)}, u32[]{:S(2)}) collective-permute-start(bf16[2,136,512]{2,1,0:T(8,128)(2,1)S(1)} %get-tuple-element.42), channel_id=1, source_target_pairs={{0,1},{1,0},{2,3},{3,2},{4,5},{5,4},{6,7},{7,6},{8,9},{9,8},{10,11... | collective-permute-start | bytes 835592 | tf_op jit(solution)/shard_map/ppermute | solution.py:198
  12.2 5.7 %collective-permute-start.1 = (bf16[16,2048]{1,0:T(8,128)(2,1)}, bf16[16,2048]{1,0:T(8,128)(2,1)S(1)}, u32[]{:S(2)}, u32[]{:S(2)}) collective-permute-start(bf16[16,2048]{1,0:T(8,128)(2,1)} %qr0.1), channel_id=1, source_target_pairs={{0,2},{1,3},{2,0},{3,1},{4,6},{5,7},{6,4},{7,5},{8,10},{9,11},{10,... | collective-permute-start | bytes 196616 | tf_op jit(solution)/shard_map/ppermute | solution.py:198
  13.6 59.9 %copy-start = (bf16[1024,7168]{1,0:T(8,128)(2,1)S(1)}, bf16[1024,7168]{1,0:T(8,128)(2,1)}, u32[]{:S(2)}) copy-start(bf16[1024,7168]{1,0:T(8,128)(2,1)} %refs_13_.1) | copy-start | bytes 44040196
  17.9 55.7 %slice-start.1 = ((s8[14680064]{0:T(1024)(128)(4,1)}), s8[4194304]{0:T(1024)(128)(4,1)S(1)}, s32[]{:S(2)}) async-start(s8[14680064]{0:T(1024)(128)(4,1)} %bitcast.3), calls=%async_computation.2 | async-start | bytes 8388608
  17.9 3.1 %collective-permute-start.6 = (bf16[16,32,512]{2,1,0:T(8,128)(2,1)S(1)}, bf16[16,32,512]{2,1,0:T(8,128)(2,1)S(1)}, u32[]{:S(2)}, u32[]{:S(2)}) collective-permute-start(bf16[16,32,512]{2,1,0:T(8,128)(2,1)S(1)} %collective-permute-done.ql0), channel_id=1, source_target_pairs={{0,1},{1,0},{2,3},{3,2},{4,5},{5,4},{6,7},{7,6},{8,9},{9,8},{10,11... | collective-permute-start | bytes 1572872 | tf_op jit(solution)/shard_map/ppermute | solution.py:198
  17.9 9.1 %collective-permute-start.8 = (bf16[2,136,512]{2,1,0:T(8,128)(2,1)S(1)}, bf16[2,136,512]{2,1,0:T(8,128)(2,1)S(1)}, u32[]{:S(2)}, u32[]{:S(2)}) collective-permute-start(bf16[2,136,512]{2,1,0:T(8,128)(2,1)S(1)} %get-tuple-element.51), channel_id=1, source_target_pairs={{0,4},{1,5},{2,6},{3,7},{4,0},{5,1},{6,2},{7,3},{8,12},{9,13},{10,... | collective-permute-start | bytes 835592 | tf_op jit(solution)/shard_map/ppermute | solution.py:198
  19.7 1.3 %collective-permute-start.7 = (bf16[16,2048]{1,0:T(8,128)(2,1)S(1)}, bf16[16,2048]{1,0:T(8,128)(2,1)S(1)}, u32[]{:S(2)}, u32[]{:S(2)}) collective-permute-start(bf16[16,2048]{1,0:T(8,128)(2,1)S(1)} %collective-permute-done.1.qr0), channel_id=1, source_target_pairs={{0,1},{1,0},{2,3},{3,2},{4,5},{5,4},{6,7},{7,6},{8,9},{9,8},{10,11... | collective-permute-start | bytes 196616 | tf_op jit(solution)/shard_map/ppermute | solution.py:198
  27.0 2.5 %collective-permute-start.9 = (bf16[2,136,512]{2,1,0:T(8,128)(2,1)S(1)}, bf16[2,136,512]{2,1,0:T(8,128)(2,1)S(1)}, u32[]{:S(2)}, u32[]{:S(2)}) collective-permute-start(bf16[2,136,512]{2,1,0:T(8,128)(2,1)S(1)} %get-tuple-element.55), channel_id=1, source_target_pairs={{0,1},{1,0},{2,3},{3,2},{4,5},{5,4},{6,7},{7,6},{8,9},{9,8},{10,11... | collective-permute-start | bytes 835592 | tf_op jit(solution)/shard_map/ppermute | solution.py:198
  27.1 2.4 %collective-permute-start.10 = (bf16[2,136,512]{2,1,0:T(8,128)(2,1)S(1)}, bf16[2,136,512]{2,1,0:T(8,128)(2,1)S(1)}, u32[]{:S(2)}, u32[]{:S(2)}) collective-permute-start(bf16[2,136,512]{2,1,0:T(8,128)(2,1)S(1)} %get-tuple-element.56), channel_id=1, source_target_pairs={{0,1},{1,0},{2,3},{3,2},{4,5},{5,4},{6,7},{7,6},{8,9},{9,8},{10,11... | collective-permute-start | bytes 835592 | tf_op jit(solution)/shard_map/ppermute | solution.py:198
  27.7 7.9 %collective-permute-start.13 = (bf16[1,136,512]{2,1,0:T(8,128)(2,1)S(1)}, bf16[1,136,512]{2,1,0:T(8,128)(2,1)S(1)}, u32[]{:S(2)}, u32[]{:S(2)}) collective-permute-start(bf16[1,136,512]{2,1,0:T(8,128)(2,1)S(1)} %get-tuple-element.59), channel_id=1, source_target_pairs={{0,2},{1,3},{2,0},{3,1},{4,6},{5,7},{6,4},{7,5},{8,10},{9,11},{10,... | collective-permute-start | bytes 417800 | tf_op jit(solution)/shard_map/ppermute | solution.py:198
  29.8 9.6 %collective-permute-start.11 = (bf16[1,136,512]{2,1,0:T(8,128)(2,1)S(1)}, bf16[1,136,512]{2,1,0:T(8,128)(2,1)S(1)}, u32[]{:S(2)}, u32[]{:S(2)}) collective-permute-start(bf16[1,136,512]{2,1,0:T(8,128)(2,1)S(1)} %get-tuple-element.57), channel_id=1, source_target_pairs={{0,2},{1,3},{2,0},{3,1},{4,6},{5,7},{6,4},{7,5},{8,10},{9,11},{10,... | collective-permute-start | bytes 417800 | tf_op jit(solution)/shard_map/ppermute | solution.py:198
  31.1 8.4 %collective-permute-start.12 = (bf16[1,136,512]{2,1,0:T(8,128)(2,1)S(1)}, bf16[1,136,512]{2,1,0:T(8,128)(2,1)S(1)}, u32[]{:S(2)}, u32[]{:S(2)}) collective-permute-start(bf16[1,136,512]{2,1,0:T(8,128)(2,1)S(1)} %get-tuple-element.58), channel_id=1, source_target_pairs={{0,6},{1,7},{2,4},{3,5},{4,2},{5,3},{6,0},{7,1},{8,14},{9,15},{10,... | collective-permute-start | bytes 417800 | tf_op jit(solution)/shard_map/ppermute | solution.py:198
  32.8 6.6 %collective-permute-start.14 = (bf16[1,136,512]{2,1,0:T(8,128)(2,1)S(1)}, bf16[1,136,512]{2,1,0:T(8,128)(2,1)S(1)}, u32[]{:S(2)}, u32[]{:S(2)}) collective-permute-start(bf16[1,136,512]{2,1,0:T(8,128)(2,1)S(1)} %get-tuple-element.61), channel_id=1, source_target_pairs={{0,4},{1,5},{2,6},{3,7},{4,0},{5,1},{6,2},{7,3},{8,12},{9,13},{10,... | collective-permute-start | bytes 417800 | tf_op jit(solution)/shard_map/ppermute | solution.py:198
  39.8 7.9 %collective-permute-start.15 = (bf16[72,512]{1,0:T(8,128)(2,1)S(1)}, bf16[72,512]{1,0:T(8,128)(2,1)S(1)}, u32[]{:S(2)}, u32[]{:S(2)}) collective-permute-start(bf16[72,512]{1,0:T(8,128)(2,1)S(1)} %get-tuple-element.63), channel_id=1, source_target_pairs={{0,24},{1,25},{2,26},{3,27},{4,28},{5,29},{6,30},{7,31},{8,16},{9,... | collective-permute-start | bytes 221192 | tf_op jit(solution)/shard_map/ppermute | solution.py:198
  43.5 5.7 %collective-permute-start.16 = (bf16[72,512]{1,0:T(8,128)(2,1)S(1)}, bf16[72,512]{1,0:T(8,128)(2,1)S(1)}, u32[]{:S(2)}, u32[]{:S(2)}) collective-permute-start(bf16[72,512]{1,0:T(8,128)(2,1)S(1)} %get-tuple-element.64), channel_id=1, source_target_pairs={{0,16},{1,17},{2,18},{3,19},{4,20},{5,21},{6,22},{7,23},{8,24},{9,... | collective-permute-start | bytes 221192 | tf_op jit(solution)/shard_map/ppermute | solution.py:198
  43.5 5.7 %collective-permute-start.17 = (bf16[72,512]{1,0:T(8,128)(2,1)S(1)}, bf16[72,512]{1,0:T(8,128)(2,1)S(1)}, u32[]{:S(2)}, u32[]{:S(2)}) collective-permute-start(bf16[72,512]{1,0:T(8,128)(2,1)S(1)} %get-tuple-element.65), channel_id=1, source_target_pairs={{0,8},{1,9},{2,10},{3,11},{4,12},{5,13},{6,14},{7,15},{8,0},{9,1},... | collective-permute-start | bytes 221192 | tf_op jit(solution)/shard_map/ppermute | solution.py:198
  44.3 29.3 %slice-start.2 = ((s8[14680064]{0:T(1024)(128)(4,1)}), s8[4194304]{0:T(1024)(128)(4,1)S(1)}, s32[]{:S(2)}) async-start(s8[14680064]{0:T(1024)(128)(4,1)} %bitcast.3), calls=%async_computation.3 | async-start | bytes 8388608
  44.3 29.3 %copy-start.1 = (bf16[16,7168]{1,0:T(8,128)(2,1)S(1)}, bf16[16,7168]{1,0:T(8,128)(2,1)}, u32[]{:S(2)}) copy-start(bf16[16,7168]{1,0:T(8,128)(2,1)} %refs_8_.1) | copy-start | bytes 688132
  44.3 29.3 %copy-start.2 = (f32[7168]{0:T(1024)S(1)}, f32[7168]{0:T(1024)}, u32[]{:S(2)}) copy-start(f32[7168]{0:T(1024)} %param.28) | copy-start | bytes 86020
  44.3 29.3 %copy-start.3 = (s32[16,8]{0,1:T(8,128)S(1)}, s32[16,8]{0,1:T(8,128)}, u32[]{:S(2)}) copy-start(s32[16,8]{0,1:T(8,128)} %param.32) | copy-start | bytes 1540
  44.3 29.3 %copy-start.4 = (f32[16,8]{0,1:T(8,128)S(1)}, f32[16,8]{0,1:T(8,128)}, u32[]{:S(2)}) copy-start(f32[16,8]{0,1:T(8,128)} %param.33) | copy-start | bytes 1540
  49.3 24.4 %slice-start.3 = ((s8[14680064]{0:T(1024)(128)(4,1)}), s8[2097152]{0:T(1024)(128)(4,1)S(1)}, s32[]{:S(2)}) async-start(s8[14680064]{0:T(1024)(128)(4,1)} %bitcast.3), calls=%async_computation.4 | async-start | bytes 4194304
  50.7 1.4 %collective-permute-start.18 = (bf16[4,16,896]{2,1,0:T(8,128)(2,1)S(1)}, bf16[4,16,896]{2,1,0:T(8,128)(2,1)S(1)}, u32[]{:S(2)}, u32[]{:S(2)}) collective-permute-start(bf16[4,16,896]{2,1,0:T(8,128)(2,1)S(1)} %get-tuple-element.69), channel_id=1, source_target_pairs={{0,1},{1,0},{2,3},{3,2},{4,5},{5,4},{6,7},{7,6},{8,9},{9,8},{10,11... | collective-permute-start | bytes 344072 | tf_op jit(solution)/shard_map/ppermute | solution.py:198
  52.1 4.8 %collective-permute-start.19 = (bf16[16,896]{1,0:T(8,128)(2,1)S(1)}, bf16[16,896]{1,0:T(8,128)(2,1)S(1)}, u32[]{:S(2)}, u32[]{:S(2)}) collective-permute-start(bf16[16,896]{1,0:T(8,128)(2,1)S(1)} %get-tuple-element.71), channel_id=1, source_target_pairs={{0,6},{1,7},{2,4},{3,5},{4,2},{5,3},{6,0},{7,1},{8,14},{9,15},{10,... | collective-permute-start | bytes 86024 | tf_op jit(solution)/shard_map/ppermute | solution.py:198
  54.6 3.9 %collective-permute-start.20 = (bf16[16,896]{1,0:T(8,128)(2,1)S(1)}, bf16[16,896]{1,0:T(8,128)(2,1)S(1)}, u32[]{:S(2)}, u32[]{:S(2)}) collective-permute-start(bf16[16,896]{1,0:T(8,128)(2,1)S(1)} %get-tuple-element.72), channel_id=1, source_target_pairs={{0,4},{1,5},{2,6},{3,7},{4,0},{5,1},{6,2},{7,3},{8,12},{9,13},{10,... | collective-permute-start | bytes 86024 | tf_op jit(solution)/shard_map/ppermute | solution.py:198
  55.2 3.9 %collective-permute-start.21 = (bf16[16,896]{1,0:T(8,128)(2,1)S(1)}, bf16[16,896]{1,0:T(8,128)(2,1)S(1)}, u32[]{:S(2)}, u32[]{:S(2)}) collective-permute-start(bf16[16,896]{1,0:T(8,128)(2,1)S(1)} %get-tuple-element.73), channel_id=1, source_target_pairs={{0,2},{1,3},{2,0},{3,1},{4,6},{5,7},{6,4},{7,5},{8,10},{9,11},{10,... | collective-permute-start | bytes 86024 | tf_op jit(solution)/shard_map/ppermute | solution.py:198
  59.1 6.0 %collective-permute-start.24 = (bf16[16,896]{1,0:T(8,128)(2,1)S(1)}, bf16[16,896]{1,0:T(8,128)(2,1)S(1)}, u32[]{:S(2)}, u32[]{:S(2)}) collective-permute-start(bf16[16,896]{1,0:T(8,128)(2,1)S(1)} %sums.4.refs_0_), channel_id=1, source_target_pairs={{0,24},{1,25},{2,26},{3,27},{4,28},{5,29},{6,30},{7,31},{8,16},{9,... | collective-permute-start | bytes 86024 | tf_op jit(solution)/shard_map/ppermute | solution.py:198
  61.6 4.8 %collective-permute-start.23 = (bf16[16,896]{1,0:T(8,128)(2,1)S(1)}, bf16[16,896]{1,0:T(8,128)(2,1)S(1)}, u32[]{:S(2)}, u32[]{:S(2)}) collective-permute-start(bf16[16,896]{1,0:T(8,128)(2,1)S(1)} %sums.4.refs_0_), channel_id=1, source_target_pairs={{0,16},{1,17},{2,18},{3,19},{4,20},{5,21},{6,22},{7,23},{8,24},{9,... | collective-permute-start | bytes 86024 | tf_op jit(solution)/shard_map/ppermute | solution.py:198
  61.6 4.8 %collective-permute-start.22 = (bf16[16,896]{1,0:T(8,128)(2,1)S(1)}, bf16[16,896]{1,0:T(8,128)(2,1)S(1)}, u32[]{:S(2)}, u32[]{:S(2)}) collective-permute-start(bf16[16,896]{1,0:T(8,128)(2,1)S(1)} %sums.4.refs_0_), channel_id=1, source_target_pairs={{0,8},{1,9},{2,10},{3,11},{4,12},{5,13},{6,14},{7,15},{8,0},{9,1},... | collective-permute-start | bytes 86024 | tf_op jit(solution)/shard_map/ppermute | solution.py:198
  66.4 4.8 %collective-permute-start.30 = (bf16[16,896]{1,0:T(8,128)(2,1)S(1)}, bf16[16,896]{1,0:T(8,128)(2,1)S(1)}, u32[]{:S(2)}, u32[]{:S(2)}) collective-permute-start(bf16[16,896]{1,0:T(8,128)(2,1)S(1)} %sums.5.refs_0_), channel_id=1, source_target_pairs={{0,6},{1,7},{2,4},{3,5},{4,2},{5,3},{6,0},{7,1},{8,14},{9,15},{10,... | collective-permute-start | bytes 86024 | tf_op jit(solution)/shard_map/ppermute | solution.py:198
  67.9 3.9 %collective-permute-start.28 = (bf16[16,896]{1,0:T(8,128)(2,1)S(1)}, bf16[16,896]{1,0:T(8,128)(2,1)S(1)}, u32[]{:S(2)}, u32[]{:S(2)}) collective-permute-start(bf16[16,896]{1,0:T(8,128)(2,1)S(1)} %sums.5.refs_0_), channel_id=1, source_target_pairs={{0,4},{1,5},{2,6},{3,7},{4,0},{5,1},{6,2},{7,3},{8,12},{9,13},{10,... | collective-permute-start | bytes 86024 | tf_op jit(solution)/shard_map/ppermute | solution.py:198
  68.5 3.9 %collective-permute-start.26 = (bf16[16,896]{1,0:T(8,128)(2,1)S(1)}, bf16[16,896]{1,0:T(8,128)(2,1)S(1)}, u32[]{:S(2)}, u32[]{:S(2)}) collective-permute-start(bf16[16,896]{1,0:T(8,128)(2,1)S(1)} %sums.5.refs_0_), channel_id=1, source_target_pairs={{0,2},{1,3},{2,0},{3,1},{4,6},{5,7},{6,4},{7,5},{8,10},{9,11},{10,... | collective-permute-start | bytes 86024 | tf_op jit(solution)/shard_map/ppermute | solution.py:198
  70.0 2.4 %collective-permute-start.25 = (bf16[16,896]{1,0:T(8,128)(2,1)S(1)}, bf16[16,896]{1,0:T(8,128)(2,1)S(1)}, u32[]{:S(2)}, u32[]{:S(2)}) collective-permute-start(bf16[16,896]{1,0:T(8,128)(2,1)S(1)} %sums.5.refs_0_), channel_id=1, source_target_pairs={{0,1},{1,0},{2,3},{3,2},{4,5},{5,4},{6,7},{7,6},{8,9},{9,8},{10,11... | collective-permute-start | bytes 86024 | tf_op jit(solution)/shard_map/ppermute | solution.py:198
  71.3 1.2 %collective-permute-start.31 = (bf16[16,896]{1,0:T(8,128)(2,1)S(1)}, bf16[16,896]{1,0:T(8,128)(2,1)S(1)}, u32[]{:S(2)}, u32[]{:S(2)}) collective-permute-start(bf16[16,896]{1,0:T(8,128)(2,1)S(1)} %collective-permute-done.30.refs_6_), channel_id=1, source_target_pairs={{0,1},{1,0},{2,3},{3,2},{4,5},{5,4},{6,7},{7,6},{8,9},{9,8},{10,11... | collective-permute-start | bytes 86024 | tf_op jit(solution)/shard_map/ppermute | solution.py:198
  71.8 1.2 %collective-permute-start.29 = (bf16[16,896]{1,0:T(8,128)(2,1)S(1)}, bf16[16,896]{1,0:T(8,128)(2,1)S(1)}, u32[]{:S(2)}, u32[]{:S(2)}) collective-permute-start(bf16[16,896]{1,0:T(8,128)(2,1)S(1)} %collective-permute-done.28.refs_4_), channel_id=1, source_target_pairs={{0,1},{1,0},{2,3},{3,2},{4,5},{5,4},{6,7},{7,6},{8,9},{9,8},{10,11... | collective-permute-start | bytes 86024 | tf_op jit(solution)/shard_map/ppermute | solution.py:198
  72.4 1.2 %collective-permute-start.27 = (bf16[16,896]{1,0:T(8,128)(2,1)S(1)}, bf16[16,896]{1,0:T(8,128)(2,1)S(1)}, u32[]{:S(2)}, u32[]{:S(2)}) collective-permute-start(bf16[16,896]{1,0:T(8,128)(2,1)S(1)} %collective-permute-done.26.refs_2_), channel_id=1, source_target_pairs={{0,1},{1,0},{2,3},{3,2},{4,5},{5,4},{6,7},{7,6},{8,9},{9,8},{10,11... | collective-permute-start | bytes 86024 | tf_op jit(solution)/shard_map/ppermute | solution.py:198
  87.2 1.4 %collective-permute-start.32 = (bf16[4,4,16,224]{3,2,1,0:T(8,128)(2,1)S(1)}, bf16[4,4,16,224]{3,2,1,0:T(8,128)(2,1)S(1)}, u32[]{:S(2)}, u32[]{:S(2)}) collective-permute-start(bf16[4,4,16,224]{3,2,1,0:T(8,128)(2,1)S(1)} %get-tuple-element.77), channel_id=1, source_target_pairs={{0,1},{1,0},{2,3},{3,2},{4,5},{5,4},{6,7},{7,6},{8,9},{9,8},{10,11... | collective-permute-start | bytes 344072 | tf_op jit(solution)/shard_map/ppermute | solution.py:198
